TPU v7x, 32 devices: a whole 2x2x4 slice. The times are simulated.
32 devices in a mesh: rows: 2 (over x), query: 16 (over z, y, core).
Axes of the slice: x: 2, y: 2, z: 4, core: 2. Of those that a mesh axis runs over, the one named last changes fastest.
Arguments:
- acts: bfloat16 [640, 28672], P('query', 'rows'), may hold values from -6 to 6
- grads: bfloat16 [640, 8192], P('query', 'rows'), may hold values from -6 to 6
- in_factors: bfloat16 [28672, 8192], P('rows', 'query')
- out_factors: bfloat16 [8192, 8192], P('rows', 'query')
Outputs:
- scores: float32 [640, 256], P('rows', 'query')
All inputs are finite; a program needn't handle non-finite values.
Results may differ from a plain program's by a relative error of at most 0.0003.
Values may be sent and summed in bfloat16 or wider, within the bound.
No kernel may reach another device: no remote copies, remote signals or barrier semaphores. Data moves between devices by JAX's collectives and lax.ppermute only.
A program may use at most 128 MiB of HBM per device.

v0:
```python
import jax
import jax.numpy as jnp
from jax import lax
from jax.sharding import PartitionSpec as P

RANK = 32


def gram_of(factors, count_queries):
    blocks = factors.reshape(factors.shape[0], count_queries, RANK)
    return jnp.einsum("hqr,hqs->qrs", blocks, blocks, preferred_element_type=jnp.float32)


def local(acts, grads, in_factors, out_factors):
    columns = in_factors.shape[1]
    count_queries = columns // RANK
    first = jnp.dot(
        lax.all_gather(acts, "query", axis=0, tiled=True),
        in_factors,
        preferred_element_type=jnp.float32,
    )
    second = jnp.dot(
        lax.all_gather(grads, "query", axis=0, tiled=True),
        out_factors,
        preferred_element_type=jnp.float32,
    )
    proj_in = first
    proj_out = second
    gram_in = gram_of(in_factors, count_queries)
    gram_out = gram_of(out_factors, count_queries)
    gram_in, gram_out = lax.psum((gram_in, gram_out), "rows")
    qnorm = jnp.sum(gram_in * gram_out, axis=(1, 2))
    inverse = 1.0 / jnp.sqrt(qnorm + 1e-06)
    proj_in, proj_out = (
        lax.psum_scatter(proj_in, "rows", scatter_dimension=0, tiled=True),
        lax.psum_scatter(proj_out, "rows", scatter_dimension=0, tiled=True),
    )
    paired = (proj_in * proj_out).reshape(proj_in.shape[0], count_queries, RANK).sum(axis=2)
    return paired * inverse[None, :]


def solution(mesh):
    return jax.shard_map(
        local,
        mesh=mesh,
        in_specs=(P("query", "rows"), P("query", "rows"), P("rows", "query"), P("rows", "query")),
        out_specs=P("rows", "query"),
        check_vma=False,
    )
```

profile of v0, /device:TPU:0, one launch (start us, length us, event | category | flops | bytes accessed | tf_op | source)
XLA Modules:
  0.0 217.8 jit_solution(1444653148876001625)
XLA Ops:
  7.4 0.7 all-gather.5.cloned.1.call-update
  8.1 0.0 all-gather.3.cloned.1.call-start
  8.1 0.7 all-gather.3.cloned.1.call-update
  8.8 0.0 all-reduce.3.cloned.1.call-start
  8.9 6.4 %copy.11 = bf16[4096,512]{0,1:T(8,128)(2,1)} copy(bf16[4096,512]{1,0:T(8,128)(2,1)} %param.7) | data formatting | bytes 8388608 | tf_op args[3]
  15.3 18.8 %copy.10 = bf16[14336,512]{0,1:T(8,128)(2,1)} copy(bf16[14336,512]{1,0:T(8,128)(2,1)} %param.6) | data formatting | bytes 29360128 | tf_op args[2]
  34.2 5.4 %fusion.3 = f32[16,32,32]{2,1,0:T(8,128)} fusion(bf16[4096,16,32]{0,2,1:T(8,128)(2,1)} %bitcast.13), kind=kOutput, calls=%fused_computation.7 | convolution fusion | flops 134217728 | bytes 4259840 | tf_op jit(solution)/shard_map/hqr,hqs->qrs/dot_general | solution.py:11
  39.6 12.8 %fusion.2 = f32[16,32,32]{2,1,0:T(8,128)} fusion(bf16[14336,16,32]{0,2,1:T(8,128)(2,1)} %bitcast.12), kind=kOutput, calls=%fused_computation.6 | convolution fusion | flops 469762048 | bytes 14745600 | tf_op jit(solution)/shard_map/hqr,hqs->qrs/dot_general | solution.py:11
  52.4 0.0 all-reduce.3.cloned.1.call-update
  52.5 0.0 reduce-scatter.5.cloned.1.call-start
  52.5 16.9 %all-gather.5.cloned.1.call-done = bf16[640,4096]{1,0:T(8,128)(2,1)} async-done(((bf16[40,4096]{1,0:T(8,128)(2,1)}), bf16[640,4096]{1,0:T(8,128)(2,1)}) %all-gather.5.cloned.1.call-update) | async-done | bytes 5242896 | tf_op jit(solution)/shard_map/all_gather | solution.py:23
  69.4 7.7 %fusion.1 = f32[640,512]{1,0:T(8,128)} fusion(bf16[640,4096]{1,0:T(8,128)(2,1)} %all-gather.5.cloned.1.call-done, bf16[4096,512]{1,0:T(8,128)(2,1)} %param.7), kind=kOutput, calls=%fused_computation.5 | convolution fusion | flops 2684354560 | bytes 10747904 | tf_op jit(solution)/shard_map/dot_general | solution.py:22
  77.1 0.0 reduce-scatter.5.cloned.1.call-update
  77.2 0.0 reduce-scatter.3.cloned.1.call-start
  77.2 88.9 %all-gather.3.cloned.1.call-done = bf16[640,14336]{1,0:T(8,128)(2,1)} async-done(((bf16[40,14336]{1,0:T(8,128)(2,1)}), bf16[640,14336]{1,0:T(8,128)(2,1)}) %all-gather.3.cloned.1.call-update) | async-done | bytes 18350096 | tf_op jit(solution)/shard_map/all_gather | solution.py:18
  166.1 18.4 %fusion = f32[640,512]{1,0:T(8,128)} fusion(bf16[640,14336]{1,0:T(8,128)(2,1)} %all-gather.3.cloned.1.call-done, bf16[14336,512]{1,0:T(8,128)(2,1)} %param.6), kind=kOutput, calls=%fused_computation.4 | convolution fusion | flops 9395240960 | bytes 34340864 | tf_op jit(solution)/shard_map/dot_general | solution.py:17
  184.5 0.0 reduce-scatter.3.cloned.1.call-update
  184.6 0.0 all-reduce.3.cloned.1.call-done
  184.6 1.2 multiply_reduce_fusion
  185.9 21.9 %reduce-scatter.3.cloned.1.call-done = f32[320,512]{1,0:T(8,128)} async-done(((f32[640,512]{1,0:T(8,128)}), f32[320,512]{1,0:T(8,128)}) %reduce-scatter.3.cloned.1.call-update) | async-done | bytes 655376 | tf_op jit(solution)/shard_map/reduce_scatter | solution.py:35
  207.7 1.4 mul.14
  209.1 0.3 copy.9
  209.4 0.1 bitcast_reduce_fusion
  209.5 0.7 broadcast_multiply_fusion
  (3 shorter events, 0.0 us)
Async XLA Ops:
  7.4 62.1 %all-gather.5.cloned.1.call-start = ((), (), s32[]{:S(2)}) async-start(), calls=%async_computation.4 | async-start | bytes 5570560 | tf_op jit(solution)/shard_map/all_gather | solution.py:23
  8.1 158.0 %all-gather.3.cloned.1.call-start = ((), (), s32[]{:S(2)}) async-start(), calls=%async_computation.2 | async-start | bytes 19496960 | tf_op jit(solution)/shard_map/all_gather | solution.py:18
  8.8 175.7 %all-reduce.3.cloned.1.call-start = ((), (), s32[]{:S(2)}) async-start(), calls=%async_computation.6 | async-start | bytes 1048576 | tf_op jit(solution)/shard_map/psum | solution.py:31
  52.5 133.4 %reduce-scatter.5.cloned.1.call-start = ((), (), s32[]{:S(2)}) async-start(), calls=%async_computation.5 | async-start | bytes 1966080 | tf_op jit(solution)/shard_map/reduce_scatter | solution.py:36
  77.2 130.6 %reduce-scatter.3.cloned.1.call-start = ((), (), s32[]{:S(2)}) async-start(), calls=%async_computation.3 | async-start | bytes 1966080 | tf_op jit(solution)/shard_map/reduce_scatter | solution.py:35
Sparse Core Ops, SparseCore 0:
  10.7 58.6 all-gather.4
  71.0 95.0 all-gather.2
Sparse Core Ops, SparseCore 1:
  52.5 31.1 all-reduce.2
  85.9 23.1 reduce-scatter.4
  184.6 23.1 reduce-scatter.2
where the time goes:
time: 219 us; the launch traced here: 218 us
  waiting for transfers between devices  129 us (59%)
  matrix products  44.3 us (20%)
  local copies, waits for them, and re-layouts  25.5 us (12%)
  between operations  15.1 us (7%)
  other arithmetic  3.41 us (2%)
    all_gather x1, waiting for transfers between devices, local(): lax.all_gather(acts, 'query', axis=0, tiled=True)  88.9 us
    unnamed x2, local copies, waits for them, and re-layouts  25.3 us
    reduce_scatter x1, waiting for transfers between devices, local(): lax.psum_scatter(proj_in, 'rows', scatter_dimension=0, tiled=True)  21.9 us
    dot_general x1, matrix products, local(): jnp.dot(lax.all_gather(acts, 'query', axis=0, tiled=True), in_factors, pr...  18.4 us
    dot_general x2, matrix products, gram_of(): jnp.einsum('hqr,hqs->qrs', blocks, blocks, preferred_element_type=jnp.flo...  18.3 us
    all_gather x1, waiting for transfers between devices, local(): lax.all_gather(grads, 'query', axis=0, tiled=True)  16.9 us
    dot_general x1, matrix products, local(): jnp.dot(lax.all_gather(grads, 'query', axis=0, tiled=True), out_factors,...  7.69 us
  transfers between devices with their start and end apart: 5, of which 3 were waited for; matrix products, arithmetic and copies ran while one was open for 33% of the time, Pallas kernels for 0%

commit v1 on v0

v1 whole, which is shorter than its diff:
```python
import functools
import math

import jax
import jax.numpy as jnp
from jax import lax
from jax.experimental import pallas as pl
from jax.experimental.pallas import tpu as pltpu
from jax.sharding import PartitionSpec as P

RANK = 32
WIDE = 256
LIGHT = pl.CostEstimate(flops=1, bytes_accessed=1, transcendentals=0)
ROOM = 24 << 20


def params():
    return pltpu.CompilerParams(vmem_limit_bytes=ROOM)


def cycle_of(first, second):
    if min(first, second) == 1:
        size = first * second
        order = list(range(0, size, 2)) + list(range(1, size, 2))[::-1]
        return [(i, 0) if second == 1 else (0, i) for i in order]
    if first % 2:
        return [(a, b) for b, a in cycle_of(second, first)] if second % 2 == 0 else [
            (a, b) for a in range(first) for b in range(second)]
    walk = []
    for a in range(first):
        inner = range(1, second)
        walk += [(a, b) for b in (inner if a % 2 == 0 else reversed(inner))]
    return walk + [(a, 0) for a in reversed(range(first))]


def ring_of(mesh):
    devices = list(mesh.devices[0])
    chips = {}
    for index, device in enumerate(devices):
        coords = getattr(device, "coords", None)
        key = tuple(coords) if coords is not None else (index // 2,)
        chips.setdefault(key, []).append(index)
    keys = list(chips)
    values = [sorted({k[i] for k in keys}) for i in range(len(keys[0]))]
    varying = [i for i in range(len(values)) if len(values[i]) > 1]
    if len(varying) == 2 and len(keys) == len(values[varying[0]]) * len(values[varying[1]]):
        one, two = sorted(varying, key=lambda i: -len(values[i]))
        at = {(values[one].index(k[one]), values[two].index(k[two])): k for k in keys}
        keys = [at[place] for place in cycle_of(len(values[one]), len(values[two]))]
    ring = [chips[k] for k in keys]
    assert all(pair[0] % 2 == 0 and pair[1] == pair[0] + 1 for pair in ring)
    return ring


def load_kernel(a_ref, b_ref, a_out, b_out, sem):
    first = pltpu.make_async_copy(a_ref, a_out, sem.at[0])
    second = pltpu.make_async_copy(b_ref, b_out, sem.at[1])
    first.start()
    second.start()
    first.wait()
    second.wait()


def load(a, b):
    return pl.pallas_call(
        load_kernel,
        in_specs=[pl.BlockSpec(memory_space=pl.ANY)] * 2,
        out_specs=[pl.BlockSpec(memory_space=pltpu.VMEM)] * 2,
        out_shape=[pltpu.VMEM(a.shape, a.dtype), pltpu.VMEM(b.shape, b.dtype)],
        scratch_shapes=[pltpu.SemaphoreType.DMA((2,))],
        compiler_params=params(),
        cost_estimate=LIGHT,
        name="load_factors",
    )(a, b)


def gram_kernel(step, a_ref, b_ref, out_ref, sums):
    columns = a_ref.shape[1]
    row = lax.broadcasted_iota(jnp.int32, (WIDE, WIDE), 0) // RANK
    col = lax.broadcasted_iota(jnp.int32, (WIDE, WIDE), 1) // RANK
    for index, ref in enumerate((a_ref, b_ref)):
        sums[...] = jnp.zeros_like(sums)

        @pl.loop(0, ref.shape[0] // step)
        def _(i, ref=ref):
            for start in range(0, columns, WIDE):
                block = ref[pl.ds(pl.multiple_of(i * step, step), step), start : start + WIDE]
                sums[:, start : start + WIDE] += lax.dot_general(
                    block, block, (((0,), (0,)), ((), ())), preferred_element_type=jnp.float32)

        for start in range(0, columns, WIDE):
            kept = jnp.where(row == col, sums[:, start : start + WIDE], 0.0)
            out_ref[index, :, start : start + WIDE] = kept.reshape(WIDE // RANK, RANK, WIDE).sum(axis=0)


def grams(a, b):
    columns = a.shape[1]
    step = math.gcd(a.shape[0], b.shape[0])
    return pl.pallas_call(
        functools.partial(gram_kernel, step),
        in_specs=[pl.BlockSpec(memory_space=pltpu.VMEM)] * 2,
        out_specs=pl.BlockSpec(memory_space=pltpu.VMEM),
        out_shape=jax.ShapeDtypeStruct((2, RANK, columns), jnp.float32),
        scratch_shapes=[pltpu.VMEM((WIDE, columns), jnp.float32)],
        compiler_params=params(),
        cost_estimate=LIGHT,
        name="grams",
    )(a, b)


def project_kernel(step, spans, *refs):
    count = sum(len(span[0]) for span in spans)
    tokens, factors, out_ref = refs[:count], refs[count : count + 2], refs[-1]
    i = pl.program_id(0)

    @pl.when(i == 0)
    def _():
        out_ref[...] = jnp.zeros_like(out_ref)

    first = 0
    taken = 0
    for widths, which, offset, steps in spans:
        held = tokens[taken : taken + len(widths)]

        @pl.when((i >= first) & (i < first + steps))
        def _(held=held, which=which, offset=offset, first=first):
            x = jnp.concatenate([h[...] for h in held], axis=0)
            at = pl.multiple_of((i - first) * step + offset, step)
            out_ref[which] += jnp.dot(x, factors[which][pl.ds(at, step), :], preferred_element_type=jnp.float32)

        first += steps
        taken += len(widths)


def project(groups, factors):
    sizes = [arrays[0].shape[1] for arrays, _, _ in groups] + [offset for _, _, offset in groups if offset]
    step = min(functools.reduce(math.gcd, sizes), 2048)
    spans, specs, operands, first = [], [], [], 0
    for arrays, which, offset in groups:
        steps = arrays[0].shape[1] // step
        spans.append((tuple(a.shape[0] for a in arrays), which, offset, steps))
        for a in arrays:
            specs.append(pl.BlockSpec(
                (a.shape[0], step), lambda i, first=first, steps=steps: (0, jnp.clip(i - first, 0, steps - 1))))
            operands.append(a)
        first += steps
    rows = sum(spans[0][0])
    columns = factors[0].shape[1]
    return pl.pallas_call(
        functools.partial(project_kernel, step, tuple(spans)),
        grid=(first,),
        in_specs=specs + [pl.BlockSpec(memory_space=pltpu.VMEM)] * 2,
        out_specs=pl.BlockSpec((2, rows, columns), lambda i: (0, 0, 0)),
        out_shape=jax.ShapeDtypeStruct((2, rows, columns), jnp.float32),
        compiler_params=params(),
        cost_estimate=LIGHT,
        name="project",
    )(*operands, *[pltpu.with_memory_space_constraint(f, pltpu.VMEM) for f in factors])


def scores_of(projected, gram, columns):
    queries = columns // RANK
    member = (lax.broadcasted_iota(jnp.int32, (columns, queries), 0) // RANK) == lax.broadcasted_iota(
        jnp.int32, (columns, queries), 1)
    member = member.astype(jnp.float32)

    def by_query(x):
        return jnp.dot(x, member, precision=lax.Precision.HIGHEST, preferred_element_type=jnp.float32)

    norms = jnp.broadcast_to((gram[0] * gram[1]).sum(axis=0, keepdims=True), (8, columns))
    inverse = 1.0 / jnp.sqrt(by_query(norms)[:1] + 1e-06)
    return by_query(projected[0] * projected[1]) * inverse


def total_of(refs):
    return sum(ref[...] for ref in refs[1:]) + refs[0][...]


def score_kernel(count, *refs):
    parts, grams_, out_ref = refs[:count], refs[count : 2 * count], refs[-1]
    out_ref[...] = scores_of(total_of(parts), total_of(grams_), out_ref.shape[1] * RANK)


def score(parts, gram_parts):
    rows, columns = parts[0].shape[1:]
    return pl.pallas_call(
        functools.partial(score_kernel, len(parts)),
        out_shape=jax.ShapeDtypeStruct((rows, columns // RANK), jnp.float32),
        compiler_params=params(),
        cost_estimate=LIGHT,
        name="score",
    )(*parts, *gram_parts)


def looked_up(table, index):
    return sum(jnp.where(index == i, value, 0) for i, value in enumerate(table))


def last_kernel(count, distances, place, tokens, at_ref, *refs):
    parts, grams_ = refs[:count], refs[count : 2 * count]
    earlier, out_ref, held = refs[2 * count : -2], refs[-2], refs[-1]
    columns = parts[0].shape[2]
    chips = len(place)
    known = [*(ref[...] for ref in earlier)]
    if parts:
        known.append(scores_of(total_of(parts), total_of(grams_), columns))
    for group, result in zip(distances, known):
        for c in range(2):
            for j, distance in enumerate(group):
                begin = (c * len(group) + j) * tokens
                held[distance % chips, c] = result[begin : begin + tokens]
    core, side = at_ref[0], at_ref[1]
    here = looked_up(place, core // 2)
    own = core % 2
    share = out_ref.shape[0] // (2 * tokens)
    for j in range(share):
        there = looked_up(place, side * share + j)
        distance = there - here
        distance = jnp.where(distance < 0, distance + chips, distance)
        for c in range(2):
            out_ref[(2 * j + c) * tokens : (2 * j + c + 1) * tokens, :] = held[distance, (own + c) % 2]


def last(parts, gram_parts, earlier, distances, place, tokens, share, at):
    queries = earlier[0].shape[1]
    return pl.pallas_call(
        functools.partial(last_kernel, len(parts), distances, place, tokens),
        in_specs=[pl.BlockSpec(memory_space=pltpu.SMEM)]
        + [pl.BlockSpec(memory_space=pltpu.VMEM)] * (len(parts) + len(gram_parts) + len(earlier)),
        out_specs=pl.BlockSpec(memory_space=pltpu.VMEM),
        out_shape=jax.ShapeDtypeStruct((share, queries), jnp.float32),
        scratch_shapes=[pltpu.VMEM((len(place), 2, tokens, queries), jnp.float32)],
        compiler_params=params(),
        cost_estimate=LIGHT,
        name="last_scores",
    )(at, *parts, *gram_parts, *earlier)


def solution(mesh):
    rows = mesh.shape["rows"]
    query = mesh.shape["query"]
    ring = ring_of(mesh)
    chips = len(ring)
    forward = [(a, b) for i in range(chips) for a, b in zip(ring[i], ring[(i + 1) % chips])]
    backward = [(b, a) for a, b in forward]
    mates = [(pair[i], pair[1 - i]) for pair in ring for i in range(2)]
    place = [0] * chips
    for i, pair in enumerate(ring):
        place[pair[0] // 2] = i
    place = tuple(place)

    def across(x):
        if rows == 2:
            return [x, lax.ppermute(x, "rows", [(0, 1), (1, 0)])]
        return [lax.psum(x, "rows")]

    def mate(x):
        return lax.ppermute(x, "query", mates)

    def ahead(x):
        return lax.ppermute(x, "query", forward)

    def behind(x):
        return lax.ppermute(x, "query", backward)

    def tied(*trees):
        return lax.optimization_barrier(trees)

    def local(acts, grads, in_factors, out_factors):
        tokens, width = acts.shape
        cut = (width + grads.shape[1]) // 2 // 128 * 128
        at = jnp.stack([lax.axis_index("query"), lax.axis_index("rows")]).astype(jnp.int32)
        full_hops = (chips - 1) // 2

        flying = ahead(acts), behind(acts), ahead(grads), behind(grads)
        a, g = mate(acts), mate(grads)
        factors = load(in_factors, out_factors)
        gram = grams(*factors)
        projected = project([([acts, a], 0, 0), ([grads, g], 1, 0)], factors)
        flying, projected, gram = tied(flying, projected, gram)
        gram_parts = across(gram)
        groups = [(0,)]
        done = []
        waiting = []
        for hop in range(1, full_hops + 1):
            a_f, a_b, g_f, g_b = flying
            if hop < full_hops:
                flying = ahead(a_f), behind(a_b), ahead(g_f), behind(g_b)
            elif chips % 2 == 0:
                flying = ahead(a_f[:, :cut]), behind(a_b[:, cut:]), behind(g_b)
            swapped = [mate(x) for x in (a_f, a_b, g_f, g_b)]
            parts = across(projected)
            if waiting:
                done.append(score(waiting, gram_parts))
            projected = project(
                [([a_f, a_b, swapped[0], swapped[1]], 0, 0), ([g_f, g_b, swapped[2], swapped[3]], 1, 0)], factors)
            groups.append((-hop, hop))
            flying, projected, waiting, gram_parts, done = tied(flying, projected, parts, gram_parts, done)
        parts = across(projected)
        done.append(score(waiting, gram_parts))
        tail = []
        if chips % 2 == 0:
            a_f, a_b, g_b = flying
            swapped = [mate(x) for x in flying]
            projected = project(
                [([g_b, swapped[2]], 1, 0), ([a_f, swapped[0]], 0, 0), ([a_b, swapped[1]], 0, cut)], factors)
            tail = across(projected)
            groups.append((chips // 2,))
        done.append(score(parts, gram_parts))
        return last(tail, gram_parts if tail else [], done, groups, place, tokens, query * tokens // rows, at)

    return jax.shard_map(
        local,
        mesh=mesh,
        in_specs=(P("query", "rows"), P("query", "rows"), P("rows", "query"), P("rows", "query")),
        out_specs=P("rows", "query"),
        check_vma=False,
    )
```

time: 219 us -> 162 us (0.74)
  Pallas kernels: 0 us -> 46.3 us
  waiting for transfers between devices: 129 us -> 83.3 us
  matrix products: 44.3 us -> 0 us
  starting transfers between devices: 0.17 us -> 28 us
  local copies, waits for them, and re-layouts: 25.5 us -> 4.08 us
  between operations: 15.1 us -> 0.23 us
  other arithmetic: 3.41 us -> 0.07 us
    all_gather x2 -> x0, waiting for transfers between devices: 106 us -> none  [the longest x1 88.9 us: local(): lax.all_gather(acts, 'query', axis=0, tiled=True)]
    ppermute x0 -> x38, waiting for transfers between devices: none -> 83.3 us  [the longest x7 43.8 us: ahead(): return lax.ppermute(x, 'query', forward)]
    pallas_call x0 -> x12, Pallas kernels: none -> 46.3 us  [the longest x5 29.5 us: project(): pl.pallas_call(functools.partial(project_kernel, step, tuple(spans)), gri...]
    dot_general x4 -> x0, matrix products: 44.3 us -> none  [the longest x1 18.4 us: local(): jnp.dot(lax.all_gather(acts, 'query', axis=0, tiled=True), in_factors, pr...]
    ppermute x0 -> x38, starting transfers between devices: none -> 28 us  [the longest x7 12.2 us: ahead(): return lax.ppermute(x, 'query', forward)]
    unnamed x2 -> x10, local copies, waits for them, and re-layouts: 25.3 us -> 3.29 us
    reduce_scatter x2 -> x0, waiting for transfers between devices: 21.9 us -> none  [the longest x1 21.9 us: local(): lax.psum_scatter(proj_in, 'rows', scatter_dimension=0, tiled=True)]
  transfers between devices with their start and end apart: 5 -> 38, of which waited for: 3 -> 16; matrix products, arithmetic and copies ran while one was open for 33% -> 0% of each run, Pallas kernels for 0% -> 28%
where the time goes in v1:
time: 162 us
  waiting for transfers between devices  83.3 us (51%)
  Pallas kernels  46.3 us (29%)
  starting transfers between devices  28 us (17%)
  local copies, waits for them, and re-layouts  4.08 us (3%)
    ppermute x7, waiting for transfers between devices, ahead(): return lax.ppermute(x, 'query', forward)  43.8 us
    pallas_call x5, Pallas kernels, project(): pl.pallas_call(functools.partial(project_kernel, step, tuple(spans)), gri...  29.5 us
    ppermute x8, waiting for transfers between devices, behind(): return lax.ppermute(x, 'query', backward)  15.1 us
    ppermute x6, waiting for transfers between devices, across(): return [x, lax.ppermute(x, 'rows', [(0, 1), (1, 0)])]  13.3 us
    ppermute x7, starting transfers between devices, ahead(): return lax.ppermute(x, 'query', forward)  12.2 us
    ppermute x17, waiting for transfers between devices, mate(): return lax.ppermute(x, 'query', mates)  11.2 us
    ppermute x6, starting transfers between devices, across(): return [x, lax.ppermute(x, 'rows', [(0, 1), (1, 0)])]  7.27 us
    pallas_call x1, Pallas kernels, grams(): pl.pallas_call(functools.partial(gram_kernel, step), in_specs=[pl.BlockSp...  6.97 us
  transfers between devices with their start and end apart: 38, of which 16 were waited for; matrix products, arithmetic and copies ran while one was open for 0% of the time, Pallas kernels for 28%

profile of v1, /device:TPU:0, one launch (start us, length us, event | category | flops | bytes accessed | tf_op | source)
XLA Modules:
  0.0 162.0 jit_solution(4878047212767095383)
XLA Ops:
  0.5 2.5 %collective-permute-start = (bf16[40,14336]{1,0:T(8,128)(2,1)}, bf16[40,14336]{1,0:T(8,128)(2,1)S(1)}, u32[]{:S(2)}, u32[]{:S(2)}) collective-permute-start(bf16[40,14336]{1,0:T(8,128)(2,1)} %refs_0_.1), channel_id=1, source_target_pairs={{2,6},{3,7},{6,10},{7,11},{10,14},{11,15},{14,12},{15,13},{12,8},{... | collective-permute-start | bytes 3440648 | tf_op jit(solution)/shard_map/ppermute | solution.py:261
  3.3 1.7 %collective-permute-start.2 = (bf16[40,4096]{1,0:T(8,128)(2,1)}, bf16[40,4096]{1,0:T(8,128)(2,1)S(1)}, u32[]{:S(2)}, u32[]{:S(2)}) collective-permute-start(bf16[40,4096]{1,0:T(8,128)(2,1)} %refs_2_.1), channel_id=1, source_target_pairs={{2,6},{3,7},{6,10},{7,11},{10,14},{11,15},{14,12},{15,13},{12,8},{... | collective-permute-start | bytes 983048 | tf_op jit(solution)/shard_map/ppermute | solution.py:261
  5.0 1.9 %collective-permute-start.3 = (bf16[40,4096]{1,0:T(8,128)(2,1)}, bf16[40,4096]{1,0:T(8,128)(2,1)S(1)}, u32[]{:S(2)}, u32[]{:S(2)}) collective-permute-start(bf16[40,4096]{1,0:T(8,128)(2,1)} %refs_2_.1), channel_id=1, source_target_pairs={{6,2},{7,3},{10,6},{11,7},{14,10},{15,11},{12,14},{13,15},{8,12},{... | collective-permute-start | bytes 983048 | tf_op jit(solution)/shard_map/ppermute | solution.py:264
  6.9 2.2 %copy-done = bf16[4096,512]{1,0:T(8,128)(2,1)S(1)} copy-done((bf16[4096,512]{1,0:T(8,128)(2,1)S(1)}, bf16[4096,512]{1,0:T(8,128)(2,1)}, u32[]{:S(2)}) %copy-start) | copy-done | bytes 4194328
  9.1 5.2 %load_factors.1 = (bf16[14336,512]{1,0:T(8,128)(2,1)S(1)}, bf16[4096,512]{1,0:T(8,128)(2,1)S(1)}) custom-call(bf16[14336,512]{1,0:T(8,128)(2,1)} %a_ref.1, bf16[4096,512]{1,0:T(8,128)(2,1)S(1)} %copy-done), custom_call_target="tpu_custom_call" | custom-call | flops 1 | bytes 1 | tf_op jit(solution)/shard_map/load_factors/pallas_call | solution.py:65
  14.3 7.0 %grams.1.refs_2_ = f32[2,32,512]{2,1,0:T(8,128)S(1)} custom-call(bf16[14336,512]{1,0:T(8,128)(2,1)S(1)} %get-tuple-element.42.refs_4_.a_ref.refs_8_.refs_6_, bf16[4096,512]{1,0:T(8,128)(2,1)S(1)} %get-tuple-element.43.refs_5_.b_ref.refs_9_.refs_7_), custom_call_target="tpu_custom_call" | custom-call | flops 1 | bytes 1 | tf_op jit(solution)/shard_map/grams/pallas_call | solution.py:99
  21.3 5.0 %project.5.refs_0_ = f32[2,80,512]{2,1,0:T(8,128)S(1)} custom-call(bf16[40,14336]{1,0:T(8,128)(2,1)S(1)} %copy-done.1, bf16[40,14336]{1,0:T(8,128)(2,1)S(1)} %collective-permute-done.4.refs_1_, bf16[40,4096]{1,0:T(8,128)(2,1)S(1)} %copy-done.4, bf16[40,4096]{1,0:T(8,128)(2,1)S(1)} %collective-permute-done.5.refs_3_, ...), custom_call_target="tpu_custom_call" | custom-call | flops 1 | bytes 1 | tf_op jit(solution)/shard_map/project/pallas_call | solution.py:149
  26.3 9.9 %collective-permute-done.2.refs_4_ = bf16[40,4096]{1,0:T(8,128)(2,1)S(1)} collective-permute-done((bf16[40,4096]{1,0:T(8,128)(2,1)}, bf16[40,4096]{1,0:T(8,128)(2,1)S(1)}, u32[]{:S(2)}, u32[]{:S(2)}) %collective-permute-start.2) | collective-permute-done | bytes 327712 | tf_op jit(solution)/shard_map/ppermute | solution.py:261
  41.6 3.5 %collective-permute-done.15.refs_3_ = f32[2,32,512]{2,1,0:T(8,128)S(1)} collective-permute-done((f32[2,32,512]{2,1,0:T(8,128)S(1)}, f32[2,32,512]{2,1,0:T(8,128)S(1)}, u32[]{:S(2)}, u32[]{:S(2)}) %collective-permute-start.15) | collective-permute-done | bytes 131104 | tf_op jit(solution)/shard_map/ppermute | solution.py:254
  45.1 1.6 %collective-permute-done.12.refs_6_ = bf16[40,4096]{1,0:T(8,128)(2,1)S(1)} collective-permute-done((bf16[40,4096]{1,0:T(8,128)(2,1)S(1)}, bf16[40,4096]{1,0:T(8,128)(2,1)S(1)}, u32[]{:S(2)}, u32[]{:S(2)}) %collective-permute-start.12) | collective-permute-done | bytes 327712 | tf_op jit(solution)/shard_map/ppermute | solution.py:258
  51.9 5.6 %project.6.refs_0_ = f32[2,160,512]{2,1,0:T(8,128)S(1)} custom-call(bf16[40,14336]{1,0:T(8,128)(2,1)S(1)} %collective-permute-done.refs_0_, bf16[40,14336]{1,0:T(8,128)(2,1)S(1)} %collective-permute-done.1.refs_1_, bf16[40,14336]{1,0:T(8,128)(2,1)S(1)} %collective-permute-done.10.refs_2_, bf16[40,14336]{1,0:T(8,128)(2,1)S(1)} %collective-permute-done.11.refs_3_, ...), custom_call_target="tpu_custom_call" | custom-call | flops 1 | bytes 1 | tf_op jit(solution)/shard_map/project/pallas_call | solution.py:149
  57.6 14.8 %collective-permute-done.8.refs_4_ = bf16[40,4096]{1,0:T(8,128)(2,1)S(1)} collective-permute-done((bf16[40,4096]{1,0:T(8,128)(2,1)S(1)}, bf16[40,4096]{1,0:T(8,128)(2,1)S(1)}, u32[]{:S(2)}, u32[]{:S(2)}) %collective-permute-start.8) | collective-permute-done | bytes 327712 | tf_op jit(solution)/shard_map/ppermute | solution.py:261
  76.4 2.3 %collective-permute-done.22.refs_6_ = bf16[40,4096]{1,0:T(8,128)(2,1)S(1)} collective-permute-done((bf16[40,4096]{1,0:T(8,128)(2,1)S(1)}, bf16[40,4096]{1,0:T(8,128)(2,1)S(1)}, u32[]{:S(2)}, u32[]{:S(2)}) %collective-permute-start.22) | collective-permute-done | bytes 327712 | tf_op jit(solution)/shard_map/ppermute | solution.py:258
  84.3 5.7 %project.7.refs_0_ = f32[2,160,512]{2,1,0:T(8,128)S(1)} custom-call(bf16[40,14336]{1,0:T(8,128)(2,1)S(1)} %collective-permute-done.6.refs_0_, bf16[40,14336]{1,0:T(8,128)(2,1)S(1)} %collective-permute-done.7.refs_1_, bf16[40,14336]{1,0:T(8,128)(2,1)S(1)} %collective-permute-done.20.refs_2_, bf16[40,14336]{1,0:T(8,128)(2,1)S(1)} %collective-permute-done.21.refs_3_, ...), custom_call_target="tpu_custom_call" | custom-call | flops 1 | bytes 1 | tf_op jit(solution)/shard_map/project/pallas_call | solution.py:149
  90.0 19.0 %collective-permute-done.18.refs_4_ = bf16[40,4096]{1,0:T(8,128)(2,1)S(1)} collective-permute-done((bf16[40,4096]{1,0:T(8,128)(2,1)S(1)}, bf16[40,4096]{1,0:T(8,128)(2,1)S(1)}, u32[]{:S(2)}, u32[]{:S(2)}) %collective-permute-start.18) | collective-permute-done | bytes 327712 | tf_op jit(solution)/shard_map/ppermute | solution.py:261
  111.4 1.6 %collective-permute-start.25 = (bf16[40,9216]{1,0:T(8,128)(2,1)S(1)}, bf16[40,9216]{1,0:T(8,128)(2,1)S(1)}, u32[]{:S(2)}, u32[]{:S(2)}) collective-permute-start(bf16[40,9216]{1,0:T(8,128)(2,1)S(1)} %slice.6), channel_id=1, source_target_pairs={{2,6},{3,7},{6,10},{7,11},{10,14},{11,15},{14,12},{15,13},{12,8},{... | collective-permute-start | bytes 2211848 | tf_op jit(solution)/shard_map/ppermute | solution.py:261
  113.1 2.2 %collective-permute-done.30.refs_6_ = bf16[40,4096]{1,0:T(8,128)(2,1)S(1)} collective-permute-done((bf16[40,4096]{1,0:T(8,128)(2,1)S(1)}, bf16[40,4096]{1,0:T(8,128)(2,1)S(1)}, u32[]{:S(2)}, u32[]{:S(2)}) %collective-permute-start.30) | collective-permute-done | bytes 327712 | tf_op jit(solution)/shard_map/ppermute | solution.py:258
  118.4 5.7 %project.8.refs_0_ = f32[2,160,512]{2,1,0:T(8,128)S(1)} custom-call(bf16[40,14336]{1,0:T(8,128)(2,1)S(1)} %collective-permute-done.16.refs_0_, bf16[40,14336]{1,0:T(8,128)(2,1)S(1)} %collective-permute-done.17.refs_1_, bf16[40,14336]{1,0:T(8,128)(2,1)S(1)} %collective-permute-done.28.refs_2_, bf16[40,14336]{1,0:T(8,128)(2,1)S(1)} %collective-permute-done.29.refs_3_, ...), custom_call_target="tpu_custom_call" | custom-call | flops 1 | bytes 1 | tf_op jit(solution)/shard_map/project/pallas_call | solution.py:149
  124.0 11.1 %collective-permute-done.27.refs_0_ = bf16[40,4096]{1,0:T(8,128)(2,1)S(1)} collective-permute-done((bf16[40,4096]{1,0:T(8,128)(2,1)S(1)}, bf16[40,4096]{1,0:T(8,128)(2,1)S(1)}, u32[]{:S(2)}, u32[]{:S(2)}) %collective-permute-start.27) | collective-permute-done | bytes 327712 | tf_op jit(solution)/shard_map/ppermute | solution.py:264
  136.4 2.0 %collective-permute-done.33.refs_1_ = bf16[40,4096]{1,0:T(8,128)(2,1)S(1)} collective-permute-done((bf16[40,4096]{1,0:T(8,128)(2,1)S(1)}, bf16[40,4096]{1,0:T(8,128)(2,1)S(1)}, u32[]{:S(2)}, u32[]{:S(2)}) %collective-permute-start.33) | collective-permute-done | bytes 327712 | tf_op jit(solution)/shard_map/ppermute | solution.py:258
  138.5 7.6 %project.9.refs_0_ = f32[2,80,512]{2,1,0:T(8,128)} custom-call(bf16[40,4096]{1,0:T(8,128)(2,1)S(1)} %collective-permute-done.27.refs_0_, bf16[40,4096]{1,0:T(8,128)(2,1)S(1)} %collective-permute-done.33.refs_1_, bf16[40,9216]{1,0:T(8,128)(2,1)S(1)} %collective-permute-done.25.refs_2_, bf16[40,9216]{1,0:T(8,128)(2,1)S(1)} %collective-permute-done.34.refs_3_, ...), custom_call_target="tpu_custom_call" | custom-call | flops 1 | bytes 1 | tf_op jit(solution)/shard_map/project/pallas_call | solution.py:149
  148.4 5.0 %collective-permute-done.37.refs_1_ = f32[2,160,512]{2,1,0:T(8,128)} collective-permute-done((f32[2,160,512]{2,1,0:T(8,128)S(1)}, f32[2,160,512]{2,1,0:T(8,128)}, u32[]{:S(2)}, u32[]{:S(2)}) %collective-permute-start.37) | collective-permute-done | bytes 655392 | tf_op jit(solution)/shard_map/ppermute | solution.py:254
  153.4 1.7 %score.7.refs_7_ = f32[160,16]{1,0:T(8,128)S(1)} custom-call(f32[2,160,512]{2,1,0:T(8,128)S(1)} %project.8.refs_0_, f32[2,160,512]{2,1,0:T(8,128)} %collective-permute-done.37.refs_1_, f32[2,32,512]{2,1,0:T(8,128)S(1)} %grams.1.refs_2_, f32[2,32,512]{2,1,0:T(8,128)S(1)} %collective-permute-done.15.refs_3_), custom_call_target="tpu_custom_call" | custom-call | flops 1 | bytes 1 | tf_op jit(solution)/shard_map/score/pallas_call | solution.py:186
  155.1 4.8 %collective-permute-done.36.refs_1_ = f32[2,80,512]{2,1,0:T(8,128)S(1)} collective-permute-done((f32[2,80,512]{2,1,0:T(8,128)}, f32[2,80,512]{2,1,0:T(8,128)S(1)}, u32[]{:S(2)}, u32[]{:S(2)}) %collective-permute-start.36) | collective-permute-done | bytes 327712 | tf_op jit(solution)/shard_map/ppermute | solution.py:254
  (78 shorter events, 32.2 us)
Async XLA Ops:
  0.0 21.3 %collective-permute-start.4 = (bf16[40,14336]{1,0:T(8,128)(2,1)}, bf16[40,14336]{1,0:T(8,128)(2,1)S(1)}, u32[]{:S(2)}, u32[]{:S(2)}) collective-permute-start(bf16[40,14336]{1,0:T(8,128)(2,1)} %refs_0_.1), channel_id=1, source_target_pairs={{2,3},{3,2},{6,7},{7,6},{10,11},{11,10},{14,15},{15,14},{12,13},{1... | collective-permute-start | bytes 3440648 | tf_op jit(solution)/shard_map/ppermute | solution.py:258
  0.5 37.2 %collective-permute-start = (bf16[40,14336]{1,0:T(8,128)(2,1)}, bf16[40,14336]{1,0:T(8,128)(2,1)S(1)}, u32[]{:S(2)}, u32[]{:S(2)}) collective-permute-start(bf16[40,14336]{1,0:T(8,128)(2,1)} %refs_0_.1), channel_id=1, source_target_pairs={{2,6},{3,7},{6,10},{7,11},{10,14},{11,15},{14,12},{15,13},{12,8},{... | collective-permute-start | bytes 3440648 | tf_op jit(solution)/shard_map/ppermute | solution.py:261
  3.0 34.6 %collective-permute-start.1 = (bf16[40,14336]{1,0:T(8,128)(2,1)}, bf16[40,14336]{1,0:T(8,128)(2,1)S(1)}, u32[]{:S(2)}, u32[]{:S(2)}) collective-permute-start(bf16[40,14336]{1,0:T(8,128)(2,1)} %refs_0_.1), channel_id=1, source_target_pairs={{6,2},{7,3},{10,6},{11,7},{14,10},{15,11},{12,14},{13,15},{8,12},{... | collective-permute-start | bytes 3440648 | tf_op jit(solution)/shard_map/ppermute | solution.py:264
  3.3 32.9 %collective-permute-start.2 = (bf16[40,4096]{1,0:T(8,128)(2,1)}, bf16[40,4096]{1,0:T(8,128)(2,1)S(1)}, u32[]{:S(2)}, u32[]{:S(2)}) collective-permute-start(bf16[40,4096]{1,0:T(8,128)(2,1)} %refs_2_.1), channel_id=1, source_target_pairs={{2,6},{3,7},{6,10},{7,11},{10,14},{11,15},{14,12},{15,13},{12,8},{... | collective-permute-start | bytes 983048 | tf_op jit(solution)/shard_map/ppermute | solution.py:261
  5.0 32.6 %collective-permute-start.3 = (bf16[40,4096]{1,0:T(8,128)(2,1)}, bf16[40,4096]{1,0:T(8,128)(2,1)S(1)}, u32[]{:S(2)}, u32[]{:S(2)}) collective-permute-start(bf16[40,4096]{1,0:T(8,128)(2,1)} %refs_2_.1), channel_id=1, source_target_pairs={{6,2},{7,3},{10,6},{11,7},{14,10},{15,11},{12,14},{13,15},{8,12},{... | collective-permute-start | bytes 983048 | tf_op jit(solution)/shard_map/ppermute | solution.py:264
  37.6 12.3 %collective-permute-start.10 = (bf16[40,14336]{1,0:T(8,128)(2,1)S(1)}, bf16[40,14336]{1,0:T(8,128)(2,1)S(1)}, u32[]{:S(2)}, u32[]{:S(2)}) collective-permute-start(bf16[40,14336]{1,0:T(8,128)(2,1)S(1)} %collective-permute-done.refs_0_), channel_id=1, source_target_pairs={{2,3},{3,2},{6,7},{7,6},{10,11},{11,10},{14,15},{15,14},{12,13},{1... | collective-permute-start | bytes 3440648 | tf_op jit(solution)/shard_map/ppermute | solution.py:258
  37.6 12.8 %collective-permute-start.11 = (bf16[40,14336]{1,0:T(8,128)(2,1)S(1)}, bf16[40,14336]{1,0:T(8,128)(2,1)S(1)}, u32[]{:S(2)}, u32[]{:S(2)}) collective-permute-start(bf16[40,14336]{1,0:T(8,128)(2,1)S(1)} %collective-permute-done.1.refs_1_), channel_id=1, source_target_pairs={{2,3},{3,2},{6,7},{7,6},{10,11},{11,10},{14,15},{15,14},{12,13},{1... | collective-permute-start | bytes 3440648 | tf_op jit(solution)/shard_map/ppermute | solution.py:258
  38.1 35.6 %collective-permute-start.6 = (bf16[40,14336]{1,0:T(8,128)(2,1)S(1)}, bf16[40,14336]{1,0:T(8,128)(2,1)S(1)}, u32[]{:S(2)}, u32[]{:S(2)}) collective-permute-start(bf16[40,14336]{1,0:T(8,128)(2,1)S(1)} %collective-permute-done.refs_0_), channel_id=1, source_target_pairs={{2,6},{3,7},{6,10},{7,11},{10,14},{11,15},{14,12},{15,13},{12,8},{... | collective-permute-start | bytes 3440648 | tf_op jit(solution)/shard_map/ppermute | solution.py:261
  39.7 34.0 %collective-permute-start.7 = (bf16[40,14336]{1,0:T(8,128)(2,1)S(1)}, bf16[40,14336]{1,0:T(8,128)(2,1)S(1)}, u32[]{:S(2)}, u32[]{:S(2)}) collective-permute-start(bf16[40,14336]{1,0:T(8,128)(2,1)S(1)} %collective-permute-done.1.refs_1_), channel_id=1, source_target_pairs={{6,2},{7,3},{10,6},{11,7},{14,10},{15,11},{12,14},{13,15},{8,12},{... | collective-permute-start | bytes 3440648 | tf_op jit(solution)/shard_map/ppermute | solution.py:264
  48.4 24.0 %collective-permute-start.8 = (bf16[40,4096]{1,0:T(8,128)(2,1)S(1)}, bf16[40,4096]{1,0:T(8,128)(2,1)S(1)}, u32[]{:S(2)}, u32[]{:S(2)}) collective-permute-start(bf16[40,4096]{1,0:T(8,128)(2,1)S(1)} %collective-permute-done.2.refs_4_), channel_id=1, source_target_pairs={{2,6},{3,7},{6,10},{7,11},{10,14},{11,15},{14,12},{15,13},{12,8},{... | collective-permute-start | bytes 983048 | tf_op jit(solution)/shard_map/ppermute | solution.py:261
  50.0 23.7 %collective-permute-start.9 = (bf16[40,4096]{1,0:T(8,128)(2,1)S(1)}, bf16[40,4096]{1,0:T(8,128)(2,1)S(1)}, u32[]{:S(2)}, u32[]{:S(2)}) collective-permute-start(bf16[40,4096]{1,0:T(8,128)(2,1)S(1)} %collective-permute-done.3.refs_5_), channel_id=1, source_target_pairs={{6,2},{7,3},{10,6},{11,7},{14,10},{15,11},{12,14},{13,15},{8,12},{... | collective-permute-start | bytes 983048 | tf_op jit(solution)/shard_map/ppermute | solution.py:264
  50.4 23.3 %collective-permute-start.14 = (f32[2,80,512]{2,1,0:T(8,128)S(1)}, f32[2,80,512]{2,1,0:T(8,128)S(1)}, u32[]{:S(2)}, u32[]{:S(2)}) collective-permute-start(f32[2,80,512]{2,1,0:T(8,128)S(1)} %project.5.refs_0_), channel_id=1, source_target_pairs={{0,16},{16,0},{1,17},{17,1},{2,18},{18,2},{3,19},{19,3},{4,20},{20... | collective-permute-start | bytes 983048 | tf_op jit(solution)/shard_map/ppermute | solution.py:254
  73.8 9.6 %collective-permute-start.21 = (bf16[40,14336]{1,0:T(8,128)(2,1)S(1)}, bf16[40,14336]{1,0:T(8,128)(2,1)S(1)}, u32[]{:S(2)}, u32[]{:S(2)}) collective-permute-start(bf16[40,14336]{1,0:T(8,128)(2,1)S(1)} %collective-permute-done.7.refs_1_), channel_id=1, source_target_pairs={{2,3},{3,2},{6,7},{7,6},{10,11},{11,10},{14,15},{15,14},{12,13},{1... | collective-permute-start | bytes 3440648 | tf_op jit(solution)/shard_map/ppermute | solution.py:258
  74.4 35.9 %collective-permute-start.16 = (bf16[40,14336]{1,0:T(8,128)(2,1)S(1)}, bf16[40,14336]{1,0:T(8,128)(2,1)S(1)}, u32[]{:S(2)}, u32[]{:S(2)}) collective-permute-start(bf16[40,14336]{1,0:T(8,128)(2,1)S(1)} %collective-permute-done.6.refs_0_), channel_id=1, source_target_pairs={{2,6},{3,7},{6,10},{7,11},{10,14},{11,15},{14,12},{15,13},{12,8},{... | collective-permute-start | bytes 3440648 | tf_op jit(solution)/shard_map/ppermute | solution.py:261
  75.9 34.4 %collective-permute-start.17 = (bf16[40,14336]{1,0:T(8,128)(2,1)S(1)}, bf16[40,14336]{1,0:T(8,128)(2,1)S(1)}, u32[]{:S(2)}, u32[]{:S(2)}) collective-permute-start(bf16[40,14336]{1,0:T(8,128)(2,1)S(1)} %collective-permute-done.7.refs_1_), channel_id=1, source_target_pairs={{6,2},{7,3},{10,6},{11,7},{14,10},{15,11},{12,14},{13,15},{8,12},{... | collective-permute-start | bytes 3440648 | tf_op jit(solution)/shard_map/ppermute | solution.py:264
  80.3 30.0 %collective-permute-start.24 = (f32[2,160,512]{2,1,0:T(8,128)S(1)}, f32[2,160,512]{2,1,0:T(8,128)S(1)}, u32[]{:S(2)}, u32[]{:S(2)}) collective-permute-start(f32[2,160,512]{2,1,0:T(8,128)S(1)} %project.6.refs_0_), channel_id=1, source_target_pairs={{0,16},{16,0},{1,17},{17,1},{2,18},{18,2},{3,19},{19,3},{4,20},{20... | collective-permute-start | bytes 1966088 | tf_op jit(solution)/shard_map/ppermute | solution.py:254
  81.8 27.2 %collective-permute-start.18 = (bf16[40,4096]{1,0:T(8,128)(2,1)S(1)}, bf16[40,4096]{1,0:T(8,128)(2,1)S(1)}, u32[]{:S(2)}, u32[]{:S(2)}) collective-permute-start(bf16[40,4096]{1,0:T(8,128)(2,1)S(1)} %collective-permute-done.8.refs_4_), channel_id=1, source_target_pairs={{2,6},{3,7},{6,10},{7,11},{10,14},{11,15},{14,12},{15,13},{12,8},{... | collective-permute-start | bytes 983048 | tf_op jit(solution)/shard_map/ppermute | solution.py:261
  83.4 26.9 %collective-permute-start.19 = (bf16[40,4096]{1,0:T(8,128)(2,1)S(1)}, bf16[40,4096]{1,0:T(8,128)(2,1)S(1)}, u32[]{:S(2)}, u32[]{:S(2)}) collective-permute-start(bf16[40,4096]{1,0:T(8,128)(2,1)S(1)} %collective-permute-done.9.refs_5_), channel_id=1, source_target_pairs={{6,2},{7,3},{10,6},{11,7},{14,10},{15,11},{12,14},{13,15},{8,12},{... | collective-permute-start | bytes 983048 | tf_op jit(solution)/shard_map/ppermute | solution.py:264
  111.4 23.7 %collective-permute-start.25 = (bf16[40,9216]{1,0:T(8,128)(2,1)S(1)}, bf16[40,9216]{1,0:T(8,128)(2,1)S(1)}, u32[]{:S(2)}, u32[]{:S(2)}) collective-permute-start(bf16[40,9216]{1,0:T(8,128)(2,1)S(1)} %slice.6), channel_id=1, source_target_pairs={{2,6},{3,7},{6,10},{7,11},{10,14},{11,15},{14,12},{15,13},{12,8},{... | collective-permute-start | bytes 2211848 | tf_op jit(solution)/shard_map/ppermute | solution.py:261
  115.3 19.8 %collective-permute-start.32 = (f32[2,160,512]{2,1,0:T(8,128)S(1)}, f32[2,160,512]{2,1,0:T(8,128)S(1)}, u32[]{:S(2)}, u32[]{:S(2)}) collective-permute-start(f32[2,160,512]{2,1,0:T(8,128)S(1)} %project.7.refs_0_), channel_id=1, source_target_pairs={{0,16},{16,0},{1,17},{17,1},{2,18},{18,2},{3,19},{19,3},{4,20},{20... | collective-permute-start | bytes 1966088 | tf_op jit(solution)/shard_map/ppermute | solution.py:254
  116.8 18.3 %collective-permute-start.26 = (bf16[40,5120]{1,0:T(8,128)(2,1)S(1)}, bf16[40,5120]{1,0:T(8,128)(2,1)S(1)}, u32[]{:S(2)}, u32[]{:S(2)}) collective-permute-start(bf16[40,5120]{1,0:T(8,128)(2,1)S(1)} %slice.7), channel_id=1, source_target_pairs={{6,2},{7,3},{10,6},{11,7},{14,10},{15,11},{12,14},{13,15},{8,12},{... | collective-permute-start | bytes 1228808 | tf_op jit(solution)/shard_map/ppermute | solution.py:264
  117.3 17.8 %collective-permute-start.27 = (bf16[40,4096]{1,0:T(8,128)(2,1)S(1)}, bf16[40,4096]{1,0:T(8,128)(2,1)S(1)}, u32[]{:S(2)}, u32[]{:S(2)}) collective-permute-start(bf16[40,4096]{1,0:T(8,128)(2,1)S(1)} %collective-permute-done.19.refs_5_), channel_id=1, source_target_pairs={{6,2},{7,3},{10,6},{11,7},{14,10},{15,11},{12,14},{13,15},{8,12},{... | collective-permute-start | bytes 983048 | tf_op jit(solution)/shard_map/ppermute | solution.py:264
  135.8 17.6 %collective-permute-start.37 = (f32[2,160,512]{2,1,0:T(8,128)S(1)}, f32[2,160,512]{2,1,0:T(8,128)}, u32[]{:S(2)}, u32[]{:S(2)}) collective-permute-start(f32[2,160,512]{2,1,0:T(8,128)S(1)} %project.8.refs_0_), channel_id=1, source_target_pairs={{0,16},{16,0},{1,17},{17,1},{2,18},{18,2},{3,19},{19,3},{4,20},{20... | collective-permute-start | bytes 1966088 | tf_op jit(solution)/shard_map/ppermute | solution.py:254
  146.0 13.9 %collective-permute-start.36 = (f32[2,80,512]{2,1,0:T(8,128)}, f32[2,80,512]{2,1,0:T(8,128)S(1)}, u32[]{:S(2)}, u32[]{:S(2)}) collective-permute-start(f32[2,80,512]{2,1,0:T(8,128)} %project.9.refs_0_), channel_id=1, source_target_pairs={{0,16},{16,0},{1,17},{17,1},{2,18},{18,2},{3,19},{19,3},{4,20},{20... | collective-permute-start | bytes 983048 | tf_op jit(solution)/shard_map/ppermute | solution.py:254
  (19 other events, 87.1 us)

commit v2 on v1

v2 whole, which is shorter than its diff:
```python
import functools
import math

import jax
import jax.numpy as jnp
from jax import lax
from jax.experimental import pallas as pl
from jax.experimental.pallas import tpu as pltpu
from jax.sharding import PartitionSpec as P

RANK = 32
WIDE = 256
LIGHT = pl.CostEstimate(flops=1, bytes_accessed=1, transcendentals=0)
ROOM = 16 << 20


def params():
    return pltpu.CompilerParams(vmem_limit_bytes=ROOM)


def in_hbm(x):
    return pltpu.with_memory_space_constraint(x, pltpu.HBM)


def in_vmem(x):
    return pltpu.with_memory_space_constraint(x, pltpu.VMEM)


def cycle_of(first, second):
    if min(first, second) == 1:
        size = first * second
        order = list(range(0, size, 2)) + list(range(1, size, 2))[::-1]
        return [(i, 0) if second == 1 else (0, i) for i in order]
    if first % 2:
        return [(a, b) for b, a in cycle_of(second, first)] if second % 2 == 0 else [
            (a, b) for a in range(first) for b in range(second)]
    walk = []
    for a in range(first):
        inner = range(1, second)
        walk += [(a, b) for b in (inner if a % 2 == 0 else reversed(inner))]
    return walk + [(a, 0) for a in reversed(range(first))]


def ring_of(mesh):
    devices = list(mesh.devices[0])
    chips = {}
    for index, device in enumerate(devices):
        coords = getattr(device, "coords", None)
        key = tuple(coords) if coords is not None else (index // 2,)
        chips.setdefault(key, []).append(index)
    keys = list(chips)
    values = [sorted({k[i] for k in keys}) for i in range(len(keys[0]))]
    varying = [i for i in range(len(values)) if len(values[i]) > 1]
    if len(varying) == 2 and len(keys) == len(values[varying[0]]) * len(values[varying[1]]):
        one, two = sorted(varying, key=lambda i: -len(values[i]))
        at = {(values[one].index(k[one]), values[two].index(k[two])): k for k in keys}
        keys = [at[place] for place in cycle_of(len(values[one]), len(values[two]))]
    ring = [chips[k] for k in keys]
    assert all(pair[0] % 2 == 0 and pair[1] == pair[0] + 1 for pair in ring)
    return ring


def load_kernel(a_ref, b_ref, a_out, b_out, sem):
    first = pltpu.make_async_copy(a_ref, a_out, sem.at[0])
    second = pltpu.make_async_copy(b_ref, b_out, sem.at[1])
    first.start()
    second.start()
    first.wait()
    second.wait()


def load(a, b):
    return pl.pallas_call(
        load_kernel,
        in_specs=[pl.BlockSpec(memory_space=pl.ANY)] * 2,
        out_specs=[pl.BlockSpec(memory_space=pltpu.VMEM)] * 2,
        out_shape=[pltpu.VMEM(a.shape, a.dtype), pltpu.VMEM(b.shape, b.dtype)],
        scratch_shapes=[pltpu.SemaphoreType.DMA((2,))],
        compiler_params=params(),
        cost_estimate=LIGHT,
        name="load_factors",
    )(in_hbm(a), in_hbm(b))


def join_kernel(a_ref, b_ref, out_ref, sem):
    width = a_ref.shape[1]
    first = pltpu.make_async_copy(a_ref, out_ref.at[:, :width], sem.at[0])
    second = pltpu.make_async_copy(b_ref, out_ref.at[:, width:], sem.at[1])
    first.start()
    second.start()
    first.wait()
    second.wait()


def joined(a, b):
    return pl.pallas_call(
        join_kernel,
        in_specs=[pl.BlockSpec(memory_space=pl.ANY)] * 2,
        out_specs=pl.BlockSpec(memory_space=pl.ANY),
        out_shape=jax.ShapeDtypeStruct((a.shape[0], a.shape[1] + b.shape[1]), a.dtype),
        scratch_shapes=[pltpu.SemaphoreType.DMA((2,))],
        compiler_params=params(),
        cost_estimate=LIGHT,
        name="join",
    )(in_hbm(a), in_hbm(b))


def pack_kernel(count, parts, step, *refs):
    arrays, outs = refs[:count], refs[count:]
    i = pl.program_id(0)
    for out, (first, steps) in zip(outs, parts):

        @pl.when((i >= first) & (i < first + steps))
        def _(out=out):
            out[...] = jnp.concatenate([x[...] for x in arrays], axis=0)


def packed(arrays, bounds, step):
    rows = sum(a.shape[0] for a in arrays)
    parts = tuple((lo // step, (hi - lo) // step) for lo, hi in zip(bounds, bounds[1:]))
    return pl.pallas_call(
        functools.partial(pack_kernel, len(arrays), parts, step),
        grid=(bounds[-1] // step,),
        in_specs=[pl.BlockSpec((a.shape[0], step), lambda i: (0, i)) for a in arrays],
        out_specs=[
            pl.BlockSpec((rows, step), lambda i, first=first, steps=steps: (0, jnp.clip(i - first, 0, steps - 1)))
            for first, steps in parts],
        out_shape=[jax.ShapeDtypeStruct((rows, hi - lo), arrays[0].dtype) for lo, hi in zip(bounds, bounds[1:])],
        compiler_params=params(),
        cost_estimate=LIGHT,
        name="pack",
    )(*arrays)


def cut_kernel(a_ref, b_ref, a_out, b_out, sem):
    width = a_out.shape[1]
    first = pltpu.make_async_copy(a_ref.at[:, :width], a_out, sem.at[0])
    second = pltpu.make_async_copy(b_ref.at[:, width:], b_out, sem.at[1])
    first.start()
    second.start()
    first.wait()
    second.wait()


def cut_halves(a, b, middle):
    return pl.pallas_call(
        cut_kernel,
        in_specs=[pl.BlockSpec(memory_space=pl.ANY)] * 2,
        out_specs=[pl.BlockSpec(memory_space=pl.ANY)] * 2,
        out_shape=[
            jax.ShapeDtypeStruct((a.shape[0], middle), a.dtype),
            jax.ShapeDtypeStruct((b.shape[0], b.shape[1] - middle), b.dtype)],
        scratch_shapes=[pltpu.SemaphoreType.DMA((2,))],
        compiler_params=params(),
        cost_estimate=LIGHT,
        name="cut",
    )(a, b)


def gram_kernel(step, a_ref, b_ref, out_ref, sums):
    columns = a_ref.shape[1]
    row = lax.broadcasted_iota(jnp.int32, (WIDE, WIDE), 0) // RANK
    col = lax.broadcasted_iota(jnp.int32, (WIDE, WIDE), 1) // RANK
    for index, ref in enumerate((a_ref, b_ref)):
        sums[...] = jnp.zeros_like(sums)

        @pl.loop(0, ref.shape[0] // step)
        def _(i, ref=ref):
            for start in range(0, columns, WIDE):
                block = ref[pl.ds(pl.multiple_of(i * step, step), step), start : start + WIDE]
                sums[:, start : start + WIDE] += lax.dot_general(
                    block, block, (((0,), (0,)), ((), ())), preferred_element_type=jnp.float32)

        for start in range(0, columns, WIDE):
            kept = jnp.where(row == col, sums[:, start : start + WIDE], 0.0)
            out_ref[index, :, start : start + WIDE] = kept.reshape(WIDE // RANK, RANK, WIDE).sum(axis=0)


def grams(a, b):
    columns = a.shape[1]
    step = math.gcd(a.shape[0], b.shape[0])
    return pl.pallas_call(
        functools.partial(gram_kernel, step),
        in_specs=[pl.BlockSpec(memory_space=pltpu.VMEM)] * 2,
        out_specs=pl.BlockSpec(memory_space=pltpu.VMEM),
        out_shape=jax.ShapeDtypeStruct((2, RANK, columns), jnp.float32),
        scratch_shapes=[pltpu.VMEM((WIDE, columns), jnp.float32)],
        compiler_params=params(),
        cost_estimate=LIGHT,
        name="grams",
    )(a, b)


def chunk_of(*sizes):
    step = functools.reduce(math.gcd, sizes)
    for least in (1024, 512, 256, 128):
        if step % least == 0:
            return least
    return step


def project_kernel(step, spans, count, split, side_ref, *refs):
    outs, sums = refs[count + 2 : -1], refs[-1]
    factors = refs[count : count + 2]
    i = pl.program_id(0)

    @pl.when(i == 0)
    def _():
        sums[...] = jnp.zeros_like(sums)

    for held, first, steps, which, offset in spans:

        @pl.when((i >= first) & (i < first + steps))
        def _(held=held, which=which, offset=offset, first=first):
            x = jnp.concatenate([refs[h][...] for h in held], axis=0)
            at = pl.multiple_of((i - first) * step + offset, step)
            sums[which if split else 0] += jnp.dot(
                x, factors[which][pl.ds(at, step), :], preferred_element_type=jnp.float32)

    @pl.when(i == pl.num_programs(0) - 1)
    def _():
        if split:
            half = sums.shape[1] // 2
            side = side_ref[0]
            for out, which in zip(outs, (side, 1 - side)):
                out[...] = sums[:, pl.ds(pl.multiple_of(which * half, 8), half), :]
        else:
            outs[0][...] = sums[0]


def project(groups, factors, side, split, step):
    specs, operands, spans, first = [], [], [], 0
    for arrays, group in groups:
        held = tuple(range(len(operands), len(operands) + len(arrays)))
        low = min(begin for begin, _, _, _ in group) // step
        high = max(begin + width for begin, width, _, _ in group) // step
        for array, base in arrays:
            specs.append(pl.BlockSpec(
                (array.shape[0], step),
                lambda i, first=first, low=low, high=high, base=base // step:
                    (0, base + jnp.clip(i - first + low, low, high - 1))))
            operands.append(array)
        for begin, width, which, offset in group:
            spans.append((held, first + begin // step - low, width // step, which, offset))
        first += high - low
    rows, columns = sum(a.shape[0] for a, _ in groups[0][0]), factors[0].shape[1]
    shape = (2, rows // 2, columns) if split else (rows, columns)
    outs = 2 if split else 1
    return pl.pallas_call(
        functools.partial(project_kernel, step, tuple(spans), len(operands), split),
        grid=(first,),
        in_specs=[pl.BlockSpec(memory_space=pltpu.SMEM)] + specs + [pl.BlockSpec(memory_space=pltpu.VMEM)] * 2,
        out_specs=[pl.BlockSpec(shape, lambda i: (0,) * len(shape))] * outs,
        out_shape=[jax.ShapeDtypeStruct(shape, jnp.float32)] * outs,
        scratch_shapes=[pltpu.VMEM((outs, rows, columns), jnp.float32)],
        compiler_params=params(),
        cost_estimate=LIGHT,
        name="project",
    )(side, *operands, *[in_vmem(f) for f in factors])


def project_last_kernel(pieces, *refs):
    count = sum(arrays for arrays, _ in pieces)
    tokens, factors, out_ref = refs[:count], refs[count : count + 2], refs[-1]
    out_ref[...] = jnp.zeros_like(out_ref)
    taken = 0
    for arrays, spans in pieces:
        held = tokens[taken : taken + arrays]
        taken += arrays
        for begin, width, which, offset in spans:
            step = chunk_of(width)

            @pl.loop(0, width // step)
            def _(i, held=held, begin=begin, which=which, offset=offset, step=step):
                at = pl.ds(pl.multiple_of(i * step + begin, 128), step)
                x = jnp.concatenate([h[:, at] for h in held], axis=0)
                w = factors[which][pl.ds(pl.multiple_of(i * step + offset, 128), step), :]
                out_ref[...] += jnp.dot(x, w, preferred_element_type=jnp.float32)


def project_last(groups, factors):
    pieces = tuple((len(arrays), tuple(spans)) for arrays, spans in groups)
    operands = [a for arrays, _ in groups for a in arrays]
    rows, columns = sum(a.shape[0] for a in groups[0][0]), factors[0].shape[1]
    given = [in_vmem(x) for x in (*operands, *factors)]
    return pl.pallas_call(
        functools.partial(project_last_kernel, pieces),
        in_specs=[pl.BlockSpec(memory_space=pltpu.VMEM)] * len(given),
        out_specs=pl.BlockSpec(memory_space=pltpu.VMEM),
        out_shape=jax.ShapeDtypeStruct((rows, columns), jnp.float32),
        compiler_params=params(),
        cost_estimate=LIGHT,
        name="project_last",
    )(*given)


def scores_of(projected, gram, columns):
    queries = columns // RANK
    member = (lax.broadcasted_iota(jnp.int32, (columns, queries), 0) // RANK) == lax.broadcasted_iota(
        jnp.int32, (columns, queries), 1)
    member = member.astype(jnp.float32)

    def by_query(x):
        return jnp.dot(x, member, precision=lax.Precision.HIGHEST, preferred_element_type=jnp.float32)

    norms = jnp.broadcast_to((gram[0] * gram[1]).sum(axis=0, keepdims=True), (8, columns))
    inverse = 1.0 / jnp.sqrt(by_query(norms)[:1] + 1e-06)
    return by_query(projected[0] * projected[1]) * inverse


def total_of(refs):
    return sum(ref[...] for ref in refs[1:]) + refs[0][...]


def score_kernel(counts, grams_count, *refs):
    grams_, out_ref = refs[-1 - grams_count : -1], refs[-1]
    columns = grams_[0].shape[2]
    taken, first = 0, 0
    for count in counts:
        parts = refs[taken : taken + count]
        taken += count
        rows = parts[0].shape[1]
        out_ref[first : first + rows] = scores_of(total_of(parts), total_of(grams_), columns)
        first += rows


def score(groups, gram_parts):
    columns = gram_parts[0].shape[2]
    return pl.pallas_call(
        functools.partial(score_kernel, tuple(len(parts) for parts in groups), len(gram_parts)),
        out_shape=jax.ShapeDtypeStruct((sum(parts[0].shape[1] for parts in groups), columns // RANK), jnp.float32),
        compiler_params=params(),
        cost_estimate=LIGHT,
        name="score",
    )(*[p for parts in groups for p in parts], *gram_parts)


def looked_up(table, index):
    return sum(jnp.where(index == i, value, 0) for i, value in enumerate(table))


def last_kernel(count, distances, place, tokens, at_ref, *refs):
    parts = refs[: 2 * count]
    grams_ = refs[2 * count : 3 * count]
    earlier, out_ref, held = refs[3 * count : -2], refs[-2], refs[-1]
    chips = len(place)
    core, side, keeper = at_ref[0], at_ref[1], at_ref[2]
    for groups, mine, other in zip(distances, earlier[0::2], earlier[1::2]):
        for j, distance in enumerate(groups):
            held[distance % chips, keeper] = mine[j * tokens : (j + 1) * tokens]
            held[distance % chips, 1 - keeper] = other[j * tokens : (j + 1) * tokens]
    if count:
        projected = [total_of(parts[:count]), total_of(parts[count:])]
        result = scores_of(projected, total_of(grams_), projected[0].shape[1])
        for c in range(2):
            held[chips // 2, c] = result[c * tokens : (c + 1) * tokens]
    here = looked_up(place, core // 2)
    own = core % 2
    share = out_ref.shape[0] // (2 * tokens)
    for j in range(share):
        there = looked_up(place, side * share + j)
        distance = there - here
        distance = jnp.where(distance < 0, distance + chips, distance)
        for c in range(2):
            out_ref[(2 * j + c) * tokens : (2 * j + c + 1) * tokens, :] = held[distance, (own + c) % 2]


def last(first, second, gram_parts, earlier, distances, place, tokens, share, at):
    queries = earlier[0].shape[1]
    return pl.pallas_call(
        functools.partial(last_kernel, len(first), distances, place, tokens),
        in_specs=[pl.BlockSpec(memory_space=pltpu.SMEM)]
        + [pl.BlockSpec(memory_space=pltpu.VMEM)] * (3 * len(first) + len(earlier)),
        out_specs=pl.BlockSpec(memory_space=pltpu.VMEM),
        out_shape=jax.ShapeDtypeStruct((share, queries), jnp.float32),
        scratch_shapes=[pltpu.VMEM((len(place), 2, tokens, queries), jnp.float32)],
        compiler_params=params(),
        cost_estimate=LIGHT,
        name="last_scores",
    )(at, *first, *second, *gram_parts[: len(first)], *earlier)


def within(spans, low, high):
    kept = []
    for begin, width, which, offset in spans:
        a, b = max(begin, low), min(begin + width, high)
        if a < b:
            kept.append((a - low, b - a, which, offset + a - begin))
    return kept


def solution(mesh):
    rows = mesh.shape["rows"]
    query = mesh.shape["query"]
    ring = ring_of(mesh)
    chips = len(ring)
    forward = [(a, b) for i in range(chips) for a, b in zip(ring[i], ring[(i + 1) % chips])]
    backward = [(b, a) for a, b in forward]
    mates = [(pair[i], pair[1 - i]) for pair in ring for i in range(2)]
    place = [0] * chips
    for i, pair in enumerate(ring):
        place[pair[0] // 2] = i
    place = tuple(place)

    def swap_rows(x):
        return lax.ppermute(x, "rows", [(0, 1), (1, 0)])

    def across(x):
        return [x, swap_rows(x)] if rows == 2 else [lax.psum(x, "rows")]

    def mate(xs):
        return [lax.ppermute(x, "query", mates) for x in xs]

    def ahead(x):
        return lax.ppermute(x, "query", forward)

    def behind(x):
        return lax.ppermute(x, "query", backward)

    def both(pair):
        return [ahead(pair[0]), behind(pair[1])]

    def tied(*trees):
        return lax.optimization_barrier(trees)

    def local(acts, grads, in_factors, out_factors):
        tokens, width = acts.shape
        depth = grads.shape[1]
        total = width + depth
        middle = total // 2 // 128 * 128
        span = [(0, depth, 1, 0), (depth, width, 0, 0)]
        query_at, row_at = lax.axis_index("query"), lax.axis_index("rows")
        keeper = row_at if rows == 2 else jnp.zeros_like(row_at)
        at = jnp.stack([query_at, row_at, keeper]).astype(jnp.int32)
        side = keeper.astype(jnp.int32).reshape(1)
        full_hops = (chips - 1) // 2

        step = math.gcd(width, depth)
        while step > 2048 and step % 2 == 0:
            step //= 2
        bounds = [total * i // 3 // step * step for i in range(4)]

        def mates_of(held):
            return mate(packed(held, bounds, step))

        def projected(held, swapped):
            groups = [
                ([(x, lo) for x in held] + [(part, 0)], within(span, lo, hi))
                for lo, hi, part in zip(bounds, bounds[1:], swapped)]
            return project(groups, factors, side, True, step)

        def exchanged(kept, sent):
            if rows == 2:
                return [[kept, swap_rows(sent)]]
            return [[x] for x in lax.psum((kept, sent), "rows")]

        def scored(held):
            return [score(list(groups), gram_parts) for groups in zip(*held)]

        at, side, acts, grads, in_factors, out_factors = tied(at, side, acts, grads, in_factors, out_factors)
        own = joined(grads, acts)
        fly = [ahead(own), behind(own)]
        swapped = mates_of([own])
        factors = load(in_factors, out_factors)
        gram = grams(*factors)
        kept, sent = projected([own], swapped)
        fly, gram, kept, sent = tied(fly, gram, kept, sent)
        own_sums = (kept, sent)
        distances, waiting = [0], []
        for hop in range(1, full_hops + 1):
            held = fly
            final = hop == full_hops
            if not final:
                fly = [ahead(held[0]), behind(held[1])]
            elif chips % 2 == 0:
                fly = cut_halves(*held, middle)
                fly = [ahead(fly[0]), behind(fly[1])]
            swapped = mates_of(held)
            kept, sent = projected(held, swapped)
            kept, sent, waiting = tied(kept, sent, waiting)
            halves = exchanged(kept, sent)
            if hop == 1:
                waiting.append(exchanged(*own_sums))
                gram_parts = across(gram)
            if not final:
                distances += [-hop, hop]
                waiting.append(halves)
            fly, halves, waiting, gram_parts = tied(fly, halves, waiting, gram_parts)
        mine, *other = scored(waiting)
        result, *second_half = scored([halves])
        if rows == 2:
            other, second_half = [swap_rows(mine)], [swap_rows(result)]
        first, second = [], []
        if chips % 2 == 0:
            parts = mate(fly)
            fly, parts = tied(fly, parts)
            low, high = within(span, 0, middle), within(span, middle, total)
            out = project_last([([fly[0], parts[0]], [s for s in low if s[2]])], factors)
            first = across(out)
            fly, parts, out, other, second_half = tied(fly, parts, out, other, second_half)
            second = across(project_last([
                ([fly[0], parts[0]], [s for s in low if not s[2]]), ([fly[1], parts[1]], high)], factors))
        return last(
            first, second, gram_parts, [mine, *other, result, *second_half],
            (tuple(distances), (-full_hops, full_hops)), place, tokens, query * tokens // rows, at)

    return jax.shard_map(
        local,
        mesh=mesh,
        in_specs=(P("query", "rows"), P("query", "rows"), P("rows", "query"), P("rows", "query")),
        out_specs=P("rows", "query"),
        check_vma=False,
    )
```

time: 162 us -> 151 us (0.932)
  waiting for transfers between devices: 83.3 us -> 74.1 us
  Pallas kernels: 46.3 us -> 52.4 us
  starting transfers between devices: 28 us -> 23.3 us
  local copies, waits for them, and re-layouts: 4.08 us -> 0.71 us
    ppermute x23, waiting for transfers between devices: 24.4 us -> 42.8 us  [the longest x9 30.7 us: swap_rows(): return lax.ppermute(x, 'rows', [(0, 1), (1, 0)])]
    ppermute x7 -> x4, waiting for transfers between devices: 43.8 us -> 26 us  [ahead(): return lax.ppermute(x, 'query', forward)]
    ppermute x8 -> x4, waiting for transfers between devices: 15.1 us -> 5.29 us  [behind(): return lax.ppermute(x, 'query', backward)]
    pallas_call x10 -> x15, Pallas kernels: 34.2 us -> 39 us  [the longest x4 25.1 us: project(): pl.pallas_call(functools.partial(project_kernel, step, tuple(spans), len(...]
    ppermute x7 -> x4, starting transfers between devices: 12.2 us -> 7.8 us  [ahead(): return lax.ppermute(x, 'query', forward)]
    unnamed x10 -> x0, local copies, waits for them, and re-layouts: 3.29 us -> none
    ppermute x8 -> x4, starting transfers between devices: 4.76 us -> 1.47 us  [behind(): return lax.ppermute(x, 'query', backward)]
    ppermute x23, starting transfers between devices: 11.1 us -> 14 us  [the longest x9 10.9 us: swap_rows(): return lax.ppermute(x, 'rows', [(0, 1), (1, 0)])]
  transfers between devices with their start and end apart: 38 -> 31, of which waited for: 16 -> 22; matrix products, arithmetic and copies ran while one was open for 0% -> 0% of each run, Pallas kernels for 28% -> 29%
where the time goes in v2:
time: 151 us
  waiting for transfers between devices  74.1 us (49%)
  Pallas kernels  52.4 us (35%)
  starting transfers between devices  23.3 us (15%)
    ppermute x9, waiting for transfers between devices, swap_rows(): return lax.ppermute(x, 'rows', [(0, 1), (1, 0)])  30.7 us
    ppermute x4, waiting for transfers between devices, ahead(): return lax.ppermute(x, 'query', forward)  26 us
    pallas_call x4, Pallas kernels, project(): pl.pallas_call(functools.partial(project_kernel, step, tuple(spans), len(...  25.1 us
    ppermute x14, waiting for transfers between devices, mate(): return [lax.ppermute(x, 'query', mates) for x in xs]  12.1 us
    ppermute x9, starting transfers between devices, swap_rows(): return lax.ppermute(x, 'rows', [(0, 1), (1, 0)])  10.9 us
    ppermute x4, starting transfers between devices, ahead(): return lax.ppermute(x, 'query', forward)  7.8 us
    pallas_call x1, Pallas kernels, grams(): pl.pallas_call(functools.partial(gram_kernel, step), in_specs=[pl.BlockSp...  6.97 us
    pallas_call x1, Pallas kernels, load(): pl.pallas_call(load_kernel, in_specs=[pl.BlockSpec(memory_space=pl.ANY)]...  6.38 us
  transfers between devices with their start and end apart: 31, of which 22 were waited for; matrix products, arithmetic and copies ran while one was open for 0% of the time, Pallas kernels for 29%

profile of v2, /device:TPU:0, one launch (start us, length us, event | category | flops | bytes accessed | tf_op | source)
XLA Modules:
  0.0 150.8 jit_solution(16840788735191234234)
XLA Ops:
  1.5 3.0 %collective-permute-start = (bf16[40,18432]{1,0:T(8,128)(2,1)S(1)}, bf16[40,18432]{1,0:T(8,128)(2,1)S(1)}, u32[]{:S(2)}, u32[]{:S(2)}) collective-permute-start(bf16[40,18432]{1,0:T(8,128)(2,1)S(1)} %join.1.refs_0_.refs_2_.refs_4_), channel_id=1, source_target_pairs={{2,6},{3,7},{6,10},{7,11},{10,14},{11,15},{14,12},{15,13},{12,8},{... | collective-permute-start | bytes 4423688 | tf_op jit(solution)/shard_map/ppermute | solution.py:415
  6.1 6.4 %load_factors.1 = (bf16[14336,512]{1,0:T(8,128)(2,1)S(1)}, bf16[4096,512]{1,0:T(8,128)(2,1)S(1)}) custom-call(bf16[14336,512]{1,0:T(8,128)(2,1)} %a_ref.1, bf16[4096,512]{1,0:T(8,128)(2,1)} %b_ref.1), custom_call_target="tpu_custom_call" | custom-call | flops 1 | bytes 1 | tf_op jit(solution)/shard_map/load_factors/pallas_call | solution.py:73
  12.5 7.0 %grams.1.refs_6_.refs_2_.refs_4_ = f32[2,32,512]{2,1,0:T(8,128)S(1)} custom-call(bf16[14336,512]{1,0:T(8,128)(2,1)S(1)} %get-tuple-element.99.a_ref.refs_6_.refs_9_.refs_2_.refs_4_, bf16[4096,512]{1,0:T(8,128)(2,1)S(1)} %get-tuple-element.100.b_ref.refs_7_.refs_10_.refs_3_.refs_5_), custom_call_target="tpu_custom_call" | custom-call | flops 1 | bytes 1 | tf_op jit(solution)/shard_map/grams/pallas_call | solution.py:182
  19.5 5.7 %project.4 = (f32[2,40,512]{2,1,0:T(8,128)S(1)}, f32[2,40,512]{2,1,0:T(8,128)S(1)}) custom-call(s32[1]{0:T(128)} %bitcast.1.side_ref, bf16[40,18432]{1,0:T(8,128)(2,1)S(1)} %join.1.refs_0_.refs_2_.refs_4_, bf16[40,6144]{1,0:T(8,128)(2,1)S(1)} %collective-permute-done.2.refs_1_, bf16[40,18432]{1,0:T(8,128)(2,1)S(1)} %join.1.refs_0_.refs_2_.refs_4_, ...), custom_call_target="tpu_custom_call" | custom-call | flops 1 | bytes 1 | tf_op jit(solution)/shard_map/project/pallas_call | solution.py:249
  25.2 11.6 %collective-permute-done.refs_0_.refs_3_.refs_6_ = bf16[40,18432]{1,0:T(8,128)(2,1)S(1)} collective-permute-done((bf16[40,18432]{1,0:T(8,128)(2,1)S(1)}, bf16[40,18432]{1,0:T(8,128)(2,1)S(1)}, u32[]{:S(2)}, u32[]{:S(2)}) %collective-permute-start) | collective-permute-done | bytes 1474592 | tf_op jit(solution)/shard_map/ppermute | solution.py:415
  38.2 1.6 %collective-permute-start.5 = (bf16[40,18432]{1,0:T(8,128)(2,1)S(1)}, bf16[40,18432]{1,0:T(8,128)(2,1)S(1)}, u32[]{:S(2)}, u32[]{:S(2)}) collective-permute-start(bf16[40,18432]{1,0:T(8,128)(2,1)S(1)} %collective-permute-done.refs_0_.refs_3_.refs_6_), channel_id=1, source_target_pairs={{2,6},{3,7},{6,10},{7,11},{10,14},{11,15},{14,12},{15,13},{12,8},{... | collective-permute-start | bytes 4423688 | tf_op jit(solution)/shard_map/ppermute | solution.py:415
  42.1 2.0 %collective-permute-done.10.refs_8_ = bf16[80,6144]{1,0:T(8,128)(2,1)S(1)} collective-permute-done((bf16[80,6144]{1,0:T(8,128)(2,1)S(1)}, bf16[80,6144]{1,0:T(8,128)(2,1)S(1)}, u32[]{:S(2)}, u32[]{:S(2)}) %collective-permute-start.10) | collective-permute-done | bytes 983072 | tf_op jit(solution)/shard_map/ppermute | solution.py:412
  46.9 6.5 %project.5 = (f32[2,80,512]{2,1,0:T(8,128)S(1)}, f32[2,80,512]{2,1,0:T(8,128)S(1)}) custom-call(s32[1]{0:T(128)} %bitcast.1.side_ref, bf16[40,18432]{1,0:T(8,128)(2,1)S(1)} %collective-permute-done.refs_0_.refs_3_.refs_6_, bf16[40,18432]{1,0:T(8,128)(2,1)S(1)} %collective-permute-done.1.refs_1_.refs_4_.refs_7_, ...), custom_call_target="tpu_custom_call" | custom-call | flops 1 | bytes 1 | tf_op jit(solution)/shard_map/project/pallas_call | solution.py:249
  53.4 1.5 %collective-permute-start.11 = (f32[2,80,512]{2,1,0:T(8,128)S(1)}, f32[2,80,512]{2,1,0:T(8,128)S(1)}, u32[]{:S(2)}, u32[]{:S(2)}) collective-permute-start(f32[2,80,512]{2,1,0:T(8,128)S(1)} %get-tuple-element.115), channel_id=1, source_target_pairs={{0,16},{16,0},{1,17},{17,1},{2,18},{18,2},{3,19},{19,3},{4,20},{20... | collective-permute-start | bytes 983048 | tf_op jit(solution)/shard_map/ppermute | solution.py:406
  57.0 12.6 %collective-permute-done.12.refs_7_.refs_3_.refs_5_ = f32[2,32,512]{2,1,0:T(8,128)S(1)} collective-permute-done((f32[2,32,512]{2,1,0:T(8,128)S(1)}, f32[2,32,512]{2,1,0:T(8,128)S(1)}, u32[]{:S(2)}, u32[]{:S(2)}) %collective-permute-start.12) | collective-permute-done | bytes 131104 | tf_op jit(solution)/shard_map/ppermute | solution.py:406
  72.4 1.6 %collective-permute-start.13 = (bf16[40,18432]{1,0:T(8,128)(2,1)S(1)}, bf16[40,18432]{1,0:T(8,128)(2,1)S(1)}, u32[]{:S(2)}, u32[]{:S(2)}) collective-permute-start(bf16[40,18432]{1,0:T(8,128)(2,1)S(1)} %collective-permute-done.5.refs_0_.refs_3_.refs_6_), channel_id=1, source_target_pairs={{2,6},{3,7},{6,10},{7,11},{10,14},{11,15},{14,12},{15,13},{12,8},{... | collective-permute-start | bytes 4423688 | tf_op jit(solution)/shard_map/ppermute | solution.py:415
  76.3 2.0 %collective-permute-done.15.refs_2_ = bf16[80,6144]{1,0:T(8,128)(2,1)S(1)} collective-permute-done((bf16[80,6144]{1,0:T(8,128)(2,1)S(1)}, bf16[80,6144]{1,0:T(8,128)(2,1)S(1)}, u32[]{:S(2)}, u32[]{:S(2)}) %collective-permute-start.15) | collective-permute-done | bytes 983072 | tf_op jit(solution)/shard_map/ppermute | solution.py:412
  81.1 6.5 %project.6 = (f32[2,80,512]{2,1,0:T(8,128)S(1)}, f32[2,80,512]{2,1,0:T(8,128)S(1)}) custom-call(s32[1]{0:T(128)} %bitcast.1.side_ref, bf16[40,18432]{1,0:T(8,128)(2,1)S(1)} %collective-permute-done.5.refs_0_.refs_3_.refs_6_, bf16[40,18432]{1,0:T(8,128)(2,1)S(1)} %collective-permute-done.6.refs_1_.refs_4_.refs_7_, ...), custom_call_target="tpu_custom_call" | custom-call | flops 1 | bytes 1 | tf_op jit(solution)/shard_map/project/pallas_call | solution.py:249
  87.5 1.6 %collective-permute-start.18 = (f32[2,80,512]{2,1,0:T(8,128)S(1)}, f32[2,80,512]{2,1,0:T(8,128)S(1)}, u32[]{:S(2)}, u32[]{:S(2)}) collective-permute-start(f32[2,80,512]{2,1,0:T(8,128)S(1)} %get-tuple-element.133), channel_id=1, source_target_pairs={{0,16},{16,0},{1,17},{17,1},{2,18},{18,2},{3,19},{19,3},{4,20},{20... | collective-permute-start | bytes 983048 | tf_op jit(solution)/shard_map/ppermute | solution.py:406
  89.1 8.2 %collective-permute-done.18.refs_5_ = f32[2,80,512]{2,1,0:T(8,128)S(1)} collective-permute-done((f32[2,80,512]{2,1,0:T(8,128)S(1)}, f32[2,80,512]{2,1,0:T(8,128)S(1)}, u32[]{:S(2)}, u32[]{:S(2)}) %collective-permute-start.18) | collective-permute-done | bytes 327712 | tf_op jit(solution)/shard_map/ppermute | solution.py:406
  97.3 6.7 %collective-permute-done.13.a_ref.refs_0_.refs_3_.refs_6_ = bf16[40,18432]{1,0:T(8,128)(2,1)S(1)} collective-permute-done((bf16[40,18432]{1,0:T(8,128)(2,1)S(1)}, bf16[40,18432]{1,0:T(8,128)(2,1)S(1)}, u32[]{:S(2)}, u32[]{:S(2)}) %collective-permute-start.13) | collective-permute-done | bytes 1474592 | tf_op jit(solution)/shard_map/ppermute | solution.py:415
  107.3 1.6 %collective-permute-start.19 = (bf16[40,9216]{1,0:T(8,128)(2,1)S(1)}, bf16[40,9216]{1,0:T(8,128)(2,1)S(1)}, u32[]{:S(2)}, u32[]{:S(2)}) collective-permute-start(bf16[40,9216]{1,0:T(8,128)(2,1)S(1)} %get-tuple-element.138), channel_id=1, source_target_pairs={{2,6},{3,7},{6,10},{7,11},{10,14},{11,15},{14,12},{15,13},{12,8},{... | collective-permute-start | bytes 2211848 | tf_op jit(solution)/shard_map/ppermute | solution.py:415
  112.0 6.5 %project.7 = (f32[2,80,512]{2,1,0:T(8,128)S(1)}, f32[2,80,512]{2,1,0:T(8,128)S(1)}) custom-call(s32[1]{0:T(128)} %bitcast.1.side_ref, bf16[40,18432]{1,0:T(8,128)(2,1)S(1)} %collective-permute-done.13.a_ref.refs_0_.refs_3_.refs_6_, bf16[40,18432]{1,0:T(8,128)(2,1)S(1)} %collective-permute-done.14.b_ref.refs_1_.refs_4_.refs_7_, ...), custom_call_target="tpu_custom_call" | custom-call | flops 1 | bytes 1 | tf_op jit(solution)/shard_map/project/pallas_call | solution.py:249
  120.0 6.2 %collective-permute-done.19.refs_0_ = bf16[40,9216]{1,0:T(8,128)(2,1)S(1)} collective-permute-done((bf16[40,9216]{1,0:T(8,128)(2,1)S(1)}, bf16[40,9216]{1,0:T(8,128)(2,1)S(1)}, u32[]{:S(2)}, u32[]{:S(2)}) %collective-permute-start.19) | collective-permute-done | bytes 737312 | tf_op jit(solution)/shard_map/ppermute | solution.py:415
  129.7 1.6 %collective-permute-start.28 = (f32[200,16]{1,0:T(8,128)S(1)}, f32[200,16]{1,0:T(8,128)S(1)}, u32[]{:S(2)}, u32[]{:S(2)}) collective-permute-start(f32[200,16]{1,0:T(8,128)S(1)} %score.2.refs_6_), channel_id=1, source_target_pairs={{0,16},{16,0},{1,17},{17,1},{2,18},{18,2},{3,19},{19,3},{4,20},{20... | collective-permute-start | bytes 38408 | tf_op jit(solution)/shard_map/ppermute | solution.py:406
  133.6 2.2 %collective-permute-done.29.refs_9_ = f32[80,16]{1,0:T(8,128)S(1)} collective-permute-done((f32[80,16]{1,0:T(8,128)S(1)}, f32[80,16]{1,0:T(8,128)S(1)}, u32[]{:S(2)}, u32[]{:S(2)}) %collective-permute-start.29) | collective-permute-done | bytes 5152 | tf_op jit(solution)/shard_map/ppermute | solution.py:406
  135.8 4.3 %project_last.3.refs_2_ = f32[80,512]{1,0:T(8,128)S(1)} custom-call(bf16[40,9216]{1,0:T(8,128)(2,1)S(1)} %collective-permute-done.19.refs_0_, bf16[40,9216]{1,0:T(8,128)(2,1)S(1)} %collective-permute-done.25.refs_1_, bf16[40,9216]{1,0:T(8,128)(2,1)S(1)} %collective-permute-done.20.refs_2_, bf16[40,9216]{1,0:T(8,128)(2,1)S(1)} %collective-permute-done.26.refs_3_, ...), custom_call_target="tpu_custom_call" | custom-call | flops 1 | bytes 1 | tf_op jit(solution)/shard_map/project_last/pallas_call | solution.py:286
  142.2 5.1 %collective-permute-done.30.refs_3_ = f32[80,512]{1,0:T(8,128)S(1)} collective-permute-done((f32[80,512]{1,0:T(8,128)S(1)}, f32[80,512]{1,0:T(8,128)S(1)}, u32[]{:S(2)}, u32[]{:S(2)}) %collective-permute-start.30) | collective-permute-done | bytes 163872 | tf_op jit(solution)/shard_map/ppermute | solution.py:406
  147.3 1.8 %collective-permute-done.27.refs_1_ = f32[80,512]{1,0:T(8,128)S(1)} collective-permute-done((f32[80,512]{1,0:T(8,128)S(1)}, f32[80,512]{1,0:T(8,128)S(1)}, u32[]{:S(2)}, u32[]{:S(2)}) %collective-permute-start.27) | collective-permute-done | bytes 163872 | tf_op jit(solution)/shard_map/ppermute | solution.py:406
  (57 shorter events, 36.9 us)
Async XLA Ops:
  1.5 35.4 %collective-permute-start = (bf16[40,18432]{1,0:T(8,128)(2,1)S(1)}, bf16[40,18432]{1,0:T(8,128)(2,1)S(1)}, u32[]{:S(2)}, u32[]{:S(2)}) collective-permute-start(bf16[40,18432]{1,0:T(8,128)(2,1)S(1)} %join.1.refs_0_.refs_2_.refs_4_), channel_id=1, source_target_pairs={{2,6},{3,7},{6,10},{7,11},{10,14},{11,15},{14,12},{15,13},{12,8},{... | collective-permute-start | bytes 4423688 | tf_op jit(solution)/shard_map/ppermute | solution.py:415
  4.5 33.7 %collective-permute-start.1 = (bf16[40,18432]{1,0:T(8,128)(2,1)S(1)}, bf16[40,18432]{1,0:T(8,128)(2,1)S(1)}, u32[]{:S(2)}, u32[]{:S(2)}) collective-permute-start(bf16[40,18432]{1,0:T(8,128)(2,1)S(1)} %join.1.refs_0_.refs_2_.refs_4_), channel_id=1, source_target_pairs={{6,2},{7,3},{10,6},{11,7},{14,10},{15,11},{12,14},{13,15},{8,12},{... | collective-permute-start | bytes 4423688 | tf_op jit(solution)/shard_map/ppermute | solution.py:418
  5.5 14.0 %collective-permute-start.2 = (bf16[40,6144]{1,0:T(8,128)(2,1)S(1)}, bf16[40,6144]{1,0:T(8,128)(2,1)S(1)}, u32[]{:S(2)}, u32[]{:S(2)}) collective-permute-start(bf16[40,6144]{1,0:T(8,128)(2,1)S(1)} %get-tuple-element.102), channel_id=1, source_target_pairs={{2,3},{3,2},{6,7},{7,6},{10,11},{11,10},{14,15},{15,14},{12,13},{1... | collective-permute-start | bytes 1474568 | tf_op jit(solution)/shard_map/ppermute | solution.py:412
  5.5 14.0 %collective-permute-start.3 = (bf16[40,6144]{1,0:T(8,128)(2,1)S(1)}, bf16[40,6144]{1,0:T(8,128)(2,1)S(1)}, u32[]{:S(2)}, u32[]{:S(2)}) collective-permute-start(bf16[40,6144]{1,0:T(8,128)(2,1)S(1)} %get-tuple-element.103), channel_id=1, source_target_pairs={{2,3},{3,2},{6,7},{7,6},{10,11},{11,10},{14,15},{15,14},{12,13},{1... | collective-permute-start | bytes 1474568 | tf_op jit(solution)/shard_map/ppermute | solution.py:412
  6.0 13.5 %collective-permute-start.4 = (bf16[40,6144]{1,0:T(8,128)(2,1)S(1)}, bf16[40,6144]{1,0:T(8,128)(2,1)S(1)}, u32[]{:S(2)}, u32[]{:S(2)}) collective-permute-start(bf16[40,6144]{1,0:T(8,128)(2,1)S(1)} %get-tuple-element.104), channel_id=1, source_target_pairs={{2,3},{3,2},{6,7},{7,6},{10,11},{11,10},{14,15},{15,14},{12,13},{1... | collective-permute-start | bytes 1474568 | tf_op jit(solution)/shard_map/ppermute | solution.py:412
  38.2 32.8 %collective-permute-start.5 = (bf16[40,18432]{1,0:T(8,128)(2,1)S(1)}, bf16[40,18432]{1,0:T(8,128)(2,1)S(1)}, u32[]{:S(2)}, u32[]{:S(2)}) collective-permute-start(bf16[40,18432]{1,0:T(8,128)(2,1)S(1)} %collective-permute-done.refs_0_.refs_3_.refs_6_), channel_id=1, source_target_pairs={{2,6},{3,7},{6,10},{7,11},{10,14},{11,15},{14,12},{15,13},{12,8},{... | collective-permute-start | bytes 4423688 | tf_op jit(solution)/shard_map/ppermute | solution.py:415
  39.8 32.6 %collective-permute-start.6 = (bf16[40,18432]{1,0:T(8,128)(2,1)S(1)}, bf16[40,18432]{1,0:T(8,128)(2,1)S(1)}, u32[]{:S(2)}, u32[]{:S(2)}) collective-permute-start(bf16[40,18432]{1,0:T(8,128)(2,1)S(1)} %collective-permute-done.1.refs_1_.refs_4_.refs_7_), channel_id=1, source_target_pairs={{6,2},{7,3},{10,6},{11,7},{14,10},{15,11},{12,14},{13,15},{8,12},{... | collective-permute-start | bytes 4423688 | tf_op jit(solution)/shard_map/ppermute | solution.py:418
  42.1 4.9 %collective-permute-start.9 = (bf16[80,6144]{1,0:T(8,128)(2,1)S(1)}, bf16[80,6144]{1,0:T(8,128)(2,1)S(1)}, u32[]{:S(2)}, u32[]{:S(2)}) collective-permute-start(bf16[80,6144]{1,0:T(8,128)(2,1)S(1)} %get-tuple-element.112), channel_id=1, source_target_pairs={{2,3},{3,2},{6,7},{7,6},{10,11},{11,10},{14,15},{15,14},{12,13},{1... | collective-permute-start | bytes 2949128 | tf_op jit(solution)/shard_map/ppermute | solution.py:412
  53.4 16.2 %collective-permute-start.11 = (f32[2,80,512]{2,1,0:T(8,128)S(1)}, f32[2,80,512]{2,1,0:T(8,128)S(1)}, u32[]{:S(2)}, u32[]{:S(2)}) collective-permute-start(f32[2,80,512]{2,1,0:T(8,128)S(1)} %get-tuple-element.115), channel_id=1, source_target_pairs={{0,16},{16,0},{1,17},{17,1},{2,18},{18,2},{3,19},{19,3},{4,20},{20... | collective-permute-start | bytes 983048 | tf_op jit(solution)/shard_map/ppermute | solution.py:406
  54.9 14.6 %collective-permute-start.7 = (f32[2,40,512]{2,1,0:T(8,128)S(1)}, f32[2,40,512]{2,1,0:T(8,128)S(1)}, u32[]{:S(2)}, u32[]{:S(2)}) collective-permute-start(f32[2,40,512]{2,1,0:T(8,128)S(1)} %get-tuple-element.110), channel_id=1, source_target_pairs={{0,16},{16,0},{1,17},{17,1},{2,18},{18,2},{3,19},{19,3},{4,20},{20... | collective-permute-start | bytes 491528 | tf_op jit(solution)/shard_map/ppermute | solution.py:406
  55.5 14.1 %collective-permute-start.12 = (f32[2,32,512]{2,1,0:T(8,128)S(1)}, f32[2,32,512]{2,1,0:T(8,128)S(1)}, u32[]{:S(2)}, u32[]{:S(2)}) collective-permute-start(f32[2,32,512]{2,1,0:T(8,128)S(1)} %grams.1.refs_6_.refs_2_.refs_4_), channel_id=1, source_target_pairs={{0,16},{16,0},{1,17},{17,1},{2,18},{18,2},{3,19},{19,3},{4,20},{20... | collective-permute-start | bytes 393224 | tf_op jit(solution)/shard_map/ppermute | solution.py:406
  72.4 31.6 %collective-permute-start.13 = (bf16[40,18432]{1,0:T(8,128)(2,1)S(1)}, bf16[40,18432]{1,0:T(8,128)(2,1)S(1)}, u32[]{:S(2)}, u32[]{:S(2)}) collective-permute-start(bf16[40,18432]{1,0:T(8,128)(2,1)S(1)} %collective-permute-done.5.refs_0_.refs_3_.refs_6_), channel_id=1, source_target_pairs={{2,6},{3,7},{6,10},{7,11},{10,14},{11,15},{14,12},{15,13},{12,8},{... | collective-permute-start | bytes 4423688 | tf_op jit(solution)/shard_map/ppermute | solution.py:415
  74.0 31.4 %collective-permute-start.14 = (bf16[40,18432]{1,0:T(8,128)(2,1)S(1)}, bf16[40,18432]{1,0:T(8,128)(2,1)S(1)}, u32[]{:S(2)}, u32[]{:S(2)}) collective-permute-start(bf16[40,18432]{1,0:T(8,128)(2,1)S(1)} %collective-permute-done.6.refs_1_.refs_4_.refs_7_), channel_id=1, source_target_pairs={{6,2},{7,3},{10,6},{11,7},{14,10},{15,11},{12,14},{13,15},{8,12},{... | collective-permute-start | bytes 4423688 | tf_op jit(solution)/shard_map/ppermute | solution.py:418
  76.2 4.9 %collective-permute-start.17 = (bf16[80,6144]{1,0:T(8,128)(2,1)S(1)}, bf16[80,6144]{1,0:T(8,128)(2,1)S(1)}, u32[]{:S(2)}, u32[]{:S(2)}) collective-permute-start(bf16[80,6144]{1,0:T(8,128)(2,1)S(1)} %get-tuple-element.121), channel_id=1, source_target_pairs={{2,3},{3,2},{6,7},{7,6},{10,11},{11,10},{14,15},{15,14},{12,13},{1... | collective-permute-start | bytes 2949128 | tf_op jit(solution)/shard_map/ppermute | solution.py:412
  87.5 9.8 %collective-permute-start.18 = (f32[2,80,512]{2,1,0:T(8,128)S(1)}, f32[2,80,512]{2,1,0:T(8,128)S(1)}, u32[]{:S(2)}, u32[]{:S(2)}) collective-permute-start(f32[2,80,512]{2,1,0:T(8,128)S(1)} %get-tuple-element.133), channel_id=1, source_target_pairs={{0,16},{16,0},{1,17},{17,1},{2,18},{18,2},{3,19},{19,3},{4,20},{20... | collective-permute-start | bytes 983048 | tf_op jit(solution)/shard_map/ppermute | solution.py:406
  107.1 4.9 %collective-permute-start.23 = (bf16[80,6144]{1,0:T(8,128)(2,1)S(1)}, bf16[80,6144]{1,0:T(8,128)(2,1)S(1)}, u32[]{:S(2)}, u32[]{:S(2)}) collective-permute-start(bf16[80,6144]{1,0:T(8,128)(2,1)S(1)} %get-tuple-element.142), channel_id=1, source_target_pairs={{2,3},{3,2},{6,7},{7,6},{10,11},{11,10},{14,15},{15,14},{12,13},{1... | collective-permute-start | bytes 2949128 | tf_op jit(solution)/shard_map/ppermute | solution.py:412
  107.3 18.9 %collective-permute-start.19 = (bf16[40,9216]{1,0:T(8,128)(2,1)S(1)}, bf16[40,9216]{1,0:T(8,128)(2,1)S(1)}, u32[]{:S(2)}, u32[]{:S(2)}) collective-permute-start(bf16[40,9216]{1,0:T(8,128)(2,1)S(1)} %get-tuple-element.138), channel_id=1, source_target_pairs={{2,6},{3,7},{6,10},{7,11},{10,14},{11,15},{14,12},{15,13},{12,8},{... | collective-permute-start | bytes 2211848 | tf_op jit(solution)/shard_map/ppermute | solution.py:415
  109.0 18.6 %collective-permute-start.20 = (bf16[40,9216]{1,0:T(8,128)(2,1)S(1)}, bf16[40,9216]{1,0:T(8,128)(2,1)S(1)}, u32[]{:S(2)}, u32[]{:S(2)}) collective-permute-start(bf16[40,9216]{1,0:T(8,128)(2,1)S(1)} %get-tuple-element.139), channel_id=1, source_target_pairs={{6,2},{7,3},{10,6},{11,7},{14,10},{15,11},{12,14},{13,15},{8,12},{... | collective-permute-start | bytes 2211848 | tf_op jit(solution)/shard_map/ppermute | solution.py:418
  118.4 9.8 %collective-permute-start.24 = (f32[2,80,512]{2,1,0:T(8,128)S(1)}, f32[2,80,512]{2,1,0:T(8,128)S(1)}, u32[]{:S(2)}, u32[]{:S(2)}) collective-permute-start(f32[2,80,512]{2,1,0:T(8,128)S(1)} %get-tuple-element.152), channel_id=1, source_target_pairs={{0,16},{16,0},{1,17},{17,1},{2,18},{18,2},{3,19},{19,3},{4,20},{20... | collective-permute-start | bytes 983048 | tf_op jit(solution)/shard_map/ppermute | solution.py:406
  128.3 4.0 %collective-permute-start.25 = (bf16[40,9216]{1,0:T(8,128)(2,1)S(1)}, bf16[40,9216]{1,0:T(8,128)(2,1)S(1)}, u32[]{:S(2)}, u32[]{:S(2)}) collective-permute-start(bf16[40,9216]{1,0:T(8,128)(2,1)S(1)} %collective-permute-done.19.refs_0_), channel_id=1, source_target_pairs={{2,3},{3,2},{6,7},{7,6},{10,11},{11,10},{14,15},{15,14},{12,13},{1... | collective-permute-start | bytes 2211848 | tf_op jit(solution)/shard_map/ppermute | solution.py:412
  129.7 6.1 %collective-permute-start.28 = (f32[200,16]{1,0:T(8,128)S(1)}, f32[200,16]{1,0:T(8,128)S(1)}, u32[]{:S(2)}, u32[]{:S(2)}) collective-permute-start(f32[200,16]{1,0:T(8,128)S(1)} %score.2.refs_6_), channel_id=1, source_target_pairs={{0,16},{16,0},{1,17},{17,1},{2,18},{18,2},{3,19},{19,3},{4,20},{20... | collective-permute-start | bytes 38408 | tf_op jit(solution)/shard_map/ppermute | solution.py:406
  131.7 4.1 %collective-permute-start.29 = (f32[80,16]{1,0:T(8,128)S(1)}, f32[80,16]{1,0:T(8,128)S(1)}, u32[]{:S(2)}, u32[]{:S(2)}) collective-permute-start(f32[80,16]{1,0:T(8,128)S(1)} %score.3.refs_8_), channel_id=1, source_target_pairs={{0,16},{16,0},{1,17},{17,1},{2,18},{18,2},{3,19},{19,3},{4,20},{20... | collective-permute-start | bytes 15368 | tf_op jit(solution)/shard_map/ppermute | solution.py:406
  140.1 7.2 %collective-permute-start.30 = (f32[80,512]{1,0:T(8,128)S(1)}, f32[80,512]{1,0:T(8,128)S(1)}, u32[]{:S(2)}, u32[]{:S(2)}) collective-permute-start(f32[80,512]{1,0:T(8,128)S(1)} %project_last.3.refs_2_), channel_id=1, source_target_pairs={{0,16},{16,0},{1,17},{17,1},{2,18},{18,2},{3,19},{19,3},{4,20},{20... | collective-permute-start | bytes 491528 | tf_op jit(solution)/shard_map/ppermute | solution.py:406
  141.3 7.7 %collective-permute-start.27 = (f32[80,512]{1,0:T(8,128)S(1)}, f32[80,512]{1,0:T(8,128)S(1)}, u32[]{:S(2)}, u32[]{:S(2)}) collective-permute-start(f32[80,512]{1,0:T(8,128)S(1)} %project_last.2.refs_0_), channel_id=1, source_target_pairs={{0,16},{16,0},{1,17},{17,1},{2,18},{18,2},{3,19},{19,3},{4,20},{20... | collective-permute-start | bytes 491528 | tf_op jit(solution)/shard_map/ppermute | solution.py:406
  (7 other events, 24.1 us)

commit v3 on v2

v3 whole, which is shorter than its diff:
```python
import functools
import math

import jax
import jax.numpy as jnp
from jax import lax
from jax.experimental import pallas as pl
from jax.experimental.pallas import tpu as pltpu
from jax.sharding import PartitionSpec as P

RANK = 32
WIDE = 256
LIGHT = pl.CostEstimate(flops=1, bytes_accessed=1, transcendentals=0)
ROOM = 16 << 20


def params():
    return pltpu.CompilerParams(vmem_limit_bytes=ROOM)


def in_hbm(x):
    return pltpu.with_memory_space_constraint(x, pltpu.HBM)


def in_vmem(x):
    return pltpu.with_memory_space_constraint(x, pltpu.VMEM)


def cycle_of(first, second):
    if min(first, second) == 1:
        size = first * second
        order = list(range(0, size, 2)) + list(range(1, size, 2))[::-1]
        return [(i, 0) if second == 1 else (0, i) for i in order]
    if first % 2:
        return [(a, b) for b, a in cycle_of(second, first)] if second % 2 == 0 else [
            (a, b) for a in range(first) for b in range(second)]
    walk = []
    for a in range(first):
        inner = range(1, second)
        walk += [(a, b) for b in (inner if a % 2 == 0 else reversed(inner))]
    return walk + [(a, 0) for a in reversed(range(first))]


def ring_of(mesh):
    devices = list(mesh.devices[0])
    chips = {}
    for index, device in enumerate(devices):
        coords = getattr(device, "coords", None)
        key = tuple(coords) if coords is not None else (index // 2,)
        chips.setdefault(key, []).append(index)
    keys = list(chips)
    values = [sorted({k[i] for k in keys}) for i in range(len(keys[0]))]
    varying = [i for i in range(len(values)) if len(values[i]) > 1]
    if len(varying) == 2 and len(keys) == len(values[varying[0]]) * len(values[varying[1]]):
        one, two = sorted(varying, key=lambda i: -len(values[i]))
        at = {(values[one].index(k[one]), values[two].index(k[two])): k for k in keys}
        keys = [at[place] for place in cycle_of(len(values[one]), len(values[two]))]
    ring = [chips[k] for k in keys]
    assert all(pair[0] % 2 == 0 and pair[1] == pair[0] + 1 for pair in ring)
    return ring


def load_kernel(a_ref, b_ref, a_out, b_out, sem):
    first = pltpu.make_async_copy(a_ref, a_out, sem.at[0])
    second = pltpu.make_async_copy(b_ref, b_out, sem.at[1])
    first.start()
    second.start()
    first.wait()
    second.wait()


def load(a, b):
    return pl.pallas_call(
        load_kernel,
        in_specs=[pl.BlockSpec(memory_space=pl.ANY)] * 2,
        out_specs=[pl.BlockSpec(memory_space=pltpu.VMEM)] * 2,
        out_shape=[pltpu.VMEM(a.shape, a.dtype), pltpu.VMEM(b.shape, b.dtype)],
        scratch_shapes=[pltpu.SemaphoreType.DMA((2,))],
        compiler_params=params(),
        cost_estimate=LIGHT,
        name="load_factors",
    )(in_hbm(a), in_hbm(b))


def join_kernel(a_ref, b_ref, out_ref, sem):
    width = a_ref.shape[1]
    first = pltpu.make_async_copy(a_ref, out_ref.at[:, :width], sem.at[0])
    second = pltpu.make_async_copy(b_ref, out_ref.at[:, width:], sem.at[1])
    first.start()
    second.start()
    first.wait()
    second.wait()


def joined(a, b):
    return pl.pallas_call(
        join_kernel,
        in_specs=[pl.BlockSpec(memory_space=pl.ANY)] * 2,
        out_specs=pl.BlockSpec(memory_space=pl.ANY),
        out_shape=jax.ShapeDtypeStruct((a.shape[0], a.shape[1] + b.shape[1]), a.dtype),
        scratch_shapes=[pltpu.SemaphoreType.DMA((2,))],
        compiler_params=params(),
        cost_estimate=LIGHT,
        name="join",
    )(in_hbm(a), in_hbm(b))


def pack_kernel(count, parts, step, *refs):
    arrays, outs = refs[:count], refs[count:]
    i = pl.program_id(0)
    for out, (first, steps) in zip(outs, parts):

        @pl.when((i >= first) & (i < first + steps))
        def _(out=out):
            out[...] = jnp.concatenate([x[...] for x in arrays], axis=0)


def packed(arrays, bounds, step):
    rows = sum(a.shape[0] for a in arrays)
    parts = tuple((lo // step, (hi - lo) // step) for lo, hi in zip(bounds, bounds[1:]))
    return pl.pallas_call(
        functools.partial(pack_kernel, len(arrays), parts, step),
        grid=(bounds[-1] // step,),
        in_specs=[pl.BlockSpec((a.shape[0], step), lambda i: (0, i)) for a in arrays],
        out_specs=[
            pl.BlockSpec((rows, step), lambda i, first=first, steps=steps: (0, jnp.clip(i - first, 0, steps - 1)))
            for first, steps in parts],
        out_shape=[jax.ShapeDtypeStruct((rows, hi - lo), arrays[0].dtype) for lo, hi in zip(bounds, bounds[1:])],
        compiler_params=params(),
        cost_estimate=LIGHT,
        name="pack",
    )(*arrays)


def cut_kernel(ranges, a_ref, b_ref, *refs):
    outs, sem = refs[:-1], refs[-1]
    copies = [
        pltpu.make_async_copy((a_ref, b_ref)[which].at[:, lo:hi], out, sem.at[index])
        for index, (out, (which, lo, hi)) in enumerate(zip(outs, ranges))]
    for copy in copies:
        copy.start()
    for copy in copies:
        copy.wait()


def column_ranges(a, b, ranges):
    return pl.pallas_call(
        functools.partial(cut_kernel, tuple(ranges)),
        in_specs=[pl.BlockSpec(memory_space=pl.ANY)] * 2,
        out_specs=[pl.BlockSpec(memory_space=pl.ANY)] * len(ranges),
        out_shape=[jax.ShapeDtypeStruct((a.shape[0], hi - lo), a.dtype) for _, lo, hi in ranges],
        scratch_shapes=[pltpu.SemaphoreType.DMA((len(ranges),))],
        compiler_params=params(),
        cost_estimate=LIGHT,
        name="cut",
    )(a, b)


def gram_kernel(step, a_ref, b_ref, out_ref, sums):
    columns = a_ref.shape[1]
    row = lax.broadcasted_iota(jnp.int32, (WIDE, WIDE), 0) // RANK
    col = lax.broadcasted_iota(jnp.int32, (WIDE, WIDE), 1) // RANK
    for index, ref in enumerate((a_ref, b_ref)):
        sums[...] = jnp.zeros_like(sums)

        @pl.loop(0, ref.shape[0] // step)
        def _(i, ref=ref):
            for start in range(0, columns, WIDE):
                block = ref[pl.ds(pl.multiple_of(i * step, step), step), start : start + WIDE]
                sums[:, start : start + WIDE] += lax.dot_general(
                    block, block, (((0,), (0,)), ((), ())), preferred_element_type=jnp.float32)

        for start in range(0, columns, WIDE):
            kept = jnp.where(row == col, sums[:, start : start + WIDE], 0.0)
            out_ref[index, :, start : start + WIDE] = kept.reshape(WIDE // RANK, RANK, WIDE).sum(axis=0)


def grams(a, b):
    columns = a.shape[1]
    step = math.gcd(a.shape[0], b.shape[0])
    return pl.pallas_call(
        functools.partial(gram_kernel, step),
        in_specs=[pl.BlockSpec(memory_space=pltpu.VMEM)] * 2,
        out_specs=pl.BlockSpec(memory_space=pltpu.VMEM),
        out_shape=jax.ShapeDtypeStruct((2, RANK, columns), jnp.float32),
        scratch_shapes=[pltpu.VMEM((WIDE, columns), jnp.float32)],
        compiler_params=params(),
        cost_estimate=LIGHT,
        name="grams",
    )(a, b)


def chunk_of(*sizes):
    step = functools.reduce(math.gcd, sizes)
    for least in (1024, 512, 256, 128):
        if step % least == 0:
            return least
    return step


def project_kernel(step, spans, count, *refs):
    factors, out_ref = refs[count : count + 2], refs[-1]
    i = pl.program_id(0)

    @pl.when(i == 0)
    def _():
        out_ref[...] = jnp.zeros_like(out_ref)

    for held, first, steps, which, offset in spans:

        @pl.when((i >= first) & (i < first + steps))
        def _(held=held, which=which, offset=offset, first=first):
            x = jnp.concatenate([refs[h][...] for h in held], axis=0)
            at = pl.multiple_of((i - first) * step + offset, step)
            out_ref[...] += jnp.dot(x, factors[which][pl.ds(at, step), :], preferred_element_type=jnp.float32)


def project(groups, factors, step):
    specs, operands, spans, first = [], [], [], 0
    for arrays, group in groups:
        held = tuple(range(len(operands), len(operands) + len(arrays)))
        low = min(begin for begin, _, _, _ in group) // step
        high = max(begin + width for begin, width, _, _ in group) // step
        for array, base in arrays:
            specs.append(pl.BlockSpec(
                (array.shape[0], step),
                lambda i, first=first, low=low, high=high, base=base // step:
                    (0, base + jnp.clip(i - first + low, low, high - 1))))
            operands.append(array)
        for begin, width, which, offset in group:
            spans.append((held, first + begin // step - low, width // step, which, offset))
        first += high - low
    shape = (sum(a.shape[0] for a, _ in groups[0][0]), factors[0].shape[1])
    return pl.pallas_call(
        functools.partial(project_kernel, step, tuple(spans), len(operands)),
        grid=(first,),
        in_specs=specs + [pl.BlockSpec(memory_space=pltpu.VMEM)] * 2,
        out_specs=pl.BlockSpec(shape, lambda i: (0, 0)),
        out_shape=jax.ShapeDtypeStruct(shape, jnp.float32),
        compiler_params=params(),
        cost_estimate=LIGHT,
        name="project",
    )(*operands, *[in_vmem(f) for f in factors])


def by_query(x):
    columns = x.shape[1]
    queries = columns // RANK
    member = (lax.broadcasted_iota(jnp.int32, (columns, queries), 0) // RANK) == lax.broadcasted_iota(
        jnp.int32, (columns, queries), 1)
    return jnp.dot(
        x, member.astype(jnp.float32), precision=lax.Precision.HIGHEST, preferred_element_type=jnp.float32)


def total_of(refs):
    return sum(ref[...] for ref in refs[1:]) + refs[0][...]


def project_last_kernel(pieces, more, pairs, *refs):
    count = sum(arrays for arrays, _ in pieces)
    tokens, factors, out_ref, sums = refs[:count], refs[count : count + 2], refs[-2], refs[-1]
    sums[...] = refs[count + 2][...] if more else jnp.zeros_like(sums)
    taken = 0
    for arrays, spans in pieces:
        held = tokens[taken : taken + arrays]
        taken += arrays
        for begin, width, which, offset in spans:
            step = chunk_of(width)

            @pl.loop(0, width // step)
            def _(i, held=held, begin=begin, which=which, offset=offset, step=step):
                at = pl.ds(pl.multiple_of(i * step + begin, 128), step)
                x = jnp.concatenate([h[:, at] for h in held], axis=0)
                w = factors[which][pl.ds(pl.multiple_of(i * step + offset, 128), step), :]
                sums[...] += jnp.dot(x, w, preferred_element_type=jnp.float32)

    if pairs:
        out_ref[...] = by_query(sums[...] * total_of(refs[count + 2 + more : -2]))
    else:
        out_ref[...] = sums[...]


def project_last(groups, factors, start=None, pairs=()):
    pieces = tuple((len(arrays), tuple(spans)) for arrays, spans in groups)
    operands = [a for arrays, _ in groups for a in arrays]
    rows, columns = sum(a.shape[0] for a in groups[0][0]), factors[0].shape[1]
    given = [in_vmem(x) for x in (*operands, *factors)]
    given += ([] if start is None else [start]) + list(pairs)
    return pl.pallas_call(
        functools.partial(project_last_kernel, pieces, int(start is not None), len(pairs)),
        in_specs=[pl.BlockSpec(memory_space=pltpu.VMEM)] * len(given),
        out_specs=pl.BlockSpec(memory_space=pltpu.VMEM),
        out_shape=jax.ShapeDtypeStruct((rows, columns // RANK if pairs else columns), jnp.float32),
        scratch_shapes=[pltpu.VMEM((rows, columns), jnp.float32)],
        compiler_params=params(),
        cost_estimate=LIGHT,
        name="project_last",
    )(*given)


def score_kernel(count, *refs):
    out_ref = refs[-1]
    found = []
    for at in range(0, len(refs) - 1, 1 + count):
        found.append(by_query(refs[at][...] * total_of(refs[at + 1 : at + 1 + count])))
    out_ref[...] = jnp.concatenate(found, axis=0).T


def score(groups):
    rows, columns = sum(one.shape[0] for one, _ in groups), groups[0][0].shape[1]
    return pl.pallas_call(
        functools.partial(score_kernel, len(groups[0][1])),
        out_shape=jax.ShapeDtypeStruct((columns // RANK, rows), jnp.float32),
        compiler_params=params(),
        cost_estimate=LIGHT,
        name="score",
    )(*[x for one, parts in groups for x in (one, *parts)])


def inverse_kernel(*refs):
    gram, out_ref = total_of(refs[:-1]), refs[-1]
    norms = jnp.broadcast_to((gram[0] * gram[1]).sum(axis=0, keepdims=True), (8, gram.shape[2]))
    out_ref[...] = 1.0 / jnp.sqrt(by_query(norms) + 1e-06)


def inverse_norms(parts):
    return pl.pallas_call(
        inverse_kernel,
        out_shape=jax.ShapeDtypeStruct((8, parts[0].shape[2] // RANK), jnp.float32),
        compiler_params=params(),
        cost_estimate=LIGHT,
        name="inverse_norms",
    )(*parts)


def looked_up(table, index):
    return sum(jnp.where(index == i, value, 0) for i, value in enumerate(table))


def last_kernel(count, groups, place, tokens, at_ref, inverse_ref, *refs):
    out_ref, held = refs[-2:]
    chips = len(place)
    for at, distances in enumerate(groups):
        scores = total_of(refs[at * count : (at + 1) * count]).T * inverse_ref[:1]
        first = 0
        for group in distances:
            for c in range(2):
                for distance in group:
                    held[distance % chips, c] = scores[first : first + tokens]
                    first += tokens
    core, side = at_ref[0], at_ref[1]
    here = looked_up(place, core // 2)
    own = core % 2
    share = out_ref.shape[1] // (2 * tokens)
    blocks = []
    for j in range(share):
        there = looked_up(place, side * share + j)
        distance = there - here
        distance = jnp.where(distance < 0, distance + chips, distance)
        blocks += [held[distance, (own + c) % 2] for c in range(2)]
    out_ref[...] = jnp.concatenate(blocks, axis=0).T


def last(results, inverse, groups, place, tokens, share, at):
    queries = inverse.shape[1]
    return pl.pallas_call(
        functools.partial(last_kernel, len(results[0]), groups, place, tokens),
        in_specs=[pl.BlockSpec(memory_space=pltpu.SMEM)]
        + [pl.BlockSpec(memory_space=pltpu.VMEM)] * (1 + sum(len(parts) for parts in results)),
        out_specs=pl.BlockSpec(memory_space=pltpu.VMEM),
        out_shape=jax.ShapeDtypeStruct((queries, share), jnp.float32),
        scratch_shapes=[pltpu.VMEM((len(place), 2, tokens, queries), jnp.float32)],
        compiler_params=params(),
        cost_estimate=LIGHT,
        name="last_scores",
    )(at, inverse, *[x for parts in results for x in parts])


def within(spans, low, high):
    kept = []
    for begin, width, which, offset in spans:
        a, b = max(begin, low), min(begin + width, high)
        if a < b:
            kept.append((a - low, b - a, which, offset + a - begin))
    return kept


def solution(mesh):
    rows = mesh.shape["rows"]
    query = mesh.shape["query"]
    ring = ring_of(mesh)
    chips = len(ring)
    forward = [(a, b) for i in range(chips) for a, b in zip(ring[i], ring[(i + 1) % chips])]
    backward = [(b, a) for a, b in forward]
    mates = [(pair[i], pair[1 - i]) for pair in ring for i in range(2)]
    place = [0] * chips
    for i, pair in enumerate(ring):
        place[pair[0] // 2] = i
    place = tuple(place)

    def swap_rows(x):
        return lax.ppermute(x, "rows", [(0, 1), (1, 0)])

    def across(x):
        return [x, swap_rows(x)] if rows == 2 else [lax.psum(x, "rows")]

    def mate(xs):
        return [lax.ppermute(x, "query", mates) for x in xs]

    def ahead(x):
        return lax.ppermute(x, "query", forward)

    def behind(x):
        return lax.ppermute(x, "query", backward)

    def both(pair):
        return [ahead(pair[0]), behind(pair[1])]

    def tied(*trees):
        return lax.optimization_barrier(trees)

    def local(acts, grads, in_factors, out_factors):
        tokens, width = acts.shape
        depth = grads.shape[1]
        total = width + depth
        step = math.gcd(width, depth)
        while step > 2048 and step % 2 == 0:
            step //= 2
        bounds = [0, depth, depth + width // 2 // step * step, total]
        span = [(0, depth, 1, 0), (depth, width, 0, 0)]
        at = jnp.stack([lax.axis_index("query"), lax.axis_index("rows")]).astype(jnp.int32)
        full_hops = (chips - 1) // 2

        def projected(held):
            swapped = mate(packed(held, bounds, step))
            groups = [
                ([(x, lo) for x in held] + [(part, 0)], within(span, lo, hi))
                for lo, hi, part in zip(bounds, bounds[1:], swapped)]
            return project(groups[1:], factors, step), across(project(groups[:1], factors, step))

        at, acts, grads, in_factors, out_factors = tied(at, acts, grads, in_factors, out_factors)
        own = joined(grads, acts)
        fly = [ahead(own), behind(own)]
        factors = load(in_factors, out_factors)
        gram_parts = across(grams(*factors))
        pairs = [projected([own])]
        distances = [(0,)]
        fly[0], pairs, gram_parts = tied(fly[0], pairs, gram_parts)
        for hop in range(1, full_hops):
            held = list(fly)
            fly[0] = ahead(held[0])
            held = tied(*held)
            fly[1] = behind(held[1])
            pairs.append(projected(held))
            distances.append((-hop, hop))
            fly[0], pairs = tied(fly[0], pairs)
        held = list(fly)
        distances.append((-full_hops, full_hops))
        even = chips % 2 == 0
        if even:
            half = total // 256 * 128
            assert depth < half
            fly = column_ranges(*held, [(0, 0, half), (1, half, total)])
            fly = [ahead(fly[0]), behind(fly[1])]
        pairs.append(projected(held))
        inverse = inverse_norms(gram_parts)
        results = []
        if even:
            inverse, pairs = tied(inverse, pairs)
            early = across(score(pairs))
            low, high, inverse, early = tied(*fly, inverse, early)
            results.append(early)
            swapped = mate([low, high])
            one, two = [low, swapped[0]], [high, swapped[1]]
            other = across(project_last([(one, within(span, 0, depth))], factors))
            mine = project_last(
                [(one, [s for s in within(span, 0, half) if not s[2]]), (two, within(span, half, total))], factors)
            results.append(across(score([(mine, other)])))
            groups = (tuple(distances), ((chips // 2,),))
        else:
            results.append(across(score(pairs)))
            groups = (tuple(distances),)
        return last(results, inverse, groups, place, tokens, query * tokens // rows, at).T

    return jax.shard_map(
        local,
        mesh=mesh,
        in_specs=(P("query", "rows"), P("query", "rows"), P("rows", "query"), P("rows", "query")),
        out_specs=P("rows", "query"),
        check_vma=False,
    )
```

time: 151 us -> 142 us (0.940)
  waiting for transfers between devices: 74.1 us -> 67.8 us
  Pallas kernels: 52.4 us -> 49.8 us
    ppermute x9 -> x8, waiting for transfers between devices: 30.7 us -> 16.1 us  [swap_rows(): return lax.ppermute(x, 'rows', [(0, 1), (1, 0)])]
    ppermute x4, waiting for transfers between devices: 26 us -> 35.7 us  [ahead(): return lax.ppermute(x, 'query', forward)]
    pallas_call x4 -> x8, Pallas kernels: 25.1 us -> 21.7 us  [project(): pl.pallas_call(functools.partial(project_kernel, step, tuple(spans), len(...]
    ppermute x4, waiting for transfers between devices: 5.29 us -> 2.07 us  [behind(): return lax.ppermute(x, 'query', backward)]
    ppermute x14, waiting for transfers between devices: 12.1 us -> 13.9 us  [mate(): return [lax.ppermute(x, 'query', mates) for x in xs]]
    pallas_call x6 -> x7, Pallas kernels: 8.07 us -> 8.9 us  [the longest x2 5.56 us: project_last(): pl.pallas_call(functools.partial(project_last_kernel, pieces, int(start i...]
    ppermute x9 -> x8, starting transfers between devices: 10.9 us -> 11.4 us  [swap_rows(): return lax.ppermute(x, 'rows', [(0, 1), (1, 0)])]
  transfers between devices with their start and end apart: 31 -> 30, of which waited for: 22 -> 17; matrix products, arithmetic and copies ran while one was open for 0% -> 0% of each run, Pallas kernels for 29% -> 32%
where the time goes in v3:
time: 142 us
  waiting for transfers between devices  67.8 us (48%)
  Pallas kernels  49.8 us (35%)
  starting transfers between devices  23.8 us (17%)
    ppermute x4, waiting for transfers between devices, ahead(): return lax.ppermute(x, 'query', forward)  35.7 us
    pallas_call x8, Pallas kernels, project(): pl.pallas_call(functools.partial(project_kernel, step, tuple(spans), len(...  21.7 us
    ppermute x8, waiting for transfers between devices, swap_rows(): return lax.ppermute(x, 'rows', [(0, 1), (1, 0)])  16.1 us
    ppermute x14, waiting for transfers between devices, mate(): return [lax.ppermute(x, 'query', mates) for x in xs]  13.9 us
    ppermute x8, starting transfers between devices, swap_rows(): return lax.ppermute(x, 'rows', [(0, 1), (1, 0)])  11.4 us
    ppermute x4, starting transfers between devices, ahead(): return lax.ppermute(x, 'query', forward)  7.7 us
    pallas_call x1, Pallas kernels, grams(): pl.pallas_call(functools.partial(gram_kernel, step), in_specs=[pl.BlockSp...  6.97 us
    pallas_call x1, Pallas kernels, load(): pl.pallas_call(load_kernel, in_specs=[pl.BlockSpec(memory_space=pl.ANY)]...  6.38 us
  transfers between devices with their start and end apart: 30, of which 17 were waited for; matrix products, arithmetic and copies ran while one was open for 0% of the time, Pallas kernels for 32%

profile of v3, /device:TPU:0, one launch (start us, length us, event | category | flops | bytes accessed | tf_op | source)
XLA Modules:
  0.0 141.7 jit_solution(8681338899516041423)
XLA Ops:
  1.5 3.0 %collective-permute-start = (bf16[40,18432]{1,0:T(8,128)(2,1)S(1)}, bf16[40,18432]{1,0:T(8,128)(2,1)S(1)}, u32[]{:S(2)}, u32[]{:S(2)}) collective-permute-start(bf16[40,18432]{1,0:T(8,128)(2,1)S(1)} %join.1.refs_0_.refs_2_), channel_id=1, source_target_pairs={{2,6},{3,7},{6,10},{7,11},{10,14},{11,15},{14,12},{15,13},{12,8},{... | collective-permute-start | bytes 4423688 | tf_op jit(solution)/shard_map/ppermute | solution.py:411
  6.1 6.4 %load_factors.1 = (bf16[14336,512]{1,0:T(8,128)(2,1)S(1)}, bf16[4096,512]{1,0:T(8,128)(2,1)S(1)}) custom-call(bf16[14336,512]{1,0:T(8,128)(2,1)} %a_ref.1, bf16[4096,512]{1,0:T(8,128)(2,1)} %b_ref.1), custom_call_target="tpu_custom_call" | custom-call | flops 1 | bytes 1 | tf_op jit(solution)/shard_map/load_factors/pallas_call | solution.py:73
  13.6 1.9 %collective-permute-start.4 = (f32[80,512]{1,0:T(8,128)S(1)}, f32[80,512]{1,0:T(8,128)S(1)}, u32[]{:S(2)}, u32[]{:S(2)}) collective-permute-start(f32[80,512]{1,0:T(8,128)S(1)} %project.9.refs_1_), channel_id=1, source_target_pairs={{0,16},{16,0},{1,17},{17,1},{2,18},{18,2},{3,19},{19,3},{4,20},{20... | collective-permute-start | bytes 491528 | tf_op jit(solution)/shard_map/ppermute | solution.py:402
  15.6 7.0 %grams.1.refs_0_ = f32[2,32,512]{2,1,0:T(8,128)S(1)} custom-call(bf16[14336,512]{1,0:T(8,128)(2,1)S(1)} %get-tuple-element.78.refs_4_.refs_2_.a_ref.refs_6_.refs_3_, bf16[4096,512]{1,0:T(8,128)(2,1)S(1)} %get-tuple-element.79.refs_5_.refs_3_.b_ref.refs_7_.refs_4_), custom_call_target="tpu_custom_call" | custom-call | flops 1 | bytes 1 | tf_op jit(solution)/shard_map/grams/pallas_call | solution.py:181
  22.8 3.9 %project.8.refs_0_ = f32[80,512]{1,0:T(8,128)S(1)} custom-call(bf16[40,18432]{1,0:T(8,128)(2,1)S(1)} %join.1.refs_0_.refs_2_, bf16[40,6144]{1,0:T(8,128)(2,1)S(1)} %collective-permute-done.1.refs_1_, bf16[40,18432]{1,0:T(8,128)(2,1)S(1)} %join.1.refs_0_.refs_2_, bf16[40,8192]{1,0:T(8,128)(2,1)S(1)} %collective-permute-done.2.refs_3_, ...), custom_call_target="tpu_custom_call" | custom-call | flops 1 | bytes 1 | tf_op jit(solution)/shard_map/project/pallas_call | solution.py:234
  28.2 8.6 %collective-permute-done.refs_0_.refs_3_ = bf16[40,18432]{1,0:T(8,128)(2,1)S(1)} collective-permute-done((bf16[40,18432]{1,0:T(8,128)(2,1)S(1)}, bf16[40,18432]{1,0:T(8,128)(2,1)S(1)}, u32[]{:S(2)}, u32[]{:S(2)}) %collective-permute-start) | collective-permute-done | bytes 1474592 | tf_op jit(solution)/shard_map/ppermute | solution.py:411
  36.8 1.7 %collective-permute-start.6 = (bf16[40,18432]{1,0:T(8,128)(2,1)S(1)}, bf16[40,18432]{1,0:T(8,128)(2,1)S(1)}, u32[]{:S(2)}, u32[]{:S(2)}) collective-permute-start(bf16[40,18432]{1,0:T(8,128)(2,1)S(1)} %collective-permute-done.refs_0_.refs_3_), channel_id=1, source_target_pairs={{2,6},{3,7},{6,10},{7,11},{10,14},{11,15},{14,12},{15,13},{12,8},{... | collective-permute-start | bytes 4423688 | tf_op jit(solution)/shard_map/ppermute | solution.py:411
  40.7 4.8 %collective-permute-done.10.refs_2_ = bf16[80,4096]{1,0:T(8,128)(2,1)S(1)} collective-permute-done((bf16[80,4096]{1,0:T(8,128)(2,1)S(1)}, bf16[80,4096]{1,0:T(8,128)(2,1)S(1)}, u32[]{:S(2)}, u32[]{:S(2)}) %collective-permute-start.10) | collective-permute-done | bytes 655392 | tf_op jit(solution)/shard_map/ppermute | solution.py:408
  46.7 1.7 %collective-permute-start.11 = (f32[160,512]{1,0:T(8,128)S(1)}, f32[160,512]{1,0:T(8,128)S(1)}, u32[]{:S(2)}, u32[]{:S(2)}) collective-permute-start(f32[160,512]{1,0:T(8,128)S(1)} %project.11.refs_4_), channel_id=1, source_target_pairs={{0,16},{16,0},{1,17},{17,1},{2,18},{18,2},{3,19},{19,3},{4,20},{20... | collective-permute-start | bytes 983048 | tf_op jit(solution)/shard_map/ppermute | solution.py:402
  48.5 4.4 %project.10.refs_3_ = f32[160,512]{1,0:T(8,128)S(1)} custom-call(bf16[40,18432]{1,0:T(8,128)(2,1)S(1)} %collective-permute-done.refs_0_.refs_3_, bf16[40,18432]{1,0:T(8,128)(2,1)S(1)} %collective-permute-done.7.refs_1_.refs_4_, bf16[80,6144]{1,0:T(8,128)(2,1)S(1)} %collective-permute-done.8.refs_2_, ...), custom_call_target="tpu_custom_call" | custom-call | flops 1 | bytes 1 | tf_op jit(solution)/shard_map/project/pallas_call | solution.py:234
  52.8 3.7 %collective-permute-done.11.refs_5_ = f32[160,512]{1,0:T(8,128)S(1)} collective-permute-done((f32[160,512]{1,0:T(8,128)S(1)}, f32[160,512]{1,0:T(8,128)S(1)}, u32[]{:S(2)}, u32[]{:S(2)}) %collective-permute-start.11) | collective-permute-done | bytes 327712 | tf_op jit(solution)/shard_map/ppermute | solution.py:402
  56.6 13.7 %collective-permute-done.6.refs_0_.refs_3_ = bf16[40,18432]{1,0:T(8,128)(2,1)S(1)} collective-permute-done((bf16[40,18432]{1,0:T(8,128)(2,1)S(1)}, bf16[40,18432]{1,0:T(8,128)(2,1)S(1)}, u32[]{:S(2)}, u32[]{:S(2)}) %collective-permute-start.6) | collective-permute-done | bytes 1474592 | tf_op jit(solution)/shard_map/ppermute | solution.py:411
  74.2 4.8 %collective-permute-done.16.refs_2_ = bf16[80,4096]{1,0:T(8,128)(2,1)S(1)} collective-permute-done((bf16[80,4096]{1,0:T(8,128)(2,1)S(1)}, bf16[80,4096]{1,0:T(8,128)(2,1)S(1)}, u32[]{:S(2)}, u32[]{:S(2)}) %collective-permute-start.16) | collective-permute-done | bytes 655392 | tf_op jit(solution)/shard_map/ppermute | solution.py:408
  81.6 4.4 %project.12.refs_6_ = f32[160,512]{1,0:T(8,128)S(1)} custom-call(bf16[40,18432]{1,0:T(8,128)(2,1)S(1)} %collective-permute-done.6.refs_0_.refs_3_, bf16[40,18432]{1,0:T(8,128)(2,1)S(1)} %collective-permute-done.13.refs_1_.refs_4_, bf16[80,6144]{1,0:T(8,128)(2,1)S(1)} %collective-permute-done.14.refs_2_, ...), custom_call_target="tpu_custom_call" | custom-call | flops 1 | bytes 1 | tf_op jit(solution)/shard_map/project/pallas_call | solution.py:234
  86.0 4.0 %collective-permute-done.17.refs_8_ = f32[160,512]{1,0:T(8,128)S(1)} collective-permute-done((f32[160,512]{1,0:T(8,128)S(1)}, f32[160,512]{1,0:T(8,128)S(1)}, u32[]{:S(2)}, u32[]{:S(2)}) %collective-permute-start.17) | collective-permute-done | bytes 327712 | tf_op jit(solution)/shard_map/ppermute | solution.py:402
  90.0 12.8 %collective-permute-done.12.a_ref.refs_0_.refs_3_ = bf16[40,18432]{1,0:T(8,128)(2,1)S(1)} collective-permute-done((bf16[40,18432]{1,0:T(8,128)(2,1)S(1)}, bf16[40,18432]{1,0:T(8,128)(2,1)S(1)}, u32[]{:S(2)}, u32[]{:S(2)}) %collective-permute-start.12) | collective-permute-done | bytes 1474592 | tf_op jit(solution)/shard_map/ppermute | solution.py:411
  105.7 1.6 %collective-permute-start.19 = (bf16[40,9216]{1,0:T(8,128)(2,1)S(1)}, bf16[40,9216]{1,0:T(8,128)(2,1)S(1)}, u32[]{:S(2)}, u32[]{:S(2)}) collective-permute-start(bf16[40,9216]{1,0:T(8,128)(2,1)S(1)} %get-tuple-element.103), channel_id=1, source_target_pairs={{2,6},{3,7},{6,10},{7,11},{10,14},{11,15},{14,12},{15,13},{12,8},{... | collective-permute-start | bytes 2211848 | tf_op jit(solution)/shard_map/ppermute | solution.py:411
  107.7 2.6 %collective-permute-done.23.refs_2_ = bf16[80,4096]{1,0:T(8,128)(2,1)S(1)} collective-permute-done((bf16[80,4096]{1,0:T(8,128)(2,1)S(1)}, bf16[80,4096]{1,0:T(8,128)(2,1)S(1)}, u32[]{:S(2)}, u32[]{:S(2)}) %collective-permute-start.23) | collective-permute-done | bytes 655392 | tf_op jit(solution)/shard_map/ppermute | solution.py:408
  111.5 1.6 %collective-permute-start.24 = (f32[160,512]{1,0:T(8,128)S(1)}, f32[160,512]{1,0:T(8,128)S(1)}, u32[]{:S(2)}, u32[]{:S(2)}) collective-permute-start(f32[160,512]{1,0:T(8,128)S(1)} %project.15.refs_10_), channel_id=1, source_target_pairs={{0,16},{16,0},{1,17},{17,1},{2,18},{18,2},{3,19},{19,3},{4,20},{20... | collective-permute-start | bytes 983048 | tf_op jit(solution)/shard_map/ppermute | solution.py:402
  113.4 4.4 %project.14.refs_9_ = f32[160,512]{1,0:T(8,128)S(1)} custom-call(bf16[40,18432]{1,0:T(8,128)(2,1)S(1)} %collective-permute-done.12.a_ref.refs_0_.refs_3_, bf16[40,18432]{1,0:T(8,128)(2,1)S(1)} %collective-permute-done.18.b_ref.refs_1_.refs_4_, bf16[80,6144]{1,0:T(8,128)(2,1)S(1)} %collective-permute-done.21.refs_2_, ...), custom_call_target="tpu_custom_call" | custom-call | flops 1 | bytes 1 | tf_op jit(solution)/shard_map/project/pallas_call | solution.py:234
  117.8 3.6 %collective-permute-done.24.refs_11_ = f32[160,512]{1,0:T(8,128)S(1)} collective-permute-done((f32[160,512]{1,0:T(8,128)S(1)}, f32[160,512]{1,0:T(8,128)S(1)}, u32[]{:S(2)}, u32[]{:S(2)}) %collective-permute-start.24) | collective-permute-done | bytes 327712 | tf_op jit(solution)/shard_map/ppermute | solution.py:402
  127.1 1.7 %collective-permute-done.26.refs_1_ = bf16[40,9216]{1,0:T(8,128)(2,1)S(1)} collective-permute-done((bf16[40,9216]{1,0:T(8,128)(2,1)S(1)}, bf16[40,9216]{1,0:T(8,128)(2,1)S(1)}, u32[]{:S(2)}, u32[]{:S(2)}) %collective-permute-start.26) | collective-permute-done | bytes 737312 | tf_op jit(solution)/shard_map/ppermute | solution.py:408
  131.5 4.3 %project_last.2.refs_0_ = f32[80,512]{1,0:T(8,128)S(1)} custom-call(bf16[40,9216]{1,0:T(8,128)(2,1)S(1)} %collective-permute-done.19.refs_0_, bf16[40,9216]{1,0:T(8,128)(2,1)S(1)} %collective-permute-done.26.refs_1_, bf16[40,9216]{1,0:T(8,128)(2,1)S(1)} %collective-permute-done.20.refs_2_, bf16[40,9216]{1,0:T(8,128)(2,1)S(1)} %collective-permute-done.27.refs_3_, ...), custom_call_target="tpu_custom_call" | custom-call | flops 1 | bytes 1 | tf_op jit(solution)/shard_map/project_last/pallas_call | solution.py:289
  138.2 2.2 %collective-permute-done.29.refs_3_ = f32[16,80]{1,0:T(8,128)S(1)} collective-permute-done((f32[16,80]{1,0:T(8,128)S(1)}, f32[16,80]{1,0:T(8,128)S(1)}, u32[]{:S(2)}, u32[]{:S(2)}) %collective-permute-start.29) | collective-permute-done | bytes 5152 | tf_op jit(solution)/shard_map/ppermute | solution.py:402
  (59 shorter events, 32.7 us)
Async XLA Ops:
  1.5 35.4 %collective-permute-start = (bf16[40,18432]{1,0:T(8,128)(2,1)S(1)}, bf16[40,18432]{1,0:T(8,128)(2,1)S(1)}, u32[]{:S(2)}, u32[]{:S(2)}) collective-permute-start(bf16[40,18432]{1,0:T(8,128)(2,1)S(1)} %join.1.refs_0_.refs_2_), channel_id=1, source_target_pairs={{2,6},{3,7},{6,10},{7,11},{10,14},{11,15},{14,12},{15,13},{12,8},{... | collective-permute-start | bytes 4423688 | tf_op jit(solution)/shard_map/ppermute | solution.py:411
  4.5 34.0 %collective-permute-start.7 = (bf16[40,18432]{1,0:T(8,128)(2,1)S(1)}, bf16[40,18432]{1,0:T(8,128)(2,1)S(1)}, u32[]{:S(2)}, u32[]{:S(2)}) collective-permute-start(bf16[40,18432]{1,0:T(8,128)(2,1)S(1)} %join.1.refs_0_.refs_2_), channel_id=1, source_target_pairs={{6,2},{7,3},{10,6},{11,7},{14,10},{15,11},{12,14},{13,15},{8,12},{... | collective-permute-start | bytes 4423688 | tf_op jit(solution)/shard_map/ppermute | solution.py:414
  5.5 17.3 %collective-permute-start.2 = (bf16[40,8192]{1,0:T(8,128)(2,1)S(1)}, bf16[40,8192]{1,0:T(8,128)(2,1)S(1)}, u32[]{:S(2)}, u32[]{:S(2)}) collective-permute-start(bf16[40,8192]{1,0:T(8,128)(2,1)S(1)} %get-tuple-element.75), channel_id=1, source_target_pairs={{2,3},{3,2},{6,7},{7,6},{10,11},{11,10},{14,15},{15,14},{12,13},{1... | collective-permute-start | bytes 1966088 | tf_op jit(solution)/shard_map/ppermute | solution.py:408
  5.5 17.0 %collective-permute-start.1 = (bf16[40,6144]{1,0:T(8,128)(2,1)S(1)}, bf16[40,6144]{1,0:T(8,128)(2,1)S(1)}, u32[]{:S(2)}, u32[]{:S(2)}) collective-permute-start(bf16[40,6144]{1,0:T(8,128)(2,1)S(1)} %get-tuple-element.74), channel_id=1, source_target_pairs={{2,3},{3,2},{6,7},{7,6},{10,11},{11,10},{14,15},{15,14},{12,13},{1... | collective-permute-start | bytes 1474568 | tf_op jit(solution)/shard_map/ppermute | solution.py:408
  6.0 6.5 %collective-permute-start.3 = (bf16[40,4096]{1,0:T(8,128)(2,1)S(1)}, bf16[40,4096]{1,0:T(8,128)(2,1)S(1)}, u32[]{:S(2)}, u32[]{:S(2)}) collective-permute-start(bf16[40,4096]{1,0:T(8,128)(2,1)S(1)} %get-tuple-element.80), channel_id=1, source_target_pairs={{2,3},{3,2},{6,7},{7,6},{10,11},{11,10},{14,15},{15,14},{12,13},{1... | collective-permute-start | bytes 983048 | tf_op jit(solution)/shard_map/ppermute | solution.py:408
  13.6 14.6 %collective-permute-start.4 = (f32[80,512]{1,0:T(8,128)S(1)}, f32[80,512]{1,0:T(8,128)S(1)}, u32[]{:S(2)}, u32[]{:S(2)}) collective-permute-start(f32[80,512]{1,0:T(8,128)S(1)} %project.9.refs_1_), channel_id=1, source_target_pairs={{0,16},{16,0},{1,17},{17,1},{2,18},{18,2},{3,19},{19,3},{4,20},{20... | collective-permute-start | bytes 491528 | tf_op jit(solution)/shard_map/ppermute | solution.py:402
  22.6 5.6 %collective-permute-start.5 = (f32[2,32,512]{2,1,0:T(8,128)S(1)}, f32[2,32,512]{2,1,0:T(8,128)S(1)}, u32[]{:S(2)}, u32[]{:S(2)}) collective-permute-start(f32[2,32,512]{2,1,0:T(8,128)S(1)} %grams.1.refs_0_), channel_id=1, source_target_pairs={{0,16},{16,0},{1,17},{17,1},{2,18},{18,2},{3,19},{19,3},{4,20},{20... | collective-permute-start | bytes 393224 | tf_op jit(solution)/shard_map/ppermute | solution.py:402
  36.8 33.5 %collective-permute-start.6 = (bf16[40,18432]{1,0:T(8,128)(2,1)S(1)}, bf16[40,18432]{1,0:T(8,128)(2,1)S(1)}, u32[]{:S(2)}, u32[]{:S(2)}) collective-permute-start(bf16[40,18432]{1,0:T(8,128)(2,1)S(1)} %collective-permute-done.refs_0_.refs_3_), channel_id=1, source_target_pairs={{2,6},{3,7},{6,10},{7,11},{10,14},{11,15},{14,12},{15,13},{12,8},{... | collective-permute-start | bytes 4423688 | tf_op jit(solution)/shard_map/ppermute | solution.py:411
  38.5 33.2 %collective-permute-start.13 = (bf16[40,18432]{1,0:T(8,128)(2,1)S(1)}, bf16[40,18432]{1,0:T(8,128)(2,1)S(1)}, u32[]{:S(2)}, u32[]{:S(2)}) collective-permute-start(bf16[40,18432]{1,0:T(8,128)(2,1)S(1)} %collective-permute-done.7.refs_1_.refs_4_), channel_id=1, source_target_pairs={{6,2},{7,3},{10,6},{11,7},{14,10},{15,11},{12,14},{13,15},{8,12},{... | collective-permute-start | bytes 4423688 | tf_op jit(solution)/shard_map/ppermute | solution.py:414
  40.1 8.4 %collective-permute-start.9 = (bf16[80,8192]{1,0:T(8,128)(2,1)S(1)}, bf16[80,8192]{1,0:T(8,128)(2,1)S(1)}, u32[]{:S(2)}, u32[]{:S(2)}) collective-permute-start(bf16[80,8192]{1,0:T(8,128)(2,1)S(1)} %get-tuple-element.88), channel_id=1, source_target_pairs={{2,3},{3,2},{6,7},{7,6},{10,11},{11,10},{14,15},{15,14},{12,13},{1... | collective-permute-start | bytes 3932168 | tf_op jit(solution)/shard_map/ppermute | solution.py:408
  40.2 8.3 %collective-permute-start.8 = (bf16[80,6144]{1,0:T(8,128)(2,1)S(1)}, bf16[80,6144]{1,0:T(8,128)(2,1)S(1)}, u32[]{:S(2)}, u32[]{:S(2)}) collective-permute-start(bf16[80,6144]{1,0:T(8,128)(2,1)S(1)} %get-tuple-element.87), channel_id=1, source_target_pairs={{2,3},{3,2},{6,7},{7,6},{10,11},{11,10},{14,15},{15,14},{12,13},{1... | collective-permute-start | bytes 2949128 | tf_op jit(solution)/shard_map/ppermute | solution.py:408
  46.7 9.8 %collective-permute-start.11 = (f32[160,512]{1,0:T(8,128)S(1)}, f32[160,512]{1,0:T(8,128)S(1)}, u32[]{:S(2)}, u32[]{:S(2)}) collective-permute-start(f32[160,512]{1,0:T(8,128)S(1)} %project.11.refs_4_), channel_id=1, source_target_pairs={{0,16},{16,0},{1,17},{17,1},{2,18},{18,2},{3,19},{19,3},{4,20},{20... | collective-permute-start | bytes 983048 | tf_op jit(solution)/shard_map/ppermute | solution.py:402
  70.3 32.6 %collective-permute-start.12 = (bf16[40,18432]{1,0:T(8,128)(2,1)S(1)}, bf16[40,18432]{1,0:T(8,128)(2,1)S(1)}, u32[]{:S(2)}, u32[]{:S(2)}) collective-permute-start(bf16[40,18432]{1,0:T(8,128)(2,1)S(1)} %collective-permute-done.6.refs_0_.refs_3_), channel_id=1, source_target_pairs={{2,6},{3,7},{6,10},{7,11},{10,14},{11,15},{14,12},{15,13},{12,8},{... | collective-permute-start | bytes 4423688 | tf_op jit(solution)/shard_map/ppermute | solution.py:411
  71.7 32.0 %collective-permute-start.18 = (bf16[40,18432]{1,0:T(8,128)(2,1)S(1)}, bf16[40,18432]{1,0:T(8,128)(2,1)S(1)}, u32[]{:S(2)}, u32[]{:S(2)}) collective-permute-start(bf16[40,18432]{1,0:T(8,128)(2,1)S(1)} %collective-permute-done.13.refs_1_.refs_4_), channel_id=1, source_target_pairs={{6,2},{7,3},{10,6},{11,7},{14,10},{15,11},{12,14},{13,15},{8,12},{... | collective-permute-start | bytes 4423688 | tf_op jit(solution)/shard_map/ppermute | solution.py:414
  73.5 8.1 %collective-permute-start.15 = (bf16[80,8192]{1,0:T(8,128)(2,1)S(1)}, bf16[80,8192]{1,0:T(8,128)(2,1)S(1)}, u32[]{:S(2)}, u32[]{:S(2)}) collective-permute-start(bf16[80,8192]{1,0:T(8,128)(2,1)S(1)} %get-tuple-element.100), channel_id=1, source_target_pairs={{2,3},{3,2},{6,7},{7,6},{10,11},{11,10},{14,15},{15,14},{12,13},{1... | collective-permute-start | bytes 3932168 | tf_op jit(solution)/shard_map/ppermute | solution.py:408
  73.6 8.0 %collective-permute-start.14 = (bf16[80,6144]{1,0:T(8,128)(2,1)S(1)}, bf16[80,6144]{1,0:T(8,128)(2,1)S(1)}, u32[]{:S(2)}, u32[]{:S(2)}) collective-permute-start(bf16[80,6144]{1,0:T(8,128)(2,1)S(1)} %get-tuple-element.99), channel_id=1, source_target_pairs={{2,3},{3,2},{6,7},{7,6},{10,11},{11,10},{14,15},{15,14},{12,13},{1... | collective-permute-start | bytes 2949128 | tf_op jit(solution)/shard_map/ppermute | solution.py:408
  80.2 9.8 %collective-permute-start.17 = (f32[160,512]{1,0:T(8,128)S(1)}, f32[160,512]{1,0:T(8,128)S(1)}, u32[]{:S(2)}, u32[]{:S(2)}) collective-permute-start(f32[160,512]{1,0:T(8,128)S(1)} %project.13.refs_7_), channel_id=1, source_target_pairs={{0,16},{16,0},{1,17},{17,1},{2,18},{18,2},{3,19},{19,3},{4,20},{20... | collective-permute-start | bytes 983048 | tf_op jit(solution)/shard_map/ppermute | solution.py:402
  104.8 8.5 %collective-permute-start.22 = (bf16[80,8192]{1,0:T(8,128)(2,1)S(1)}, bf16[80,8192]{1,0:T(8,128)(2,1)S(1)}, u32[]{:S(2)}, u32[]{:S(2)}) collective-permute-start(bf16[80,8192]{1,0:T(8,128)(2,1)S(1)} %get-tuple-element.117), channel_id=1, source_target_pairs={{2,3},{3,2},{6,7},{7,6},{10,11},{11,10},{14,15},{15,14},{12,13},{1... | collective-permute-start | bytes 3932168 | tf_op jit(solution)/shard_map/ppermute | solution.py:408
  104.9 8.4 %collective-permute-start.21 = (bf16[80,6144]{1,0:T(8,128)(2,1)S(1)}, bf16[80,6144]{1,0:T(8,128)(2,1)S(1)}, u32[]{:S(2)}, u32[]{:S(2)}) collective-permute-start(bf16[80,6144]{1,0:T(8,128)(2,1)S(1)} %get-tuple-element.116), channel_id=1, source_target_pairs={{2,3},{3,2},{6,7},{7,6},{10,11},{11,10},{14,15},{15,14},{12,13},{1... | collective-permute-start | bytes 2949128 | tf_op jit(solution)/shard_map/ppermute | solution.py:408
  105.7 18.9 %collective-permute-start.19 = (bf16[40,9216]{1,0:T(8,128)(2,1)S(1)}, bf16[40,9216]{1,0:T(8,128)(2,1)S(1)}, u32[]{:S(2)}, u32[]{:S(2)}) collective-permute-start(bf16[40,9216]{1,0:T(8,128)(2,1)S(1)} %get-tuple-element.103), channel_id=1, source_target_pairs={{2,6},{3,7},{6,10},{7,11},{10,14},{11,15},{14,12},{15,13},{12,8},{... | collective-permute-start | bytes 2211848 | tf_op jit(solution)/shard_map/ppermute | solution.py:411
  107.3 18.6 %collective-permute-start.20 = (bf16[40,9216]{1,0:T(8,128)(2,1)S(1)}, bf16[40,9216]{1,0:T(8,128)(2,1)S(1)}, u32[]{:S(2)}, u32[]{:S(2)}) collective-permute-start(bf16[40,9216]{1,0:T(8,128)(2,1)S(1)} %get-tuple-element.104), channel_id=1, source_target_pairs={{6,2},{7,3},{10,6},{11,7},{14,10},{15,11},{12,14},{13,15},{8,12},{... | collective-permute-start | bytes 2211848 | tf_op jit(solution)/shard_map/ppermute | solution.py:414
  111.5 9.8 %collective-permute-start.24 = (f32[160,512]{1,0:T(8,128)S(1)}, f32[160,512]{1,0:T(8,128)S(1)}, u32[]{:S(2)}, u32[]{:S(2)}) collective-permute-start(f32[160,512]{1,0:T(8,128)S(1)} %project.15.refs_10_), channel_id=1, source_target_pairs={{0,16},{16,0},{1,17},{17,1},{2,18},{18,2},{3,19},{19,3},{4,20},{20... | collective-permute-start | bytes 983048 | tf_op jit(solution)/shard_map/ppermute | solution.py:402
  126.5 5.0 %collective-permute-start.27 = (bf16[40,9216]{1,0:T(8,128)(2,1)S(1)}, bf16[40,9216]{1,0:T(8,128)(2,1)S(1)}, u32[]{:S(2)}, u32[]{:S(2)}) collective-permute-start(bf16[40,9216]{1,0:T(8,128)(2,1)S(1)} %collective-permute-done.20.refs_2_), channel_id=1, source_target_pairs={{2,3},{3,2},{6,7},{7,6},{10,11},{11,10},{14,15},{15,14},{12,13},{1... | collective-permute-start | bytes 2211848 | tf_op jit(solution)/shard_map/ppermute | solution.py:408
  130.0 6.3 %collective-permute-start.28 = (f32[80,512]{1,0:T(8,128)S(1)}, f32[80,512]{1,0:T(8,128)S(1)}, u32[]{:S(2)}, u32[]{:S(2)}) collective-permute-start(f32[80,512]{1,0:T(8,128)S(1)} %project_last.3.refs_1_), channel_id=1, source_target_pairs={{0,16},{16,0},{1,17},{17,1},{2,18},{18,2},{3,19},{19,3},{4,20},{20... | collective-permute-start | bytes 491528 | tf_op jit(solution)/shard_map/ppermute | solution.py:402
  (6 other events, 24.5 us)

commit v4 on v0

v4 whole, which is shorter than its diff:
```python
import functools
import math

import jax
import jax.numpy as jnp
from jax import lax
from jax.experimental import pallas as pl
from jax.experimental.pallas import tpu as pltpu
from jax.sharding import PartitionSpec as P

RANK = 32
WIDE = 256
LIGHT = pl.CostEstimate(flops=1, bytes_accessed=1, transcendentals=0)
ROOM = 6 << 20


def params():
    return pltpu.CompilerParams(vmem_limit_bytes=ROOM)


def in_hbm(x):
    return pltpu.with_memory_space_constraint(x, pltpu.HBM)


def in_vmem(x):
    return pltpu.with_memory_space_constraint(x, pltpu.VMEM)


def cycle_of(first, second):
    if min(first, second) == 1:
        size = first * second
        order = list(range(0, size, 2)) + list(range(1, size, 2))[::-1]
        return [(i, 0) if second == 1 else (0, i) for i in order]
    if first % 2:
        return [(a, b) for b, a in cycle_of(second, first)] if second % 2 == 0 else [
            (a, b) for a in range(first) for b in range(second)]
    walk = []
    for a in range(first):
        inner = range(1, second)
        walk += [(a, b) for b in (inner if a % 2 == 0 else reversed(inner))]
    return walk + [(a, 0) for a in reversed(range(first))]


def ring_of(mesh):
    devices = list(mesh.devices[0])
    chips = {}
    for index, device in enumerate(devices):
        coords = getattr(device, "coords", None)
        key = tuple(coords) if coords is not None else (index // 2,)
        chips.setdefault(key, []).append(index)
    keys = list(chips)
    values = [sorted({k[i] for k in keys}) for i in range(len(keys[0]))]
    varying = [i for i in range(len(values)) if len(values[i]) > 1]
    if len(varying) == 2 and len(keys) == len(values[varying[0]]) * len(values[varying[1]]):
        one, two = sorted(varying, key=lambda i: -len(values[i]))
        at = {(values[one].index(k[one]), values[two].index(k[two])): k for k in keys}
        keys = [at[place] for place in cycle_of(len(values[one]), len(values[two]))]
    ring = [chips[k] for k in keys]
    assert all(pair[0] % 2 == 0 and pair[1] == pair[0] + 1 for pair in ring)
    return ring


def chunk_of(*sizes):
    whole = functools.reduce(math.gcd, sizes)
    return next(step for step in range(2048, 0, -128) if whole % step == 0)


def copy_kernel(plan, count, *refs):
    sem = refs[-1]
    copies = [
        pltpu.make_async_copy(
            refs[source].at[:, pl.ds(begin, width)], refs[count + target].at[:, pl.ds(put, width)], sem.at[index])
        for index, (source, begin, target, put, width) in enumerate(plan)]
    for copy in copies:
        copy.start()
    for copy in copies:
        copy.wait()


def columns_of(arrays, outputs, vmem=False):
    kind, space = (pltpu.VMEM, pltpu.VMEM) if vmem else (jax.ShapeDtypeStruct, pl.ANY)
    plan, widths = [], []
    for target, ranges in enumerate(outputs):
        put = 0
        for source, lo, hi in ranges:
            plan.append((source, lo, target, put, hi - lo))
            put += hi - lo
        widths.append(put)
    return pl.pallas_call(
        functools.partial(copy_kernel, tuple(plan), len(arrays)),
        in_specs=[pl.BlockSpec(memory_space=pl.ANY)] * len(arrays),
        out_specs=[pl.BlockSpec(memory_space=space)] * len(outputs),
        out_shape=[kind((arrays[0].shape[0], width), arrays[0].dtype) for width in widths],
        scratch_shapes=[pltpu.SemaphoreType.DMA((len(plan),))],
        compiler_params=params(),
        cost_estimate=LIGHT,
        name="columns",
    )(*arrays)


def load_kernel(step, a_ref, b_ref, a_out, b_out, gram_ref, sums, sem):
    columns = a_ref.shape[1]
    row = lax.broadcasted_iota(jnp.int32, (WIDE, WIDE), 0) // RANK
    col = lax.broadcasted_iota(jnp.int32, (WIDE, WIDE), 1) // RANK
    counts = [a_ref.shape[0] // step, b_ref.shape[0] // step]
    pairs = ((a_ref, a_out), (b_ref, b_out))

    def chunk(index, i):
        source, target = pairs[index]
        at = pl.ds(pl.multiple_of(i * step, step), step)
        return pltpu.make_async_copy(source.at[at], target.at[at], sem.at[index * counts[0] + i])

    for index in range(2):
        for i in range(counts[index]):
            chunk(index, i).start()
    for index in range(2):
        held = pairs[index][1]
        sums[...] = jnp.zeros_like(sums)

        @pl.loop(0, counts[index])
        def _(i, index=index, held=held):
            chunk(index, i).wait()
            for start in range(0, columns, WIDE):
                block = held[pl.ds(pl.multiple_of(i * step, step), step), start : start + WIDE]
                sums[:, start : start + WIDE] += lax.dot_general(
                    block, block, (((0,), (0,)), ((), ())), preferred_element_type=jnp.float32)

        for start in range(0, columns, WIDE):
            kept = jnp.where(row == col, sums[:, start : start + WIDE], 0.0)
            gram_ref[index, :, start : start + WIDE] = kept.reshape(WIDE // RANK, RANK, WIDE).sum(axis=0)


def load(a, b):
    columns = a.shape[1]
    step = chunk_of(math.gcd(a.shape[0], b.shape[0]))
    return pl.pallas_call(
        functools.partial(load_kernel, step),
        in_specs=[pl.BlockSpec(memory_space=pl.ANY)] * 2,
        out_specs=[pl.BlockSpec(memory_space=pltpu.VMEM)] * 3,
        out_shape=[
            pltpu.VMEM(a.shape, a.dtype), pltpu.VMEM(b.shape, b.dtype),
            jax.ShapeDtypeStruct((2, RANK, columns), jnp.float32)],
        scratch_shapes=[
            pltpu.VMEM((WIDE, columns), jnp.float32),
            pltpu.SemaphoreType.DMA(((a.shape[0] + b.shape[0]) // step,))],
        compiler_params=params(),
        cost_estimate=LIGHT,
        name="load_factors",
    )(in_hbm(a), in_hbm(b))


def pack_kernel(count, *refs):
    arrays, out_ref = refs[:count], refs[count]
    packed = jnp.concatenate([x[...] for x in arrays], axis=0)
    for copy in range(2):
        out_ref[copy] = packed


def twice(arrays):
    rows, width = sum(a.shape[0] for a in arrays), arrays[0].shape[1]
    step = chunk_of(width)
    return pl.pallas_call(
        functools.partial(pack_kernel, len(arrays)),
        grid=(width // step,),
        in_specs=[pl.BlockSpec((a.shape[0], step), lambda i: (0, i)) for a in arrays],
        out_specs=pl.BlockSpec((2, rows, step), lambda i: (0, 0, i)),
        out_shape=jax.ShapeDtypeStruct((2, rows, width), arrays[0].dtype),
        compiler_params=params(),
        cost_estimate=LIGHT,
        name="pack",
    )(*arrays)


def beside_kernel(*refs):
    arrays, out_ref, sem = refs[:-2], refs[-2], refs[-1]
    copies, put = [], 0
    for array in arrays:
        for copy in range(2):
            copies.append(pltpu.make_async_copy(
                array, out_ref.at[copy, :, pl.ds(put, array.shape[1])], sem.at[len(copies)]))
        put += array.shape[1]
    for copy in copies:
        copy.start()
    for copy in copies:
        copy.wait()


def beside_twice(arrays):
    shape = (2, arrays[0].shape[0], sum(a.shape[1] for a in arrays))
    return pl.pallas_call(
        beside_kernel,
        in_specs=[pl.BlockSpec(memory_space=pl.ANY)] * len(arrays),
        out_specs=pl.BlockSpec(memory_space=pl.ANY),
        out_shape=jax.ShapeDtypeStruct(shape, arrays[0].dtype),
        scratch_shapes=[pltpu.SemaphoreType.DMA((2 * len(arrays),))],
        compiler_params=params(),
        cost_estimate=LIGHT,
        name="pack",
    )(*arrays)


def project_kernel(step, spans, count, outs, more, *refs):
    held, factors = refs[:count], refs[count : count + 2]
    given, sums = refs[count + 2 : count + 2 + more], refs[-outs:]
    i = pl.program_id(0)

    @pl.when(i == 0)
    def _():
        for index, out in enumerate(sums):
            out[...] = given[index][...] if more else jnp.zeros_like(out)

    for begin, width, which, offset in spans:
        first, steps = begin // step, width // step

        @pl.when((i >= first) & (i < first + steps))
        def _(which=which, offset=offset, first=first):
            x = jnp.concatenate(
                [x for h in held for x in ((h[0], h[1]) if len(h.shape) == 3 else (h[...],))], axis=0)
            at = pl.multiple_of((i - first) * step + offset, step)
            sums[which if outs == 2 else 0][...] += jnp.dot(
                x, factors[which][pl.ds(at, step), :], preferred_element_type=jnp.float32)


def project(arrays, span, factors, outs, start=None):
    width = sum(size for _, size, _, _ in span)
    step = chunk_of(*(size for _, size, _, _ in span))
    shape = (sum(math.prod(a.shape[:-1]) for a in arrays), factors[0].shape[1])
    extra = [] if start is None else [start]
    result = pl.pallas_call(
        functools.partial(project_kernel, step, tuple(span), len(arrays), outs, len(extra)),
        grid=(width // step,),
        in_specs=[
            pl.BlockSpec((*a.shape[:-1], step), lambda i, zeros=(0,) * (a.ndim - 1): (*zeros, i)) for a in arrays]
        + [pl.BlockSpec(memory_space=pltpu.VMEM)] * (2 + len(extra)),
        out_specs=[pl.BlockSpec(shape, lambda i: (0, 0))] * outs,
        out_shape=[jax.ShapeDtypeStruct(shape, jnp.float32)] * outs,
        compiler_params=params(),
        cost_estimate=LIGHT,
        name="project",
    )(*arrays, *[in_vmem(f) for f in factors], *extra)
    return result if outs == 2 else result[0]


def by_query(x):
    columns = x.shape[1]
    queries = columns // RANK
    member = (lax.broadcasted_iota(jnp.int32, (columns, queries), 0) // RANK) == lax.broadcasted_iota(
        jnp.int32, (columns, queries), 1)
    return jnp.dot(
        x, member.astype(jnp.float32), precision=lax.Precision.HIGHEST, preferred_element_type=jnp.float32)


def total_of(refs):
    return sum(ref[...] for ref in refs[1:]) + refs[0][...]


def project_last_kernel(spans, *refs):
    count = len(spans)
    held, mates = refs[:count], refs[count : 2 * count]
    factors, out_ref = refs[2 * count : 2 * count + 2], refs[-1]
    out_ref[...] = jnp.zeros_like(out_ref)
    for mine, other, pieces in zip(held, mates, spans):
        for begin, width, which, offset in pieces:
            step = chunk_of(width)

            @pl.loop(0, width // step)
            def _(i, mine=mine, other=other, begin=begin, which=which, offset=offset, step=step):
                at = pl.ds(pl.multiple_of(i * step + begin, 128), step)
                x = jnp.concatenate([mine[:, at], other[:, at]], axis=0)
                w = factors[which][pl.ds(pl.multiple_of(i * step + offset, 128), step), :]
                out_ref[...] += jnp.dot(x, w, preferred_element_type=jnp.float32)


def project_last(held, mates, spans, factors):
    given = [in_vmem(x) for x in (*held, *mates, *factors)]
    return pl.pallas_call(
        functools.partial(project_last_kernel, tuple(tuple(s) for s in spans)),
        in_specs=[pl.BlockSpec(memory_space=pltpu.VMEM)] * len(given),
        out_specs=pl.BlockSpec(memory_space=pltpu.VMEM),
        out_shape=jax.ShapeDtypeStruct((2 * held[0].shape[0], factors[0].shape[1]), jnp.float32),
        compiler_params=params(),
        cost_estimate=LIGHT,
        name="project_last",
    )(*given)


def score_kernel(counts, earlier, *refs):
    out_ref = refs[-1]
    found, taken = [], earlier
    for count in counts:
        found.append(by_query(refs[taken][...] * total_of(refs[taken + 1 : taken + 1 + count])))
        taken += 1 + count
    out_ref[...] = jnp.concatenate([*[ref[...] for ref in refs[:earlier]], jnp.concatenate(found, axis=0).T], axis=1)


def score(groups, *earlier):
    rows, columns = sum(one.shape[0] for one, _ in groups), groups[0][0].shape[1]
    return pl.pallas_call(
        functools.partial(score_kernel, tuple(len(parts) for _, parts in groups), len(earlier)),
        out_shape=jax.ShapeDtypeStruct((columns // RANK, rows + sum(x.shape[1] for x in earlier)), jnp.float32),
        compiler_params=params(),
        cost_estimate=LIGHT,
        name="score",
    )(*earlier, *[x for one, parts in groups for x in (one, *parts)])


def inverse_kernel(*refs):
    gram, out_ref = total_of(refs[:-1]), refs[-1]
    norms = jnp.broadcast_to((gram[0] * gram[1]).sum(axis=0, keepdims=True), (8, gram.shape[2]))
    out_ref[...] = 1.0 / jnp.sqrt(by_query(norms) + 1e-06)


def inverse_norms(parts):
    return pl.pallas_call(
        inverse_kernel,
        out_shape=jax.ShapeDtypeStruct((8, parts[0].shape[2] // RANK), jnp.float32),
        compiler_params=params(),
        cost_estimate=LIGHT,
        name="inverse_norms",
    )(*parts)


def looked_up(table, index):
    return sum(jnp.where(index == i, value, 0) for i, value in enumerate(table))


def last_kernel(count, groups, place, tokens, at_ref, inverse_ref, *refs):
    out_ref, held = refs[-2:]
    chips = len(place)
    scores = total_of(refs[:count]).T * inverse_ref[:1]
    first = 0
    for group in groups:
        for c in range(2):
            for distance in group:
                core = (at_ref[0] + c) % 2 if distance == chips // 2 else c
                held[distance % chips, core] = scores[first : first + tokens]
                first += tokens
    here = looked_up(place, at_ref[0] // 2)
    side = at_ref[1]
    share = out_ref.shape[1] // (2 * tokens)
    blocks = []
    for j in range(share):
        there = looked_up(place, side * share + j)
        distance = there - here
        distance = jnp.where(distance < 0, distance + chips, distance)
        blocks += [held[distance, c] for c in range(2)]
    out_ref[...] = jnp.concatenate(blocks, axis=0).T


def last(parts, inverse, groups, place, tokens, share, at):
    queries = inverse.shape[1]
    return pl.pallas_call(
        functools.partial(last_kernel, len(parts), groups, place, tokens),
        in_specs=[pl.BlockSpec(memory_space=pltpu.SMEM)] + [pl.BlockSpec(memory_space=pltpu.VMEM)] * (1 + len(parts)),
        out_specs=pl.BlockSpec(memory_space=pltpu.VMEM),
        out_shape=jax.ShapeDtypeStruct((queries, share), jnp.float32),
        scratch_shapes=[pltpu.VMEM((len(place), 2, tokens, queries), jnp.float32)],
        compiler_params=params(),
        cost_estimate=LIGHT,
        name="last_scores",
    )(at, inverse, *parts)


def within(spans, low, high):
    kept = []
    for begin, width, which, offset in spans:
        a, b = max(begin, low), min(begin + width, high)
        if a < b:
            kept.append((a - low, b - a, which, offset + a - begin))
    return kept


def solution(mesh):
    rows = mesh.shape["rows"]
    query = mesh.shape["query"]
    ring = ring_of(mesh)
    chips = len(ring)
    assert chips % 2 == 0 and chips >= 4
    forward = [(a, b) for i in range(chips) for a, b in zip(ring[i], ring[(i + 1) % chips])]
    backward = [(b, a) for a, b in forward]
    mates = [(pair[i], pair[1 - i]) for pair in ring for i in range(2)]
    place = [0] * chips
    for i, pair in enumerate(ring):
        place[pair[0] // 2] = i
    place = tuple(place)

    def across(x):
        if rows == 2:
            return [x, lax.ppermute(x, "rows", [(0, 1), (1, 0)])]
        return [lax.psum(x, "rows")]

    def both_cores(x):
        return lax.all_to_all(x, "query", 0, 0, axis_index_groups=sorted(ring))

    def round_ring(pair):
        return [lax.ppermute(pair[0], "query", forward), lax.ppermute(pair[1], "query", backward)]

    def tied(*trees):
        return lax.optimization_barrier(trees)

    def local(acts, grads, in_factors, out_factors):
        tokens, width = acts.shape
        depth = grads.shape[1]
        half = (width + depth) // 256 * 128
        cut = half - depth
        assert cut > 0
        spans = [[(0, depth, 1, 0), (depth, cut, 0, 0)], [(0, width - cut, 0, cut)]]
        middles = [sum(s[1] for s in span) // 256 * 128 for span in spans]
        at = jnp.stack([lax.axis_index("query"), lax.axis_index("rows")]).astype(jnp.int32)
        last_hop = chips // 2

        def next_of(pair, hop, stream):
            if hop + 1 == last_hop:
                middle = middles[stream]
                pair = columns_of(pair, [[(0, 0, middle)], [(1, middle, pair[1].shape[1])]], True)
            return round_ring(pair)

        at, acts, grads, in_factors, out_factors = tied(at, acts, grads, in_factors, out_factors)
        (own0,) = columns_of([in_hbm(grads), in_hbm(acts)], [[(0, 0, depth), (1, 0, cut)]], True)
        fly0 = round_ring([own0, own0])
        (own1,) = columns_of([in_hbm(acts)], [[(0, cut, width)]], True)
        fly1 = round_ring([own1, own1])
        *factors, gram = load(in_factors, out_factors)
        fly0, own0, own1, gram = tied(fly0, own0, own1, gram)
        groups, pairs, found, gram_parts = [], [], [], []
        for hop in range(1, last_hop):
            extra = hop == 1
            groups.append((-hop, hop) + (0,) * extra)
            held = fly0
            fly0 = next_of(held, hop, 0)
            other, part = project([both_cores(twice(held + [own0] * extra))], spans[0], factors, 2)[::-1]
            if pairs:
                part, pairs, gram = tied(part, pairs, gram)
                found = [score(pairs, *found)]
                gram_parts = gram_parts or across(gram)
            fly1, other, part, found, gram_parts = tied(fly1, other, part, found, gram_parts)
            held = fly1
            fly1 = next_of(held, hop, 1)
            one = project([both_cores(twice(held + [own1] * extra))], spans[1], factors, 1, part)
            other = across(other)
            if hop + 1 < last_hop:
                fly0, one, other = tied(fly0, one, other)
            else:
                fly0, fly1, one, other, gram_parts = tied(fly0, fly1, one, other, gram_parts)
            pairs = [(one, other)]
        groups.append((last_hop,))
        held = [*fly0, *fly1]
        swapped = [lax.ppermute(x, "query", mates) for x in held]
        pieces = [
            within(span, lo, hi)
            for span, middle in zip(spans, middles) for lo, hi in ((0, middle), (middle, sum(s[1] for s in span)))]
        chosen = [[[s for s in piece if s[2] == which] for piece in pieces] for which in range(2)]
        used = [[i for i, piece in enumerate(c) if piece] for c in chosen]
        one, other = [
            project_last([held[i] for i in u], [swapped[i] for i in u], [c[i] for i in u], factors)
            for u, c in zip(used, chosen)]
        found = score(pairs, *found)
        inverse = inverse_norms(gram_parts)
        scores = score([(one, across(other))], found)
        return last(across(scores), inverse, tuple(groups), place, tokens, query * tokens // rows, at).T

    return jax.shard_map(
        local,
        mesh=mesh,
        in_specs=(P("query", "rows"), P("query", "rows"), P("rows", "query"), P("rows", "query")),
        out_specs=P("rows", "query"),
        check_vma=False,
    )
```

time: 219 us -> 133 us (0.61)
  waiting for transfers between devices: 129 us -> 24 us
  Pallas kernels: 0 us -> 45.2 us
  matrix products: 44.3 us -> 0 us
  blocking collectives: 0 us -> 38.9 us
  local copies, waits for them, and re-layouts: 25.5 us -> 0 us
  starting transfers between devices: 0.17 us -> 24.7 us
  between operations: 15.1 us -> 0.24 us
  other arithmetic: 3.41 us -> 0.07 us
    all_gather x2 -> x0, waiting for transfers between devices: 106 us -> none  [the longest x1 88.9 us: local(): lax.all_gather(acts, 'query', axis=0, tiled=True)]
    pallas_call x0 -> x25, Pallas kernels: none -> 45.2 us  [the longest x6 21.1 us: project(): pl.pallas_call(functools.partial(project_kernel, step, tuple(span), len(a...]
    dot_general x4 -> x0, matrix products: 44.3 us -> none  [the longest x1 18.4 us: local(): jnp.dot(lax.all_gather(acts, 'query', axis=0, tiled=True), in_factors, pr...]
    all_to_all x0 -> x6, blocking collectives: none -> 38.9 us  [both_cores(): return lax.all_to_all(x, 'query', 0, 0, axis_index_groups=sorted(ring))]
    unnamed x2 -> x0, local copies, waits for them, and re-layouts: 25.3 us -> none
    ppermute x0 -> x26, starting transfers between devices: none -> 24.7 us  [the longest x8 14.5 us: round_ring(): lax.ppermute(pair[0], 'query', forward)]
    ppermute x0 -> x26, waiting for transfers between devices: none -> 24 us  [the longest x8 9.25 us: round_ring(): lax.ppermute(pair[0], 'query', forward)]
    reduce_scatter x2 -> x0, waiting for transfers between devices: 21.9 us -> none  [the longest x1 21.9 us: local(): lax.psum_scatter(proj_in, 'rows', scatter_dimension=0, tiled=True)]
  transfers between devices with their start and end apart: 5 -> 26, of which waited for: 3 -> 14; matrix products, arithmetic and copies ran while one was open for 33% -> 0% of each run, Pallas kernels for 0% -> 32%
where the time goes in v4:
time: 133 us
  Pallas kernels  45.2 us (34%)
  blocking collectives  38.9 us (29%)
  starting transfers between devices  24.7 us (19%)
  waiting for transfers between devices  24 us (18%)
    all_to_all x6, blocking collectives, both_cores(): return lax.all_to_all(x, 'query', 0, 0, axis_index_groups=sorted(ring))  38.9 us
    pallas_call x6, Pallas kernels, project(): pl.pallas_call(functools.partial(project_kernel, step, tuple(span), len(a...  21.1 us
    ppermute x8, starting transfers between devices, round_ring(): lax.ppermute(pair[0], 'query', forward)  14.5 us
    ppermute x8, waiting for transfers between devices, round_ring(): lax.ppermute(pair[0], 'query', forward)  9.25 us
    pallas_call x1, Pallas kernels, load(): pl.pallas_call(functools.partial(load_kernel, step), in_specs=[pl.BlockSp...  8.62 us
    ppermute x8, waiting for transfers between devices, round_ring(): lax.ppermute(pair[1], 'query', backward)  8.18 us
    ppermute x6, starting transfers between devices, across(): return [x, lax.ppermute(x, 'rows', [(0, 1), (1, 0)])]  6.21 us
    ppermute x6, waiting for transfers between devices, across(): return [x, lax.ppermute(x, 'rows', [(0, 1), (1, 0)])]  5.85 us
  transfers between devices with their start and end apart: 26, of which 14 were waited for; matrix products, arithmetic and copies ran while one was open for 0% of the time, Pallas kernels for 32%

profile of v4, /device:TPU:0, one launch (start us, length us, event | category | flops | bytes accessed | tf_op | source)
XLA Modules:
  0.0 133.1 jit_solution(8817283169611938280)
XLA Ops:
  1.2 3.0 %collective-permute-start = (bf16[40,9216]{1,0:T(8,128)(2,1)S(1)}, bf16[40,9216]{1,0:T(8,128)(2,1)S(1)}, u32[]{:S(2)}, u32[]{:S(2)}) collective-permute-start(bf16[40,9216]{1,0:T(8,128)(2,1)S(1)} %columns.4.refs_2_), channel_id=1, source_target_pairs={{2,6},{3,7},{6,10},{7,11},{10,14},{11,15},{14,12},{15,13},{12,8},{... | collective-permute-start | bytes 2211848 | tf_op jit(solution)/shard_map/ppermute | solution.py:396
  5.5 2.0 %collective-permute-start.4 = (bf16[40,9216]{1,0:T(8,128)(2,1)S(1)}, bf16[40,9216]{1,0:T(8,128)(2,1)S(1)}, u32[]{:S(2)}, u32[]{:S(2)}) collective-permute-start(bf16[40,9216]{1,0:T(8,128)(2,1)S(1)} %columns.5.refs_2_), channel_id=1, source_target_pairs={{2,6},{3,7},{6,10},{7,11},{10,14},{11,15},{14,12},{15,13},{12,8},{... | collective-permute-start | bytes 2211848 | tf_op jit(solution)/shard_map/ppermute | solution.py:396
  7.6 8.6 %load_factors.1 = (bf16[14336,512]{1,0:T(8,128)(2,1)S(1)}, bf16[4096,512]{1,0:T(8,128)(2,1)S(1)}, f32[2,32,512]{2,1,0:T(8,128)S(1)}) custom-call(bf16[14336,512]{1,0:T(8,128)(2,1)} %a_ref, bf16[4096,512]{1,0:T(8,128)(2,1)} %b_ref), custom_call_target="tpu_custom_call" | custom-call | flops 1 | bytes 1 | tf_op jit(solution)/shard_map/load_factors/pallas_call | solution.py:136
  16.2 5.4 %collective-permute-done.refs_0_ = bf16[40,9216]{1,0:T(8,128)(2,1)S(1)} collective-permute-done((bf16[40,9216]{1,0:T(8,128)(2,1)S(1)}, bf16[40,9216]{1,0:T(8,128)(2,1)S(1)}, u32[]{:S(2)}, u32[]{:S(2)}) %collective-permute-start) | collective-permute-done | bytes 737312 | tf_op jit(solution)/shard_map/ppermute | solution.py:396
  21.6 2.0 %collective-permute-done.1.refs_1_ = bf16[40,9216]{1,0:T(8,128)(2,1)S(1)} collective-permute-done((bf16[40,9216]{1,0:T(8,128)(2,1)S(1)}, bf16[40,9216]{1,0:T(8,128)(2,1)S(1)}, u32[]{:S(2)}, u32[]{:S(2)}) %collective-permute-start.1) | collective-permute-done | bytes 737312 | tf_op jit(solution)/shard_map/ppermute | solution.py:396
  26.5 7.3 %all_to_all.30.refs_0_ = bf16[2,120,9216]{2,1,0:T(8,128)(2,1)S(1)} all-to-all(bf16[2,120,9216]{2,1,0:T(8,128)(2,1)S(1)} %pack.6), channel_id=1, replica_groups={{0,1},{2,3},{4,5},{6,7},{8,9},{10,11},{12,13},{14,15},{16,17},{18,19},{..., dimensions={0} | all-to-all | bytes 8847360 | tf_op jit(solution)/shard_map/all_to_all | solution.py:393
  33.8 4.4 %project.6 = (f32[240,512]{1,0:T(8,128)S(1)}, f32[240,512]{1,0:T(8,128)S(1)}) custom-call(bf16[2,120,9216]{2,1,0:T(8,128)(2,1)S(1)} %all_to_all.30.refs_0_, bf16[14336,512]{1,0:T(8,128)(2,1)S(1)} %get-tuple-element.83.refs_1_.refs_8_.refs_2_, bf16[4096,512]{1,0:T(8,128)(2,1)S(1)} %get-tuple-element.84.refs_2_.refs_9_.refs_3_), custom_call_target="tpu_custom_call" | custom-call | flops 1 | bytes 1 | tf_op jit(solution)/shard_map/project/pallas_call | solution.py:229
  43.8 7.3 %all_to_all.31.refs_0_ = bf16[2,120,9216]{2,1,0:T(8,128)(2,1)S(1)} all-to-all(bf16[2,120,9216]{2,1,0:T(8,128)(2,1)S(1)} %pack.7), channel_id=1, replica_groups={{0,1},{2,3},{4,5},{6,7},{8,9},{10,11},{12,13},{14,15},{16,17},{18,19},{..., dimensions={0} | all-to-all | bytes 8847360 | tf_op jit(solution)/shard_map/all_to_all | solution.py:393
  51.1 3.7 %project.7.refs_0_ = f32[240,512]{1,0:T(8,128)S(1)} custom-call(bf16[2,120,9216]{2,1,0:T(8,128)(2,1)S(1)} %all_to_all.31.refs_0_, bf16[14336,512]{1,0:T(8,128)(2,1)S(1)} %get-tuple-element.83.refs_1_.refs_8_.refs_2_, bf16[4096,512]{1,0:T(8,128)(2,1)S(1)} %get-tuple-element.84.refs_2_.refs_9_.refs_3_, f32[240,512]{1,0:T(8,128)S(1)} %get-tuple-element.90.refs_3_), custom_call_target="tpu_custom_call" | custom-call | flops 1 | bytes 1 | tf_op jit(solution)/shard_map/project/pallas_call | solution.py:229
  55.9 6.1 %all_to_all.32.refs_0_ = bf16[2,80,9216]{2,1,0:T(8,128)(2,1)S(1)} all-to-all(bf16[2,80,9216]{2,1,0:T(8,128)(2,1)S(1)} %pack.8), channel_id=1, replica_groups={{0,1},{2,3},{4,5},{6,7},{8,9},{10,11},{12,13},{14,15},{16,17},{18,19},{..., dimensions={0} | all-to-all | bytes 5898240 | tf_op jit(solution)/shard_map/all_to_all | solution.py:393
  62.0 3.6 %project.8 = (f32[160,512]{1,0:T(8,128)S(1)}, f32[160,512]{1,0:T(8,128)S(1)}) custom-call(bf16[2,80,9216]{2,1,0:T(8,128)(2,1)S(1)} %all_to_all.32.refs_0_, bf16[14336,512]{1,0:T(8,128)(2,1)S(1)} %get-tuple-element.83.refs_1_.refs_8_.refs_2_, bf16[4096,512]{1,0:T(8,128)(2,1)S(1)} %get-tuple-element.84.refs_2_.refs_9_.refs_3_), custom_call_target="tpu_custom_call" | custom-call | flops 1 | bytes 1 | tf_op jit(solution)/shard_map/project/pallas_call | solution.py:229
  75.3 6.1 %all_to_all.33.refs_0_ = bf16[2,80,9216]{2,1,0:T(8,128)(2,1)S(1)} all-to-all(bf16[2,80,9216]{2,1,0:T(8,128)(2,1)S(1)} %pack.9), channel_id=1, replica_groups={{0,1},{2,3},{4,5},{6,7},{8,9},{10,11},{12,13},{14,15},{16,17},{18,19},{..., dimensions={0} | all-to-all | bytes 5898240 | tf_op jit(solution)/shard_map/all_to_all | solution.py:393
  81.4 2.9 %project.9.refs_1_ = f32[160,512]{1,0:T(8,128)S(1)} custom-call(bf16[2,80,9216]{2,1,0:T(8,128)(2,1)S(1)} %all_to_all.33.refs_0_, bf16[14336,512]{1,0:T(8,128)(2,1)S(1)} %get-tuple-element.83.refs_1_.refs_8_.refs_2_, bf16[4096,512]{1,0:T(8,128)(2,1)S(1)} %get-tuple-element.84.refs_2_.refs_9_.refs_3_, f32[160,512]{1,0:T(8,128)S(1)} %get-tuple-element.107.refs_3_), custom_call_target="tpu_custom_call" | custom-call | flops 1 | bytes 1 | tf_op jit(solution)/shard_map/project/pallas_call | solution.py:229
  84.4 2.1 %collective-permute-done.7.refs_0_ = bf16[40,9216]{1,0:T(8,128)(2,1)S(1)} collective-permute-done((bf16[40,9216]{1,0:T(8,128)(2,1)S(1)}, bf16[40,9216]{1,0:T(8,128)(2,1)S(1)}, u32[]{:S(2)}, u32[]{:S(2)}) %collective-permute-start.7) | collective-permute-done | bytes 737312 | tf_op jit(solution)/shard_map/ppermute | solution.py:396
  86.5 1.6 %collective-permute-done.8.refs_1_ = bf16[40,9216]{1,0:T(8,128)(2,1)S(1)} collective-permute-done((bf16[40,9216]{1,0:T(8,128)(2,1)S(1)}, bf16[40,9216]{1,0:T(8,128)(2,1)S(1)}, u32[]{:S(2)}, u32[]{:S(2)}) %collective-permute-start.8) | collective-permute-done | bytes 737312 | tf_op jit(solution)/shard_map/ppermute | solution.py:396
  88.9 1.6 %collective-permute-start.13 = (bf16[40,4608]{1,0:T(8,128)(2,1)S(1)}, bf16[40,4608]{1,0:T(8,128)(2,1)S(1)}, u32[]{:S(2)}, u32[]{:S(2)}) collective-permute-start(bf16[40,4608]{1,0:T(8,128)(2,1)S(1)} %get-tuple-element.111), channel_id=1, source_target_pairs={{2,6},{3,7},{6,10},{7,11},{10,14},{11,15},{14,12},{15,13},{12,8},{... | collective-permute-start | bytes 1105928 | tf_op jit(solution)/shard_map/ppermute | solution.py:396
  90.9 6.1 %all_to_all.34.refs_0_ = bf16[2,80,9216]{2,1,0:T(8,128)(2,1)S(1)} all-to-all(bf16[2,80,9216]{2,1,0:T(8,128)(2,1)S(1)} %pack.10), channel_id=1, replica_groups={{0,1},{2,3},{4,5},{6,7},{8,9},{10,11},{12,13},{14,15},{16,17},{18,19},{..., dimensions={0} | all-to-all | bytes 5898240 | tf_op jit(solution)/shard_map/all_to_all | solution.py:393
  97.0 3.6 %project.10 = (f32[160,512]{1,0:T(8,128)S(1)}, f32[160,512]{1,0:T(8,128)S(1)}) custom-call(bf16[2,80,9216]{2,1,0:T(8,128)(2,1)S(1)} %all_to_all.34.refs_0_, bf16[14336,512]{1,0:T(8,128)(2,1)S(1)} %get-tuple-element.83.refs_1_.refs_8_.refs_2_, bf16[4096,512]{1,0:T(8,128)(2,1)S(1)} %get-tuple-element.84.refs_2_.refs_9_.refs_3_), custom_call_target="tpu_custom_call" | custom-call | flops 1 | bytes 1 | tf_op jit(solution)/shard_map/project/pallas_call | solution.py:229
  102.3 1.6 %collective-permute-done.16.refs_1_ = bf16[40,9216]{1,0:T(8,128)(2,1)S(1)} collective-permute-done((bf16[40,9216]{1,0:T(8,128)(2,1)S(1)}, bf16[40,9216]{1,0:T(8,128)(2,1)S(1)}, u32[]{:S(2)}, u32[]{:S(2)}) %collective-permute-start.16) | collective-permute-done | bytes 737312 | tf_op jit(solution)/shard_map/ppermute | solution.py:396
  104.0 1.6 %collective-permute-start.17 = (bf16[40,4608]{1,0:T(8,128)(2,1)S(1)}, bf16[40,4608]{1,0:T(8,128)(2,1)S(1)}, u32[]{:S(2)}, u32[]{:S(2)}) collective-permute-start(bf16[40,4608]{1,0:T(8,128)(2,1)S(1)} %get-tuple-element.127), channel_id=1, source_target_pairs={{2,6},{3,7},{6,10},{7,11},{10,14},{11,15},{14,12},{15,13},{12,8},{... | collective-permute-start | bytes 1105928 | tf_op jit(solution)/shard_map/ppermute | solution.py:396
  107.3 6.1 %all_to_all.35.refs_0_ = bf16[2,80,9216]{2,1,0:T(8,128)(2,1)S(1)} all-to-all(bf16[2,80,9216]{2,1,0:T(8,128)(2,1)S(1)} %pack.11), channel_id=1, replica_groups={{0,1},{2,3},{4,5},{6,7},{8,9},{10,11},{12,13},{14,15},{16,17},{18,19},{..., dimensions={0} | all-to-all | bytes 5898240 | tf_op jit(solution)/shard_map/all_to_all | solution.py:393
  113.4 2.9 %project.11.refs_1_ = f32[160,512]{1,0:T(8,128)S(1)} custom-call(bf16[2,80,9216]{2,1,0:T(8,128)(2,1)S(1)} %all_to_all.35.refs_0_, bf16[14336,512]{1,0:T(8,128)(2,1)S(1)} %get-tuple-element.83.refs_1_.refs_8_.refs_2_, bf16[4096,512]{1,0:T(8,128)(2,1)S(1)} %get-tuple-element.84.refs_2_.refs_9_.refs_3_, f32[160,512]{1,0:T(8,128)S(1)} %get-tuple-element.129.refs_3_), custom_call_target="tpu_custom_call" | custom-call | flops 1 | bytes 1 | tf_op jit(solution)/shard_map/project/pallas_call | solution.py:229
  122.2 3.8 %project_last.2.refs_1_ = f32[80,512]{1,0:T(8,128)S(1)} custom-call(bf16[40,4608]{1,0:T(8,128)(2,1)S(1)} %collective-permute-done.13.refs_0_, bf16[40,4608]{1,0:T(8,128)(2,1)S(1)} %collective-permute-done.14.refs_1_, bf16[40,4608]{1,0:T(8,128)(2,1)S(1)} %collective-permute-done.17.refs_2_, bf16[40,4608]{1,0:T(8,128)(2,1)S(1)} %collective-permute-done.18.refs_3_, ...), custom_call_target="tpu_custom_call" | custom-call | flops 1 | bytes 1 | tf_op jit(solution)/shard_map/project_last/pallas_call | solution.py:276
  128.5 3.2 %collective-permute-done.25.refs_1_ = f32[16,640]{1,0:T(8,128)S(1)} collective-permute-done((f32[16,640]{1,0:T(8,128)S(1)}, f32[16,640]{1,0:T(8,128)S(1)}, u32[]{:S(2)}, u32[]{:S(2)}) %collective-permute-start.25) | collective-permute-done | bytes 40992 | tf_op jit(solution)/shard_map/ppermute | solution.py:389
  (60 shorter events, 36.2 us)
Async XLA Ops:
  1.2 20.4 %collective-permute-start = (bf16[40,9216]{1,0:T(8,128)(2,1)S(1)}, bf16[40,9216]{1,0:T(8,128)(2,1)S(1)}, u32[]{:S(2)}, u32[]{:S(2)}) collective-permute-start(bf16[40,9216]{1,0:T(8,128)(2,1)S(1)} %columns.4.refs_2_), channel_id=1, source_target_pairs={{2,6},{3,7},{6,10},{7,11},{10,14},{11,15},{14,12},{15,13},{12,8},{... | collective-permute-start | bytes 2211848 | tf_op jit(solution)/shard_map/ppermute | solution.py:396
  4.2 19.4 %collective-permute-start.1 = (bf16[40,9216]{1,0:T(8,128)(2,1)S(1)}, bf16[40,9216]{1,0:T(8,128)(2,1)S(1)}, u32[]{:S(2)}, u32[]{:S(2)}) collective-permute-start(bf16[40,9216]{1,0:T(8,128)(2,1)S(1)} %columns.4.refs_2_), channel_id=1, source_target_pairs={{6,2},{7,3},{10,6},{11,7},{14,10},{15,11},{12,14},{13,15},{8,12},{... | collective-permute-start | bytes 2211848 | tf_op jit(solution)/shard_map/ppermute | solution.py:396
  5.5 32.7 %collective-permute-start.4 = (bf16[40,9216]{1,0:T(8,128)(2,1)S(1)}, bf16[40,9216]{1,0:T(8,128)(2,1)S(1)}, u32[]{:S(2)}, u32[]{:S(2)}) collective-permute-start(bf16[40,9216]{1,0:T(8,128)(2,1)S(1)} %columns.5.refs_2_), channel_id=1, source_target_pairs={{2,6},{3,7},{6,10},{7,11},{10,14},{11,15},{14,12},{15,13},{12,8},{... | collective-permute-start | bytes 2211848 | tf_op jit(solution)/shard_map/ppermute | solution.py:396
  7.4 32.0 %collective-permute-start.5 = (bf16[40,9216]{1,0:T(8,128)(2,1)S(1)}, bf16[40,9216]{1,0:T(8,128)(2,1)S(1)}, u32[]{:S(2)}, u32[]{:S(2)}) collective-permute-start(bf16[40,9216]{1,0:T(8,128)(2,1)S(1)} %columns.5.refs_2_), channel_id=1, source_target_pairs={{6,2},{7,3},{10,6},{11,7},{14,10},{15,11},{12,14},{13,15},{8,12},{... | collective-permute-start | bytes 2211848 | tf_op jit(solution)/shard_map/ppermute | solution.py:396
  23.6 31.2 %collective-permute-start.2 = (bf16[40,9216]{1,0:T(8,128)(2,1)S(1)}, bf16[40,9216]{1,0:T(8,128)(2,1)S(1)}, u32[]{:S(2)}, u32[]{:S(2)}) collective-permute-start(bf16[40,9216]{1,0:T(8,128)(2,1)S(1)} %collective-permute-done.refs_0_), channel_id=1, source_target_pairs={{2,6},{3,7},{6,10},{7,11},{10,14},{11,15},{14,12},{15,13},{12,8},{... | collective-permute-start | bytes 2211848 | tf_op jit(solution)/shard_map/ppermute | solution.py:396
  25.2 30.0 %collective-permute-start.3 = (bf16[40,9216]{1,0:T(8,128)(2,1)S(1)}, bf16[40,9216]{1,0:T(8,128)(2,1)S(1)}, u32[]{:S(2)}, u32[]{:S(2)}) collective-permute-start(bf16[40,9216]{1,0:T(8,128)(2,1)S(1)} %collective-permute-done.1.refs_1_), channel_id=1, source_target_pairs={{6,2},{7,3},{10,6},{11,7},{14,10},{15,11},{12,14},{13,15},{8,12},{... | collective-permute-start | bytes 2211848 | tf_op jit(solution)/shard_map/ppermute | solution.py:396
  39.4 30.4 %collective-permute-start.9 = (bf16[40,9216]{1,0:T(8,128)(2,1)S(1)}, bf16[40,9216]{1,0:T(8,128)(2,1)S(1)}, u32[]{:S(2)}, u32[]{:S(2)}) collective-permute-start(bf16[40,9216]{1,0:T(8,128)(2,1)S(1)} %collective-permute-done.4.refs_0_), channel_id=1, source_target_pairs={{2,6},{3,7},{6,10},{7,11},{10,14},{11,15},{14,12},{15,13},{12,8},{... | collective-permute-start | bytes 2211848 | tf_op jit(solution)/shard_map/ppermute | solution.py:396
  41.0 28.8 %collective-permute-start.10 = (bf16[40,9216]{1,0:T(8,128)(2,1)S(1)}, bf16[40,9216]{1,0:T(8,128)(2,1)S(1)}, u32[]{:S(2)}, u32[]{:S(2)}) collective-permute-start(bf16[40,9216]{1,0:T(8,128)(2,1)S(1)} %collective-permute-done.5.refs_1_), channel_id=1, source_target_pairs={{6,2},{7,3},{10,6},{11,7},{14,10},{15,11},{12,14},{13,15},{8,12},{... | collective-permute-start | bytes 2211848 | tf_op jit(solution)/shard_map/ppermute | solution.py:396
  41.5 13.4 %collective-permute-start.6 = (f32[240,512]{1,0:T(8,128)S(1)}, f32[240,512]{1,0:T(8,128)S(1)}, u32[]{:S(2)}, u32[]{:S(2)}) collective-permute-start(f32[240,512]{1,0:T(8,128)S(1)} %get-tuple-element.102.refs_1_), channel_id=1, source_target_pairs={{0,16},{16,0},{1,17},{17,1},{2,18},{18,2},{3,19},{19,3},{4,20},{20... | collective-permute-start | bytes 1474568 | tf_op jit(solution)/shard_map/ppermute | solution.py:389
  65.6 5.6 %collective-permute-start.11 = (f32[2,32,512]{2,1,0:T(8,128)S(1)}, f32[2,32,512]{2,1,0:T(8,128)S(1)}, u32[]{:S(2)}, u32[]{:S(2)}) collective-permute-start(f32[2,32,512]{2,1,0:T(8,128)S(1)} %get-tuple-element.133.refs_0_), channel_id=1, source_target_pairs={{0,16},{16,0},{1,17},{17,1},{2,18},{18,2},{3,19},{19,3},{4,20},{20... | collective-permute-start | bytes 393224 | tf_op jit(solution)/shard_map/ppermute | solution.py:389
  67.1 19.4 %collective-permute-start.7 = (bf16[40,9216]{1,0:T(8,128)(2,1)S(1)}, bf16[40,9216]{1,0:T(8,128)(2,1)S(1)}, u32[]{:S(2)}, u32[]{:S(2)}) collective-permute-start(bf16[40,9216]{1,0:T(8,128)(2,1)S(1)} %collective-permute-done.2.refs_0_), channel_id=1, source_target_pairs={{2,6},{3,7},{6,10},{7,11},{10,14},{11,15},{14,12},{15,13},{12,8},{... | collective-permute-start | bytes 2211848 | tf_op jit(solution)/shard_map/ppermute | solution.py:396
  68.7 19.4 %collective-permute-start.8 = (bf16[40,9216]{1,0:T(8,128)(2,1)S(1)}, bf16[40,9216]{1,0:T(8,128)(2,1)S(1)}, u32[]{:S(2)}, u32[]{:S(2)}) collective-permute-start(bf16[40,9216]{1,0:T(8,128)(2,1)S(1)} %collective-permute-done.3.refs_1_), channel_id=1, source_target_pairs={{6,2},{7,3},{10,6},{11,7},{14,10},{15,11},{12,14},{13,15},{8,12},{... | collective-permute-start | bytes 2211848 | tf_op jit(solution)/shard_map/ppermute | solution.py:396
  71.2 31.1 %collective-permute-start.15 = (bf16[40,9216]{1,0:T(8,128)(2,1)S(1)}, bf16[40,9216]{1,0:T(8,128)(2,1)S(1)}, u32[]{:S(2)}, u32[]{:S(2)}) collective-permute-start(bf16[40,9216]{1,0:T(8,128)(2,1)S(1)} %collective-permute-done.9.refs_0_), channel_id=1, source_target_pairs={{2,6},{3,7},{6,10},{7,11},{10,14},{11,15},{14,12},{15,13},{12,8},{... | collective-permute-start | bytes 2211848 | tf_op jit(solution)/shard_map/ppermute | solution.py:396
  72.7 31.2 %collective-permute-start.16 = (bf16[40,9216]{1,0:T(8,128)(2,1)S(1)}, bf16[40,9216]{1,0:T(8,128)(2,1)S(1)}, u32[]{:S(2)}, u32[]{:S(2)}) collective-permute-start(bf16[40,9216]{1,0:T(8,128)(2,1)S(1)} %collective-permute-done.10.refs_1_), channel_id=1, source_target_pairs={{6,2},{7,3},{10,6},{11,7},{14,10},{15,11},{12,14},{13,15},{8,12},{... | collective-permute-start | bytes 2211848 | tf_op jit(solution)/shard_map/ppermute | solution.py:396
  73.2 11.2 %collective-permute-start.12 = (f32[160,512]{1,0:T(8,128)S(1)}, f32[160,512]{1,0:T(8,128)S(1)}, u32[]{:S(2)}, u32[]{:S(2)}) collective-permute-start(f32[160,512]{1,0:T(8,128)S(1)} %get-tuple-element.121.refs_2_), channel_id=1, source_target_pairs={{0,16},{16,0},{1,17},{17,1},{2,18},{18,2},{3,19},{19,3},{4,20},{20... | collective-permute-start | bytes 983048 | tf_op jit(solution)/shard_map/ppermute | solution.py:389
  88.9 27.4 %collective-permute-start.13 = (bf16[40,4608]{1,0:T(8,128)(2,1)S(1)}, bf16[40,4608]{1,0:T(8,128)(2,1)S(1)}, u32[]{:S(2)}, u32[]{:S(2)}) collective-permute-start(bf16[40,4608]{1,0:T(8,128)(2,1)S(1)} %get-tuple-element.111), channel_id=1, source_target_pairs={{2,6},{3,7},{6,10},{7,11},{10,14},{11,15},{14,12},{15,13},{12,8},{... | collective-permute-start | bytes 1105928 | tf_op jit(solution)/shard_map/ppermute | solution.py:396
  90.5 25.8 %collective-permute-start.14 = (bf16[40,4608]{1,0:T(8,128)(2,1)S(1)}, bf16[40,4608]{1,0:T(8,128)(2,1)S(1)}, u32[]{:S(2)}, u32[]{:S(2)}) collective-permute-start(bf16[40,4608]{1,0:T(8,128)(2,1)S(1)} %get-tuple-element.112), channel_id=1, source_target_pairs={{6,2},{7,3},{10,6},{11,7},{14,10},{15,11},{12,14},{13,15},{8,12},{... | collective-permute-start | bytes 1105928 | tf_op jit(solution)/shard_map/ppermute | solution.py:396
  104.0 13.0 %collective-permute-start.17 = (bf16[40,4608]{1,0:T(8,128)(2,1)S(1)}, bf16[40,4608]{1,0:T(8,128)(2,1)S(1)}, u32[]{:S(2)}, u32[]{:S(2)}) collective-permute-start(bf16[40,4608]{1,0:T(8,128)(2,1)S(1)} %get-tuple-element.127), channel_id=1, source_target_pairs={{2,6},{3,7},{6,10},{7,11},{10,14},{11,15},{14,12},{15,13},{12,8},{... | collective-permute-start | bytes 1105928 | tf_op jit(solution)/shard_map/ppermute | solution.py:396
  105.6 12.6 %collective-permute-start.18 = (bf16[40,4608]{1,0:T(8,128)(2,1)S(1)}, bf16[40,4608]{1,0:T(8,128)(2,1)S(1)}, u32[]{:S(2)}, u32[]{:S(2)}) collective-permute-start(bf16[40,4608]{1,0:T(8,128)(2,1)S(1)} %get-tuple-element.128), channel_id=1, source_target_pairs={{6,2},{7,3},{10,6},{11,7},{14,10},{15,11},{12,14},{13,15},{8,12},{... | collective-permute-start | bytes 1105928 | tf_op jit(solution)/shard_map/ppermute | solution.py:396
  106.1 10.2 %collective-permute-start.19 = (f32[160,512]{1,0:T(8,128)S(1)}, f32[160,512]{1,0:T(8,128)S(1)}, u32[]{:S(2)}, u32[]{:S(2)}) collective-permute-start(f32[160,512]{1,0:T(8,128)S(1)} %get-tuple-element.137.refs_2_), channel_id=1, source_target_pairs={{0,16},{16,0},{1,17},{17,1},{2,18},{18,2},{3,19},{19,3},{4,20},{20... | collective-permute-start | bytes 983048 | tf_op jit(solution)/shard_map/ppermute | solution.py:389
  118.3 3.9 %collective-permute-start.21 = (bf16[40,4608]{1,0:T(8,128)(2,1)S(1)}, bf16[40,4608]{1,0:T(8,128)(2,1)S(1)}, u32[]{:S(2)}, u32[]{:S(2)}) collective-permute-start(bf16[40,4608]{1,0:T(8,128)(2,1)S(1)} %collective-permute-done.14.refs_1_), channel_id=1, source_target_pairs={{2,3},{3,2},{6,7},{7,6},{10,11},{11,10},{14,15},{15,14},{12,13},{1... | collective-permute-start | bytes 1105928 | tf_op jit(solution)/shard_map/ppermute | solution.py:448
  118.8 3.4 %collective-permute-start.22 = (bf16[40,4608]{1,0:T(8,128)(2,1)S(1)}, bf16[40,4608]{1,0:T(8,128)(2,1)S(1)}, u32[]{:S(2)}, u32[]{:S(2)}) collective-permute-start(bf16[40,4608]{1,0:T(8,128)(2,1)S(1)} %collective-permute-done.17.refs_2_), channel_id=1, source_target_pairs={{2,3},{3,2},{6,7},{7,6},{10,11},{11,10},{14,15},{15,14},{12,13},{1... | collective-permute-start | bytes 1105928 | tf_op jit(solution)/shard_map/ppermute | solution.py:448
  120.9 6.3 %collective-permute-start.24 = (f32[80,512]{1,0:T(8,128)S(1)}, f32[80,512]{1,0:T(8,128)S(1)}, u32[]{:S(2)}, u32[]{:S(2)}) collective-permute-start(f32[80,512]{1,0:T(8,128)S(1)} %project_last.3.refs_2_), channel_id=1, source_target_pairs={{0,16},{16,0},{1,17},{17,1},{2,18},{18,2},{3,19},{19,3},{4,20},{20... | collective-permute-start | bytes 491528 | tf_op jit(solution)/shard_map/ppermute | solution.py:389
  127.7 4.0 %collective-permute-start.25 = (f32[16,640]{1,0:T(8,128)S(1)}, f32[16,640]{1,0:T(8,128)S(1)}, u32[]{:S(2)}, u32[]{:S(2)}) collective-permute-start(f32[16,640]{1,0:T(8,128)S(1)} %score.7.refs_0_), channel_id=1, source_target_pairs={{0,16},{16,0},{1,17},{17,1},{2,18},{18,2},{3,19},{19,3},{4,20},{20... | collective-permute-start | bytes 122888 | tf_op jit(solution)/shard_map/ppermute | solution.py:389
  (2 other events, 5.1 us)

commit v5 on v4

--- a/solution.py
+++ b/solution.py
@@ -203,11 +203,18 @@
     held, factors = refs[:count], refs[count : count + 2]
     given, sums = refs[count + 2 : count + 2 + more], refs[-outs:]
     i = pl.program_id(0)
+    rows = sums[0].shape[0]
 
     @pl.when(i == 0)
     def _():
         for index, out in enumerate(sums):
-            out[...] = given[index][...] if more else jnp.zeros_like(out)
+            if outs == 1 and more:
+                out[...] = given[0][...]
+            else:
+                out[:rows] = jnp.zeros((rows, out.shape[1]), out.dtype)
+        if outs == 2 and more:
+            for j in range(2):
+                sums[1][rows + j * RANK : rows + (j + 1) * RANK] = given[0][j]
 
     for begin, width, which, offset in spans:
         first, steps = begin // step, width // step
@@ -217,7 +224,7 @@
             x = jnp.concatenate(
                 [x for h in held for x in ((h[0], h[1]) if len(h.shape) == 3 else (h[...],))], axis=0)
             at = pl.multiple_of((i - first) * step + offset, step)
-            sums[which if outs == 2 else 0][...] += jnp.dot(
+            sums[which if outs == 2 else 0][:rows] += jnp.dot(
                 x, factors[which][pl.ds(at, step), :], preferred_element_type=jnp.float32)
 
 
@@ -226,14 +233,17 @@
     step = chunk_of(*(size for _, size, _, _ in span))
     shape = (sum(math.prod(a.shape[:-1]) for a in arrays), factors[0].shape[1])
     extra = [] if start is None else [start]
+    shapes = [shape] * outs
+    if outs == 2 and extra:
+        shapes[1] = (shape[0] + 2 * RANK, shape[1])
     result = pl.pallas_call(
         functools.partial(project_kernel, step, tuple(span), len(arrays), outs, len(extra)),
         grid=(width // step,),
         in_specs=[
             pl.BlockSpec((*a.shape[:-1], step), lambda i, zeros=(0,) * (a.ndim - 1): (*zeros, i)) for a in arrays]
         + [pl.BlockSpec(memory_space=pltpu.VMEM)] * (2 + len(extra)),
-        out_specs=[pl.BlockSpec(shape, lambda i: (0, 0))] * outs,
-        out_shape=[jax.ShapeDtypeStruct(shape, jnp.float32)] * outs,
+        out_specs=[pl.BlockSpec(x, lambda i: (0, 0)) for x in shapes],
+        out_shape=[jax.ShapeDtypeStruct(x, jnp.float32) for x in shapes],
         compiler_params=params(),
         cost_estimate=LIGHT,
         name="project",
@@ -250,70 +260,84 @@
         x, member.astype(jnp.float32), precision=lax.Precision.HIGHEST, preferred_element_type=jnp.float32)
 
 
-def total_of(refs):
-    return sum(ref[...] for ref in refs[1:]) + refs[0][...]
-
-
-def project_last_kernel(spans, *refs):
-    count = len(spans)
-    held, mates = refs[:count], refs[count : 2 * count]
-    factors, out_ref = refs[2 * count : 2 * count + 2], refs[-1]
-    out_ref[...] = jnp.zeros_like(out_ref)
-    for mine, other, pieces in zip(held, mates, spans):
-        for begin, width, which, offset in pieces:
-            step = chunk_of(width)
-
-            @pl.loop(0, width // step)
-            def _(i, mine=mine, other=other, begin=begin, which=which, offset=offset, step=step):
+def total_of(refs, rows=None):
+    return sum(ref[:rows] for ref in refs[1:]) + refs[0][:rows]
+
+
+def project_last_kernel(plan, counts, *refs):
+    arrays, factors = refs[: counts[0]], refs[counts[0] : counts[0] + 2]
+    starts, out_ref = refs[counts[0] + 2 : -1], refs[-1]
+    if counts[1]:
+        first = 0
+        for start in starts:
+            out_ref[first : first + start.shape[0]] = start[...]
+            first += start.shape[0]
+    else:
+        out_ref[...] = jnp.zeros_like(out_ref)
+    for held, width, which, offset in plan:
+        step = chunk_of(width)
+
+        @pl.loop(0, width // step)
+        def _(i, held=held, which=which, offset=offset, step=step):
+            x = []
+            for index, begin in held:
                 at = pl.ds(pl.multiple_of(i * step + begin, 128), step)
-                x = jnp.concatenate([mine[:, at], other[:, at]], axis=0)
-                w = factors[which][pl.ds(pl.multiple_of(i * step + offset, 128), step), :]
-                out_ref[...] += jnp.dot(x, w, preferred_element_type=jnp.float32)
-
-
-def project_last(held, mates, spans, factors):
-    given = [in_vmem(x) for x in (*held, *mates, *factors)]
-    return pl.pallas_call(
-        functools.partial(project_last_kernel, tuple(tuple(s) for s in spans)),
+                ref = arrays[index]
+                x += [ref[0, :, at], ref[1, :, at]] if len(ref.shape) == 3 else [ref[:, at]]
+            w = factors[which][pl.ds(pl.multiple_of(i * step + offset, 128), step), :]
+            out_ref[...] += jnp.dot(jnp.concatenate(x, axis=0), w, preferred_element_type=jnp.float32)
+
+
+def project_last(arrays, plan, factors, starts=()):
+    rows = sum(math.prod(arrays[index].shape[:-1]) for index, _ in plan[0][0])
+    given = [in_vmem(x) for x in (*arrays, *factors)] + list(starts)
+    return pl.pallas_call(
+        functools.partial(project_last_kernel, tuple(plan), (len(arrays), len(starts))),
         in_specs=[pl.BlockSpec(memory_space=pltpu.VMEM)] * len(given),
         out_specs=pl.BlockSpec(memory_space=pltpu.VMEM),
-        out_shape=jax.ShapeDtypeStruct((2 * held[0].shape[0], factors[0].shape[1]), jnp.float32),
+        out_shape=jax.ShapeDtypeStruct((rows, factors[0].shape[1]), jnp.float32),
         compiler_params=params(),
         cost_estimate=LIGHT,
         name="project_last",
     )(*given)
 
 
-def score_kernel(counts, earlier, *refs):
+def score_kernel(plan, earlier, *refs):
     out_ref = refs[-1]
-    found, taken = [], earlier
-    for count in counts:
-        found.append(by_query(refs[taken][...] * total_of(refs[taken + 1 : taken + 1 + count])))
-        taken += 1 + count
+    one, found, first = refs[earlier][...], [], 0
+    taken = earlier + 1
+    for count, rows in plan:
+        found.append(by_query(one[first : first + rows] * total_of(refs[taken : taken + count], rows)))
+        taken += count
+        first += rows
     out_ref[...] = jnp.concatenate([*[ref[...] for ref in refs[:earlier]], jnp.concatenate(found, axis=0).T], axis=1)
 
 
-def score(groups, *earlier):
-    rows, columns = sum(one.shape[0] for one, _ in groups), groups[0][0].shape[1]
-    return pl.pallas_call(
-        functools.partial(score_kernel, tuple(len(parts) for _, parts in groups), len(earlier)),
-        out_shape=jax.ShapeDtypeStruct((columns // RANK, rows + sum(x.shape[1] for x in earlier)), jnp.float32),
+def score(one, others, earlier=()):
+    rows = one.shape[0]
+    plan = tuple((len(parts), count) for parts, count in others)
+    return pl.pallas_call(
+        functools.partial(score_kernel, plan, len(earlier)),
+        out_shape=jax.ShapeDtypeStruct(
+            (one.shape[1] // RANK, rows + sum(x.shape[1] for x in earlier)), jnp.float32),
         compiler_params=params(),
         cost_estimate=LIGHT,
         name="score",
-    )(*earlier, *[x for one, parts in groups for x in (one, *parts)])
+    )(*earlier, one, *[x for parts, _ in others for x in parts])
 
 
 def inverse_kernel(*refs):
-    gram, out_ref = total_of(refs[:-1]), refs[-1]
-    norms = jnp.broadcast_to((gram[0] * gram[1]).sum(axis=0, keepdims=True), (8, gram.shape[2]))
-    out_ref[...] = 1.0 / jnp.sqrt(by_query(norms) + 1e-06)
+    out_ref = refs[-1]
+    gram = total_of(refs[:-1])[-2 * RANK :]
+    norms = jnp.broadcast_to((gram[:RANK] * gram[RANK:]).sum(axis=0, keepdims=True), (8, gram.shape[1]))
+    inverse = 1.0 / jnp.sqrt(by_query(norms) + 1e-06)
+    out_ref[...] = jnp.broadcast_to(inverse.T[:, :1], out_ref.shape)
 
 
 def inverse_norms(parts):
     return pl.pallas_call(
         inverse_kernel,
-        out_shape=jax.ShapeDtypeStruct((8, parts[0].shape[2] // RANK), jnp.float32),
+        out_shape=jax.ShapeDtypeStruct((parts[0].shape[1] // RANK, 128), jnp.float32),
         compiler_params=params(),
         cost_estimate=LIGHT,
         name="inverse_norms",
@@ -324,50 +348,47 @@
     return sum(jnp.where(index == i, value, 0) for i, value in enumerate(table))
 
 
-def last_kernel(count, groups, place, tokens, at_ref, inverse_ref, *refs):
-    out_ref, held = refs[-2:]
+def last_kernel(count, groups, place, tokens, inverse_ref, *refs):
+    out_ref = refs[-1]
     chips = len(place)
-    scores = total_of(refs[:count]).T * inverse_ref[:1]
+    scores = jnp.concatenate([total_of(refs[i : i + count]) for i in range(0, len(refs) - 1, count)], axis=1)
+    width = scores.shape[1]
+    starts = [[0] * chips for _ in range(2)]
     first = 0
     for group in groups:
         for c in range(2):
             for distance in group:
-                core = (at_ref[0] + c) % 2 if distance == chips // 2 else c
-                held[distance % chips, core] = scores[first : first + tokens]
+                starts[c][distance % chips] = first
                 first += tokens
-    here = looked_up(place, at_ref[0] // 2)
-    side = at_ref[1]
+    query_at, side = lax.axis_index("query"), lax.axis_index("rows")
+    core = query_at % 2
+    here = looked_up(place, query_at // 2)
     share = out_ref.shape[1] // (2 * tokens)
-    blocks = []
+    lane = lax.broadcasted_iota(jnp.int32, scores.shape, 1) // tokens
+    result = jnp.zeros_like(scores)
     for j in range(share):
-        there = looked_up(place, side * share + j)
-        distance = there - here
+        distance = looked_up(place, side * share + j) - here
         distance = jnp.where(distance < 0, distance + chips, distance)
-        blocks += [held[distance, c] for c in range(2)]
-    out_ref[...] = jnp.concatenate(blocks, axis=0).T
-
-
-def last(parts, inverse, groups, place, tokens, share, at):
-    queries = inverse.shape[1]
-    return pl.pallas_call(
-        functools.partial(last_kernel, len(parts), groups, place, tokens),
-        in_specs=[pl.BlockSpec(memory_space=pltpu.SMEM)] + [pl.BlockSpec(memory_space=pltpu.VMEM)] * (1 + len(parts)),
+        firsts = [looked_up(starts[c], distance) for c in range(2)]
+        turned = (distance == chips // 2) & (core == 1)
+        firsts = [jnp.where(turned, firsts[1 - c], firsts[c]) for c in range(2)]
+        for c in range(2):
+            shift = (2 * j + c) * tokens - firsts[c]
+            shift = jnp.where(shift < 0, shift + width, shift)
+            result = jnp.where(lane == 2 * j + c, pltpu.roll(scores, shift, 1), result)
+    out_ref[...] = result[:, : out_ref.shape[1]] * inverse_ref[:, :1]
+
+
+def last(results, inverse, groups, place, tokens, share):
+    return pl.pallas_call(
+        functools.partial(last_kernel, len(results[0]), groups, place, tokens),
+        in_specs=[pl.BlockSpec(memory_space=pltpu.VMEM)] * (1 + sum(len(parts) for parts in results)),
         out_specs=pl.BlockSpec(memory_space=pltpu.VMEM),
-        out_shape=jax.ShapeDtypeStruct((queries, share), jnp.float32),
-        scratch_shapes=[pltpu.VMEM((len(place), 2, tokens, queries), jnp.float32)],
+        out_shape=jax.ShapeDtypeStruct((inverse.shape[0], share), jnp.float32),
         compiler_params=params(),
         cost_estimate=LIGHT,
         name="last_scores",
-    )(at, inverse, *parts)
-
-
-def within(spans, low, high):
-    kept = []
-    for begin, width, which, offset in spans:
-        a, b = max(begin, low), min(begin + width, high)
-        if a < b:
-            kept.append((a - low, b - a, which, offset + a - begin))
-    return kept
+    )(inverse, *[x for parts in results for x in parts])
 
 
 def solution(mesh):
@@ -392,6 +413,9 @@
     def both_cores(x):
         return lax.all_to_all(x, "query", 0, 0, axis_index_groups=sorted(ring))
 
+    def mate(xs):
+        return [lax.ppermute(x, "query", mates) for x in xs]
+
     def round_ring(pair):
         return [lax.ppermute(pair[0], "query", forward), lax.ppermute(pair[1], "query", backward)]
 
@@ -405,59 +429,68 @@
         cut = half - depth
         assert cut > 0
         spans = [[(0, depth, 1, 0), (depth, cut, 0, 0)], [(0, width - cut, 0, cut)]]
-        middles = [sum(s[1] for s in span) // 256 * 128 for span in spans]
-        at = jnp.stack([lax.axis_index("query"), lax.axis_index("rows")]).astype(jnp.int32)
         last_hop = chips // 2
 
-        def next_of(pair, hop, stream):
-            if hop + 1 == last_hop:
-                middle = middles[stream]
-                pair = columns_of(pair, [[(0, 0, middle)], [(1, middle, pair[1].shape[1])]], True)
-            return round_ring(pair)
-
-        at, acts, grads, in_factors, out_factors = tied(at, acts, grads, in_factors, out_factors)
         (own0,) = columns_of([in_hbm(grads), in_hbm(acts)], [[(0, 0, depth), (1, 0, cut)]], True)
         fly0 = round_ring([own0, own0])
         (own1,) = columns_of([in_hbm(acts)], [[(0, cut, width)]], True)
         fly1 = round_ring([own1, own1])
         *factors, gram = load(in_factors, out_factors)
         fly0, own0, own1, gram = tied(fly0, own0, own1, gram)
-        groups, pairs, found, gram_parts = [], [], [], []
+        groups, pair, found = [], [], []
         for hop in range(1, last_hop):
             extra = hop == 1
+            final = hop + 1 == last_hop
             groups.append((-hop, hop) + (0,) * extra)
-            held = fly0
-            fly0 = next_of(held, hop, 0)
-            other, part = project([both_cores(twice(held + [own0] * extra))], spans[0], factors, 2)[::-1]
-            if pairs:
-                part, pairs, gram = tied(part, pairs, gram)
-                found = [score(pairs, *found)]
-                gram_parts = gram_parts or across(gram)
-            fly1, other, part, found, gram_parts = tied(fly1, other, part, found, gram_parts)
-            held = fly1
-            fly1 = next_of(held, hop, 1)
-            one = project([both_cores(twice(held + [own1] * extra))], spans[1], factors, 1, part)
-            other = across(other)
-            if hop + 1 < last_hop:
+            held0 = fly0
+            if final:
+                middle, low = depth // 256 * 128, cut // 256 * 128
+                fly0 = columns_of(held0, [
+                    [(0, 0, middle), (0, depth, depth + low)], [(1, middle, depth), (1, depth + low, half)]], True)
+            fly0 = round_ring(fly0)
+            other, part = project(
+                [both_cores(twice(held0 + [own0] * extra))], spans[0], factors, 2,
+                gram if hop == min(2, last_hop - 1) else None)[::-1]
+            if pair:
+                part, pair = tied(part, pair)
+                found = [score(pair[0], [(pair[1], pair[0].shape[0])], found)]
+            fly1, other, part, found = tied(fly1, other, part, found)
+            held1 = fly1
+            if final:
+                high = (width - cut) // 256 * 128
+                fly1 = columns_of(held1, [[(0, 0, high)], [(1, high, width - cut)]], True)
+            fly1 = round_ring(fly1)
+            swapped = both_cores(twice(held1 + [own1] * extra))
+            if final:
+                other = across(other)
+                fly0, swapped, other, part = tied(fly0, swapped, other, part)
+            else:
+                one = project([swapped], spans[1], factors, 1, part)
+                other = across(other)
                 fly0, one, other = tied(fly0, one, other)
-            else:
-                fly0, fly1, one, other, gram_parts = tied(fly0, fly1, one, other, gram_parts)
-            pairs = [(one, other)]
+                pair = (one, other)
+            if hop == min(2, last_hop - 1):
+                gram_parts = other
         groups.append((last_hop,))
-        held = [*fly0, *fly1]
-        swapped = [lax.ppermute(x, "query", mates) for x in held]
-        pieces = [
-            within(span, lo, hi)
-            for span, middle in zip(spans, middles) for lo, hi in ((0, middle), (middle, sum(s[1] for s in span)))]
-        chosen = [[[s for s in piece if s[2] == which] for piece in pieces] for which in range(2)]
-        used = [[i for i, piece in enumerate(c) if piece] for c in chosen]
-        one, other = [
-            project_last([held[i] for i in u], [swapped[i] for i in u], [c[i] for i in u], factors)
-            for u, c in zip(used, chosen)]
-        found = score(pairs, *found)
+        arrays = [swapped]
+        held = columns_of(fly0, [
+            [(0, 0, middle), (1, 0, depth - middle)],
+            [(0, middle, middle + low)], [(1, depth - middle, half - middle - low)]], True)
+        swapped = mate(held)
+        last_other = project_last([held[0], swapped[0]], [(((0, 0), (1, 0)), depth, 1, 0)], factors)
+        last_part = project_last([*held[1:], *swapped[1:]], [
+            (((0, 0), (2, 0)), low, 0, 0), (((1, 0), (3, 0)), cut - low, 0, low)], factors)
         inverse = inverse_norms(gram_parts)
-        scores = score([(one, across(other))], found)
-        return last(across(scores), inverse, tuple(groups), place, tokens, query * tokens // rows, at).T
+        results = [across(x) for x in found]
+        fly1, arrays, part, last_part, last_other, inverse, results = tied(
+            fly1, arrays, part, last_part, last_other, inverse, results)
+        swapped = mate(fly1)
+        last_other = across(last_other)
+        one = project_last([*arrays, *fly1, *swapped], [
+            (((0, 0), (1, 0), (3, 0)), high, 0, cut),
+            (((0, high), (2, 0), (4, 0)), width - cut - high, 0, cut + high)], factors, [part, last_part])
+        results.append(across(score(one, [(other, part.shape[0]), (last_other, 2 * tokens)])))
+        return last(results, inverse, tuple(groups), place, tokens, query * tokens // rows).T
 
     return jax.shard_map(
         local,

time: 133 us -> 131 us (0.985)
  Pallas kernels: 45.2 us -> 42.8 us
    pallas_call x6 -> x5, Pallas kernels: 21.1 us -> 18.2 us  [project(): pl.pallas_call(functools.partial(project_kernel, step, tuple(span), len(a...]
    ppermute x8, waiting for transfers between devices: 9.25 us -> 6.71 us  [round_ring(): lax.ppermute(pair[0], 'query', forward)]
    ppermute x8, waiting for transfers between devices: 8.18 us -> 10.3 us  [round_ring(): lax.ppermute(pair[1], 'query', backward)]
    ppermute x6, waiting for transfers between devices: 5.85 us -> 4.41 us  [across(): return [x, lax.ppermute(x, 'rows', [(0, 1), (1, 0)])]]
    pallas_call x4 -> x5, Pallas kernels: 2.4 us -> 2.78 us  [columns_of(): pl.pallas_call(functools.partial(copy_kernel, tuple(plan), len(arrays)),...]
  transfers between devices with their start and end apart: 26 -> 27, of which waited for: 14 -> 15; matrix products, arithmetic and copies ran while one was open for 0% -> 0% of each run, Pallas kernels for 32% -> 31%
where the time goes in v5:
time: 131 us
  Pallas kernels  42.8 us (33%)
  blocking collectives  38.9 us (30%)
  starting transfers between devices  25.8 us (20%)
  waiting for transfers between devices  23.3 us (18%)
    all_to_all x6, blocking collectives, both_cores(): return lax.all_to_all(x, 'query', 0, 0, axis_index_groups=sorted(ring))  38.9 us
    pallas_call x5, Pallas kernels, project(): pl.pallas_call(functools.partial(project_kernel, step, tuple(span), len(a...  18.2 us
    ppermute x8, starting transfers between devices, round_ring(): lax.ppermute(pair[0], 'query', forward)  14.9 us
    ppermute x8, waiting for transfers between devices, round_ring(): lax.ppermute(pair[1], 'query', backward)  10.3 us
    pallas_call x1, Pallas kernels, load(): pl.pallas_call(functools.partial(load_kernel, step), in_specs=[pl.BlockSp...  8.62 us
    ppermute x6, starting transfers between devices, across(): return [x, lax.ppermute(x, 'rows', [(0, 1), (1, 0)])]  7.1 us
    ppermute x8, waiting for transfers between devices, round_ring(): lax.ppermute(pair[0], 'query', forward)  6.71 us
    pallas_call x3, Pallas kernels, project_last(): pl.pallas_call(functools.partial(project_last_kernel, tuple(plan), (len(a...  5.76 us
  transfers between devices with their start and end apart: 27, of which 15 were waited for; matrix products, arithmetic and copies ran while one was open for 0% of the time, Pallas kernels for 31%

profile of v5, /device:TPU:0, one launch (start us, length us, event | category | flops | bytes accessed | tf_op | source)
XLA Modules:
  0.0 131.1 jit_solution(16655826723915271359)
XLA Ops:
  1.1 3.0 %collective-permute-start.2 = (bf16[40,9216]{1,0:T(8,128)(2,1)S(1)}, bf16[40,9216]{1,0:T(8,128)(2,1)S(1)}, u32[]{:S(2)}, u32[]{:S(2)}) collective-permute-start(bf16[40,9216]{1,0:T(8,128)(2,1)S(1)} %columns.6.refs_2_), channel_id=1, source_target_pairs={{2,6},{3,7},{6,10},{7,11},{10,14},{11,15},{14,12},{15,13},{12,8},{... | collective-permute-start | bytes 2211848 | tf_op jit(solution)/shard_map/ppermute | solution.py:420
  5.4 2.0 %collective-permute-start = (bf16[40,9216]{1,0:T(8,128)(2,1)S(1)}, bf16[40,9216]{1,0:T(8,128)(2,1)S(1)}, u32[]{:S(2)}, u32[]{:S(2)}) collective-permute-start(bf16[40,9216]{1,0:T(8,128)(2,1)S(1)} %columns.5.refs_2_), channel_id=1, source_target_pairs={{2,6},{3,7},{6,10},{7,11},{10,14},{11,15},{14,12},{15,13},{12,8},{... | collective-permute-start | bytes 2211848 | tf_op jit(solution)/shard_map/ppermute | solution.py:420
  7.5 8.6 %load_factors.1 = (bf16[14336,512]{1,0:T(8,128)(2,1)S(1)}, bf16[4096,512]{1,0:T(8,128)(2,1)S(1)}, f32[2,32,512]{2,1,0:T(8,128)S(1)}) custom-call(bf16[14336,512]{1,0:T(8,128)(2,1)} %a_ref.1, bf16[4096,512]{1,0:T(8,128)(2,1)} %b_ref.1), custom_call_target="tpu_custom_call" | custom-call | flops 1 | bytes 1 | tf_op jit(solution)/shard_map/load_factors/pallas_call | solution.py:136
  16.1 5.4 %collective-permute-done.2.refs_0_ = bf16[40,9216]{1,0:T(8,128)(2,1)S(1)} collective-permute-done((bf16[40,9216]{1,0:T(8,128)(2,1)S(1)}, bf16[40,9216]{1,0:T(8,128)(2,1)S(1)}, u32[]{:S(2)}, u32[]{:S(2)}) %collective-permute-start.2) | collective-permute-done | bytes 737312 | tf_op jit(solution)/shard_map/ppermute | solution.py:420
  21.5 2.0 %collective-permute-done.3.refs_1_ = bf16[40,9216]{1,0:T(8,128)(2,1)S(1)} collective-permute-done((bf16[40,9216]{1,0:T(8,128)(2,1)S(1)}, bf16[40,9216]{1,0:T(8,128)(2,1)S(1)}, u32[]{:S(2)}, u32[]{:S(2)}) %collective-permute-start.3) | collective-permute-done | bytes 737312 | tf_op jit(solution)/shard_map/ppermute | solution.py:420
  26.5 7.3 %all_to_all.30.refs_0_ = bf16[2,120,9216]{2,1,0:T(8,128)(2,1)S(1)} all-to-all(bf16[2,120,9216]{2,1,0:T(8,128)(2,1)S(1)} %pack.6), channel_id=1, replica_groups={{0,1},{2,3},{4,5},{6,7},{8,9},{10,11},{12,13},{14,15},{16,17},{18,19},{..., dimensions={0} | all-to-all | bytes 8847360 | tf_op jit(solution)/shard_map/all_to_all | solution.py:414
  33.7 4.4 %project.5 = (f32[240,512]{1,0:T(8,128)S(1)}, f32[240,512]{1,0:T(8,128)S(1)}) custom-call(bf16[2,120,9216]{2,1,0:T(8,128)(2,1)S(1)} %all_to_all.30.refs_0_, bf16[14336,512]{1,0:T(8,128)(2,1)S(1)} %get-tuple-element.77.refs_1_.refs_4_.refs_2_.refs_5_, bf16[4096,512]{1,0:T(8,128)(2,1)S(1)} %get-tuple-element.78.refs_2_.refs_5_.refs_3_.refs_6_), custom_call_target="tpu_custom_call" | custom-call | flops 1 | bytes 1 | tf_op jit(solution)/shard_map/project/pallas_call | solution.py:239
  43.8 7.3 %all_to_all.31.refs_0_ = bf16[2,120,9216]{2,1,0:T(8,128)(2,1)S(1)} all-to-all(bf16[2,120,9216]{2,1,0:T(8,128)(2,1)S(1)} %pack.7), channel_id=1, replica_groups={{0,1},{2,3},{4,5},{6,7},{8,9},{10,11},{12,13},{14,15},{16,17},{18,19},{..., dimensions={0} | all-to-all | bytes 8847360 | tf_op jit(solution)/shard_map/all_to_all | solution.py:414
  51.0 3.7 %project.6.refs_0_ = f32[240,512]{1,0:T(8,128)S(1)} custom-call(bf16[2,120,9216]{2,1,0:T(8,128)(2,1)S(1)} %all_to_all.31.refs_0_, bf16[14336,512]{1,0:T(8,128)(2,1)S(1)} %get-tuple-element.77.refs_1_.refs_4_.refs_2_.refs_5_, bf16[4096,512]{1,0:T(8,128)(2,1)S(1)} %get-tuple-element.78.refs_2_.refs_5_.refs_3_.refs_6_, f32[240,512]{1,0:T(8,128)S(1)} %get-tuple-element.84.refs_3_), custom_call_target="tpu_custom_call" | custom-call | flops 1 | bytes 1 | tf_op jit(solution)/shard_map/project/pallas_call | solution.py:239
  57.8 6.1 %all_to_all.32.refs_0_ = bf16[2,80,9216]{2,1,0:T(8,128)(2,1)S(1)} all-to-all(bf16[2,80,9216]{2,1,0:T(8,128)(2,1)S(1)} %pack.8), channel_id=1, replica_groups={{0,1},{2,3},{4,5},{6,7},{8,9},{10,11},{12,13},{14,15},{16,17},{18,19},{..., dimensions={0} | all-to-all | bytes 5898240 | tf_op jit(solution)/shard_map/all_to_all | solution.py:414
  63.9 3.6 %project.7 = (f32[160,512]{1,0:T(8,128)S(1)}, f32[224,512]{1,0:T(8,128)S(1)}) custom-call(bf16[2,80,9216]{2,1,0:T(8,128)(2,1)S(1)} %all_to_all.32.refs_0_, bf16[14336,512]{1,0:T(8,128)(2,1)S(1)} %get-tuple-element.77.refs_1_.refs_4_.refs_2_.refs_5_, bf16[4096,512]{1,0:T(8,128)(2,1)S(1)} %get-tuple-element.78.refs_2_.refs_5_.refs_3_.refs_6_, ...), custom_call_target="tpu_custom_call" | custom-call | flops 1 | bytes 1 | tf_op jit(solution)/shard_map/project/pallas_call | solution.py:239
  68.9 2.0 %collective-permute-done.5.refs_1_ = bf16[40,9216]{1,0:T(8,128)(2,1)S(1)} collective-permute-done((bf16[40,9216]{1,0:T(8,128)(2,1)S(1)}, bf16[40,9216]{1,0:T(8,128)(2,1)S(1)}, u32[]{:S(2)}, u32[]{:S(2)}) %collective-permute-start.5) | collective-permute-done | bytes 737312 | tf_op jit(solution)/shard_map/ppermute | solution.py:420
  71.0 1.9 %collective-permute-start.9 = (bf16[40,9216]{1,0:T(8,128)(2,1)S(1)}, bf16[40,9216]{1,0:T(8,128)(2,1)S(1)}, u32[]{:S(2)}, u32[]{:S(2)}) collective-permute-start(bf16[40,9216]{1,0:T(8,128)(2,1)S(1)} %collective-permute-done.4.refs_0_), channel_id=1, source_target_pairs={{2,6},{3,7},{6,10},{7,11},{10,14},{11,15},{14,12},{15,13},{12,8},{... | collective-permute-start | bytes 2211848 | tf_op jit(solution)/shard_map/ppermute | solution.py:420
  75.1 6.1 %all_to_all.33.refs_0_ = bf16[2,80,9216]{2,1,0:T(8,128)(2,1)S(1)} all-to-all(bf16[2,80,9216]{2,1,0:T(8,128)(2,1)S(1)} %pack.9), channel_id=1, replica_groups={{0,1},{2,3},{4,5},{6,7},{8,9},{10,11},{12,13},{14,15},{16,17},{18,19},{..., dimensions={0} | all-to-all | bytes 5898240 | tf_op jit(solution)/shard_map/all_to_all | solution.py:414
  81.2 2.9 %project.8.refs_1_ = f32[160,512]{1,0:T(8,128)S(1)} custom-call(bf16[2,80,9216]{2,1,0:T(8,128)(2,1)S(1)} %all_to_all.33.refs_0_, bf16[14336,512]{1,0:T(8,128)(2,1)S(1)} %get-tuple-element.77.refs_1_.refs_4_.refs_2_.refs_5_, bf16[4096,512]{1,0:T(8,128)(2,1)S(1)} %get-tuple-element.78.refs_2_.refs_5_.refs_3_.refs_6_, f32[160,512]{1,0:T(8,128)S(1)} %get-tuple-element.100.refs_3_), custom_call_target="tpu_custom_call" | custom-call | flops 1 | bytes 1 | tf_op jit(solution)/shard_map/project/pallas_call | solution.py:239
  84.7 2.0 %collective-permute-done.12.refs_1_ = bf16[40,9216]{1,0:T(8,128)(2,1)S(1)} collective-permute-done((bf16[40,9216]{1,0:T(8,128)(2,1)S(1)}, bf16[40,9216]{1,0:T(8,128)(2,1)S(1)}, u32[]{:S(2)}, u32[]{:S(2)}) %collective-permute-start.12) | collective-permute-done | bytes 737312 | tf_op jit(solution)/shard_map/ppermute | solution.py:420
  87.0 1.6 %collective-permute-start.16 = (bf16[40,4608]{1,0:T(8,128)(2,1)S(1)}, bf16[40,4608]{1,0:T(8,128)(2,1)S(1)}, u32[]{:S(2)}, u32[]{:S(2)}) collective-permute-start(bf16[40,4608]{1,0:T(8,128)(2,1)S(1)} %get-tuple-element.118), channel_id=1, source_target_pairs={{2,6},{3,7},{6,10},{7,11},{10,14},{11,15},{14,12},{15,13},{12,8},{... | collective-permute-start | bytes 1105928 | tf_op jit(solution)/shard_map/ppermute | solution.py:420
  89.7 6.1 %all_to_all.34.refs_0_ = bf16[2,80,9216]{2,1,0:T(8,128)(2,1)S(1)} all-to-all(bf16[2,80,9216]{2,1,0:T(8,128)(2,1)S(1)} %pack.10), channel_id=1, replica_groups={{0,1},{2,3},{4,5},{6,7},{8,9},{10,11},{12,13},{14,15},{16,17},{18,19},{..., dimensions={0} | all-to-all | bytes 5898240 | tf_op jit(solution)/shard_map/all_to_all | solution.py:414
  95.8 3.6 %project.9 = (f32[160,512]{1,0:T(8,128)S(1)}, f32[160,512]{1,0:T(8,128)S(1)}) custom-call(bf16[2,80,9216]{2,1,0:T(8,128)(2,1)S(1)} %all_to_all.34.refs_0_, bf16[14336,512]{1,0:T(8,128)(2,1)S(1)} %get-tuple-element.77.refs_1_.refs_4_.refs_2_.refs_5_, bf16[4096,512]{1,0:T(8,128)(2,1)S(1)} %get-tuple-element.78.refs_2_.refs_5_.refs_3_.refs_6_), custom_call_target="tpu_custom_call" | custom-call | flops 1 | bytes 1 | tf_op jit(solution)/shard_map/project/pallas_call | solution.py:239
  100.0 2.5 %collective-permute-done.10.refs_1_ = bf16[40,9216]{1,0:T(8,128)(2,1)S(1)} collective-permute-done((bf16[40,9216]{1,0:T(8,128)(2,1)S(1)}, bf16[40,9216]{1,0:T(8,128)(2,1)S(1)}, u32[]{:S(2)}, u32[]{:S(2)}) %collective-permute-start.10) | collective-permute-done | bytes 737312 | tf_op jit(solution)/shard_map/ppermute | solution.py:420
  104.1 1.6 %collective-permute-start.14 = (bf16[40,4608]{1,0:T(8,128)(2,1)S(1)}, bf16[40,4608]{1,0:T(8,128)(2,1)S(1)}, u32[]{:S(2)}, u32[]{:S(2)}) collective-permute-start(bf16[40,4608]{1,0:T(8,128)(2,1)S(1)} %get-tuple-element.116), channel_id=1, source_target_pairs={{2,6},{3,7},{6,10},{7,11},{10,14},{11,15},{14,12},{15,13},{12,8},{... | collective-permute-start | bytes 1105928 | tf_op jit(solution)/shard_map/ppermute | solution.py:420
  106.9 6.1 %all_to_all.35.refs_0_ = bf16[2,80,9216]{2,1,0:T(8,128)(2,1)S(1)} all-to-all(bf16[2,80,9216]{2,1,0:T(8,128)(2,1)S(1)} %pack.11), channel_id=1, replica_groups={{0,1},{2,3},{4,5},{6,7},{8,9},{10,11},{12,13},{14,15},{16,17},{18,19},{..., dimensions={0} | all-to-all | bytes 5898240 | tf_op jit(solution)/shard_map/all_to_all | solution.py:414
  121.4 3.3 %project_last.5.refs_0_ = f32[240,512]{1,0:T(8,128)S(1)} custom-call(bf16[2,80,9216]{2,1,0:T(8,128)(2,1)S(1)} %all_to_all.35.refs_0_, bf16[40,4608]{1,0:T(8,128)(2,1)S(1)} %collective-permute-done.14.refs_1_, bf16[40,4608]{1,0:T(8,128)(2,1)S(1)} %collective-permute-done.15.refs_2_, bf16[40,4608]{1,0:T(8,128)(2,1)S(1)} %collective-permute-done.23.refs_3_, ...), custom_call_target="tpu_custom_call" | custom-call | flops 1 | bytes 1 | tf_op jit(solution)/shard_map/project_last/pallas_call | solution.py:294
  127.5 2.7 %collective-permute-done.26.refs_3_ = f32[16,240]{1,0:T(8,128)S(1)} collective-permute-done((f32[16,240]{1,0:T(8,128)S(1)}, f32[16,240]{1,0:T(8,128)S(1)}, u32[]{:S(2)}, u32[]{:S(2)}) %collective-permute-start.26) | collective-permute-done | bytes 15392 | tf_op jit(solution)/shard_map/ppermute | solution.py:410
  (61 shorter events, 34.9 us)
Async XLA Ops:
  1.1 20.4 %collective-permute-start.2 = (bf16[40,9216]{1,0:T(8,128)(2,1)S(1)}, bf16[40,9216]{1,0:T(8,128)(2,1)S(1)}, u32[]{:S(2)}, u32[]{:S(2)}) collective-permute-start(bf16[40,9216]{1,0:T(8,128)(2,1)S(1)} %columns.6.refs_2_), channel_id=1, source_target_pairs={{2,6},{3,7},{6,10},{7,11},{10,14},{11,15},{14,12},{15,13},{12,8},{... | collective-permute-start | bytes 2211848 | tf_op jit(solution)/shard_map/ppermute | solution.py:420
  4.1 19.4 %collective-permute-start.3 = (bf16[40,9216]{1,0:T(8,128)(2,1)S(1)}, bf16[40,9216]{1,0:T(8,128)(2,1)S(1)}, u32[]{:S(2)}, u32[]{:S(2)}) collective-permute-start(bf16[40,9216]{1,0:T(8,128)(2,1)S(1)} %columns.6.refs_2_), channel_id=1, source_target_pairs={{6,2},{7,3},{10,6},{11,7},{14,10},{15,11},{12,14},{13,15},{8,12},{... | collective-permute-start | bytes 2211848 | tf_op jit(solution)/shard_map/ppermute | solution.py:420
  5.4 32.7 %collective-permute-start = (bf16[40,9216]{1,0:T(8,128)(2,1)S(1)}, bf16[40,9216]{1,0:T(8,128)(2,1)S(1)}, u32[]{:S(2)}, u32[]{:S(2)}) collective-permute-start(bf16[40,9216]{1,0:T(8,128)(2,1)S(1)} %columns.5.refs_2_), channel_id=1, source_target_pairs={{2,6},{3,7},{6,10},{7,11},{10,14},{11,15},{14,12},{15,13},{12,8},{... | collective-permute-start | bytes 2211848 | tf_op jit(solution)/shard_map/ppermute | solution.py:420
  7.4 32.0 %collective-permute-start.1 = (bf16[40,9216]{1,0:T(8,128)(2,1)S(1)}, bf16[40,9216]{1,0:T(8,128)(2,1)S(1)}, u32[]{:S(2)}, u32[]{:S(2)}) collective-permute-start(bf16[40,9216]{1,0:T(8,128)(2,1)S(1)} %columns.5.refs_2_), channel_id=1, source_target_pairs={{6,2},{7,3},{10,6},{11,7},{14,10},{15,11},{12,14},{13,15},{8,12},{... | collective-permute-start | bytes 2211848 | tf_op jit(solution)/shard_map/ppermute | solution.py:420
  23.6 31.2 %collective-permute-start.6 = (bf16[40,9216]{1,0:T(8,128)(2,1)S(1)}, bf16[40,9216]{1,0:T(8,128)(2,1)S(1)}, u32[]{:S(2)}, u32[]{:S(2)}) collective-permute-start(bf16[40,9216]{1,0:T(8,128)(2,1)S(1)} %collective-permute-done.2.refs_0_), channel_id=1, source_target_pairs={{2,6},{3,7},{6,10},{7,11},{10,14},{11,15},{14,12},{15,13},{12,8},{... | collective-permute-start | bytes 2211848 | tf_op jit(solution)/shard_map/ppermute | solution.py:420
  25.1 30.0 %collective-permute-start.7 = (bf16[40,9216]{1,0:T(8,128)(2,1)S(1)}, bf16[40,9216]{1,0:T(8,128)(2,1)S(1)}, u32[]{:S(2)}, u32[]{:S(2)}) collective-permute-start(bf16[40,9216]{1,0:T(8,128)(2,1)S(1)} %collective-permute-done.3.refs_1_), channel_id=1, source_target_pairs={{6,2},{7,3},{10,6},{11,7},{14,10},{15,11},{12,14},{13,15},{8,12},{... | collective-permute-start | bytes 2211848 | tf_op jit(solution)/shard_map/ppermute | solution.py:420
  39.4 29.6 %collective-permute-start.4 = (bf16[40,9216]{1,0:T(8,128)(2,1)S(1)}, bf16[40,9216]{1,0:T(8,128)(2,1)S(1)}, u32[]{:S(2)}, u32[]{:S(2)}) collective-permute-start(bf16[40,9216]{1,0:T(8,128)(2,1)S(1)} %collective-permute-done.refs_0_), channel_id=1, source_target_pairs={{2,6},{3,7},{6,10},{7,11},{10,14},{11,15},{14,12},{15,13},{12,8},{... | collective-permute-start | bytes 2211848 | tf_op jit(solution)/shard_map/ppermute | solution.py:420
  40.9 30.0 %collective-permute-start.5 = (bf16[40,9216]{1,0:T(8,128)(2,1)S(1)}, bf16[40,9216]{1,0:T(8,128)(2,1)S(1)}, u32[]{:S(2)}, u32[]{:S(2)}) collective-permute-start(bf16[40,9216]{1,0:T(8,128)(2,1)S(1)} %collective-permute-done.1.refs_1_), channel_id=1, source_target_pairs={{6,2},{7,3},{10,6},{11,7},{14,10},{15,11},{12,14},{13,15},{8,12},{... | collective-permute-start | bytes 2211848 | tf_op jit(solution)/shard_map/ppermute | solution.py:420
  41.4 13.4 %collective-permute-start.8 = (f32[240,512]{1,0:T(8,128)S(1)}, f32[240,512]{1,0:T(8,128)S(1)}, u32[]{:S(2)}, u32[]{:S(2)}) collective-permute-start(f32[240,512]{1,0:T(8,128)S(1)} %get-tuple-element.96.refs_1_), channel_id=1, source_target_pairs={{0,16},{16,0},{1,17},{17,1},{2,18},{18,2},{3,19},{19,3},{4,20},{20... | collective-permute-start | bytes 1474568 | tf_op jit(solution)/shard_map/ppermute | solution.py:410
  55.2 29.6 %collective-permute-start.11 = (bf16[40,9216]{1,0:T(8,128)(2,1)S(1)}, bf16[40,9216]{1,0:T(8,128)(2,1)S(1)}, u32[]{:S(2)}, u32[]{:S(2)}) collective-permute-start(bf16[40,9216]{1,0:T(8,128)(2,1)S(1)} %collective-permute-done.6.refs_0_), channel_id=1, source_target_pairs={{2,6},{3,7},{6,10},{7,11},{10,14},{11,15},{14,12},{15,13},{12,8},{... | collective-permute-start | bytes 2211848 | tf_op jit(solution)/shard_map/ppermute | solution.py:420
  56.7 30.0 %collective-permute-start.12 = (bf16[40,9216]{1,0:T(8,128)(2,1)S(1)}, bf16[40,9216]{1,0:T(8,128)(2,1)S(1)}, u32[]{:S(2)}, u32[]{:S(2)}) collective-permute-start(bf16[40,9216]{1,0:T(8,128)(2,1)S(1)} %collective-permute-done.7.refs_1_), channel_id=1, source_target_pairs={{6,2},{7,3},{10,6},{11,7},{14,10},{15,11},{12,14},{13,15},{8,12},{... | collective-permute-start | bytes 2211848 | tf_op jit(solution)/shard_map/ppermute | solution.py:420
  71.0 31.6 %collective-permute-start.10 = (bf16[40,9216]{1,0:T(8,128)(2,1)S(1)}, bf16[40,9216]{1,0:T(8,128)(2,1)S(1)}, u32[]{:S(2)}, u32[]{:S(2)}) collective-permute-start(bf16[40,9216]{1,0:T(8,128)(2,1)S(1)} %collective-permute-done.5.refs_1_), channel_id=1, source_target_pairs={{6,2},{7,3},{10,6},{11,7},{14,10},{15,11},{12,14},{13,15},{8,12},{... | collective-permute-start | bytes 2211848 | tf_op jit(solution)/shard_map/ppermute | solution.py:420
  71.0 31.5 %collective-permute-start.9 = (bf16[40,9216]{1,0:T(8,128)(2,1)S(1)}, bf16[40,9216]{1,0:T(8,128)(2,1)S(1)}, u32[]{:S(2)}, u32[]{:S(2)}) collective-permute-start(bf16[40,9216]{1,0:T(8,128)(2,1)S(1)} %collective-permute-done.4.refs_0_), channel_id=1, source_target_pairs={{2,6},{3,7},{6,10},{7,11},{10,14},{11,15},{14,12},{15,13},{12,8},{... | collective-permute-start | bytes 2211848 | tf_op jit(solution)/shard_map/ppermute | solution.py:420
  73.0 11.2 %collective-permute-start.13 = (f32[224,512]{1,0:T(8,128)S(1)}, f32[224,512]{1,0:T(8,128)S(1)}, u32[]{:S(2)}, u32[]{:S(2)}) collective-permute-start(f32[224,512]{1,0:T(8,128)S(1)} %get-tuple-element.112.refs_2_.refs_0_), channel_id=1, source_target_pairs={{0,16},{16,0},{1,17},{17,1},{2,18},{18,2},{3,19},{19,3},{4,20},{20... | collective-permute-start | bytes 1376264 | tf_op jit(solution)/shard_map/ppermute | solution.py:410
  87.0 26.0 %collective-permute-start.16 = (bf16[40,4608]{1,0:T(8,128)(2,1)S(1)}, bf16[40,4608]{1,0:T(8,128)(2,1)S(1)}, u32[]{:S(2)}, u32[]{:S(2)}) collective-permute-start(bf16[40,4608]{1,0:T(8,128)(2,1)S(1)} %get-tuple-element.118), channel_id=1, source_target_pairs={{2,6},{3,7},{6,10},{7,11},{10,14},{11,15},{14,12},{15,13},{12,8},{... | collective-permute-start | bytes 1105928 | tf_op jit(solution)/shard_map/ppermute | solution.py:420
  88.6 24.4 %collective-permute-start.17 = (bf16[40,4608]{1,0:T(8,128)(2,1)S(1)}, bf16[40,4608]{1,0:T(8,128)(2,1)S(1)}, u32[]{:S(2)}, u32[]{:S(2)}) collective-permute-start(bf16[40,4608]{1,0:T(8,128)(2,1)S(1)} %get-tuple-element.119), channel_id=1, source_target_pairs={{6,2},{7,3},{10,6},{11,7},{14,10},{15,11},{12,14},{13,15},{8,12},{... | collective-permute-start | bytes 1105928 | tf_op jit(solution)/shard_map/ppermute | solution.py:420
  102.6 10.4 %collective-permute-start.18 = (f32[160,512]{1,0:T(8,128)S(1)}, f32[160,512]{1,0:T(8,128)S(1)}, u32[]{:S(2)}, u32[]{:S(2)}) collective-permute-start(f32[160,512]{1,0:T(8,128)S(1)} %get-tuple-element.138.refs_1_), channel_id=1, source_target_pairs={{0,16},{16,0},{1,17},{17,1},{2,18},{18,2},{3,19},{19,3},{4,20},{20... | collective-permute-start | bytes 983048 | tf_op jit(solution)/shard_map/ppermute | solution.py:410
  104.1 15.0 %collective-permute-start.14 = (bf16[40,4608]{1,0:T(8,128)(2,1)S(1)}, bf16[40,4608]{1,0:T(8,128)(2,1)S(1)}, u32[]{:S(2)}, u32[]{:S(2)}) collective-permute-start(bf16[40,4608]{1,0:T(8,128)(2,1)S(1)} %get-tuple-element.116), channel_id=1, source_target_pairs={{2,6},{3,7},{6,10},{7,11},{10,14},{11,15},{14,12},{15,13},{12,8},{... | collective-permute-start | bytes 1105928 | tf_op jit(solution)/shard_map/ppermute | solution.py:420
  105.8 13.4 %collective-permute-start.15 = (bf16[40,4608]{1,0:T(8,128)(2,1)S(1)}, bf16[40,4608]{1,0:T(8,128)(2,1)S(1)}, u32[]{:S(2)}, u32[]{:S(2)}) collective-permute-start(bf16[40,4608]{1,0:T(8,128)(2,1)S(1)} %get-tuple-element.117), channel_id=1, source_target_pairs={{6,2},{7,3},{10,6},{11,7},{14,10},{15,11},{12,14},{13,15},{8,12},{... | collective-permute-start | bytes 1105928 | tf_op jit(solution)/shard_map/ppermute | solution.py:420
  113.2 4.4 %collective-permute-start.21 = (bf16[40,4096]{1,0:T(8,128)(2,1)S(1)}, bf16[40,4096]{1,0:T(8,128)(2,1)S(1)}, u32[]{:S(2)}, u32[]{:S(2)}) collective-permute-start(bf16[40,4096]{1,0:T(8,128)(2,1)S(1)} %get-tuple-element.128.refs_0_), channel_id=1, source_target_pairs={{2,3},{3,2},{6,7},{7,6},{10,11},{11,10},{14,15},{15,14},{12,13},{1... | collective-permute-start | bytes 983048 | tf_op jit(solution)/shard_map/ppermute | solution.py:417
  113.8 2.3 %collective-permute-start.20 = (bf16[40,2560]{1,0:T(8,128)(2,1)S(1)}, bf16[40,2560]{1,0:T(8,128)(2,1)S(1)}, u32[]{:S(2)}, u32[]{:S(2)}) collective-permute-start(bf16[40,2560]{1,0:T(8,128)(2,1)S(1)} %get-tuple-element.127.refs_1_), channel_id=1, source_target_pairs={{2,3},{3,2},{6,7},{7,6},{10,11},{11,10},{14,15},{15,14},{12,13},{1... | collective-permute-start | bytes 614408 | tf_op jit(solution)/shard_map/ppermute | solution.py:417
  115.2 3.9 %collective-permute-start.22 = (f32[16,400]{1,0:T(8,128)S(1)}, f32[16,400]{1,0:T(8,128)S(1)}, u32[]{:S(2)}, u32[]{:S(2)}) collective-permute-start(f32[16,400]{1,0:T(8,128)S(1)} %score.4.refs_0_), channel_id=1, source_target_pairs={{0,16},{16,0},{1,17},{17,1},{2,18},{18,2},{3,19},{19,3},{4,20},{20... | collective-permute-start | bytes 76808 | tf_op jit(solution)/shard_map/ppermute | solution.py:410
  119.7 6.2 %collective-permute-start.25 = (f32[80,512]{1,0:T(8,128)S(1)}, f32[80,512]{1,0:T(8,128)S(1)}, u32[]{:S(2)}, u32[]{:S(2)}) collective-permute-start(f32[80,512]{1,0:T(8,128)S(1)} %project_last.4.refs_3_), channel_id=1, source_target_pairs={{0,16},{16,0},{1,17},{17,1},{2,18},{18,2},{3,19},{19,3},{4,20},{20... | collective-permute-start | bytes 491528 | tf_op jit(solution)/shard_map/ppermute | solution.py:410
  126.4 3.8 %collective-permute-start.26 = (f32[16,240]{1,0:T(8,128)S(1)}, f32[16,240]{1,0:T(8,128)S(1)}, u32[]{:S(2)}, u32[]{:S(2)}) collective-permute-start(f32[16,240]{1,0:T(8,128)S(1)} %score.5.refs_2_), channel_id=1, source_target_pairs={{0,16},{16,0},{1,17},{17,1},{2,18},{18,2},{3,19},{19,3},{4,20},{20... | collective-permute-start | bytes 46088 | tf_op jit(solution)/shard_map/ppermute | solution.py:410
  (3 other events, 5.7 us)

commit v6 on v5

--- a/solution.py
+++ b/solution.py
@@ -328,8 +328,9 @@
 
 def inverse_kernel(*refs):
     out_ref = refs[-1]
-    gram = total_of(refs[:-1])[-2 * RANK :]
-    norms = jnp.broadcast_to((gram[:RANK] * gram[RANK:]).sum(axis=0, keepdims=True), (8, gram.shape[1]))
+    gram = total_of(refs[:-1])
+    first, second = (gram[0], gram[1]) if gram.ndim == 3 else (gram[-2 * RANK : -RANK], gram[-RANK:])
+    norms = jnp.broadcast_to((first * second).sum(axis=0, keepdims=True), (8, gram.shape[-1]))
     inverse = 1.0 / jnp.sqrt(by_query(norms) + 1e-06)
     out_ref[...] = jnp.broadcast_to(inverse.T[:, :1], out_ref.shape)
 
@@ -337,7 +338,7 @@
 def inverse_norms(parts):
     return pl.pallas_call(
         inverse_kernel,
-        out_shape=jax.ShapeDtypeStruct((parts[0].shape[1] // RANK, 128), jnp.float32),
+        out_shape=jax.ShapeDtypeStruct((parts[0].shape[-1] // RANK, 128), jnp.float32),
         compiler_params=params(),
         cost_estimate=LIGHT,
         name="inverse_norms",
@@ -348,10 +349,10 @@
     return sum(jnp.where(index == i, value, 0) for i, value in enumerate(table))
 
 
-def last_kernel(count, groups, place, tokens, inverse_ref, *refs):
+def last_kernel(groups, place, tokens, inverse_ref, *refs):
     out_ref = refs[-1]
     chips = len(place)
-    scores = jnp.concatenate([total_of(refs[i : i + count]) for i in range(0, len(refs) - 1, count)], axis=1)
+    scores = total_of(refs[:-1])
     width = scores.shape[1]
     starts = [[0] * chips for _ in range(2)]
     first = 0
@@ -379,16 +380,16 @@
     out_ref[...] = result[:, : out_ref.shape[1]] * inverse_ref[:, :1]
 
 
-def last(results, inverse, groups, place, tokens, share):
-    return pl.pallas_call(
-        functools.partial(last_kernel, len(results[0]), groups, place, tokens),
-        in_specs=[pl.BlockSpec(memory_space=pltpu.VMEM)] * (1 + sum(len(parts) for parts in results)),
+def last(parts, inverse, groups, place, tokens, share):
+    return pl.pallas_call(
+        functools.partial(last_kernel, groups, place, tokens),
+        in_specs=[pl.BlockSpec(memory_space=pltpu.VMEM)] * (1 + len(parts)),
         out_specs=pl.BlockSpec(memory_space=pltpu.VMEM),
         out_shape=jax.ShapeDtypeStruct((inverse.shape[0], share), jnp.float32),
         compiler_params=params(),
         cost_estimate=LIGHT,
         name="last_scores",
-    )(inverse, *[x for parts in results for x in parts])
+    )(inverse, *parts)
 
 
 def solution(mesh):
@@ -437,7 +438,7 @@
         fly1 = round_ring([own1, own1])
         *factors, gram = load(in_factors, out_factors)
         fly0, own0, own1, gram = tied(fly0, own0, own1, gram)
-        groups, pair, found = [], [], []
+        groups, pair, found, gram_parts = [], [], [], []
         for hop in range(1, last_hop):
             extra = hop == 1
             final = hop + 1 == last_hop
@@ -450,14 +451,17 @@
             fly0 = round_ring(fly0)
             other, part = project(
                 [both_cores(twice(held0 + [own0] * extra))], spans[0], factors, 2,
-                gram if hop == min(2, last_hop - 1) else None)[::-1]
+                gram if hop == 2 and not final else None)[::-1]
             if pair:
-                part, pair = tied(part, pair)
+                part, pair, gram_parts = tied(part, pair, gram_parts)
                 found = [score(pair[0], [(pair[1], pair[0].shape[0])], found)]
+            if final:
+                inverse = inverse_norms(gram_parts or across(gram))
+                found.append(inverse)
             fly1, other, part, found = tied(fly1, other, part, found)
             held1 = fly1
             if final:
-                high = (width - cut) // 256 * 128
+                high = (width - cut) // 256 * 128 + (width - cut) // 24 // 128 * 128
                 fly1 = columns_of(held1, [[(0, 0, high)], [(1, high, width - cut)]], True)
             fly1 = round_ring(fly1)
             swapped = both_cores(twice(held1 + [own1] * extra))
@@ -469,7 +473,7 @@
                 other = across(other)
                 fly0, one, other = tied(fly0, one, other)
                 pair = (one, other)
-            if hop == min(2, last_hop - 1):
+            if hop == 2 and not final:
                 gram_parts = other
         groups.append((last_hop,))
         arrays = [swapped]
@@ -478,18 +482,18 @@
             [(0, middle, middle + low)], [(1, depth - middle, half - middle - low)]], True)
         swapped = mate(held)
         last_other = project_last([held[0], swapped[0]], [(((0, 0), (1, 0)), depth, 1, 0)], factors)
+        *found, inverse = found
+        fly1, arrays, part, held, swapped, last_other, inverse, found = tied(
+            fly1, arrays, part, held, swapped, last_other, inverse, found)
         last_part = project_last([*held[1:], *swapped[1:]], [
             (((0, 0), (2, 0)), low, 0, 0), (((1, 0), (3, 0)), cut - low, 0, low)], factors)
-        inverse = inverse_norms(gram_parts)
-        results = [across(x) for x in found]
-        fly1, arrays, part, last_part, last_other, inverse, results = tied(
-            fly1, arrays, part, last_part, last_other, inverse, results)
         swapped = mate(fly1)
         last_other = across(last_other)
+        fly1, swapped, last_part = tied(fly1, swapped, last_part)
         one = project_last([*arrays, *fly1, *swapped], [
             (((0, 0), (1, 0), (3, 0)), high, 0, cut),
             (((0, high), (2, 0), (4, 0)), width - cut - high, 0, cut + high)], factors, [part, last_part])
-        results.append(across(score(one, [(other, part.shape[0]), (last_other, 2 * tokens)])))
+        results = across(score(one, [(other, part.shape[0]), (last_other, 2 * tokens)], found))
         return last(results, inverse, tuple(groups), place, tokens, query * tokens // rows).T
 
     return jax.shard_map(

time: 131 us -> 129 us (0.985)
  waiting for transfers between devices: 23.3 us -> 20.7 us
    ppermute x6 -> x5, waiting for transfers between devices: 4.41 us -> 2.85 us  [across(): return [x, lax.ppermute(x, 'rows', [(0, 1), (1, 0)])]]
    ppermute x6 -> x5, starting transfers between devices: 7.1 us -> 7.19 us  [across(): return [x, lax.ppermute(x, 'rows', [(0, 1), (1, 0)])]]
  transfers between devices with their start and end apart: 27 -> 26, of which waited for: 15 -> 12; matrix products, arithmetic and copies ran while one was open for 0% -> 0% of each run, Pallas kernels for 31% -> 31%
where the time goes in v6:
time: 129 us
  Pallas kernels  43 us (33%)
  blocking collectives  38.9 us (30%)
  starting transfers between devices  25.9 us (20%)
  waiting for transfers between devices  20.7 us (16%)
    all_to_all x6, blocking collectives, both_cores(): return lax.all_to_all(x, 'query', 0, 0, axis_index_groups=sorted(ring))  38.9 us
    pallas_call x5, Pallas kernels, project(): pl.pallas_call(functools.partial(project_kernel, step, tuple(span), len(a...  18.2 us
    ppermute x8, starting transfers between devices, round_ring(): lax.ppermute(pair[0], 'query', forward)  14.9 us
    ppermute x8, waiting for transfers between devices, round_ring(): lax.ppermute(pair[1], 'query', backward)  10.2 us
    pallas_call x1, Pallas kernels, load(): pl.pallas_call(functools.partial(load_kernel, step), in_specs=[pl.BlockSp...  8.62 us
    ppermute x5, starting transfers between devices, across(): return [x, lax.ppermute(x, 'rows', [(0, 1), (1, 0)])]  7.19 us
    ppermute x8, waiting for transfers between devices, round_ring(): lax.ppermute(pair[0], 'query', forward)  6.71 us
    pallas_call x3, Pallas kernels, project_last(): pl.pallas_call(functools.partial(project_last_kernel, tuple(plan), (len(a...  5.96 us
  transfers between devices with their start and end apart: 26, of which 12 were waited for; matrix products, arithmetic and copies ran while one was open for 0% of the time, Pallas kernels for 31%

profile of v6, /device:TPU:0, one launch (start us, length us, event | category | flops | bytes accessed | tf_op | source)
XLA Modules:
  0.0 128.9 jit_solution(4784959528403831865)
XLA Ops:
  1.1 3.0 %collective-permute-start.2 = (bf16[40,9216]{1,0:T(8,128)(2,1)S(1)}, bf16[40,9216]{1,0:T(8,128)(2,1)S(1)}, u32[]{:S(2)}, u32[]{:S(2)}) collective-permute-start(bf16[40,9216]{1,0:T(8,128)(2,1)S(1)} %columns.6.refs_2_), channel_id=1, source_target_pairs={{2,6},{3,7},{6,10},{7,11},{10,14},{11,15},{14,12},{15,13},{12,8},{... | collective-permute-start | bytes 2211848 | tf_op jit(solution)/shard_map/ppermute | solution.py:421
  5.4 2.0 %collective-permute-start = (bf16[40,9216]{1,0:T(8,128)(2,1)S(1)}, bf16[40,9216]{1,0:T(8,128)(2,1)S(1)}, u32[]{:S(2)}, u32[]{:S(2)}) collective-permute-start(bf16[40,9216]{1,0:T(8,128)(2,1)S(1)} %columns.5.refs_2_), channel_id=1, source_target_pairs={{2,6},{3,7},{6,10},{7,11},{10,14},{11,15},{14,12},{15,13},{12,8},{... | collective-permute-start | bytes 2211848 | tf_op jit(solution)/shard_map/ppermute | solution.py:421
  7.5 8.6 %load_factors.1 = (bf16[14336,512]{1,0:T(8,128)(2,1)S(1)}, bf16[4096,512]{1,0:T(8,128)(2,1)S(1)}, f32[2,32,512]{2,1,0:T(8,128)S(1)}) custom-call(bf16[14336,512]{1,0:T(8,128)(2,1)} %a_ref.1, bf16[4096,512]{1,0:T(8,128)(2,1)} %b_ref.1), custom_call_target="tpu_custom_call" | custom-call | flops 1 | bytes 1 | tf_op jit(solution)/shard_map/load_factors/pallas_call | solution.py:136
  16.1 5.4 %collective-permute-done.2.refs_0_ = bf16[40,9216]{1,0:T(8,128)(2,1)S(1)} collective-permute-done((bf16[40,9216]{1,0:T(8,128)(2,1)S(1)}, bf16[40,9216]{1,0:T(8,128)(2,1)S(1)}, u32[]{:S(2)}, u32[]{:S(2)}) %collective-permute-start.2) | collective-permute-done | bytes 737312 | tf_op jit(solution)/shard_map/ppermute | solution.py:421
  21.5 2.0 %collective-permute-done.3.refs_1_ = bf16[40,9216]{1,0:T(8,128)(2,1)S(1)} collective-permute-done((bf16[40,9216]{1,0:T(8,128)(2,1)S(1)}, bf16[40,9216]{1,0:T(8,128)(2,1)S(1)}, u32[]{:S(2)}, u32[]{:S(2)}) %collective-permute-start.3) | collective-permute-done | bytes 737312 | tf_op jit(solution)/shard_map/ppermute | solution.py:421
  26.5 7.3 %all_to_all.30.refs_0_ = bf16[2,120,9216]{2,1,0:T(8,128)(2,1)S(1)} all-to-all(bf16[2,120,9216]{2,1,0:T(8,128)(2,1)S(1)} %pack.6), channel_id=1, replica_groups={{0,1},{2,3},{4,5},{6,7},{8,9},{10,11},{12,13},{14,15},{16,17},{18,19},{..., dimensions={0} | all-to-all | bytes 8847360 | tf_op jit(solution)/shard_map/all_to_all | solution.py:415
  33.7 4.4 %project.5 = (f32[240,512]{1,0:T(8,128)S(1)}, f32[240,512]{1,0:T(8,128)S(1)}) custom-call(bf16[2,120,9216]{2,1,0:T(8,128)(2,1)S(1)} %all_to_all.30.refs_0_, bf16[14336,512]{1,0:T(8,128)(2,1)S(1)} %get-tuple-element.87.refs_1_.refs_2_.refs_4_.refs_5_, bf16[4096,512]{1,0:T(8,128)(2,1)S(1)} %get-tuple-element.88.refs_2_.refs_3_.refs_5_.refs_6_), custom_call_target="tpu_custom_call" | custom-call | flops 1 | bytes 1 | tf_op jit(solution)/shard_map/project/pallas_call | solution.py:239
  43.8 7.3 %all_to_all.31.refs_0_ = bf16[2,120,9216]{2,1,0:T(8,128)(2,1)S(1)} all-to-all(bf16[2,120,9216]{2,1,0:T(8,128)(2,1)S(1)} %pack.7), channel_id=1, replica_groups={{0,1},{2,3},{4,5},{6,7},{8,9},{10,11},{12,13},{14,15},{16,17},{18,19},{..., dimensions={0} | all-to-all | bytes 8847360 | tf_op jit(solution)/shard_map/all_to_all | solution.py:415
  51.0 3.7 %project.6.refs_0_ = f32[240,512]{1,0:T(8,128)S(1)} custom-call(bf16[2,120,9216]{2,1,0:T(8,128)(2,1)S(1)} %all_to_all.31.refs_0_, bf16[14336,512]{1,0:T(8,128)(2,1)S(1)} %get-tuple-element.87.refs_1_.refs_2_.refs_4_.refs_5_, bf16[4096,512]{1,0:T(8,128)(2,1)S(1)} %get-tuple-element.88.refs_2_.refs_3_.refs_5_.refs_6_, f32[240,512]{1,0:T(8,128)S(1)} %get-tuple-element.94.refs_3_), custom_call_target="tpu_custom_call" | custom-call | flops 1 | bytes 1 | tf_op jit(solution)/shard_map/project/pallas_call | solution.py:239
  57.8 6.1 %all_to_all.32.refs_0_ = bf16[2,80,9216]{2,1,0:T(8,128)(2,1)S(1)} all-to-all(bf16[2,80,9216]{2,1,0:T(8,128)(2,1)S(1)} %pack.8), channel_id=1, replica_groups={{0,1},{2,3},{4,5},{6,7},{8,9},{10,11},{12,13},{14,15},{16,17},{18,19},{..., dimensions={0} | all-to-all | bytes 5898240 | tf_op jit(solution)/shard_map/all_to_all | solution.py:415
  63.9 3.6 %project.7 = (f32[160,512]{1,0:T(8,128)S(1)}, f32[224,512]{1,0:T(8,128)S(1)}) custom-call(bf16[2,80,9216]{2,1,0:T(8,128)(2,1)S(1)} %all_to_all.32.refs_0_, bf16[14336,512]{1,0:T(8,128)(2,1)S(1)} %get-tuple-element.87.refs_1_.refs_2_.refs_4_.refs_5_, bf16[4096,512]{1,0:T(8,128)(2,1)S(1)} %get-tuple-element.88.refs_2_.refs_3_.refs_5_.refs_6_, ...), custom_call_target="tpu_custom_call" | custom-call | flops 1 | bytes 1 | tf_op jit(solution)/shard_map/project/pallas_call | solution.py:239
  68.9 2.0 %collective-permute-done.5.refs_1_ = bf16[40,9216]{1,0:T(8,128)(2,1)S(1)} collective-permute-done((bf16[40,9216]{1,0:T(8,128)(2,1)S(1)}, bf16[40,9216]{1,0:T(8,128)(2,1)S(1)}, u32[]{:S(2)}, u32[]{:S(2)}) %collective-permute-start.5) | collective-permute-done | bytes 737312 | tf_op jit(solution)/shard_map/ppermute | solution.py:421
  71.0 1.9 %collective-permute-start.9 = (bf16[40,9216]{1,0:T(8,128)(2,1)S(1)}, bf16[40,9216]{1,0:T(8,128)(2,1)S(1)}, u32[]{:S(2)}, u32[]{:S(2)}) collective-permute-start(bf16[40,9216]{1,0:T(8,128)(2,1)S(1)} %collective-permute-done.4.refs_0_), channel_id=1, source_target_pairs={{2,6},{3,7},{6,10},{7,11},{10,14},{11,15},{14,12},{15,13},{12,8},{... | collective-permute-start | bytes 2211848 | tf_op jit(solution)/shard_map/ppermute | solution.py:421
  75.1 6.1 %all_to_all.33.refs_0_ = bf16[2,80,9216]{2,1,0:T(8,128)(2,1)S(1)} all-to-all(bf16[2,80,9216]{2,1,0:T(8,128)(2,1)S(1)} %pack.9), channel_id=1, replica_groups={{0,1},{2,3},{4,5},{6,7},{8,9},{10,11},{12,13},{14,15},{16,17},{18,19},{..., dimensions={0} | all-to-all | bytes 5898240 | tf_op jit(solution)/shard_map/all_to_all | solution.py:415
  81.2 2.9 %project.8.refs_1_ = f32[160,512]{1,0:T(8,128)S(1)} custom-call(bf16[2,80,9216]{2,1,0:T(8,128)(2,1)S(1)} %all_to_all.33.refs_0_, bf16[14336,512]{1,0:T(8,128)(2,1)S(1)} %get-tuple-element.87.refs_1_.refs_2_.refs_4_.refs_5_, bf16[4096,512]{1,0:T(8,128)(2,1)S(1)} %get-tuple-element.88.refs_2_.refs_3_.refs_5_.refs_6_, f32[160,512]{1,0:T(8,128)S(1)} %get-tuple-element.110.refs_3_), custom_call_target="tpu_custom_call" | custom-call | flops 1 | bytes 1 | tf_op jit(solution)/shard_map/project/pallas_call | solution.py:239
  84.7 2.0 %collective-permute-done.12.refs_1_ = bf16[40,9216]{1,0:T(8,128)(2,1)S(1)} collective-permute-done((bf16[40,9216]{1,0:T(8,128)(2,1)S(1)}, bf16[40,9216]{1,0:T(8,128)(2,1)S(1)}, u32[]{:S(2)}, u32[]{:S(2)}) %collective-permute-start.12) | collective-permute-done | bytes 737312 | tf_op jit(solution)/shard_map/ppermute | solution.py:421
  87.0 1.6 %collective-permute-start.16 = (bf16[40,4608]{1,0:T(8,128)(2,1)S(1)}, bf16[40,4608]{1,0:T(8,128)(2,1)S(1)}, u32[]{:S(2)}, u32[]{:S(2)}) collective-permute-start(bf16[40,4608]{1,0:T(8,128)(2,1)S(1)} %get-tuple-element.130), channel_id=1, source_target_pairs={{2,6},{3,7},{6,10},{7,11},{10,14},{11,15},{14,12},{15,13},{12,8},{... | collective-permute-start | bytes 1105928 | tf_op jit(solution)/shard_map/ppermute | solution.py:421
  89.7 6.1 %all_to_all.34.refs_0_ = bf16[2,80,9216]{2,1,0:T(8,128)(2,1)S(1)} all-to-all(bf16[2,80,9216]{2,1,0:T(8,128)(2,1)S(1)} %pack.10), channel_id=1, replica_groups={{0,1},{2,3},{4,5},{6,7},{8,9},{10,11},{12,13},{14,15},{16,17},{18,19},{..., dimensions={0} | all-to-all | bytes 5898240 | tf_op jit(solution)/shard_map/all_to_all | solution.py:415
  95.8 3.6 %project.9 = (f32[160,512]{1,0:T(8,128)S(1)}, f32[160,512]{1,0:T(8,128)S(1)}) custom-call(bf16[2,80,9216]{2,1,0:T(8,128)(2,1)S(1)} %all_to_all.34.refs_0_, bf16[14336,512]{1,0:T(8,128)(2,1)S(1)} %get-tuple-element.87.refs_1_.refs_2_.refs_4_.refs_5_, bf16[4096,512]{1,0:T(8,128)(2,1)S(1)} %get-tuple-element.88.refs_2_.refs_3_.refs_5_.refs_6_), custom_call_target="tpu_custom_call" | custom-call | flops 1 | bytes 1 | tf_op jit(solution)/shard_map/project/pallas_call | solution.py:239
  100.4 2.1 %collective-permute-done.10.refs_1_ = bf16[40,9216]{1,0:T(8,128)(2,1)S(1)} collective-permute-done((bf16[40,9216]{1,0:T(8,128)(2,1)S(1)}, bf16[40,9216]{1,0:T(8,128)(2,1)S(1)}, u32[]{:S(2)}, u32[]{:S(2)}) %collective-permute-start.10) | collective-permute-done | bytes 737312 | tf_op jit(solution)/shard_map/ppermute | solution.py:421
  104.1 1.6 %collective-permute-start.14 = (bf16[40,4992]{1,0:T(8,128)(2,1)S(1)}, bf16[40,4992]{1,0:T(8,128)(2,1)S(1)}, u32[]{:S(2)}, u32[]{:S(2)}) collective-permute-start(bf16[40,4992]{1,0:T(8,128)(2,1)S(1)} %get-tuple-element.128), channel_id=1, source_target_pairs={{2,6},{3,7},{6,10},{7,11},{10,14},{11,15},{14,12},{15,13},{12,8},{... | collective-permute-start | bytes 1198088 | tf_op jit(solution)/shard_map/ppermute | solution.py:421
  106.9 6.1 %all_to_all.35.refs_0_ = bf16[2,80,9216]{2,1,0:T(8,128)(2,1)S(1)} all-to-all(bf16[2,80,9216]{2,1,0:T(8,128)(2,1)S(1)} %pack.11), channel_id=1, replica_groups={{0,1},{2,3},{4,5},{6,7},{8,9},{10,11},{12,13},{14,15},{16,17},{18,19},{..., dimensions={0} | all-to-all | bytes 5898240 | tf_op jit(solution)/shard_map/all_to_all | solution.py:415
  119.8 3.6 %project_last.5.refs_1_ = f32[240,512]{1,0:T(8,128)S(1)} custom-call(bf16[2,80,9216]{2,1,0:T(8,128)(2,1)S(1)} %all_to_all.35.refs_0_, bf16[40,4992]{1,0:T(8,128)(2,1)S(1)} %collective-permute-done.14.refs_1_, bf16[40,4224]{1,0:T(8,128)(2,1)S(1)} %collective-permute-done.15.refs_2_, bf16[40,4992]{1,0:T(8,128)(2,1)S(1)} %collective-permute-done.22.refs_3_, ...), custom_call_target="tpu_custom_call" | custom-call | flops 1 | bytes 1 | tf_op jit(solution)/shard_map/project_last/pallas_call | solution.py:294
  125.2 2.8 %collective-permute-done.25.refs_1_ = f32[16,640]{1,0:T(8,128)S(1)} collective-permute-done((f32[16,640]{1,0:T(8,128)S(1)}, f32[16,640]{1,0:T(8,128)S(1)}, u32[]{:S(2)}, u32[]{:S(2)}) %collective-permute-start.25) | collective-permute-done | bytes 40992 | tf_op jit(solution)/shard_map/ppermute | solution.py:411
  (59 shorter events, 32.7 us)
Async XLA Ops:
  1.1 20.4 %collective-permute-start.2 = (bf16[40,9216]{1,0:T(8,128)(2,1)S(1)}, bf16[40,9216]{1,0:T(8,128)(2,1)S(1)}, u32[]{:S(2)}, u32[]{:S(2)}) collective-permute-start(bf16[40,9216]{1,0:T(8,128)(2,1)S(1)} %columns.6.refs_2_), channel_id=1, source_target_pairs={{2,6},{3,7},{6,10},{7,11},{10,14},{11,15},{14,12},{15,13},{12,8},{... | collective-permute-start | bytes 2211848 | tf_op jit(solution)/shard_map/ppermute | solution.py:421
  4.1 19.4 %collective-permute-start.3 = (bf16[40,9216]{1,0:T(8,128)(2,1)S(1)}, bf16[40,9216]{1,0:T(8,128)(2,1)S(1)}, u32[]{:S(2)}, u32[]{:S(2)}) collective-permute-start(bf16[40,9216]{1,0:T(8,128)(2,1)S(1)} %columns.6.refs_2_), channel_id=1, source_target_pairs={{6,2},{7,3},{10,6},{11,7},{14,10},{15,11},{12,14},{13,15},{8,12},{... | collective-permute-start | bytes 2211848 | tf_op jit(solution)/shard_map/ppermute | solution.py:421
  5.4 32.7 %collective-permute-start = (bf16[40,9216]{1,0:T(8,128)(2,1)S(1)}, bf16[40,9216]{1,0:T(8,128)(2,1)S(1)}, u32[]{:S(2)}, u32[]{:S(2)}) collective-permute-start(bf16[40,9216]{1,0:T(8,128)(2,1)S(1)} %columns.5.refs_2_), channel_id=1, source_target_pairs={{2,6},{3,7},{6,10},{7,11},{10,14},{11,15},{14,12},{15,13},{12,8},{... | collective-permute-start | bytes 2211848 | tf_op jit(solution)/shard_map/ppermute | solution.py:421
  7.4 32.0 %collective-permute-start.1 = (bf16[40,9216]{1,0:T(8,128)(2,1)S(1)}, bf16[40,9216]{1,0:T(8,128)(2,1)S(1)}, u32[]{:S(2)}, u32[]{:S(2)}) collective-permute-start(bf16[40,9216]{1,0:T(8,128)(2,1)S(1)} %columns.5.refs_2_), channel_id=1, source_target_pairs={{6,2},{7,3},{10,6},{11,7},{14,10},{15,11},{12,14},{13,15},{8,12},{... | collective-permute-start | bytes 2211848 | tf_op jit(solution)/shard_map/ppermute | solution.py:421
  23.6 31.2 %collective-permute-start.6 = (bf16[40,9216]{1,0:T(8,128)(2,1)S(1)}, bf16[40,9216]{1,0:T(8,128)(2,1)S(1)}, u32[]{:S(2)}, u32[]{:S(2)}) collective-permute-start(bf16[40,9216]{1,0:T(8,128)(2,1)S(1)} %collective-permute-done.2.refs_0_), channel_id=1, source_target_pairs={{2,6},{3,7},{6,10},{7,11},{10,14},{11,15},{14,12},{15,13},{12,8},{... | collective-permute-start | bytes 2211848 | tf_op jit(solution)/shard_map/ppermute | solution.py:421
  25.1 30.0 %collective-permute-start.7 = (bf16[40,9216]{1,0:T(8,128)(2,1)S(1)}, bf16[40,9216]{1,0:T(8,128)(2,1)S(1)}, u32[]{:S(2)}, u32[]{:S(2)}) collective-permute-start(bf16[40,9216]{1,0:T(8,128)(2,1)S(1)} %collective-permute-done.3.refs_1_), channel_id=1, source_target_pairs={{6,2},{7,3},{10,6},{11,7},{14,10},{15,11},{12,14},{13,15},{8,12},{... | collective-permute-start | bytes 2211848 | tf_op jit(solution)/shard_map/ppermute | solution.py:421
  39.4 29.6 %collective-permute-start.4 = (bf16[40,9216]{1,0:T(8,128)(2,1)S(1)}, bf16[40,9216]{1,0:T(8,128)(2,1)S(1)}, u32[]{:S(2)}, u32[]{:S(2)}) collective-permute-start(bf16[40,9216]{1,0:T(8,128)(2,1)S(1)} %collective-permute-done.refs_0_), channel_id=1, source_target_pairs={{2,6},{3,7},{6,10},{7,11},{10,14},{11,15},{14,12},{15,13},{12,8},{... | collective-permute-start | bytes 2211848 | tf_op jit(solution)/shard_map/ppermute | solution.py:421
  40.9 30.0 %collective-permute-start.5 = (bf16[40,9216]{1,0:T(8,128)(2,1)S(1)}, bf16[40,9216]{1,0:T(8,128)(2,1)S(1)}, u32[]{:S(2)}, u32[]{:S(2)}) collective-permute-start(bf16[40,9216]{1,0:T(8,128)(2,1)S(1)} %collective-permute-done.1.refs_1_), channel_id=1, source_target_pairs={{6,2},{7,3},{10,6},{11,7},{14,10},{15,11},{12,14},{13,15},{8,12},{... | collective-permute-start | bytes 2211848 | tf_op jit(solution)/shard_map/ppermute | solution.py:421
  41.4 13.4 %collective-permute-start.8 = (f32[240,512]{1,0:T(8,128)S(1)}, f32[240,512]{1,0:T(8,128)S(1)}, u32[]{:S(2)}, u32[]{:S(2)}) collective-permute-start(f32[240,512]{1,0:T(8,128)S(1)} %get-tuple-element.106.refs_1_), channel_id=1, source_target_pairs={{0,16},{16,0},{1,17},{17,1},{2,18},{18,2},{3,19},{19,3},{4,20},{20... | collective-permute-start | bytes 1474568 | tf_op jit(solution)/shard_map/ppermute | solution.py:411
  55.2 29.6 %collective-permute-start.11 = (bf16[40,9216]{1,0:T(8,128)(2,1)S(1)}, bf16[40,9216]{1,0:T(8,128)(2,1)S(1)}, u32[]{:S(2)}, u32[]{:S(2)}) collective-permute-start(bf16[40,9216]{1,0:T(8,128)(2,1)S(1)} %collective-permute-done.6.refs_0_), channel_id=1, source_target_pairs={{2,6},{3,7},{6,10},{7,11},{10,14},{11,15},{14,12},{15,13},{12,8},{... | collective-permute-start | bytes 2211848 | tf_op jit(solution)/shard_map/ppermute | solution.py:421
  56.7 30.0 %collective-permute-start.12 = (bf16[40,9216]{1,0:T(8,128)(2,1)S(1)}, bf16[40,9216]{1,0:T(8,128)(2,1)S(1)}, u32[]{:S(2)}, u32[]{:S(2)}) collective-permute-start(bf16[40,9216]{1,0:T(8,128)(2,1)S(1)} %collective-permute-done.7.refs_1_), channel_id=1, source_target_pairs={{6,2},{7,3},{10,6},{11,7},{14,10},{15,11},{12,14},{13,15},{8,12},{... | collective-permute-start | bytes 2211848 | tf_op jit(solution)/shard_map/ppermute | solution.py:421
  71.0 31.6 %collective-permute-start.10 = (bf16[40,9216]{1,0:T(8,128)(2,1)S(1)}, bf16[40,9216]{1,0:T(8,128)(2,1)S(1)}, u32[]{:S(2)}, u32[]{:S(2)}) collective-permute-start(bf16[40,9216]{1,0:T(8,128)(2,1)S(1)} %collective-permute-done.5.refs_1_), channel_id=1, source_target_pairs={{6,2},{7,3},{10,6},{11,7},{14,10},{15,11},{12,14},{13,15},{8,12},{... | collective-permute-start | bytes 2211848 | tf_op jit(solution)/shard_map/ppermute | solution.py:421
  71.0 31.5 %collective-permute-start.9 = (bf16[40,9216]{1,0:T(8,128)(2,1)S(1)}, bf16[40,9216]{1,0:T(8,128)(2,1)S(1)}, u32[]{:S(2)}, u32[]{:S(2)}) collective-permute-start(bf16[40,9216]{1,0:T(8,128)(2,1)S(1)} %collective-permute-done.4.refs_0_), channel_id=1, source_target_pairs={{2,6},{3,7},{6,10},{7,11},{10,14},{11,15},{14,12},{15,13},{12,8},{... | collective-permute-start | bytes 2211848 | tf_op jit(solution)/shard_map/ppermute | solution.py:421
  73.0 11.2 %collective-permute-start.13 = (f32[224,512]{1,0:T(8,128)S(1)}, f32[224,512]{1,0:T(8,128)S(1)}, u32[]{:S(2)}, u32[]{:S(2)}) collective-permute-start(f32[224,512]{1,0:T(8,128)S(1)} %get-tuple-element.124.refs_2_.refs_0_), channel_id=1, source_target_pairs={{0,16},{16,0},{1,17},{17,1},{2,18},{18,2},{3,19},{19,3},{4,20},{20... | collective-permute-start | bytes 1376264 | tf_op jit(solution)/shard_map/ppermute | solution.py:411
  87.0 26.0 %collective-permute-start.16 = (bf16[40,4608]{1,0:T(8,128)(2,1)S(1)}, bf16[40,4608]{1,0:T(8,128)(2,1)S(1)}, u32[]{:S(2)}, u32[]{:S(2)}) collective-permute-start(bf16[40,4608]{1,0:T(8,128)(2,1)S(1)} %get-tuple-element.130), channel_id=1, source_target_pairs={{2,6},{3,7},{6,10},{7,11},{10,14},{11,15},{14,12},{15,13},{12,8},{... | collective-permute-start | bytes 1105928 | tf_op jit(solution)/shard_map/ppermute | solution.py:421
  88.6 24.4 %collective-permute-start.17 = (bf16[40,4608]{1,0:T(8,128)(2,1)S(1)}, bf16[40,4608]{1,0:T(8,128)(2,1)S(1)}, u32[]{:S(2)}, u32[]{:S(2)}) collective-permute-start(bf16[40,4608]{1,0:T(8,128)(2,1)S(1)} %get-tuple-element.131), channel_id=1, source_target_pairs={{6,2},{7,3},{10,6},{11,7},{14,10},{15,11},{12,14},{13,15},{8,12},{... | collective-permute-start | bytes 1105928 | tf_op jit(solution)/shard_map/ppermute | solution.py:421
  102.6 10.4 %collective-permute-start.18 = (f32[160,512]{1,0:T(8,128)S(1)}, f32[160,512]{1,0:T(8,128)S(1)}, u32[]{:S(2)}, u32[]{:S(2)}) collective-permute-start(f32[160,512]{1,0:T(8,128)S(1)} %get-tuple-element.158.refs_2_), channel_id=1, source_target_pairs={{0,16},{16,0},{1,17},{17,1},{2,18},{18,2},{3,19},{19,3},{4,20},{20... | collective-permute-start | bytes 983048 | tf_op jit(solution)/shard_map/ppermute | solution.py:411
  104.1 12.1 %collective-permute-start.14 = (bf16[40,4992]{1,0:T(8,128)(2,1)S(1)}, bf16[40,4992]{1,0:T(8,128)(2,1)S(1)}, u32[]{:S(2)}, u32[]{:S(2)}) collective-permute-start(bf16[40,4992]{1,0:T(8,128)(2,1)S(1)} %get-tuple-element.128), channel_id=1, source_target_pairs={{2,6},{3,7},{6,10},{7,11},{10,14},{11,15},{14,12},{15,13},{12,8},{... | collective-permute-start | bytes 1198088 | tf_op jit(solution)/shard_map/ppermute | solution.py:421
  105.8 10.5 %collective-permute-start.15 = (bf16[40,4224]{1,0:T(8,128)(2,1)S(1)}, bf16[40,4224]{1,0:T(8,128)(2,1)S(1)}, u32[]{:S(2)}, u32[]{:S(2)}) collective-permute-start(bf16[40,4224]{1,0:T(8,128)(2,1)S(1)} %get-tuple-element.129), channel_id=1, source_target_pairs={{6,2},{7,3},{10,6},{11,7},{14,10},{15,11},{12,14},{13,15},{8,12},{... | collective-permute-start | bytes 1013768 | tf_op jit(solution)/shard_map/ppermute | solution.py:421
  113.4 2.8 %collective-permute-start.20 = (bf16[40,2560]{1,0:T(8,128)(2,1)S(1)}, bf16[40,2560]{1,0:T(8,128)(2,1)S(1)}, u32[]{:S(2)}, u32[]{:S(2)}) collective-permute-start(bf16[40,2560]{1,0:T(8,128)(2,1)S(1)} %get-tuple-element.148.refs_0_), channel_id=1, source_target_pairs={{2,3},{3,2},{6,7},{7,6},{10,11},{11,10},{14,15},{15,14},{12,13},{1... | collective-permute-start | bytes 614408 | tf_op jit(solution)/shard_map/ppermute | solution.py:418
  116.2 3.5 %collective-permute-start.22 = (bf16[40,4992]{1,0:T(8,128)(2,1)S(1)}, bf16[40,4992]{1,0:T(8,128)(2,1)S(1)}, u32[]{:S(2)}, u32[]{:S(2)}) collective-permute-start(bf16[40,4992]{1,0:T(8,128)(2,1)S(1)} %collective-permute-done.14.refs_1_), channel_id=1, source_target_pairs={{2,3},{3,2},{6,7},{7,6},{10,11},{11,10},{14,15},{15,14},{12,13},{1... | collective-permute-start | bytes 1198088 | tf_op jit(solution)/shard_map/ppermute | solution.py:418
  116.3 3.4 %collective-permute-start.23 = (bf16[40,4224]{1,0:T(8,128)(2,1)S(1)}, bf16[40,4224]{1,0:T(8,128)(2,1)S(1)}, u32[]{:S(2)}, u32[]{:S(2)}) collective-permute-start(bf16[40,4224]{1,0:T(8,128)(2,1)S(1)} %collective-permute-done.15.refs_2_), channel_id=1, source_target_pairs={{2,3},{3,2},{6,7},{7,6},{10,11},{11,10},{14,15},{15,14},{12,13},{1... | collective-permute-start | bytes 1013768 | tf_op jit(solution)/shard_map/ppermute | solution.py:418
  116.8 6.5 %collective-permute-start.24 = (f32[80,512]{1,0:T(8,128)S(1)}, f32[80,512]{1,0:T(8,128)S(1)}, u32[]{:S(2)}, u32[]{:S(2)}) collective-permute-start(f32[80,512]{1,0:T(8,128)S(1)} %project_last.3.refs_4_), channel_id=1, source_target_pairs={{0,16},{16,0},{1,17},{17,1},{2,18},{18,2},{3,19},{19,3},{4,20},{20... | collective-permute-start | bytes 491528 | tf_op jit(solution)/shard_map/ppermute | solution.py:411
  124.1 4.0 %collective-permute-start.25 = (f32[16,640]{1,0:T(8,128)S(1)}, f32[16,640]{1,0:T(8,128)S(1)}, u32[]{:S(2)}, u32[]{:S(2)}) collective-permute-start(f32[16,640]{1,0:T(8,128)S(1)} %score.5.refs_0_), channel_id=1, source_target_pairs={{0,16},{16,0},{1,17},{17,1},{2,18},{18,2},{3,19},{19,3},{4,20},{20... | collective-permute-start | bytes 122888 | tf_op jit(solution)/shard_map/ppermute | solution.py:411
  (2 other events, 4.1 us)

commit v7 on v6

--- a/solution.py
+++ b/solution.py
@@ -60,9 +60,9 @@
     return ring
 
 
-def chunk_of(*sizes):
+def chunk_of(*sizes, most=2048):
     whole = functools.reduce(math.gcd, sizes)
-    return next(step for step in range(2048, 0, -128) if whole % step == 0)
+    return next(step for step in range(most, 0, -128) if whole % step == 0)
 
 
 def copy_kernel(plan, count, *refs):
@@ -230,7 +230,7 @@
 
 def project(arrays, span, factors, outs, start=None):
     width = sum(size for _, size, _, _ in span)
-    step = chunk_of(*(size for _, size, _, _ in span))
+    step = chunk_of(*(size for _, size, _, _ in span), most=3072)
     shape = (sum(math.prod(a.shape[:-1]) for a in arrays), factors[0].shape[1])
     extra = [] if start is None else [start]
     shapes = [shape] * outs
@@ -275,7 +275,7 @@
     else:
         out_ref[...] = jnp.zeros_like(out_ref)
     for held, width, which, offset in plan:
-        step = chunk_of(width)
+        step = chunk_of(width, most=5120)
 
         @pl.loop(0, width // step)
         def _(i, held=held, which=which, offset=offset, step=step):
@@ -302,28 +302,22 @@
     )(*given)
 
 
-def score_kernel(plan, earlier, *refs):
-    out_ref = refs[-1]
-    one, found, first = refs[earlier][...], [], 0
-    taken = earlier + 1
-    for count, rows in plan:
-        found.append(by_query(one[first : first + rows] * total_of(refs[taken : taken + count], rows)))
-        taken += count
-        first += rows
-    out_ref[...] = jnp.concatenate([*[ref[...] for ref in refs[:earlier]], jnp.concatenate(found, axis=0).T], axis=1)
-
-
-def score(one, others, earlier=()):
-    rows = one.shape[0]
-    plan = tuple((len(parts), count) for parts, count in others)
-    return pl.pallas_call(
-        functools.partial(score_kernel, plan, len(earlier)),
+def score_kernel(first, rows, count, earlier, *refs):
+    one, parts, out_ref = refs[earlier], refs[earlier + 1 : earlier + 1 + count], refs[-1]
+    found = by_query(one[first : first + rows] * total_of(parts, rows)).T
+    out_ref[...] = jnp.concatenate([*[ref[...] for ref in refs[:earlier]], found], axis=1)
+
+
+def score(one, parts, earlier=(), first=0, rows=None):
+    rows = rows or one.shape[0]
+    return pl.pallas_call(
+        functools.partial(score_kernel, first, rows, len(parts), len(earlier)),
         out_shape=jax.ShapeDtypeStruct(
             (one.shape[1] // RANK, rows + sum(x.shape[1] for x in earlier)), jnp.float32),
         compiler_params=params(),
         cost_estimate=LIGHT,
         name="score",
-    )(*earlier, one, *[x for parts, _ in others for x in parts])
+    )(*earlier, one, *parts)
 
 
 def inverse_kernel(*refs):
@@ -454,7 +448,7 @@
                 gram if hop == 2 and not final else None)[::-1]
             if pair:
                 part, pair, gram_parts = tied(part, pair, gram_parts)
-                found = [score(pair[0], [(pair[1], pair[0].shape[0])], found)]
+                found = [score(pair[0], pair[1], found)]
             if final:
                 inverse = inverse_norms(gram_parts or across(gram))
                 found.append(inverse)
@@ -493,7 +487,8 @@
         one = project_last([*arrays, *fly1, *swapped], [
             (((0, 0), (1, 0), (3, 0)), high, 0, cut),
             (((0, high), (2, 0), (4, 0)), width - cut - high, 0, cut + high)], factors, [part, last_part])
-        results = across(score(one, [(other, part.shape[0]), (last_other, 2 * tokens)], found))
+        found = [score(one, other, found, 0, part.shape[0])]
+        results = across(score(one, last_other, found, part.shape[0], 2 * tokens))
         return last(results, inverse, tuple(groups), place, tokens, query * tokens // rows).T
 
     return jax.shard_map(

time: 129 us -> 129 us (level)
  Pallas kernels: 43 us -> 40.6 us
  waiting for transfers between devices: 20.7 us -> 22.1 us
    pallas_call x3, Pallas kernels: 5.96 us -> 4.36 us  [project_last(): pl.pallas_call(functools.partial(project_last_kernel, tuple(plan), (len(a...]
  transfers between devices with their start and end apart: 26 -> 26, of which waited for: 12 -> 13; matrix products, arithmetic and copies ran while one was open for 0% -> 0% of each run, Pallas kernels for 31% -> 30%
where the time goes in v7:
time: 129 us; the launch traced here: 128 us
  Pallas kernels  40.6 us (31%)
  blocking collectives  39 us (30%)
  starting transfers between devices  26.3 us (20%)
  waiting for transfers between devices  22.1 us (17%)
    all_to_all x6, blocking collectives, both_cores(): return lax.all_to_all(x, 'query', 0, 0, axis_index_groups=sorted(ring))  39 us
    pallas_call x5, Pallas kernels, project(): pl.pallas_call(functools.partial(project_kernel, step, tuple(span), len(a...  17 us
    ppermute x8, starting transfers between devices, round_ring(): lax.ppermute(pair[0], 'query', forward)  14.9 us
    ppermute x8, waiting for transfers between devices, round_ring(): lax.ppermute(pair[1], 'query', backward)  10.9 us
    pallas_call x1, Pallas kernels, load(): pl.pallas_call(functools.partial(load_kernel, step), in_specs=[pl.BlockSp...  8.62 us
    ppermute x5, starting transfers between devices, across(): return [x, lax.ppermute(x, 'rows', [(0, 1), (1, 0)])]  7.52 us
    ppermute x8, waiting for transfers between devices, round_ring(): lax.ppermute(pair[0], 'query', forward)  7.3 us
    pallas_call x3, Pallas kernels, project_last(): pl.pallas_call(functools.partial(project_last_kernel, tuple(plan), (len(a...  4.36 us
  transfers between devices with their start and end apart: 26, of which 13 were waited for; matrix products, arithmetic and copies ran while one was open for 0% of the time, Pallas kernels for 30%

profile of v7, /device:TPU:0, one launch (start us, length us, event | category | flops | bytes accessed | tf_op | source)
XLA Modules:
  0.0 128.2 jit_solution(12432329728754801666)
XLA Ops:
  1.1 3.0 %collective-permute-start.2 = (bf16[40,9216]{1,0:T(8,128)(2,1)S(1)}, bf16[40,9216]{1,0:T(8,128)(2,1)S(1)}, u32[]{:S(2)}, u32[]{:S(2)}) collective-permute-start(bf16[40,9216]{1,0:T(8,128)(2,1)S(1)} %columns.6.refs_2_), channel_id=1, source_target_pairs={{2,6},{3,7},{6,10},{7,11},{10,14},{11,15},{14,12},{15,13},{12,8},{... | collective-permute-start | bytes 2211848 | tf_op jit(solution)/shard_map/ppermute | solution.py:415
  5.4 2.0 %collective-permute-start = (bf16[40,9216]{1,0:T(8,128)(2,1)S(1)}, bf16[40,9216]{1,0:T(8,128)(2,1)S(1)}, u32[]{:S(2)}, u32[]{:S(2)}) collective-permute-start(bf16[40,9216]{1,0:T(8,128)(2,1)S(1)} %columns.5.refs_2_), channel_id=1, source_target_pairs={{2,6},{3,7},{6,10},{7,11},{10,14},{11,15},{14,12},{15,13},{12,8},{... | collective-permute-start | bytes 2211848 | tf_op jit(solution)/shard_map/ppermute | solution.py:415
  7.5 8.6 %load_factors.1 = (bf16[14336,512]{1,0:T(8,128)(2,1)S(1)}, bf16[4096,512]{1,0:T(8,128)(2,1)S(1)}, f32[2,32,512]{2,1,0:T(8,128)S(1)}) custom-call(bf16[14336,512]{1,0:T(8,128)(2,1)} %a_ref.1, bf16[4096,512]{1,0:T(8,128)(2,1)} %b_ref.1), custom_call_target="tpu_custom_call" | custom-call | flops 1 | bytes 1 | tf_op jit(solution)/shard_map/load_factors/pallas_call | solution.py:136
  16.1 5.4 %collective-permute-done.2.refs_0_ = bf16[40,9216]{1,0:T(8,128)(2,1)S(1)} collective-permute-done((bf16[40,9216]{1,0:T(8,128)(2,1)S(1)}, bf16[40,9216]{1,0:T(8,128)(2,1)S(1)}, u32[]{:S(2)}, u32[]{:S(2)}) %collective-permute-start.2) | collective-permute-done | bytes 737312 | tf_op jit(solution)/shard_map/ppermute | solution.py:415
  21.5 2.0 %collective-permute-done.3.refs_1_ = bf16[40,9216]{1,0:T(8,128)(2,1)S(1)} collective-permute-done((bf16[40,9216]{1,0:T(8,128)(2,1)S(1)}, bf16[40,9216]{1,0:T(8,128)(2,1)S(1)}, u32[]{:S(2)}, u32[]{:S(2)}) %collective-permute-start.3) | collective-permute-done | bytes 737312 | tf_op jit(solution)/shard_map/ppermute | solution.py:415
  26.5 7.3 %all_to_all.30.refs_0_ = bf16[2,120,9216]{2,1,0:T(8,128)(2,1)S(1)} all-to-all(bf16[2,120,9216]{2,1,0:T(8,128)(2,1)S(1)} %pack.6), channel_id=1, replica_groups={{0,1},{2,3},{4,5},{6,7},{8,9},{10,11},{12,13},{14,15},{16,17},{18,19},{..., dimensions={0} | all-to-all | bytes 8847360 | tf_op jit(solution)/shard_map/all_to_all | solution.py:409
  33.7 4.4 %project.5 = (f32[240,512]{1,0:T(8,128)S(1)}, f32[240,512]{1,0:T(8,128)S(1)}) custom-call(bf16[2,120,9216]{2,1,0:T(8,128)(2,1)S(1)} %all_to_all.30.refs_0_, bf16[14336,512]{1,0:T(8,128)(2,1)S(1)} %get-tuple-element.87.refs_1_.refs_2_.refs_4_.refs_5_, bf16[4096,512]{1,0:T(8,128)(2,1)S(1)} %get-tuple-element.88.refs_2_.refs_3_.refs_5_.refs_6_), custom_call_target="tpu_custom_call" | custom-call | flops 1 | bytes 1 | tf_op jit(solution)/shard_map/project/pallas_call | solution.py:239
  43.8 7.3 %all_to_all.31.refs_0_ = bf16[2,120,9216]{2,1,0:T(8,128)(2,1)S(1)} all-to-all(bf16[2,120,9216]{2,1,0:T(8,128)(2,1)S(1)} %pack.7), channel_id=1, replica_groups={{0,1},{2,3},{4,5},{6,7},{8,9},{10,11},{12,13},{14,15},{16,17},{18,19},{..., dimensions={0} | all-to-all | bytes 8847360 | tf_op jit(solution)/shard_map/all_to_all | solution.py:409
  51.0 3.2 %project.6.refs_0_ = f32[240,512]{1,0:T(8,128)S(1)} custom-call(bf16[2,120,9216]{2,1,0:T(8,128)(2,1)S(1)} %all_to_all.31.refs_0_, bf16[14336,512]{1,0:T(8,128)(2,1)S(1)} %get-tuple-element.87.refs_1_.refs_2_.refs_4_.refs_5_, bf16[4096,512]{1,0:T(8,128)(2,1)S(1)} %get-tuple-element.88.refs_2_.refs_3_.refs_5_.refs_6_, f32[240,512]{1,0:T(8,128)S(1)} %get-tuple-element.94.refs_3_), custom_call_target="tpu_custom_call" | custom-call | flops 1 | bytes 1 | tf_op jit(solution)/shard_map/project/pallas_call | solution.py:239
  57.8 6.1 %all_to_all.32.refs_0_ = bf16[2,80,9216]{2,1,0:T(8,128)(2,1)S(1)} all-to-all(bf16[2,80,9216]{2,1,0:T(8,128)(2,1)S(1)} %pack.8), channel_id=1, replica_groups={{0,1},{2,3},{4,5},{6,7},{8,9},{10,11},{12,13},{14,15},{16,17},{18,19},{..., dimensions={0} | all-to-all | bytes 5898240 | tf_op jit(solution)/shard_map/all_to_all | solution.py:409
  63.9 3.6 %project.7 = (f32[160,512]{1,0:T(8,128)S(1)}, f32[224,512]{1,0:T(8,128)S(1)}) custom-call(bf16[2,80,9216]{2,1,0:T(8,128)(2,1)S(1)} %all_to_all.32.refs_0_, bf16[14336,512]{1,0:T(8,128)(2,1)S(1)} %get-tuple-element.87.refs_1_.refs_2_.refs_4_.refs_5_, bf16[4096,512]{1,0:T(8,128)(2,1)S(1)} %get-tuple-element.88.refs_2_.refs_3_.refs_5_.refs_6_, ...), custom_call_target="tpu_custom_call" | custom-call | flops 1 | bytes 1 | tf_op jit(solution)/shard_map/project/pallas_call | solution.py:239
  68.9 2.0 %collective-permute-done.5.refs_1_ = bf16[40,9216]{1,0:T(8,128)(2,1)S(1)} collective-permute-done((bf16[40,9216]{1,0:T(8,128)(2,1)S(1)}, bf16[40,9216]{1,0:T(8,128)(2,1)S(1)}, u32[]{:S(2)}, u32[]{:S(2)}) %collective-permute-start.5) | collective-permute-done | bytes 737312 | tf_op jit(solution)/shard_map/ppermute | solution.py:415
  71.0 1.9 %collective-permute-start.9 = (bf16[40,9216]{1,0:T(8,128)(2,1)S(1)}, bf16[40,9216]{1,0:T(8,128)(2,1)S(1)}, u32[]{:S(2)}, u32[]{:S(2)}) collective-permute-start(bf16[40,9216]{1,0:T(8,128)(2,1)S(1)} %collective-permute-done.4.refs_0_), channel_id=1, source_target_pairs={{2,6},{3,7},{6,10},{7,11},{10,14},{11,15},{14,12},{15,13},{12,8},{... | collective-permute-start | bytes 2211848 | tf_op jit(solution)/shard_map/ppermute | solution.py:415
  75.1 6.1 %all_to_all.33.refs_0_ = bf16[2,80,9216]{2,1,0:T(8,128)(2,1)S(1)} all-to-all(bf16[2,80,9216]{2,1,0:T(8,128)(2,1)S(1)} %pack.9), channel_id=1, replica_groups={{0,1},{2,3},{4,5},{6,7},{8,9},{10,11},{12,13},{14,15},{16,17},{18,19},{..., dimensions={0} | all-to-all | bytes 5898240 | tf_op jit(solution)/shard_map/all_to_all | solution.py:409
  81.2 2.3 %project.8.refs_1_ = f32[160,512]{1,0:T(8,128)S(1)} custom-call(bf16[2,80,9216]{2,1,0:T(8,128)(2,1)S(1)} %all_to_all.33.refs_0_, bf16[14336,512]{1,0:T(8,128)(2,1)S(1)} %get-tuple-element.87.refs_1_.refs_2_.refs_4_.refs_5_, bf16[4096,512]{1,0:T(8,128)(2,1)S(1)} %get-tuple-element.88.refs_2_.refs_3_.refs_5_.refs_6_, f32[160,512]{1,0:T(8,128)S(1)} %get-tuple-element.110.refs_3_), custom_call_target="tpu_custom_call" | custom-call | flops 1 | bytes 1 | tf_op jit(solution)/shard_map/project/pallas_call | solution.py:239
  84.7 2.0 %collective-permute-done.12.refs_1_ = bf16[40,9216]{1,0:T(8,128)(2,1)S(1)} collective-permute-done((bf16[40,9216]{1,0:T(8,128)(2,1)S(1)}, bf16[40,9216]{1,0:T(8,128)(2,1)S(1)}, u32[]{:S(2)}, u32[]{:S(2)}) %collective-permute-start.12) | collective-permute-done | bytes 737312 | tf_op jit(solution)/shard_map/ppermute | solution.py:415
  87.0 1.6 %collective-permute-start.16 = (bf16[40,4608]{1,0:T(8,128)(2,1)S(1)}, bf16[40,4608]{1,0:T(8,128)(2,1)S(1)}, u32[]{:S(2)}, u32[]{:S(2)}) collective-permute-start(bf16[40,4608]{1,0:T(8,128)(2,1)S(1)} %get-tuple-element.130), channel_id=1, source_target_pairs={{2,6},{3,7},{6,10},{7,11},{10,14},{11,15},{14,12},{15,13},{12,8},{... | collective-permute-start | bytes 1105928 | tf_op jit(solution)/shard_map/ppermute | solution.py:415
  89.7 6.1 %all_to_all.34.refs_0_ = bf16[2,80,9216]{2,1,0:T(8,128)(2,1)S(1)} all-to-all(bf16[2,80,9216]{2,1,0:T(8,128)(2,1)S(1)} %pack.10), channel_id=1, replica_groups={{0,1},{2,3},{4,5},{6,7},{8,9},{10,11},{12,13},{14,15},{16,17},{18,19},{..., dimensions={0} | all-to-all | bytes 5898240 | tf_op jit(solution)/shard_map/all_to_all | solution.py:409
  95.8 3.6 %project.9 = (f32[160,512]{1,0:T(8,128)S(1)}, f32[160,512]{1,0:T(8,128)S(1)}) custom-call(bf16[2,80,9216]{2,1,0:T(8,128)(2,1)S(1)} %all_to_all.34.refs_0_, bf16[14336,512]{1,0:T(8,128)(2,1)S(1)} %get-tuple-element.87.refs_1_.refs_2_.refs_4_.refs_5_, bf16[4096,512]{1,0:T(8,128)(2,1)S(1)} %get-tuple-element.88.refs_2_.refs_3_.refs_5_.refs_6_), custom_call_target="tpu_custom_call" | custom-call | flops 1 | bytes 1 | tf_op jit(solution)/shard_map/project/pallas_call | solution.py:239
  100.4 2.1 %collective-permute-done.10.refs_1_ = bf16[40,9216]{1,0:T(8,128)(2,1)S(1)} collective-permute-done((bf16[40,9216]{1,0:T(8,128)(2,1)S(1)}, bf16[40,9216]{1,0:T(8,128)(2,1)S(1)}, u32[]{:S(2)}, u32[]{:S(2)}) %collective-permute-start.10) | collective-permute-done | bytes 737312 | tf_op jit(solution)/shard_map/ppermute | solution.py:415
  104.1 1.6 %collective-permute-start.14 = (bf16[40,4992]{1,0:T(8,128)(2,1)S(1)}, bf16[40,4992]{1,0:T(8,128)(2,1)S(1)}, u32[]{:S(2)}, u32[]{:S(2)}) collective-permute-start(bf16[40,4992]{1,0:T(8,128)(2,1)S(1)} %get-tuple-element.128), channel_id=1, source_target_pairs={{2,6},{3,7},{6,10},{7,11},{10,14},{11,15},{14,12},{15,13},{12,8},{... | collective-permute-start | bytes 1198088 | tf_op jit(solution)/shard_map/ppermute | solution.py:415
  106.9 6.1 %all_to_all.35.refs_0_ = bf16[2,80,9216]{2,1,0:T(8,128)(2,1)S(1)} all-to-all(bf16[2,80,9216]{2,1,0:T(8,128)(2,1)S(1)} %pack.11), channel_id=1, replica_groups={{0,1},{2,3},{4,5},{6,7},{8,9},{10,11},{12,13},{14,15},{16,17},{18,19},{..., dimensions={0} | all-to-all | bytes 5898240 | tf_op jit(solution)/shard_map/all_to_all | solution.py:409
  119.4 2.5 %project_last.5.refs_1_ = f32[240,512]{1,0:T(8,128)S(1)} custom-call(bf16[2,80,9216]{2,1,0:T(8,128)(2,1)S(1)} %all_to_all.35.refs_0_, bf16[40,4992]{1,0:T(8,128)(2,1)S(1)} %collective-permute-done.14.refs_1_, bf16[40,4224]{1,0:T(8,128)(2,1)S(1)} %collective-permute-done.15.refs_2_, bf16[40,4992]{1,0:T(8,128)(2,1)S(1)} %collective-permute-done.22.refs_3_, ...), custom_call_target="tpu_custom_call" | custom-call | flops 1 | bytes 1 | tf_op jit(solution)/shard_map/project_last/pallas_call | solution.py:294
  125.0 2.5 %collective-permute-done.25.refs_1_ = f32[16,640]{1,0:T(8,128)S(1)} collective-permute-done((f32[16,640]{1,0:T(8,128)S(1)}, f32[16,640]{1,0:T(8,128)S(1)}, u32[]{:S(2)}, u32[]{:S(2)}) %collective-permute-start.25) | collective-permute-done | bytes 40992 | tf_op jit(solution)/shard_map/ppermute | solution.py:405
  (60 shorter events, 34.6 us)
Async XLA Ops:
  1.1 20.4 %collective-permute-start.2 = (bf16[40,9216]{1,0:T(8,128)(2,1)S(1)}, bf16[40,9216]{1,0:T(8,128)(2,1)S(1)}, u32[]{:S(2)}, u32[]{:S(2)}) collective-permute-start(bf16[40,9216]{1,0:T(8,128)(2,1)S(1)} %columns.6.refs_2_), channel_id=1, source_target_pairs={{2,6},{3,7},{6,10},{7,11},{10,14},{11,15},{14,12},{15,13},{12,8},{... | collective-permute-start | bytes 2211848 | tf_op jit(solution)/shard_map/ppermute | solution.py:415
  4.1 19.4 %collective-permute-start.3 = (bf16[40,9216]{1,0:T(8,128)(2,1)S(1)}, bf16[40,9216]{1,0:T(8,128)(2,1)S(1)}, u32[]{:S(2)}, u32[]{:S(2)}) collective-permute-start(bf16[40,9216]{1,0:T(8,128)(2,1)S(1)} %columns.6.refs_2_), channel_id=1, source_target_pairs={{6,2},{7,3},{10,6},{11,7},{14,10},{15,11},{12,14},{13,15},{8,12},{... | collective-permute-start | bytes 2211848 | tf_op jit(solution)/shard_map/ppermute | solution.py:415
  5.4 32.7 %collective-permute-start = (bf16[40,9216]{1,0:T(8,128)(2,1)S(1)}, bf16[40,9216]{1,0:T(8,128)(2,1)S(1)}, u32[]{:S(2)}, u32[]{:S(2)}) collective-permute-start(bf16[40,9216]{1,0:T(8,128)(2,1)S(1)} %columns.5.refs_2_), channel_id=1, source_target_pairs={{2,6},{3,7},{6,10},{7,11},{10,14},{11,15},{14,12},{15,13},{12,8},{... | collective-permute-start | bytes 2211848 | tf_op jit(solution)/shard_map/ppermute | solution.py:415
  7.4 32.0 %collective-permute-start.1 = (bf16[40,9216]{1,0:T(8,128)(2,1)S(1)}, bf16[40,9216]{1,0:T(8,128)(2,1)S(1)}, u32[]{:S(2)}, u32[]{:S(2)}) collective-permute-start(bf16[40,9216]{1,0:T(8,128)(2,1)S(1)} %columns.5.refs_2_), channel_id=1, source_target_pairs={{6,2},{7,3},{10,6},{11,7},{14,10},{15,11},{12,14},{13,15},{8,12},{... | collective-permute-start | bytes 2211848 | tf_op jit(solution)/shard_map/ppermute | solution.py:415
  23.6 30.7 %collective-permute-start.6 = (bf16[40,9216]{1,0:T(8,128)(2,1)S(1)}, bf16[40,9216]{1,0:T(8,128)(2,1)S(1)}, u32[]{:S(2)}, u32[]{:S(2)}) collective-permute-start(bf16[40,9216]{1,0:T(8,128)(2,1)S(1)} %collective-permute-done.2.refs_0_), channel_id=1, source_target_pairs={{2,6},{3,7},{6,10},{7,11},{10,14},{11,15},{14,12},{15,13},{12,8},{... | collective-permute-start | bytes 2211848 | tf_op jit(solution)/shard_map/ppermute | solution.py:415
  25.1 30.0 %collective-permute-start.7 = (bf16[40,9216]{1,0:T(8,128)(2,1)S(1)}, bf16[40,9216]{1,0:T(8,128)(2,1)S(1)}, u32[]{:S(2)}, u32[]{:S(2)}) collective-permute-start(bf16[40,9216]{1,0:T(8,128)(2,1)S(1)} %collective-permute-done.3.refs_1_), channel_id=1, source_target_pairs={{6,2},{7,3},{10,6},{11,7},{14,10},{15,11},{12,14},{13,15},{8,12},{... | collective-permute-start | bytes 2211848 | tf_op jit(solution)/shard_map/ppermute | solution.py:415
  39.4 29.6 %collective-permute-start.4 = (bf16[40,9216]{1,0:T(8,128)(2,1)S(1)}, bf16[40,9216]{1,0:T(8,128)(2,1)S(1)}, u32[]{:S(2)}, u32[]{:S(2)}) collective-permute-start(bf16[40,9216]{1,0:T(8,128)(2,1)S(1)} %collective-permute-done.refs_0_), channel_id=1, source_target_pairs={{2,6},{3,7},{6,10},{7,11},{10,14},{11,15},{14,12},{15,13},{12,8},{... | collective-permute-start | bytes 2211848 | tf_op jit(solution)/shard_map/ppermute | solution.py:415
  40.9 30.0 %collective-permute-start.5 = (bf16[40,9216]{1,0:T(8,128)(2,1)S(1)}, bf16[40,9216]{1,0:T(8,128)(2,1)S(1)}, u32[]{:S(2)}, u32[]{:S(2)}) collective-permute-start(bf16[40,9216]{1,0:T(8,128)(2,1)S(1)} %collective-permute-done.1.refs_1_), channel_id=1, source_target_pairs={{6,2},{7,3},{10,6},{11,7},{14,10},{15,11},{12,14},{13,15},{8,12},{... | collective-permute-start | bytes 2211848 | tf_op jit(solution)/shard_map/ppermute | solution.py:415
  41.4 12.8 %collective-permute-start.8 = (f32[240,512]{1,0:T(8,128)S(1)}, f32[240,512]{1,0:T(8,128)S(1)}, u32[]{:S(2)}, u32[]{:S(2)}) collective-permute-start(f32[240,512]{1,0:T(8,128)S(1)} %get-tuple-element.106.refs_1_), channel_id=1, source_target_pairs={{0,16},{16,0},{1,17},{17,1},{2,18},{18,2},{3,19},{19,3},{4,20},{20... | collective-permute-start | bytes 1474568 | tf_op jit(solution)/shard_map/ppermute | solution.py:405
  55.2 29.6 %collective-permute-start.11 = (bf16[40,9216]{1,0:T(8,128)(2,1)S(1)}, bf16[40,9216]{1,0:T(8,128)(2,1)S(1)}, u32[]{:S(2)}, u32[]{:S(2)}) collective-permute-start(bf16[40,9216]{1,0:T(8,128)(2,1)S(1)} %collective-permute-done.6.refs_0_), channel_id=1, source_target_pairs={{2,6},{3,7},{6,10},{7,11},{10,14},{11,15},{14,12},{15,13},{12,8},{... | collective-permute-start | bytes 2211848 | tf_op jit(solution)/shard_map/ppermute | solution.py:415
  56.7 30.0 %collective-permute-start.12 = (bf16[40,9216]{1,0:T(8,128)(2,1)S(1)}, bf16[40,9216]{1,0:T(8,128)(2,1)S(1)}, u32[]{:S(2)}, u32[]{:S(2)}) collective-permute-start(bf16[40,9216]{1,0:T(8,128)(2,1)S(1)} %collective-permute-done.7.refs_1_), channel_id=1, source_target_pairs={{6,2},{7,3},{10,6},{11,7},{14,10},{15,11},{12,14},{13,15},{8,12},{... | collective-permute-start | bytes 2211848 | tf_op jit(solution)/shard_map/ppermute | solution.py:415
  71.0 31.6 %collective-permute-start.10 = (bf16[40,9216]{1,0:T(8,128)(2,1)S(1)}, bf16[40,9216]{1,0:T(8,128)(2,1)S(1)}, u32[]{:S(2)}, u32[]{:S(2)}) collective-permute-start(bf16[40,9216]{1,0:T(8,128)(2,1)S(1)} %collective-permute-done.5.refs_1_), channel_id=1, source_target_pairs={{6,2},{7,3},{10,6},{11,7},{14,10},{15,11},{12,14},{13,15},{8,12},{... | collective-permute-start | bytes 2211848 | tf_op jit(solution)/shard_map/ppermute | solution.py:415
  71.0 31.5 %collective-permute-start.9 = (bf16[40,9216]{1,0:T(8,128)(2,1)S(1)}, bf16[40,9216]{1,0:T(8,128)(2,1)S(1)}, u32[]{:S(2)}, u32[]{:S(2)}) collective-permute-start(bf16[40,9216]{1,0:T(8,128)(2,1)S(1)} %collective-permute-done.4.refs_0_), channel_id=1, source_target_pairs={{2,6},{3,7},{6,10},{7,11},{10,14},{11,15},{14,12},{15,13},{12,8},{... | collective-permute-start | bytes 2211848 | tf_op jit(solution)/shard_map/ppermute | solution.py:415
  73.0 10.6 %collective-permute-start.13 = (f32[224,512]{1,0:T(8,128)S(1)}, f32[224,512]{1,0:T(8,128)S(1)}, u32[]{:S(2)}, u32[]{:S(2)}) collective-permute-start(f32[224,512]{1,0:T(8,128)S(1)} %get-tuple-element.124.refs_2_.refs_0_), channel_id=1, source_target_pairs={{0,16},{16,0},{1,17},{17,1},{2,18},{18,2},{3,19},{19,3},{4,20},{20... | collective-permute-start | bytes 1376264 | tf_op jit(solution)/shard_map/ppermute | solution.py:405
  87.0 26.0 %collective-permute-start.16 = (bf16[40,4608]{1,0:T(8,128)(2,1)S(1)}, bf16[40,4608]{1,0:T(8,128)(2,1)S(1)}, u32[]{:S(2)}, u32[]{:S(2)}) collective-permute-start(bf16[40,4608]{1,0:T(8,128)(2,1)S(1)} %get-tuple-element.130), channel_id=1, source_target_pairs={{2,6},{3,7},{6,10},{7,11},{10,14},{11,15},{14,12},{15,13},{12,8},{... | collective-permute-start | bytes 1105928 | tf_op jit(solution)/shard_map/ppermute | solution.py:415
  88.6 24.4 %collective-permute-start.17 = (bf16[40,4608]{1,0:T(8,128)(2,1)S(1)}, bf16[40,4608]{1,0:T(8,128)(2,1)S(1)}, u32[]{:S(2)}, u32[]{:S(2)}) collective-permute-start(bf16[40,4608]{1,0:T(8,128)(2,1)S(1)} %get-tuple-element.131), channel_id=1, source_target_pairs={{6,2},{7,3},{10,6},{11,7},{14,10},{15,11},{12,14},{13,15},{8,12},{... | collective-permute-start | bytes 1105928 | tf_op jit(solution)/shard_map/ppermute | solution.py:415
  102.6 10.4 %collective-permute-start.18 = (f32[160,512]{1,0:T(8,128)S(1)}, f32[160,512]{1,0:T(8,128)S(1)}, u32[]{:S(2)}, u32[]{:S(2)}) collective-permute-start(f32[160,512]{1,0:T(8,128)S(1)} %get-tuple-element.158.refs_2_), channel_id=1, source_target_pairs={{0,16},{16,0},{1,17},{17,1},{2,18},{18,2},{3,19},{19,3},{4,20},{20... | collective-permute-start | bytes 983048 | tf_op jit(solution)/shard_map/ppermute | solution.py:405
  104.1 12.1 %collective-permute-start.14 = (bf16[40,4992]{1,0:T(8,128)(2,1)S(1)}, bf16[40,4992]{1,0:T(8,128)(2,1)S(1)}, u32[]{:S(2)}, u32[]{:S(2)}) collective-permute-start(bf16[40,4992]{1,0:T(8,128)(2,1)S(1)} %get-tuple-element.128), channel_id=1, source_target_pairs={{2,6},{3,7},{6,10},{7,11},{10,14},{11,15},{14,12},{15,13},{12,8},{... | collective-permute-start | bytes 1198088 | tf_op jit(solution)/shard_map/ppermute | solution.py:415
  105.8 10.5 %collective-permute-start.15 = (bf16[40,4224]{1,0:T(8,128)(2,1)S(1)}, bf16[40,4224]{1,0:T(8,128)(2,1)S(1)}, u32[]{:S(2)}, u32[]{:S(2)}) collective-permute-start(bf16[40,4224]{1,0:T(8,128)(2,1)S(1)} %get-tuple-element.129), channel_id=1, source_target_pairs={{6,2},{7,3},{10,6},{11,7},{14,10},{15,11},{12,14},{13,15},{8,12},{... | collective-permute-start | bytes 1013768 | tf_op jit(solution)/shard_map/ppermute | solution.py:415
  113.5 2.8 %collective-permute-start.20 = (bf16[40,2560]{1,0:T(8,128)(2,1)S(1)}, bf16[40,2560]{1,0:T(8,128)(2,1)S(1)}, u32[]{:S(2)}, u32[]{:S(2)}) collective-permute-start(bf16[40,2560]{1,0:T(8,128)(2,1)S(1)} %get-tuple-element.148.refs_0_), channel_id=1, source_target_pairs={{2,3},{3,2},{6,7},{7,6},{10,11},{11,10},{14,15},{15,14},{12,13},{1... | collective-permute-start | bytes 614408 | tf_op jit(solution)/shard_map/ppermute | solution.py:412
  116.2 3.1 %collective-permute-start.22 = (bf16[40,4992]{1,0:T(8,128)(2,1)S(1)}, bf16[40,4992]{1,0:T(8,128)(2,1)S(1)}, u32[]{:S(2)}, u32[]{:S(2)}) collective-permute-start(bf16[40,4992]{1,0:T(8,128)(2,1)S(1)} %collective-permute-done.14.refs_1_), channel_id=1, source_target_pairs={{2,3},{3,2},{6,7},{7,6},{10,11},{11,10},{14,15},{15,14},{12,13},{1... | collective-permute-start | bytes 1198088 | tf_op jit(solution)/shard_map/ppermute | solution.py:412
  116.3 3.0 %collective-permute-start.23 = (bf16[40,4224]{1,0:T(8,128)(2,1)S(1)}, bf16[40,4224]{1,0:T(8,128)(2,1)S(1)}, u32[]{:S(2)}, u32[]{:S(2)}) collective-permute-start(bf16[40,4224]{1,0:T(8,128)(2,1)S(1)} %collective-permute-done.15.refs_2_), channel_id=1, source_target_pairs={{2,3},{3,2},{6,7},{7,6},{10,11},{11,10},{14,15},{15,14},{12,13},{1... | collective-permute-start | bytes 1013768 | tf_op jit(solution)/shard_map/ppermute | solution.py:412
  116.8 6.2 %collective-permute-start.24 = (f32[80,512]{1,0:T(8,128)S(1)}, f32[80,512]{1,0:T(8,128)S(1)}, u32[]{:S(2)}, u32[]{:S(2)}) collective-permute-start(f32[80,512]{1,0:T(8,128)S(1)} %project_last.3.refs_2_), channel_id=1, source_target_pairs={{0,16},{16,0},{1,17},{17,1},{2,18},{18,2},{3,19},{19,3},{4,20},{20... | collective-permute-start | bytes 491528 | tf_op jit(solution)/shard_map/ppermute | solution.py:405
  123.4 4.0 %collective-permute-start.25 = (f32[16,640]{1,0:T(8,128)S(1)}, f32[16,640]{1,0:T(8,128)S(1)}, u32[]{:S(2)}, u32[]{:S(2)}) collective-permute-start(f32[16,640]{1,0:T(8,128)S(1)} %score.7.refs_0_), channel_id=1, source_target_pairs={{0,16},{16,0},{1,17},{17,1},{2,18},{18,2},{3,19},{19,3},{4,20},{20... | collective-permute-start | bytes 122888 | tf_op jit(solution)/shard_map/ppermute | solution.py:405
  (2 other events, 4.1 us)

commit v8 on v7

--- a/solution.py
+++ b/solution.py
@@ -481,12 +481,12 @@
             fly1, arrays, part, held, swapped, last_other, inverse, found)
         last_part = project_last([*held[1:], *swapped[1:]], [
             (((0, 0), (2, 0)), low, 0, 0), (((1, 0), (3, 0)), cut - low, 0, low)], factors)
-        swapped = mate(fly1)
+        joined = columns_of(fly1, [[(0, 0, high), (1, 0, width - cut - high)]], True)
+        swapped = mate(joined)
         last_other = across(last_other)
-        fly1, swapped, last_part = tied(fly1, swapped, last_part)
-        one = project_last([*arrays, *fly1, *swapped], [
-            (((0, 0), (1, 0), (3, 0)), high, 0, cut),
-            (((0, high), (2, 0), (4, 0)), width - cut - high, 0, cut + high)], factors, [part, last_part])
+        joined, swapped, last_part = tied(joined, swapped, last_part)
+        one = project_last([*arrays, *joined, *swapped], [
+            (((0, 0), (1, 0), (2, 0)), width - cut, 0, cut)], factors, [part, last_part])
         found = [score(one, other, found, 0, part.shape[0])]
         results = across(score(one, last_other, found, part.shape[0], 2 * tokens))
         return last(results, inverse, tuple(groups), place, tokens, query * tokens // rows).T

time: 129 us -> 129 us (level)
    pallas_call x5 -> x6, Pallas kernels: 2.78 us -> 2.86 us  [columns_of(): pl.pallas_call(functools.partial(copy_kernel, tuple(plan), len(arrays)),...]
  transfers between devices with their start and end apart: 26 -> 25, of which waited for: 13 -> 13; matrix products, arithmetic and copies ran while one was open for 0% -> 0% of each run, Pallas kernels for 30% -> 30%
where the time goes in v8:
time: 129 us; the launch traced here: 128 us
  Pallas kernels  40.9 us (32%)
  blocking collectives  39 us (30%)
  starting transfers between devices  26 us (20%)
  waiting for transfers between devices  22.2 us (17%)
    all_to_all x6, blocking collectives, both_cores(): return lax.all_to_all(x, 'query', 0, 0, axis_index_groups=sorted(ring))  39 us
    pallas_call x5, Pallas kernels, project(): pl.pallas_call(functools.partial(project_kernel, step, tuple(span), len(a...  17 us
    ppermute x8, starting transfers between devices, round_ring(): lax.ppermute(pair[0], 'query', forward)  14.9 us
    ppermute x8, waiting for transfers between devices, round_ring(): lax.ppermute(pair[1], 'query', backward)  10.9 us
    pallas_call x1, Pallas kernels, load(): pl.pallas_call(functools.partial(load_kernel, step), in_specs=[pl.BlockSp...  8.62 us
    ppermute x5, starting transfers between devices, across(): return [x, lax.ppermute(x, 'rows', [(0, 1), (1, 0)])]  7.66 us
    ppermute x8, waiting for transfers between devices, round_ring(): lax.ppermute(pair[0], 'query', forward)  7.3 us
    pallas_call x3, Pallas kernels, project_last(): pl.pallas_call(functools.partial(project_last_kernel, tuple(plan), (len(a...  4.52 us
  transfers between devices with their start and end apart: 25, of which 13 were waited for; matrix products, arithmetic and copies ran while one was open for 0% of the time, Pallas kernels for 30%

profile of v8, /device:TPU:0, one launch (start us, length us, event | category | flops | bytes accessed | tf_op | source)
XLA Modules:
  0.0 128.3 jit_solution(3159154824569534044)
XLA Ops:
  1.1 3.0 %collective-permute-start.2 = (bf16[40,9216]{1,0:T(8,128)(2,1)S(1)}, bf16[40,9216]{1,0:T(8,128)(2,1)S(1)}, u32[]{:S(2)}, u32[]{:S(2)}) collective-permute-start(bf16[40,9216]{1,0:T(8,128)(2,1)S(1)} %columns.7.refs_2_), channel_id=1, source_target_pairs={{2,6},{3,7},{6,10},{7,11},{10,14},{11,15},{14,12},{15,13},{12,8},{... | collective-permute-start | bytes 2211848 | tf_op jit(solution)/shard_map/ppermute | solution.py:415
  5.4 2.0 %collective-permute-start = (bf16[40,9216]{1,0:T(8,128)(2,1)S(1)}, bf16[40,9216]{1,0:T(8,128)(2,1)S(1)}, u32[]{:S(2)}, u32[]{:S(2)}) collective-permute-start(bf16[40,9216]{1,0:T(8,128)(2,1)S(1)} %columns.6.refs_2_), channel_id=1, source_target_pairs={{2,6},{3,7},{6,10},{7,11},{10,14},{11,15},{14,12},{15,13},{12,8},{... | collective-permute-start | bytes 2211848 | tf_op jit(solution)/shard_map/ppermute | solution.py:415
  7.5 8.6 %load_factors.1 = (bf16[14336,512]{1,0:T(8,128)(2,1)S(1)}, bf16[4096,512]{1,0:T(8,128)(2,1)S(1)}, f32[2,32,512]{2,1,0:T(8,128)S(1)}) custom-call(bf16[14336,512]{1,0:T(8,128)(2,1)} %a_ref.1, bf16[4096,512]{1,0:T(8,128)(2,1)} %b_ref.1), custom_call_target="tpu_custom_call" | custom-call | flops 1 | bytes 1 | tf_op jit(solution)/shard_map/load_factors/pallas_call | solution.py:136
  16.1 5.4 %collective-permute-done.2.refs_0_ = bf16[40,9216]{1,0:T(8,128)(2,1)S(1)} collective-permute-done((bf16[40,9216]{1,0:T(8,128)(2,1)S(1)}, bf16[40,9216]{1,0:T(8,128)(2,1)S(1)}, u32[]{:S(2)}, u32[]{:S(2)}) %collective-permute-start.2) | collective-permute-done | bytes 737312 | tf_op jit(solution)/shard_map/ppermute | solution.py:415
  21.5 2.0 %collective-permute-done.3.refs_1_ = bf16[40,9216]{1,0:T(8,128)(2,1)S(1)} collective-permute-done((bf16[40,9216]{1,0:T(8,128)(2,1)S(1)}, bf16[40,9216]{1,0:T(8,128)(2,1)S(1)}, u32[]{:S(2)}, u32[]{:S(2)}) %collective-permute-start.3) | collective-permute-done | bytes 737312 | tf_op jit(solution)/shard_map/ppermute | solution.py:415
  26.5 7.3 %all_to_all.30.refs_0_ = bf16[2,120,9216]{2,1,0:T(8,128)(2,1)S(1)} all-to-all(bf16[2,120,9216]{2,1,0:T(8,128)(2,1)S(1)} %pack.6), channel_id=1, replica_groups={{0,1},{2,3},{4,5},{6,7},{8,9},{10,11},{12,13},{14,15},{16,17},{18,19},{..., dimensions={0} | all-to-all | bytes 8847360 | tf_op jit(solution)/shard_map/all_to_all | solution.py:409
  33.7 4.4 %project.5 = (f32[240,512]{1,0:T(8,128)S(1)}, f32[240,512]{1,0:T(8,128)S(1)}) custom-call(bf16[2,120,9216]{2,1,0:T(8,128)(2,1)S(1)} %all_to_all.30.refs_0_, bf16[14336,512]{1,0:T(8,128)(2,1)S(1)} %get-tuple-element.85.refs_1_.refs_2_.refs_4_.refs_3_, bf16[4096,512]{1,0:T(8,128)(2,1)S(1)} %get-tuple-element.86.refs_2_.refs_3_.refs_5_.refs_4_), custom_call_target="tpu_custom_call" | custom-call | flops 1 | bytes 1 | tf_op jit(solution)/shard_map/project/pallas_call | solution.py:239
  43.8 7.3 %all_to_all.31.refs_0_ = bf16[2,120,9216]{2,1,0:T(8,128)(2,1)S(1)} all-to-all(bf16[2,120,9216]{2,1,0:T(8,128)(2,1)S(1)} %pack.7), channel_id=1, replica_groups={{0,1},{2,3},{4,5},{6,7},{8,9},{10,11},{12,13},{14,15},{16,17},{18,19},{..., dimensions={0} | all-to-all | bytes 8847360 | tf_op jit(solution)/shard_map/all_to_all | solution.py:409
  51.0 3.2 %project.6.refs_0_ = f32[240,512]{1,0:T(8,128)S(1)} custom-call(bf16[2,120,9216]{2,1,0:T(8,128)(2,1)S(1)} %all_to_all.31.refs_0_, bf16[14336,512]{1,0:T(8,128)(2,1)S(1)} %get-tuple-element.85.refs_1_.refs_2_.refs_4_.refs_3_, bf16[4096,512]{1,0:T(8,128)(2,1)S(1)} %get-tuple-element.86.refs_2_.refs_3_.refs_5_.refs_4_, f32[240,512]{1,0:T(8,128)S(1)} %get-tuple-element.92.refs_3_), custom_call_target="tpu_custom_call" | custom-call | flops 1 | bytes 1 | tf_op jit(solution)/shard_map/project/pallas_call | solution.py:239
  57.8 6.1 %all_to_all.32.refs_0_ = bf16[2,80,9216]{2,1,0:T(8,128)(2,1)S(1)} all-to-all(bf16[2,80,9216]{2,1,0:T(8,128)(2,1)S(1)} %pack.8), channel_id=1, replica_groups={{0,1},{2,3},{4,5},{6,7},{8,9},{10,11},{12,13},{14,15},{16,17},{18,19},{..., dimensions={0} | all-to-all | bytes 5898240 | tf_op jit(solution)/shard_map/all_to_all | solution.py:409
  63.9 3.6 %project.7 = (f32[160,512]{1,0:T(8,128)S(1)}, f32[224,512]{1,0:T(8,128)S(1)}) custom-call(bf16[2,80,9216]{2,1,0:T(8,128)(2,1)S(1)} %all_to_all.32.refs_0_, bf16[14336,512]{1,0:T(8,128)(2,1)S(1)} %get-tuple-element.85.refs_1_.refs_2_.refs_4_.refs_3_, bf16[4096,512]{1,0:T(8,128)(2,1)S(1)} %get-tuple-element.86.refs_2_.refs_3_.refs_5_.refs_4_, ...), custom_call_target="tpu_custom_call" | custom-call | flops 1 | bytes 1 | tf_op jit(solution)/shard_map/project/pallas_call | solution.py:239
  68.9 2.0 %collective-permute-done.5.refs_1_ = bf16[40,9216]{1,0:T(8,128)(2,1)S(1)} collective-permute-done((bf16[40,9216]{1,0:T(8,128)(2,1)S(1)}, bf16[40,9216]{1,0:T(8,128)(2,1)S(1)}, u32[]{:S(2)}, u32[]{:S(2)}) %collective-permute-start.5) | collective-permute-done | bytes 737312 | tf_op jit(solution)/shard_map/ppermute | solution.py:415
  71.0 1.9 %collective-permute-start.9 = (bf16[40,9216]{1,0:T(8,128)(2,1)S(1)}, bf16[40,9216]{1,0:T(8,128)(2,1)S(1)}, u32[]{:S(2)}, u32[]{:S(2)}) collective-permute-start(bf16[40,9216]{1,0:T(8,128)(2,1)S(1)} %collective-permute-done.4.refs_0_), channel_id=1, source_target_pairs={{2,6},{3,7},{6,10},{7,11},{10,14},{11,15},{14,12},{15,13},{12,8},{... | collective-permute-start | bytes 2211848 | tf_op jit(solution)/shard_map/ppermute | solution.py:415
  75.1 6.1 %all_to_all.33.refs_0_ = bf16[2,80,9216]{2,1,0:T(8,128)(2,1)S(1)} all-to-all(bf16[2,80,9216]{2,1,0:T(8,128)(2,1)S(1)} %pack.9), channel_id=1, replica_groups={{0,1},{2,3},{4,5},{6,7},{8,9},{10,11},{12,13},{14,15},{16,17},{18,19},{..., dimensions={0} | all-to-all | bytes 5898240 | tf_op jit(solution)/shard_map/all_to_all | solution.py:409
  81.2 2.3 %project.8.refs_1_ = f32[160,512]{1,0:T(8,128)S(1)} custom-call(bf16[2,80,9216]{2,1,0:T(8,128)(2,1)S(1)} %all_to_all.33.refs_0_, bf16[14336,512]{1,0:T(8,128)(2,1)S(1)} %get-tuple-element.85.refs_1_.refs_2_.refs_4_.refs_3_, bf16[4096,512]{1,0:T(8,128)(2,1)S(1)} %get-tuple-element.86.refs_2_.refs_3_.refs_5_.refs_4_, f32[160,512]{1,0:T(8,128)S(1)} %get-tuple-element.108.refs_3_), custom_call_target="tpu_custom_call" | custom-call | flops 1 | bytes 1 | tf_op jit(solution)/shard_map/project/pallas_call | solution.py:239
  84.7 2.0 %collective-permute-done.12.refs_1_ = bf16[40,9216]{1,0:T(8,128)(2,1)S(1)} collective-permute-done((bf16[40,9216]{1,0:T(8,128)(2,1)S(1)}, bf16[40,9216]{1,0:T(8,128)(2,1)S(1)}, u32[]{:S(2)}, u32[]{:S(2)}) %collective-permute-start.12) | collective-permute-done | bytes 737312 | tf_op jit(solution)/shard_map/ppermute | solution.py:415
  87.0 1.6 %collective-permute-start.16 = (bf16[40,4608]{1,0:T(8,128)(2,1)S(1)}, bf16[40,4608]{1,0:T(8,128)(2,1)S(1)}, u32[]{:S(2)}, u32[]{:S(2)}) collective-permute-start(bf16[40,4608]{1,0:T(8,128)(2,1)S(1)} %get-tuple-element.128), channel_id=1, source_target_pairs={{2,6},{3,7},{6,10},{7,11},{10,14},{11,15},{14,12},{15,13},{12,8},{... | collective-permute-start | bytes 1105928 | tf_op jit(solution)/shard_map/ppermute | solution.py:415
  89.7 6.1 %all_to_all.34.refs_0_ = bf16[2,80,9216]{2,1,0:T(8,128)(2,1)S(1)} all-to-all(bf16[2,80,9216]{2,1,0:T(8,128)(2,1)S(1)} %pack.10), channel_id=1, replica_groups={{0,1},{2,3},{4,5},{6,7},{8,9},{10,11},{12,13},{14,15},{16,17},{18,19},{..., dimensions={0} | all-to-all | bytes 5898240 | tf_op jit(solution)/shard_map/all_to_all | solution.py:409
  95.8 3.6 %project.9 = (f32[160,512]{1,0:T(8,128)S(1)}, f32[160,512]{1,0:T(8,128)S(1)}) custom-call(bf16[2,80,9216]{2,1,0:T(8,128)(2,1)S(1)} %all_to_all.34.refs_0_, bf16[14336,512]{1,0:T(8,128)(2,1)S(1)} %get-tuple-element.85.refs_1_.refs_2_.refs_4_.refs_3_, bf16[4096,512]{1,0:T(8,128)(2,1)S(1)} %get-tuple-element.86.refs_2_.refs_3_.refs_5_.refs_4_), custom_call_target="tpu_custom_call" | custom-call | flops 1 | bytes 1 | tf_op jit(solution)/shard_map/project/pallas_call | solution.py:239
  100.4 2.1 %collective-permute-done.10.refs_1_ = bf16[40,9216]{1,0:T(8,128)(2,1)S(1)} collective-permute-done((bf16[40,9216]{1,0:T(8,128)(2,1)S(1)}, bf16[40,9216]{1,0:T(8,128)(2,1)S(1)}, u32[]{:S(2)}, u32[]{:S(2)}) %collective-permute-start.10) | collective-permute-done | bytes 737312 | tf_op jit(solution)/shard_map/ppermute | solution.py:415
  104.1 1.6 %collective-permute-start.14 = (bf16[40,4992]{1,0:T(8,128)(2,1)S(1)}, bf16[40,4992]{1,0:T(8,128)(2,1)S(1)}, u32[]{:S(2)}, u32[]{:S(2)}) collective-permute-start(bf16[40,4992]{1,0:T(8,128)(2,1)S(1)} %get-tuple-element.126), channel_id=1, source_target_pairs={{2,6},{3,7},{6,10},{7,11},{10,14},{11,15},{14,12},{15,13},{12,8},{... | collective-permute-start | bytes 1198088 | tf_op jit(solution)/shard_map/ppermute | solution.py:415
  106.9 6.1 %all_to_all.35.refs_0_ = bf16[2,80,9216]{2,1,0:T(8,128)(2,1)S(1)} all-to-all(bf16[2,80,9216]{2,1,0:T(8,128)(2,1)S(1)} %pack.11), channel_id=1, replica_groups={{0,1},{2,3},{4,5},{6,7},{8,9},{10,11},{12,13},{14,15},{16,17},{18,19},{..., dimensions={0} | all-to-all | bytes 5898240 | tf_op jit(solution)/shard_map/all_to_all | solution.py:409
  119.1 2.7 %project_last.5.refs_1_ = f32[240,512]{1,0:T(8,128)S(1)} custom-call(bf16[2,80,9216]{2,1,0:T(8,128)(2,1)S(1)} %all_to_all.35.refs_0_, bf16[40,9216]{1,0:T(8,128)(2,1)S(1)} %columns.11.refs_1_, bf16[40,9216]{1,0:T(8,128)(2,1)S(1)} %collective-permute-done.22.refs_2_, bf16[14336,512]{1,0:T(8,128)(2,1)S(1)} %get-tuple-element.85.refs_1_.refs_2_.refs_4_.refs_3_, ...), custom_call_target="tpu_custom_call" | custom-call | flops 1 | bytes 1 | tf_op jit(solution)/shard_map/project_last/pallas_call | solution.py:294
  125.0 2.4 %collective-permute-done.24.refs_1_ = f32[16,640]{1,0:T(8,128)S(1)} collective-permute-done((f32[16,640]{1,0:T(8,128)S(1)}, f32[16,640]{1,0:T(8,128)S(1)}, u32[]{:S(2)}, u32[]{:S(2)}) %collective-permute-start.24) | collective-permute-done | bytes 40992 | tf_op jit(solution)/shard_map/ppermute | solution.py:405
  (59 shorter events, 34.5 us)
Async XLA Ops:
  1.1 20.4 %collective-permute-start.2 = (bf16[40,9216]{1,0:T(8,128)(2,1)S(1)}, bf16[40,9216]{1,0:T(8,128)(2,1)S(1)}, u32[]{:S(2)}, u32[]{:S(2)}) collective-permute-start(bf16[40,9216]{1,0:T(8,128)(2,1)S(1)} %columns.7.refs_2_), channel_id=1, source_target_pairs={{2,6},{3,7},{6,10},{7,11},{10,14},{11,15},{14,12},{15,13},{12,8},{... | collective-permute-start | bytes 2211848 | tf_op jit(solution)/shard_map/ppermute | solution.py:415
  4.1 19.4 %collective-permute-start.3 = (bf16[40,9216]{1,0:T(8,128)(2,1)S(1)}, bf16[40,9216]{1,0:T(8,128)(2,1)S(1)}, u32[]{:S(2)}, u32[]{:S(2)}) collective-permute-start(bf16[40,9216]{1,0:T(8,128)(2,1)S(1)} %columns.7.refs_2_), channel_id=1, source_target_pairs={{6,2},{7,3},{10,6},{11,7},{14,10},{15,11},{12,14},{13,15},{8,12},{... | collective-permute-start | bytes 2211848 | tf_op jit(solution)/shard_map/ppermute | solution.py:415
  5.4 32.7 %collective-permute-start = (bf16[40,9216]{1,0:T(8,128)(2,1)S(1)}, bf16[40,9216]{1,0:T(8,128)(2,1)S(1)}, u32[]{:S(2)}, u32[]{:S(2)}) collective-permute-start(bf16[40,9216]{1,0:T(8,128)(2,1)S(1)} %columns.6.refs_2_), channel_id=1, source_target_pairs={{2,6},{3,7},{6,10},{7,11},{10,14},{11,15},{14,12},{15,13},{12,8},{... | collective-permute-start | bytes 2211848 | tf_op jit(solution)/shard_map/ppermute | solution.py:415
  7.4 32.0 %collective-permute-start.1 = (bf16[40,9216]{1,0:T(8,128)(2,1)S(1)}, bf16[40,9216]{1,0:T(8,128)(2,1)S(1)}, u32[]{:S(2)}, u32[]{:S(2)}) collective-permute-start(bf16[40,9216]{1,0:T(8,128)(2,1)S(1)} %columns.6.refs_2_), channel_id=1, source_target_pairs={{6,2},{7,3},{10,6},{11,7},{14,10},{15,11},{12,14},{13,15},{8,12},{... | collective-permute-start | bytes 2211848 | tf_op jit(solution)/shard_map/ppermute | solution.py:415
  23.6 30.7 %collective-permute-start.6 = (bf16[40,9216]{1,0:T(8,128)(2,1)S(1)}, bf16[40,9216]{1,0:T(8,128)(2,1)S(1)}, u32[]{:S(2)}, u32[]{:S(2)}) collective-permute-start(bf16[40,9216]{1,0:T(8,128)(2,1)S(1)} %collective-permute-done.2.refs_0_), channel_id=1, source_target_pairs={{2,6},{3,7},{6,10},{7,11},{10,14},{11,15},{14,12},{15,13},{12,8},{... | collective-permute-start | bytes 2211848 | tf_op jit(solution)/shard_map/ppermute | solution.py:415
  25.1 30.0 %collective-permute-start.7 = (bf16[40,9216]{1,0:T(8,128)(2,1)S(1)}, bf16[40,9216]{1,0:T(8,128)(2,1)S(1)}, u32[]{:S(2)}, u32[]{:S(2)}) collective-permute-start(bf16[40,9216]{1,0:T(8,128)(2,1)S(1)} %collective-permute-done.3.refs_1_), channel_id=1, source_target_pairs={{6,2},{7,3},{10,6},{11,7},{14,10},{15,11},{12,14},{13,15},{8,12},{... | collective-permute-start | bytes 2211848 | tf_op jit(solution)/shard_map/ppermute | solution.py:415
  39.4 29.6 %collective-permute-start.4 = (bf16[40,9216]{1,0:T(8,128)(2,1)S(1)}, bf16[40,9216]{1,0:T(8,128)(2,1)S(1)}, u32[]{:S(2)}, u32[]{:S(2)}) collective-permute-start(bf16[40,9216]{1,0:T(8,128)(2,1)S(1)} %collective-permute-done.refs_0_), channel_id=1, source_target_pairs={{2,6},{3,7},{6,10},{7,11},{10,14},{11,15},{14,12},{15,13},{12,8},{... | collective-permute-start | bytes 2211848 | tf_op jit(solution)/shard_map/ppermute | solution.py:415
  40.9 30.0 %collective-permute-start.5 = (bf16[40,9216]{1,0:T(8,128)(2,1)S(1)}, bf16[40,9216]{1,0:T(8,128)(2,1)S(1)}, u32[]{:S(2)}, u32[]{:S(2)}) collective-permute-start(bf16[40,9216]{1,0:T(8,128)(2,1)S(1)} %collective-permute-done.1.refs_1_), channel_id=1, source_target_pairs={{6,2},{7,3},{10,6},{11,7},{14,10},{15,11},{12,14},{13,15},{8,12},{... | collective-permute-start | bytes 2211848 | tf_op jit(solution)/shard_map/ppermute | solution.py:415
  41.4 12.8 %collective-permute-start.8 = (f32[240,512]{1,0:T(8,128)S(1)}, f32[240,512]{1,0:T(8,128)S(1)}, u32[]{:S(2)}, u32[]{:S(2)}) collective-permute-start(f32[240,512]{1,0:T(8,128)S(1)} %get-tuple-element.104.refs_1_), channel_id=1, source_target_pairs={{0,16},{16,0},{1,17},{17,1},{2,18},{18,2},{3,19},{19,3},{4,20},{20... | collective-permute-start | bytes 1474568 | tf_op jit(solution)/shard_map/ppermute | solution.py:405
  55.2 29.6 %collective-permute-start.11 = (bf16[40,9216]{1,0:T(8,128)(2,1)S(1)}, bf16[40,9216]{1,0:T(8,128)(2,1)S(1)}, u32[]{:S(2)}, u32[]{:S(2)}) collective-permute-start(bf16[40,9216]{1,0:T(8,128)(2,1)S(1)} %collective-permute-done.6.refs_0_), channel_id=1, source_target_pairs={{2,6},{3,7},{6,10},{7,11},{10,14},{11,15},{14,12},{15,13},{12,8},{... | collective-permute-start | bytes 2211848 | tf_op jit(solution)/shard_map/ppermute | solution.py:415
  56.7 30.0 %collective-permute-start.12 = (bf16[40,9216]{1,0:T(8,128)(2,1)S(1)}, bf16[40,9216]{1,0:T(8,128)(2,1)S(1)}, u32[]{:S(2)}, u32[]{:S(2)}) collective-permute-start(bf16[40,9216]{1,0:T(8,128)(2,1)S(1)} %collective-permute-done.7.refs_1_), channel_id=1, source_target_pairs={{6,2},{7,3},{10,6},{11,7},{14,10},{15,11},{12,14},{13,15},{8,12},{... | collective-permute-start | bytes 2211848 | tf_op jit(solution)/shard_map/ppermute | solution.py:415
  71.0 31.6 %collective-permute-start.10 = (bf16[40,9216]{1,0:T(8,128)(2,1)S(1)}, bf16[40,9216]{1,0:T(8,128)(2,1)S(1)}, u32[]{:S(2)}, u32[]{:S(2)}) collective-permute-start(bf16[40,9216]{1,0:T(8,128)(2,1)S(1)} %collective-permute-done.5.refs_1_), channel_id=1, source_target_pairs={{6,2},{7,3},{10,6},{11,7},{14,10},{15,11},{12,14},{13,15},{8,12},{... | collective-permute-start | bytes 2211848 | tf_op jit(solution)/shard_map/ppermute | solution.py:415
  71.0 31.5 %collective-permute-start.9 = (bf16[40,9216]{1,0:T(8,128)(2,1)S(1)}, bf16[40,9216]{1,0:T(8,128)(2,1)S(1)}, u32[]{:S(2)}, u32[]{:S(2)}) collective-permute-start(bf16[40,9216]{1,0:T(8,128)(2,1)S(1)} %collective-permute-done.4.refs_0_), channel_id=1, source_target_pairs={{2,6},{3,7},{6,10},{7,11},{10,14},{11,15},{14,12},{15,13},{12,8},{... | collective-permute-start | bytes 2211848 | tf_op jit(solution)/shard_map/ppermute | solution.py:415
  73.0 10.6 %collective-permute-start.13 = (f32[224,512]{1,0:T(8,128)S(1)}, f32[224,512]{1,0:T(8,128)S(1)}, u32[]{:S(2)}, u32[]{:S(2)}) collective-permute-start(f32[224,512]{1,0:T(8,128)S(1)} %get-tuple-element.122.refs_2_.refs_0_), channel_id=1, source_target_pairs={{0,16},{16,0},{1,17},{17,1},{2,18},{18,2},{3,19},{19,3},{4,20},{20... | collective-permute-start | bytes 1376264 | tf_op jit(solution)/shard_map/ppermute | solution.py:405
  87.0 26.0 %collective-permute-start.16 = (bf16[40,4608]{1,0:T(8,128)(2,1)S(1)}, bf16[40,4608]{1,0:T(8,128)(2,1)S(1)}, u32[]{:S(2)}, u32[]{:S(2)}) collective-permute-start(bf16[40,4608]{1,0:T(8,128)(2,1)S(1)} %get-tuple-element.128), channel_id=1, source_target_pairs={{2,6},{3,7},{6,10},{7,11},{10,14},{11,15},{14,12},{15,13},{12,8},{... | collective-permute-start | bytes 1105928 | tf_op jit(solution)/shard_map/ppermute | solution.py:415
  88.6 24.4 %collective-permute-start.17 = (bf16[40,4608]{1,0:T(8,128)(2,1)S(1)}, bf16[40,4608]{1,0:T(8,128)(2,1)S(1)}, u32[]{:S(2)}, u32[]{:S(2)}) collective-permute-start(bf16[40,4608]{1,0:T(8,128)(2,1)S(1)} %get-tuple-element.129), channel_id=1, source_target_pairs={{6,2},{7,3},{10,6},{11,7},{14,10},{15,11},{12,14},{13,15},{8,12},{... | collective-permute-start | bytes 1105928 | tf_op jit(solution)/shard_map/ppermute | solution.py:415
  102.6 10.4 %collective-permute-start.18 = (f32[160,512]{1,0:T(8,128)S(1)}, f32[160,512]{1,0:T(8,128)S(1)}, u32[]{:S(2)}, u32[]{:S(2)}) collective-permute-start(f32[160,512]{1,0:T(8,128)S(1)} %get-tuple-element.154.refs_2_), channel_id=1, source_target_pairs={{0,16},{16,0},{1,17},{17,1},{2,18},{18,2},{3,19},{19,3},{4,20},{20... | collective-permute-start | bytes 983048 | tf_op jit(solution)/shard_map/ppermute | solution.py:405
  104.1 12.1 %collective-permute-start.14 = (bf16[40,4992]{1,0:T(8,128)(2,1)S(1)}, bf16[40,4992]{1,0:T(8,128)(2,1)S(1)}, u32[]{:S(2)}, u32[]{:S(2)}) collective-permute-start(bf16[40,4992]{1,0:T(8,128)(2,1)S(1)} %get-tuple-element.126), channel_id=1, source_target_pairs={{2,6},{3,7},{6,10},{7,11},{10,14},{11,15},{14,12},{15,13},{12,8},{... | collective-permute-start | bytes 1198088 | tf_op jit(solution)/shard_map/ppermute | solution.py:415
  105.8 10.5 %collective-permute-start.15 = (bf16[40,4224]{1,0:T(8,128)(2,1)S(1)}, bf16[40,4224]{1,0:T(8,128)(2,1)S(1)}, u32[]{:S(2)}, u32[]{:S(2)}) collective-permute-start(bf16[40,4224]{1,0:T(8,128)(2,1)S(1)} %get-tuple-element.127), channel_id=1, source_target_pairs={{6,2},{7,3},{10,6},{11,7},{14,10},{15,11},{12,14},{13,15},{8,12},{... | collective-permute-start | bytes 1013768 | tf_op jit(solution)/shard_map/ppermute | solution.py:415
  113.5 2.8 %collective-permute-start.20 = (bf16[40,2560]{1,0:T(8,128)(2,1)S(1)}, bf16[40,2560]{1,0:T(8,128)(2,1)S(1)}, u32[]{:S(2)}, u32[]{:S(2)}) collective-permute-start(bf16[40,2560]{1,0:T(8,128)(2,1)S(1)} %get-tuple-element.146.refs_0_), channel_id=1, source_target_pairs={{2,3},{3,2},{6,7},{7,6},{10,11},{11,10},{14,15},{15,14},{12,13},{1... | collective-permute-start | bytes 614408 | tf_op jit(solution)/shard_map/ppermute | solution.py:412
  113.8 2.4 %collective-permute-start.21 = (bf16[40,2560]{1,0:T(8,128)(2,1)S(1)}, bf16[40,2560]{1,0:T(8,128)(2,1)S(1)}, u32[]{:S(2)}, u32[]{:S(2)}) collective-permute-start(bf16[40,2560]{1,0:T(8,128)(2,1)S(1)} %get-tuple-element.147.refs_1_), channel_id=1, source_target_pairs={{2,3},{3,2},{6,7},{7,6},{10,11},{11,10},{14,15},{15,14},{12,13},{1... | collective-permute-start | bytes 614408 | tf_op jit(solution)/shard_map/ppermute | solution.py:412
  116.3 2.7 %collective-permute-start.22 = (bf16[40,9216]{1,0:T(8,128)(2,1)S(1)}, bf16[40,9216]{1,0:T(8,128)(2,1)S(1)}, u32[]{:S(2)}, u32[]{:S(2)}) collective-permute-start(bf16[40,9216]{1,0:T(8,128)(2,1)S(1)} %columns.11.refs_1_), channel_id=1, source_target_pairs={{2,3},{3,2},{6,7},{7,6},{10,11},{11,10},{14,15},{15,14},{12,13},{1... | collective-permute-start | bytes 2211848 | tf_op jit(solution)/shard_map/ppermute | solution.py:412
  116.4 6.6 %collective-permute-start.23 = (f32[80,512]{1,0:T(8,128)S(1)}, f32[80,512]{1,0:T(8,128)S(1)}, u32[]{:S(2)}, u32[]{:S(2)}) collective-permute-start(f32[80,512]{1,0:T(8,128)S(1)} %project_last.3.refs_2_), channel_id=1, source_target_pairs={{0,16},{16,0},{1,17},{17,1},{2,18},{18,2},{3,19},{19,3},{4,20},{20... | collective-permute-start | bytes 491528 | tf_op jit(solution)/shard_map/ppermute | solution.py:405
  123.5 4.0 %collective-permute-start.24 = (f32[16,640]{1,0:T(8,128)S(1)}, f32[16,640]{1,0:T(8,128)S(1)}, u32[]{:S(2)}, u32[]{:S(2)}) collective-permute-start(f32[16,640]{1,0:T(8,128)S(1)} %score.7.refs_0_), channel_id=1, source_target_pairs={{0,16},{16,0},{1,17},{17,1},{2,18},{18,2},{3,19},{19,3},{4,20},{20... | collective-permute-start | bytes 122888 | tf_op jit(solution)/shard_map/ppermute | solution.py:405
  (1 other events, 1.7 us)

commit v9 on v7

--- a/solution.py
+++ b/solution.py
@@ -11,7 +11,7 @@
 RANK = 32
 WIDE = 256
 LIGHT = pl.CostEstimate(flops=1, bytes_accessed=1, transcendentals=0)
-ROOM = 6 << 20
+ROOM = 10 << 20
 
 
 def params():
@@ -230,7 +230,7 @@
 
 def project(arrays, span, factors, outs, start=None):
     width = sum(size for _, size, _, _ in span)
-    step = chunk_of(*(size for _, size, _, _ in span), most=3072)
+    step = chunk_of(*(size for _, size, _, _ in span), most=4608)
     shape = (sum(math.prod(a.shape[:-1]) for a in arrays), factors[0].shape[1])
     extra = [] if start is None else [start]
     shapes = [shape] * outs

time: 129 us -> 129 us (level)
  no operation moved by 1% of the time
where the time goes in v9:
time: 129 us; the launch traced here: 128 us
  Pallas kernels  40.2 us (31%)
  blocking collectives  39 us (30%)
  starting transfers between devices  26.3 us (20%)
  waiting for transfers between devices  22.5 us (17%)
    all_to_all x6, blocking collectives, both_cores(): return lax.all_to_all(x, 'query', 0, 0, axis_index_groups=sorted(ring))  39 us
    pallas_call x5, Pallas kernels, project(): pl.pallas_call(functools.partial(project_kernel, step, tuple(span), len(a...  16.6 us
    ppermute x8, starting transfers between devices, round_ring(): lax.ppermute(pair[0], 'query', forward)  14.9 us
    ppermute x8, waiting for transfers between devices, round_ring(): lax.ppermute(pair[1], 'query', backward)  11.1 us
    pallas_call x1, Pallas kernels, load(): pl.pallas_call(functools.partial(load_kernel, step), in_specs=[pl.BlockSp...  8.62 us
    ppermute x5, starting transfers between devices, across(): return [x, lax.ppermute(x, 'rows', [(0, 1), (1, 0)])]  7.52 us
    ppermute x8, waiting for transfers between devices, round_ring(): lax.ppermute(pair[0], 'query', forward)  7.49 us
    pallas_call x3, Pallas kernels, project_last(): pl.pallas_call(functools.partial(project_last_kernel, tuple(plan), (len(a...  4.36 us
  transfers between devices with their start and end apart: 26, of which 13 were waited for; matrix products, arithmetic and copies ran while one was open for 0% of the time, Pallas kernels for 30%

profile of v9, /device:TPU:0, one launch (start us, length us, event | category | flops | bytes accessed | tf_op | source)
XLA Modules:
  0.0 128.2 jit_solution(13633393618312426061)
XLA Ops:
  1.1 3.0 %collective-permute-start.2 = (bf16[40,9216]{1,0:T(8,128)(2,1)S(1)}, bf16[40,9216]{1,0:T(8,128)(2,1)S(1)}, u32[]{:S(2)}, u32[]{:S(2)}) collective-permute-start(bf16[40,9216]{1,0:T(8,128)(2,1)S(1)} %columns.6.refs_2_), channel_id=1, source_target_pairs={{2,6},{3,7},{6,10},{7,11},{10,14},{11,15},{14,12},{15,13},{12,8},{... | collective-permute-start | bytes 2211848 | tf_op jit(solution)/shard_map/ppermute | solution.py:415
  5.4 2.0 %collective-permute-start = (bf16[40,9216]{1,0:T(8,128)(2,1)S(1)}, bf16[40,9216]{1,0:T(8,128)(2,1)S(1)}, u32[]{:S(2)}, u32[]{:S(2)}) collective-permute-start(bf16[40,9216]{1,0:T(8,128)(2,1)S(1)} %columns.5.refs_2_), channel_id=1, source_target_pairs={{2,6},{3,7},{6,10},{7,11},{10,14},{11,15},{14,12},{15,13},{12,8},{... | collective-permute-start | bytes 2211848 | tf_op jit(solution)/shard_map/ppermute | solution.py:415
  7.5 8.6 %load_factors.1 = (bf16[14336,512]{1,0:T(8,128)(2,1)S(1)}, bf16[4096,512]{1,0:T(8,128)(2,1)S(1)}, f32[2,32,512]{2,1,0:T(8,128)S(1)}) custom-call(bf16[14336,512]{1,0:T(8,128)(2,1)} %a_ref.1, bf16[4096,512]{1,0:T(8,128)(2,1)} %b_ref.1), custom_call_target="tpu_custom_call" | custom-call | flops 1 | bytes 1 | tf_op jit(solution)/shard_map/load_factors/pallas_call | solution.py:136
  16.1 5.4 %collective-permute-done.2.refs_0_ = bf16[40,9216]{1,0:T(8,128)(2,1)S(1)} collective-permute-done((bf16[40,9216]{1,0:T(8,128)(2,1)S(1)}, bf16[40,9216]{1,0:T(8,128)(2,1)S(1)}, u32[]{:S(2)}, u32[]{:S(2)}) %collective-permute-start.2) | collective-permute-done | bytes 737312 | tf_op jit(solution)/shard_map/ppermute | solution.py:415
  21.5 2.0 %collective-permute-done.3.refs_1_ = bf16[40,9216]{1,0:T(8,128)(2,1)S(1)} collective-permute-done((bf16[40,9216]{1,0:T(8,128)(2,1)S(1)}, bf16[40,9216]{1,0:T(8,128)(2,1)S(1)}, u32[]{:S(2)}, u32[]{:S(2)}) %collective-permute-start.3) | collective-permute-done | bytes 737312 | tf_op jit(solution)/shard_map/ppermute | solution.py:415
  26.5 7.3 %all_to_all.30.refs_0_ = bf16[2,120,9216]{2,1,0:T(8,128)(2,1)S(1)} all-to-all(bf16[2,120,9216]{2,1,0:T(8,128)(2,1)S(1)} %pack.6), channel_id=1, replica_groups={{0,1},{2,3},{4,5},{6,7},{8,9},{10,11},{12,13},{14,15},{16,17},{18,19},{..., dimensions={0} | all-to-all | bytes 8847360 | tf_op jit(solution)/shard_map/all_to_all | solution.py:409
  33.7 4.4 %project.5 = (f32[240,512]{1,0:T(8,128)S(1)}, f32[240,512]{1,0:T(8,128)S(1)}) custom-call(bf16[2,120,9216]{2,1,0:T(8,128)(2,1)S(1)} %all_to_all.30.refs_0_, bf16[14336,512]{1,0:T(8,128)(2,1)S(1)} %get-tuple-element.87.refs_1_.refs_2_.refs_4_.refs_5_, bf16[4096,512]{1,0:T(8,128)(2,1)S(1)} %get-tuple-element.88.refs_2_.refs_3_.refs_5_.refs_6_), custom_call_target="tpu_custom_call" | custom-call | flops 1 | bytes 1 | tf_op jit(solution)/shard_map/project/pallas_call | solution.py:239
  43.8 7.3 %all_to_all.31.refs_0_ = bf16[2,120,9216]{2,1,0:T(8,128)(2,1)S(1)} all-to-all(bf16[2,120,9216]{2,1,0:T(8,128)(2,1)S(1)} %pack.7), channel_id=1, replica_groups={{0,1},{2,3},{4,5},{6,7},{8,9},{10,11},{12,13},{14,15},{16,17},{18,19},{..., dimensions={0} | all-to-all | bytes 8847360 | tf_op jit(solution)/shard_map/all_to_all | solution.py:409
  51.0 3.0 %project.6.refs_0_ = f32[240,512]{1,0:T(8,128)S(1)} custom-call(bf16[2,120,9216]{2,1,0:T(8,128)(2,1)S(1)} %all_to_all.31.refs_0_, bf16[14336,512]{1,0:T(8,128)(2,1)S(1)} %get-tuple-element.87.refs_1_.refs_2_.refs_4_.refs_5_, bf16[4096,512]{1,0:T(8,128)(2,1)S(1)} %get-tuple-element.88.refs_2_.refs_3_.refs_5_.refs_6_, f32[240,512]{1,0:T(8,128)S(1)} %get-tuple-element.94.refs_3_), custom_call_target="tpu_custom_call" | custom-call | flops 1 | bytes 1 | tf_op jit(solution)/shard_map/project/pallas_call | solution.py:239
  57.8 6.1 %all_to_all.32.refs_0_ = bf16[2,80,9216]{2,1,0:T(8,128)(2,1)S(1)} all-to-all(bf16[2,80,9216]{2,1,0:T(8,128)(2,1)S(1)} %pack.8), channel_id=1, replica_groups={{0,1},{2,3},{4,5},{6,7},{8,9},{10,11},{12,13},{14,15},{16,17},{18,19},{..., dimensions={0} | all-to-all | bytes 5898240 | tf_op jit(solution)/shard_map/all_to_all | solution.py:409
  63.9 3.6 %project.7 = (f32[160,512]{1,0:T(8,128)S(1)}, f32[224,512]{1,0:T(8,128)S(1)}) custom-call(bf16[2,80,9216]{2,1,0:T(8,128)(2,1)S(1)} %all_to_all.32.refs_0_, bf16[14336,512]{1,0:T(8,128)(2,1)S(1)} %get-tuple-element.87.refs_1_.refs_2_.refs_4_.refs_5_, bf16[4096,512]{1,0:T(8,128)(2,1)S(1)} %get-tuple-element.88.refs_2_.refs_3_.refs_5_.refs_6_, ...), custom_call_target="tpu_custom_call" | custom-call | flops 1 | bytes 1 | tf_op jit(solution)/shard_map/project/pallas_call | solution.py:239
  68.9 2.0 %collective-permute-done.5.refs_1_ = bf16[40,9216]{1,0:T(8,128)(2,1)S(1)} collective-permute-done((bf16[40,9216]{1,0:T(8,128)(2,1)S(1)}, bf16[40,9216]{1,0:T(8,128)(2,1)S(1)}, u32[]{:S(2)}, u32[]{:S(2)}) %collective-permute-start.5) | collective-permute-done | bytes 737312 | tf_op jit(solution)/shard_map/ppermute | solution.py:415
  71.0 1.9 %collective-permute-start.9 = (bf16[40,9216]{1,0:T(8,128)(2,1)S(1)}, bf16[40,9216]{1,0:T(8,128)(2,1)S(1)}, u32[]{:S(2)}, u32[]{:S(2)}) collective-permute-start(bf16[40,9216]{1,0:T(8,128)(2,1)S(1)} %collective-permute-done.4.refs_0_), channel_id=1, source_target_pairs={{2,6},{3,7},{6,10},{7,11},{10,14},{11,15},{14,12},{15,13},{12,8},{... | collective-permute-start | bytes 2211848 | tf_op jit(solution)/shard_map/ppermute | solution.py:415
  75.1 6.1 %all_to_all.33.refs_0_ = bf16[2,80,9216]{2,1,0:T(8,128)(2,1)S(1)} all-to-all(bf16[2,80,9216]{2,1,0:T(8,128)(2,1)S(1)} %pack.9), channel_id=1, replica_groups={{0,1},{2,3},{4,5},{6,7},{8,9},{10,11},{12,13},{14,15},{16,17},{18,19},{..., dimensions={0} | all-to-all | bytes 5898240 | tf_op jit(solution)/shard_map/all_to_all | solution.py:409
  81.2 2.1 %project.8.refs_1_ = f32[160,512]{1,0:T(8,128)S(1)} custom-call(bf16[2,80,9216]{2,1,0:T(8,128)(2,1)S(1)} %all_to_all.33.refs_0_, bf16[14336,512]{1,0:T(8,128)(2,1)S(1)} %get-tuple-element.87.refs_1_.refs_2_.refs_4_.refs_5_, bf16[4096,512]{1,0:T(8,128)(2,1)S(1)} %get-tuple-element.88.refs_2_.refs_3_.refs_5_.refs_6_, f32[160,512]{1,0:T(8,128)S(1)} %get-tuple-element.110.refs_3_), custom_call_target="tpu_custom_call" | custom-call | flops 1 | bytes 1 | tf_op jit(solution)/shard_map/project/pallas_call | solution.py:239
  84.7 2.0 %collective-permute-done.12.refs_1_ = bf16[40,9216]{1,0:T(8,128)(2,1)S(1)} collective-permute-done((bf16[40,9216]{1,0:T(8,128)(2,1)S(1)}, bf16[40,9216]{1,0:T(8,128)(2,1)S(1)}, u32[]{:S(2)}, u32[]{:S(2)}) %collective-permute-start.12) | collective-permute-done | bytes 737312 | tf_op jit(solution)/shard_map/ppermute | solution.py:415
  87.0 1.6 %collective-permute-start.16 = (bf16[40,4608]{1,0:T(8,128)(2,1)S(1)}, bf16[40,4608]{1,0:T(8,128)(2,1)S(1)}, u32[]{:S(2)}, u32[]{:S(2)}) collective-permute-start(bf16[40,4608]{1,0:T(8,128)(2,1)S(1)} %get-tuple-element.130), channel_id=1, source_target_pairs={{2,6},{3,7},{6,10},{7,11},{10,14},{11,15},{14,12},{15,13},{12,8},{... | collective-permute-start | bytes 1105928 | tf_op jit(solution)/shard_map/ppermute | solution.py:415
  89.7 6.1 %all_to_all.34.refs_0_ = bf16[2,80,9216]{2,1,0:T(8,128)(2,1)S(1)} all-to-all(bf16[2,80,9216]{2,1,0:T(8,128)(2,1)S(1)} %pack.10), channel_id=1, replica_groups={{0,1},{2,3},{4,5},{6,7},{8,9},{10,11},{12,13},{14,15},{16,17},{18,19},{..., dimensions={0} | all-to-all | bytes 5898240 | tf_op jit(solution)/shard_map/all_to_all | solution.py:409
  95.8 3.6 %project.9 = (f32[160,512]{1,0:T(8,128)S(1)}, f32[160,512]{1,0:T(8,128)S(1)}) custom-call(bf16[2,80,9216]{2,1,0:T(8,128)(2,1)S(1)} %all_to_all.34.refs_0_, bf16[14336,512]{1,0:T(8,128)(2,1)S(1)} %get-tuple-element.87.refs_1_.refs_2_.refs_4_.refs_5_, bf16[4096,512]{1,0:T(8,128)(2,1)S(1)} %get-tuple-element.88.refs_2_.refs_3_.refs_5_.refs_6_), custom_call_target="tpu_custom_call" | custom-call | flops 1 | bytes 1 | tf_op jit(solution)/shard_map/project/pallas_call | solution.py:239
  100.4 2.1 %collective-permute-done.10.refs_1_ = bf16[40,9216]{1,0:T(8,128)(2,1)S(1)} collective-permute-done((bf16[40,9216]{1,0:T(8,128)(2,1)S(1)}, bf16[40,9216]{1,0:T(8,128)(2,1)S(1)}, u32[]{:S(2)}, u32[]{:S(2)}) %collective-permute-start.10) | collective-permute-done | bytes 737312 | tf_op jit(solution)/shard_map/ppermute | solution.py:415
  104.1 1.6 %collective-permute-start.14 = (bf16[40,4992]{1,0:T(8,128)(2,1)S(1)}, bf16[40,4992]{1,0:T(8,128)(2,1)S(1)}, u32[]{:S(2)}, u32[]{:S(2)}) collective-permute-start(bf16[40,4992]{1,0:T(8,128)(2,1)S(1)} %get-tuple-element.128), channel_id=1, source_target_pairs={{2,6},{3,7},{6,10},{7,11},{10,14},{11,15},{14,12},{15,13},{12,8},{... | collective-permute-start | bytes 1198088 | tf_op jit(solution)/shard_map/ppermute | solution.py:415
  106.9 6.1 %all_to_all.35.refs_0_ = bf16[2,80,9216]{2,1,0:T(8,128)(2,1)S(1)} all-to-all(bf16[2,80,9216]{2,1,0:T(8,128)(2,1)S(1)} %pack.11), channel_id=1, replica_groups={{0,1},{2,3},{4,5},{6,7},{8,9},{10,11},{12,13},{14,15},{16,17},{18,19},{..., dimensions={0} | all-to-all | bytes 5898240 | tf_op jit(solution)/shard_map/all_to_all | solution.py:409
  119.4 2.5 %project_last.5.refs_1_ = f32[240,512]{1,0:T(8,128)S(1)} custom-call(bf16[2,80,9216]{2,1,0:T(8,128)(2,1)S(1)} %all_to_all.35.refs_0_, bf16[40,4992]{1,0:T(8,128)(2,1)S(1)} %collective-permute-done.14.refs_1_, bf16[40,4224]{1,0:T(8,128)(2,1)S(1)} %collective-permute-done.15.refs_2_, bf16[40,4992]{1,0:T(8,128)(2,1)S(1)} %collective-permute-done.22.refs_3_, ...), custom_call_target="tpu_custom_call" | custom-call | flops 1 | bytes 1 | tf_op jit(solution)/shard_map/project_last/pallas_call | solution.py:294
  125.0 2.5 %collective-permute-done.25.refs_1_ = f32[16,640]{1,0:T(8,128)S(1)} collective-permute-done((f32[16,640]{1,0:T(8,128)S(1)}, f32[16,640]{1,0:T(8,128)S(1)}, u32[]{:S(2)}, u32[]{:S(2)}) %collective-permute-start.25) | collective-permute-done | bytes 40992 | tf_op jit(solution)/shard_map/ppermute | solution.py:405
  (60 shorter events, 35.0 us)
Async XLA Ops:
  1.1 20.4 %collective-permute-start.2 = (bf16[40,9216]{1,0:T(8,128)(2,1)S(1)}, bf16[40,9216]{1,0:T(8,128)(2,1)S(1)}, u32[]{:S(2)}, u32[]{:S(2)}) collective-permute-start(bf16[40,9216]{1,0:T(8,128)(2,1)S(1)} %columns.6.refs_2_), channel_id=1, source_target_pairs={{2,6},{3,7},{6,10},{7,11},{10,14},{11,15},{14,12},{15,13},{12,8},{... | collective-permute-start | bytes 2211848 | tf_op jit(solution)/shard_map/ppermute | solution.py:415
  4.1 19.4 %collective-permute-start.3 = (bf16[40,9216]{1,0:T(8,128)(2,1)S(1)}, bf16[40,9216]{1,0:T(8,128)(2,1)S(1)}, u32[]{:S(2)}, u32[]{:S(2)}) collective-permute-start(bf16[40,9216]{1,0:T(8,128)(2,1)S(1)} %columns.6.refs_2_), channel_id=1, source_target_pairs={{6,2},{7,3},{10,6},{11,7},{14,10},{15,11},{12,14},{13,15},{8,12},{... | collective-permute-start | bytes 2211848 | tf_op jit(solution)/shard_map/ppermute | solution.py:415
  5.4 32.7 %collective-permute-start = (bf16[40,9216]{1,0:T(8,128)(2,1)S(1)}, bf16[40,9216]{1,0:T(8,128)(2,1)S(1)}, u32[]{:S(2)}, u32[]{:S(2)}) collective-permute-start(bf16[40,9216]{1,0:T(8,128)(2,1)S(1)} %columns.5.refs_2_), channel_id=1, source_target_pairs={{2,6},{3,7},{6,10},{7,11},{10,14},{11,15},{14,12},{15,13},{12,8},{... | collective-permute-start | bytes 2211848 | tf_op jit(solution)/shard_map/ppermute | solution.py:415
  7.4 32.0 %collective-permute-start.1 = (bf16[40,9216]{1,0:T(8,128)(2,1)S(1)}, bf16[40,9216]{1,0:T(8,128)(2,1)S(1)}, u32[]{:S(2)}, u32[]{:S(2)}) collective-permute-start(bf16[40,9216]{1,0:T(8,128)(2,1)S(1)} %columns.5.refs_2_), channel_id=1, source_target_pairs={{6,2},{7,3},{10,6},{11,7},{14,10},{15,11},{12,14},{13,15},{8,12},{... | collective-permute-start | bytes 2211848 | tf_op jit(solution)/shard_map/ppermute | solution.py:415
  23.6 30.5 %collective-permute-start.6 = (bf16[40,9216]{1,0:T(8,128)(2,1)S(1)}, bf16[40,9216]{1,0:T(8,128)(2,1)S(1)}, u32[]{:S(2)}, u32[]{:S(2)}) collective-permute-start(bf16[40,9216]{1,0:T(8,128)(2,1)S(1)} %collective-permute-done.2.refs_0_), channel_id=1, source_target_pairs={{2,6},{3,7},{6,10},{7,11},{10,14},{11,15},{14,12},{15,13},{12,8},{... | collective-permute-start | bytes 2211848 | tf_op jit(solution)/shard_map/ppermute | solution.py:415
  25.1 30.0 %collective-permute-start.7 = (bf16[40,9216]{1,0:T(8,128)(2,1)S(1)}, bf16[40,9216]{1,0:T(8,128)(2,1)S(1)}, u32[]{:S(2)}, u32[]{:S(2)}) collective-permute-start(bf16[40,9216]{1,0:T(8,128)(2,1)S(1)} %collective-permute-done.3.refs_1_), channel_id=1, source_target_pairs={{6,2},{7,3},{10,6},{11,7},{14,10},{15,11},{12,14},{13,15},{8,12},{... | collective-permute-start | bytes 2211848 | tf_op jit(solution)/shard_map/ppermute | solution.py:415
  39.4 29.6 %collective-permute-start.4 = (bf16[40,9216]{1,0:T(8,128)(2,1)S(1)}, bf16[40,9216]{1,0:T(8,128)(2,1)S(1)}, u32[]{:S(2)}, u32[]{:S(2)}) collective-permute-start(bf16[40,9216]{1,0:T(8,128)(2,1)S(1)} %collective-permute-done.refs_0_), channel_id=1, source_target_pairs={{2,6},{3,7},{6,10},{7,11},{10,14},{11,15},{14,12},{15,13},{12,8},{... | collective-permute-start | bytes 2211848 | tf_op jit(solution)/shard_map/ppermute | solution.py:415
  40.9 30.0 %collective-permute-start.5 = (bf16[40,9216]{1,0:T(8,128)(2,1)S(1)}, bf16[40,9216]{1,0:T(8,128)(2,1)S(1)}, u32[]{:S(2)}, u32[]{:S(2)}) collective-permute-start(bf16[40,9216]{1,0:T(8,128)(2,1)S(1)} %collective-permute-done.1.refs_1_), channel_id=1, source_target_pairs={{6,2},{7,3},{10,6},{11,7},{14,10},{15,11},{12,14},{13,15},{8,12},{... | collective-permute-start | bytes 2211848 | tf_op jit(solution)/shard_map/ppermute | solution.py:415
  41.4 12.6 %collective-permute-start.8 = (f32[240,512]{1,0:T(8,128)S(1)}, f32[240,512]{1,0:T(8,128)S(1)}, u32[]{:S(2)}, u32[]{:S(2)}) collective-permute-start(f32[240,512]{1,0:T(8,128)S(1)} %get-tuple-element.106.refs_1_), channel_id=1, source_target_pairs={{0,16},{16,0},{1,17},{17,1},{2,18},{18,2},{3,19},{19,3},{4,20},{20... | collective-permute-start | bytes 1474568 | tf_op jit(solution)/shard_map/ppermute | solution.py:405
  55.2 29.6 %collective-permute-start.11 = (bf16[40,9216]{1,0:T(8,128)(2,1)S(1)}, bf16[40,9216]{1,0:T(8,128)(2,1)S(1)}, u32[]{:S(2)}, u32[]{:S(2)}) collective-permute-start(bf16[40,9216]{1,0:T(8,128)(2,1)S(1)} %collective-permute-done.6.refs_0_), channel_id=1, source_target_pairs={{2,6},{3,7},{6,10},{7,11},{10,14},{11,15},{14,12},{15,13},{12,8},{... | collective-permute-start | bytes 2211848 | tf_op jit(solution)/shard_map/ppermute | solution.py:415
  56.7 30.0 %collective-permute-start.12 = (bf16[40,9216]{1,0:T(8,128)(2,1)S(1)}, bf16[40,9216]{1,0:T(8,128)(2,1)S(1)}, u32[]{:S(2)}, u32[]{:S(2)}) collective-permute-start(bf16[40,9216]{1,0:T(8,128)(2,1)S(1)} %collective-permute-done.7.refs_1_), channel_id=1, source_target_pairs={{6,2},{7,3},{10,6},{11,7},{14,10},{15,11},{12,14},{13,15},{8,12},{... | collective-permute-start | bytes 2211848 | tf_op jit(solution)/shard_map/ppermute | solution.py:415
  71.0 31.6 %collective-permute-start.10 = (bf16[40,9216]{1,0:T(8,128)(2,1)S(1)}, bf16[40,9216]{1,0:T(8,128)(2,1)S(1)}, u32[]{:S(2)}, u32[]{:S(2)}) collective-permute-start(bf16[40,9216]{1,0:T(8,128)(2,1)S(1)} %collective-permute-done.5.refs_1_), channel_id=1, source_target_pairs={{6,2},{7,3},{10,6},{11,7},{14,10},{15,11},{12,14},{13,15},{8,12},{... | collective-permute-start | bytes 2211848 | tf_op jit(solution)/shard_map/ppermute | solution.py:415
  71.0 31.5 %collective-permute-start.9 = (bf16[40,9216]{1,0:T(8,128)(2,1)S(1)}, bf16[40,9216]{1,0:T(8,128)(2,1)S(1)}, u32[]{:S(2)}, u32[]{:S(2)}) collective-permute-start(bf16[40,9216]{1,0:T(8,128)(2,1)S(1)} %collective-permute-done.4.refs_0_), channel_id=1, source_target_pairs={{2,6},{3,7},{6,10},{7,11},{10,14},{11,15},{14,12},{15,13},{12,8},{... | collective-permute-start | bytes 2211848 | tf_op jit(solution)/shard_map/ppermute | solution.py:415
  73.0 10.4 %collective-permute-start.13 = (f32[224,512]{1,0:T(8,128)S(1)}, f32[224,512]{1,0:T(8,128)S(1)}, u32[]{:S(2)}, u32[]{:S(2)}) collective-permute-start(f32[224,512]{1,0:T(8,128)S(1)} %get-tuple-element.124.refs_2_.refs_0_), channel_id=1, source_target_pairs={{0,16},{16,0},{1,17},{17,1},{2,18},{18,2},{3,19},{19,3},{4,20},{20... | collective-permute-start | bytes 1376264 | tf_op jit(solution)/shard_map/ppermute | solution.py:405
  87.0 26.0 %collective-permute-start.16 = (bf16[40,4608]{1,0:T(8,128)(2,1)S(1)}, bf16[40,4608]{1,0:T(8,128)(2,1)S(1)}, u32[]{:S(2)}, u32[]{:S(2)}) collective-permute-start(bf16[40,4608]{1,0:T(8,128)(2,1)S(1)} %get-tuple-element.130), channel_id=1, source_target_pairs={{2,6},{3,7},{6,10},{7,11},{10,14},{11,15},{14,12},{15,13},{12,8},{... | collective-permute-start | bytes 1105928 | tf_op jit(solution)/shard_map/ppermute | solution.py:415
  88.6 24.4 %collective-permute-start.17 = (bf16[40,4608]{1,0:T(8,128)(2,1)S(1)}, bf16[40,4608]{1,0:T(8,128)(2,1)S(1)}, u32[]{:S(2)}, u32[]{:S(2)}) collective-permute-start(bf16[40,4608]{1,0:T(8,128)(2,1)S(1)} %get-tuple-element.131), channel_id=1, source_target_pairs={{6,2},{7,3},{10,6},{11,7},{14,10},{15,11},{12,14},{13,15},{8,12},{... | collective-permute-start | bytes 1105928 | tf_op jit(solution)/shard_map/ppermute | solution.py:415
  102.6 10.4 %collective-permute-start.18 = (f32[160,512]{1,0:T(8,128)S(1)}, f32[160,512]{1,0:T(8,128)S(1)}, u32[]{:S(2)}, u32[]{:S(2)}) collective-permute-start(f32[160,512]{1,0:T(8,128)S(1)} %get-tuple-element.158.refs_2_), channel_id=1, source_target_pairs={{0,16},{16,0},{1,17},{17,1},{2,18},{18,2},{3,19},{19,3},{4,20},{20... | collective-permute-start | bytes 983048 | tf_op jit(solution)/shard_map/ppermute | solution.py:405
  104.1 12.1 %collective-permute-start.14 = (bf16[40,4992]{1,0:T(8,128)(2,1)S(1)}, bf16[40,4992]{1,0:T(8,128)(2,1)S(1)}, u32[]{:S(2)}, u32[]{:S(2)}) collective-permute-start(bf16[40,4992]{1,0:T(8,128)(2,1)S(1)} %get-tuple-element.128), channel_id=1, source_target_pairs={{2,6},{3,7},{6,10},{7,11},{10,14},{11,15},{14,12},{15,13},{12,8},{... | collective-permute-start | bytes 1198088 | tf_op jit(solution)/shard_map/ppermute | solution.py:415
  105.8 10.5 %collective-permute-start.15 = (bf16[40,4224]{1,0:T(8,128)(2,1)S(1)}, bf16[40,4224]{1,0:T(8,128)(2,1)S(1)}, u32[]{:S(2)}, u32[]{:S(2)}) collective-permute-start(bf16[40,4224]{1,0:T(8,128)(2,1)S(1)} %get-tuple-element.129), channel_id=1, source_target_pairs={{6,2},{7,3},{10,6},{11,7},{14,10},{15,11},{12,14},{13,15},{8,12},{... | collective-permute-start | bytes 1013768 | tf_op jit(solution)/shard_map/ppermute | solution.py:415
  113.5 2.8 %collective-permute-start.20 = (bf16[40,2560]{1,0:T(8,128)(2,1)S(1)}, bf16[40,2560]{1,0:T(8,128)(2,1)S(1)}, u32[]{:S(2)}, u32[]{:S(2)}) collective-permute-start(bf16[40,2560]{1,0:T(8,128)(2,1)S(1)} %get-tuple-element.148.refs_0_), channel_id=1, source_target_pairs={{2,3},{3,2},{6,7},{7,6},{10,11},{11,10},{14,15},{15,14},{12,13},{1... | collective-permute-start | bytes 614408 | tf_op jit(solution)/shard_map/ppermute | solution.py:412
  116.2 3.1 %collective-permute-start.22 = (bf16[40,4992]{1,0:T(8,128)(2,1)S(1)}, bf16[40,4992]{1,0:T(8,128)(2,1)S(1)}, u32[]{:S(2)}, u32[]{:S(2)}) collective-permute-start(bf16[40,4992]{1,0:T(8,128)(2,1)S(1)} %collective-permute-done.14.refs_1_), channel_id=1, source_target_pairs={{2,3},{3,2},{6,7},{7,6},{10,11},{11,10},{14,15},{15,14},{12,13},{1... | collective-permute-start | bytes 1198088 | tf_op jit(solution)/shard_map/ppermute | solution.py:412
  116.3 3.0 %collective-permute-start.23 = (bf16[40,4224]{1,0:T(8,128)(2,1)S(1)}, bf16[40,4224]{1,0:T(8,128)(2,1)S(1)}, u32[]{:S(2)}, u32[]{:S(2)}) collective-permute-start(bf16[40,4224]{1,0:T(8,128)(2,1)S(1)} %collective-permute-done.15.refs_2_), channel_id=1, source_target_pairs={{2,3},{3,2},{6,7},{7,6},{10,11},{11,10},{14,15},{15,14},{12,13},{1... | collective-permute-start | bytes 1013768 | tf_op jit(solution)/shard_map/ppermute | solution.py:412
  116.8 6.2 %collective-permute-start.24 = (f32[80,512]{1,0:T(8,128)S(1)}, f32[80,512]{1,0:T(8,128)S(1)}, u32[]{:S(2)}, u32[]{:S(2)}) collective-permute-start(f32[80,512]{1,0:T(8,128)S(1)} %project_last.3.refs_2_), channel_id=1, source_target_pairs={{0,16},{16,0},{1,17},{17,1},{2,18},{18,2},{3,19},{19,3},{4,20},{20... | collective-permute-start | bytes 491528 | tf_op jit(solution)/shard_map/ppermute | solution.py:405
  123.4 4.0 %collective-permute-start.25 = (f32[16,640]{1,0:T(8,128)S(1)}, f32[16,640]{1,0:T(8,128)S(1)}, u32[]{:S(2)}, u32[]{:S(2)}) collective-permute-start(f32[16,640]{1,0:T(8,128)S(1)} %score.7.refs_0_), channel_id=1, source_target_pairs={{0,16},{16,0},{1,17},{17,1},{2,18},{18,2},{3,19},{19,3},{4,20},{20... | collective-permute-start | bytes 122888 | tf_op jit(solution)/shard_map/ppermute | solution.py:405
  (2 other events, 4.1 us)
